TPU v7x, 256 devices: a whole 4x4x8 slice. The times are simulated.
256 devices in a mesh: dp: 32 (over z, x), tensor: 8 (over y, core).
Axes of the slice: x: 4, y: 4, z: 8, core: 2. Of those that a mesh axis runs over, the one named last changes fastest.
Arguments:
- normed_input_rows: bfloat16 [16384, 8192], P('dp', 'tensor'), may hold values from -6 to 6
- key_value_cotangent: bfloat16 [16384, 2, 1024], P('dp', None, 'tensor'), may hold values from -24 to 24
- key_value_weight: bfloat16 [2, 8192, 1024], P(None, None, 'tensor'), may hold values from -0.0625 to 0.0625
- adapter_down_factors: bfloat16 [512, 8192], P('dp', 'tensor'), may hold values from -0.0625 to 0.0625
- adapter_up_factors: bfloat16 [512, 1024], P('dp', 'tensor'), may hold values from -0.1875 to 0.1875
- slot_adapter: int32 [8], replicated, may hold values from 0 to 7, each once
- adapter_of_block: int32 [128], P('dp'), may hold values from 0 to 7, as said below
- live_rows_of_block: int32 [128], P('dp'), may hold values from 16 to 128
- prompt_of_block: int32 [128], P('dp'), may hold values from 0 to 15, as said below
- reward_of_block: float32 [128], P('dp'), may hold values from 0 to 4
Outputs:
- input_gradient: bfloat16 [16384, 8192], P('dp', 'tensor')
- grad_a: float32 [512, 8192], P('dp', 'tensor')
- grad_b: float32 [512, 1024], P('dp', 'tensor')
Inputs may be any that keep to these rules, and one draw needn't show every extreme that they name: `slot_adapter`: each adapter appears once. `adapter_of_block`: among the blocks of one index of dp an adapter repeats only after all 8 have appeared. `prompt_of_block`: each prompt has exactly 8 blocks.
All inputs are finite; a program needn't handle non-finite values.
Results may differ from a plain program's by a relative error of at most 0.0051.
Values may be sent and summed in bfloat16 or wider, within the bound.
No kernel may reach another device: no remote copies, remote signals or barrier semaphores. Data moves between devices by JAX's collectives and lax.ppermute only.
A program may use at most 128 MiB of HBM per device.

v0:
```python
import jax
import jax.numpy as jnp
from jax import lax
from jax.sharding import PartitionSpec as P

BLOCK = 128
GSIZE = 8


lowrank_multiplier = 2.0


def shards(
    normed_input_rows,
    key_value_cotangent,
    key_value_weight,
    adapter_down_factors,
    adapter_up_factors,
    slot_adapter,
    adapter_of_block,
    live_rows_of_block,
    prompt_of_block,
    reward_of_block,
):
    block_count = adapter_of_block.shape[0]
    row_total = normed_input_rows.shape[0]
    width_window = normed_input_rows.shape[1]
    column_count = key_value_cotangent.shape[2]
    adapter_count = slot_adapter.shape[0]
    group_count = block_count * lax.axis_size("dp") // GSIZE
    member = (prompt_of_block[:, None] == jnp.arange(group_count, dtype=jnp.int32)[None, :]).astype(
        jnp.float32
    )
    totals, squares = lax.psum(
        (
            jnp.sum(member * reward_of_block[:, None], axis=0),
            jnp.sum(member * (reward_of_block * reward_of_block)[:, None], axis=0),
        ),
        "dp",
    )
    mean_g = totals / GSIZE
    spread_g = jnp.sqrt(jnp.maximum(squares / GSIZE - mean_g * mean_g, 1.0))
    segment_average = jnp.sum(member * mean_g[None, :], axis=1)
    spread_blk = jnp.sum(member * spread_g[None, :], axis=1)
    advantage = (reward_of_block - segment_average) / spread_blk
    live_mask = jnp.arange(BLOCK, dtype=jnp.int32)[None, :] < live_rows_of_block[:, None]
    coef = jnp.where(live_mask, -advantage[:, None] / GSIZE, 0.0)
    weighted = (
        key_value_cotangent.reshape(block_count, BLOCK, 2, column_count).astype(jnp.float32)
        * coef[:, :, None, None]
    ).astype(jnp.bfloat16)
    value_cotangent = weighted[:, :, 1, :]
    a_flat, b_flat = (
        lax.all_gather(adapter_down_factors, "dp", axis=0, tiled=True),
        lax.all_gather(adapter_up_factors, "dp", axis=0, tiled=True),
    )
    rank_width = a_flat.shape[0] // adapter_count
    a_every = a_flat.reshape(adapter_count, rank_width, width_window)
    b_every = b_flat.reshape(adapter_count, rank_width, column_count)
    selected_member = (slot_adapter[None, :] == adapter_of_block[:, None]).astype(jnp.bfloat16)
    segment_shrink_matrix = jnp.einsum(
        "ba,ard->brd", selected_member, a_every, preferred_element_type=jnp.float32
    ).astype(jnp.bfloat16)
    b_block = jnp.einsum(
        "ba,arc->brc", selected_member, b_every, preferred_element_type=jnp.float32
    ).astype(jnp.bfloat16)
    block_input_rows = normed_input_rows.reshape(block_count, BLOCK, width_window)
    low_terms = jnp.concatenate(
        [
            jnp.einsum(
                "xqg,xlg->xql",
                block_input_rows,
                segment_shrink_matrix,
                preferred_element_type=jnp.float32,
            ),
            jnp.einsum(
                "bkc,brc->bkr", value_cotangent, b_block, preferred_element_type=jnp.float32
            ),
        ],
        axis=2,
    )
    low_sums = lax.psum(low_terms, "tensor")
    rank_hidden = low_sums[:, :, :rank_width].astype(jnp.bfloat16)
    narrow_derivative = low_sums[:, :, rank_width:].astype(jnp.bfloat16)
    weighted_flat = weighted.reshape(row_total, 2, column_count)
    partial_terms = jnp.einsum(
        "tjc,jdc->td", weighted_flat, key_value_weight, preferred_element_type=jnp.float32
    )
    frozen_term = lax.psum_scatter(partial_terms, "tensor", scatter_dimension=1, tiled=True)
    correction_summand = lowrank_multiplier * jnp.einsum(
        "dbq,dqz->dbz", narrow_derivative, segment_shrink_matrix, preferred_element_type=jnp.float32
    )
    input_gradient = (frozen_term + correction_summand.reshape(row_total, width_window)).astype(
        jnp.bfloat16
    )
    block_down_gradient = lowrank_multiplier * jnp.einsum(
        "veg,vei->vgi", narrow_derivative, block_input_rows, preferred_element_type=jnp.float32
    )
    segment_lift_derivative = lowrank_multiplier * jnp.einsum(
        "sqn,sqx->snx", rank_hidden, value_cotangent, preferred_element_type=jnp.float32
    )
    chosen_wide = selected_member.astype(jnp.float32)
    owner_terms_a = jnp.einsum(
        "ba,brd->ard", chosen_wide, block_down_gradient, precision=lax.Precision.HIGHEST
    ).reshape(adapter_count * rank_width, width_window)
    owner_terms_b = jnp.einsum(
        "ba,brc->arc", chosen_wide, segment_lift_derivative, precision=lax.Precision.HIGHEST
    ).reshape(adapter_count * rank_width, column_count)
    grad_a, grad_b = (
        lax.psum_scatter(owner_terms_a, "dp", scatter_dimension=0, tiled=True),
        lax.psum_scatter(owner_terms_b, "dp", scatter_dimension=0, tiled=True),
    )
    return (input_gradient, grad_a, grad_b)


def solution(mesh):
    in_specs = (
        P("dp", "tensor"),
        P("dp", None, "tensor"),
        P(None, None, "tensor"),
        P("dp", "tensor"),
        P("dp", "tensor"),
        P(),
        P("dp"),
        P("dp"),
        P("dp"),
        P("dp"),
    )
    out_specs = (P("dp", "tensor"), P("dp", "tensor"), P("dp", "tensor"))
    return jax.shard_map(shards, mesh=mesh, in_specs=in_specs, out_specs=out_specs, check_vma=False)
```

profile of v0, /device:TPU:1, one launch (start us, length us, event | category | flops | bytes accessed | tf_op | source)
XLA Modules:
  0.0 633.9 jit_solution(7735193744007907350)
XLA Ops:
  8.0 0.0 copy-start
  8.0 0.0 all-gather.2.cloned.1.call-start
  8.1 0.7 all-gather.2.cloned.1.call-update
  8.7 0.0 reduce-scatter.4.cloned.1.call-start
  8.8 0.7 mul.73
  9.5 0.8 select_reduce_fusion.3
  10.3 64.4 %all-reduce = (f32[16]{0:T(128)S(1)}, f32[16]{0:T(128)S(1)}) all-reduce(f32[16]{0:T(128)S(1)} %get-tuple-element.5, f32[16]{0:T(128)S(1)} %get-tuple-element.6), channel_id=1, replica_groups=mesh['dp'=32,'tensor'=8] {'dp'}, use_global_device_ids=true, to_apply=%region_1.0 | all-reduce | flops 32 | bytes 256 | tf_op jit(solution)/shard_map/psum | solution.py:34
  74.7 0.9 select_reduce_fusion.2
  75.6 0.7 negate_multiply_fusion
  76.3 0.7 fusion.19
  77.0 2.4 multiply_convert_fusion
  79.4 10.3 %convolution_bitcast_fusion = f32[512,8192]{1,0:T(8,128)} fusion(bf16[2,8192,128]{2,1,0:T(8,128)(2,1)} %param.12, bf16[512,2,128]{2,1,0:T(2,128)(2,1)S(1)} %multiply_convert_fusion), kind=kOutput, calls=%fused_computation | convolution fusion | flops 2147483648 | bytes 21233664 | tf_op jit(solution)/shard_map/tjc,jdc->td/dot_general | solution.py:86
  89.7 0.0 copy-start.2
  89.7 0.0 copy-start.5
  89.7 0.0 copy-start.3
  89.7 0.0 copy-start.4
  89.7 0.0 reduce-scatter.4.cloned.1.call-update
  89.7 0.0 reduce-scatter.8.cloned.1.call-start
  89.8 0.9 copy-done.2
  90.7 0.0 copy-done.5
  90.7 31.3 %all_gather.7 = bf16[512,128]{1,0:T(8,128)(2,1)S(1)} all-gather(bf16[16,128]{1,0:T(8,128)(2,1)S(1)} %copy-done.5), channel_id=1, replica_groups=mesh['dp'=32,'tensor'=8] {'dp'}, dimensions={0}, use_global_device_ids=true | all-gather | bytes 135168 | tf_op jit(solution)/shard_map/all_gather | solution.py:55
  122.0 0.0 copy-done.3
  122.0 0.0 copy-done.4
  122.0 0.2 convolution_convert_fusion.1
  122.2 0.3 fusion.13
  122.5 0.0 all-gather.2.cloned.1.call-done
  122.5 2.0 convolution_convert_fusion
  124.5 0.0 copy-done
  124.5 0.0 copy-start.1
  124.5 0.8 copy-done.1
  125.3 0.5 convolution_bitcast_fusion.1
  125.8 50.2 %all-reduce.2 = bf16[4,128,128]{1,2,0:T(8,128)(2,1)S(1)} all-reduce(f32[4,128,128]{1,2,0:T(8,128)S(1)} %pad_maximum_fusion), channel_id=1, replica_groups=mesh['dp'=32,'tensor'=8] {'tensor'}, use_global_device_ids=true, to_apply=%region_7.8 | all-reduce | flops 65536 | bytes 393216 | tf_op jit(solution)/shard_map/psum | solution.py:82
  176.1 0.3 convolution_multiply_fusion.2
  176.3 0.4 fusion.9
  176.7 0.7 copy.44
  177.5 0.0 reduce-scatter.8.cloned.1.call-update
  177.5 0.0 reduce-scatter.6.cloned.1.call-start
  177.6 0.3 convolution_multiply_fusion.1
  177.9 1.9 fusion.1
  179.8 2.5 copy.42
  182.3 0.0 reduce-scatter.6.cloned.1.call-update
  182.3 1.6 convolution_multiply_fusion
  183.9 11.0 %reduce-scatter.4.cloned.1.call-done = f32[512,1024]{1,0:T(8,128)} async-done(((f32[512,8192]{1,0:T(8,128)}), f32[512,1024]{1,0:T(8,128)}) %reduce-scatter.4.cloned.1.call-update) | async-done | bytes 2097168 | tf_op jit(solution)/shard_map/reduce_scatter | solution.py:89
  194.9 2.9 fusion
  197.7 209.1 %reduce-scatter.8.cloned.1.call-done = f32[16,128]{1,0:T(8,128)} async-done(((f32[512,128]{1,0:T(8,128)}), f32[16,128]{1,0:T(8,128)}) %reduce-scatter.8.cloned.1.call-update) | async-done | bytes 8208 | tf_op jit(solution)/shard_map/reduce_scatter | solution.py:111
  406.8 219.5 %reduce-scatter.6.cloned.1.call-done = f32[16,1024]{1,0:T(8,128)} async-done(((f32[512,1024]{1,0:T(8,128)}), f32[16,1024]{1,0:T(8,128)}) %reduce-scatter.6.cloned.1.call-update) | async-done | bytes 65552 | tf_op jit(solution)/shard_map/reduce_scatter | solution.py:110
  (3 shorter events, 0.1 us)
Async XLA Ops:
  8.0 116.5 %copy-start = (bf16[512,1024]{1,0:T(8,128)(2,1)S(1)}, bf16[512,1024]{1,0:T(8,128)(2,1)}, u32[]{:S(2)}) copy-start(bf16[512,1024]{1,0:T(8,128)(2,1)} %param.10) | copy-start | bytes 3145732
  8.0 114.5 %all-gather.2.cloned.1.call-start = ((), (), s32[]{:S(2)}) async-start(), calls=%async_computation.4 | async-start | bytes 1081344 | tf_op jit(solution)/shard_map/all_gather | solution.py:54
  8.7 186.1 %reduce-scatter.4.cloned.1.call-start = ((), (), s32[]{:S(2)}) async-start(), calls=%async_computation.3 | async-start | bytes 18874368 | tf_op jit(solution)/shard_map/reduce_scatter | solution.py:89
  89.7 0.9 copy-start.2
  89.7 1.0 copy-start.5
  89.7 32.3 %copy-start.3 = (s32[8]{0:T(128)S(1)}, s32[8]{0:T(128)}, u32[]{:S(2)}) copy-start(s32[8]{0:T(128)} %param.15) | copy-start | bytes 100
  89.7 32.3 %copy-start.4 = (s32[4]{0:T(128)S(1)}, s32[4]{0:T(128)}, u32[]{:S(2)}) copy-start(s32[4]{0:T(128)} %param.16) | copy-start | bytes 52
  89.7 317.0 %reduce-scatter.8.cloned.1.call-start = ((), (), s32[]{:S(2)}) async-start(), calls=%async_computation.6 | async-start | bytes 270336 | tf_op jit(solution)/shard_map/reduce_scatter | solution.py:111
  124.5 0.8 copy-start.1
  177.5 448.8 %reduce-scatter.6.cloned.1.call-start = ((), (), s32[]{:S(2)}) async-start(), calls=%async_computation.5 | async-start | bytes 2162688 | tf_op jit(solution)/shard_map/reduce_scatter | solution.py:110
Sparse Core Ops, SparseCore 0:
  11.4 75.6 all-gather.1
Sparse Core Ops, SparseCore 1:
  89.8 105.0 reduce-scatter.3
  199.1 207.6 reduce-scatter.7
  411.6 214.7 reduce-scatter.5
where the time goes:
time: 639 us; the launch traced here: 634 us
  waiting for transfers between devices  440 us (69%)
  blocking collectives  146 us (23%)
  matrix products  17.7 us (3%)
  between operations  15.8 us (2%)
  other arithmetic  9.05 us (1%)
    reduce_scatter x1, waiting for transfers between devices, shards(): lax.psum_scatter(owner_terms_a, 'dp', scatter_dimension=0, tiled=True)  220 us
    reduce_scatter x1, waiting for transfers between devices, shards(): lax.psum_scatter(owner_terms_b, 'dp', scatter_dimension=0, tiled=True)  209 us
    psum x1, blocking collectives, shards(): lax.psum((jnp.sum(member * reward_of_block[:, None], axis=0), jnp.sum(mem...  64.4 us
    psum x1, blocking collectives, shards(): low_sums = lax.psum(low_terms, 'tensor')  50.2 us
    all_gather x1, blocking collectives, shards(): lax.all_gather(adapter_up_factors, 'dp', axis=0, tiled=True)  31.3 us
  transfers between devices with their start and end apart: 4, of which 3 were waited for; matrix products, arithmetic and copies ran while one was open for 5% of the time, Pallas kernels for 0%

commit v1 on v0

v1 whole, which is shorter than its diff:
```python
import jax
import jax.numpy as jnp
from jax import lax
from jax.sharding import PartitionSpec as P

BLOCK = 128
GSIZE = 8
GROUPS = 16
SLOTS = 8
RANK = 64
LOWRANK_MULTIPLIER = 2.0
BF = jnp.bfloat16
F32 = jnp.float32


def tensor_pairs(chip_step, core_flip):
    return [
        (y * 2 + c, ((y + chip_step) % 4) * 2 + (c ^ core_flip)) for y in range(4) for c in range(2)
    ]


def dot(a, b, ca, cb):
    return lax.dot_general(a, b, (((ca,), (cb,)), ((), ())), preferred_element_type=F32)


def shards(
    normed_input_rows,
    key_value_cotangent,
    key_value_weight,
    adapter_down_factors,
    adapter_up_factors,
    slot_adapter,
    adapter_of_block,
    live_rows_of_block,
    prompt_of_block,
    reward_of_block,
):
    rows, window = normed_input_rows.shape
    columns = key_value_cotangent.shape[2]
    dp = lax.axis_size("dp")
    owned = adapter_down_factors.shape[0]
    blocks = reward_of_block.shape[0]
    te = lax.axis_index("tensor")
    chip, core = te // 2, te % 2

    others = [(s, e) for s in (1, 3, 2, 0) for e in (0, 1) if (s, e) != (0, 0)]
    cotangents = [key_value_cotangent]
    slabs = [lax.dynamic_slice_in_dim(key_value_weight, te * window, window, 1)]
    for s, e in others:
        pairs = tensor_pairs(s, e)
        target = ((chip + s) % 4) * 2 + (core + e) % 2
        cotangents.append(lax.ppermute(key_value_cotangent, "tensor", pairs))
        slab = lax.dynamic_slice_in_dim(key_value_weight, target * window, window, 1)
        slabs.append(lax.ppermute(slab, "tensor", pairs))

    part_hi = lax.reduce_precision(reward_of_block, 8, 7)
    rest = reward_of_block - part_hi
    part_mid = lax.reduce_precision(rest, 8, 7)
    part_lo = rest - part_mid
    facts = jnp.concatenate([part_hi, part_mid, part_lo, prompt_of_block.astype(F32)]).astype(BF)
    facts = jnp.pad(facts[None, :], ((0, owned - 1), (0, 128 - 4 * blocks)))
    packed = jnp.concatenate([adapter_down_factors, adapter_up_factors, facts], axis=1)
    packed = jnp.broadcast_to(packed[None], (dp, *packed.shape))
    gathered = lax.all_to_all(packed, "dp", 0, 0)
    a_all = gathered[:, :, :window].reshape(SLOTS * RANK, window)
    b_all = gathered[:, :, window : window + columns].reshape(SLOTS * RANK, columns)
    facts_all = gathered[:, 0, window + columns : window + columns + 4 * blocks].astype(F32)
    facts_all = facts_all.reshape(dp, 4, blocks)
    reward_all = ((facts_all[:, 0] + facts_all[:, 1]) + facts_all[:, 2]).reshape(-1)
    prompt_all = facts_all[:, 3].astype(jnp.int32).reshape(-1)

    member_all = prompt_all[:, None] == jnp.arange(GROUPS, dtype=jnp.int32)[None, :]
    totals = jnp.sum(jnp.where(member_all, reward_all[:, None], 0.0), axis=0)
    squares = jnp.sum(jnp.where(member_all, (reward_all * reward_all)[:, None], 0.0), axis=0)
    mean_g = totals / GSIZE
    spread_g = jnp.sqrt(jnp.maximum(squares / GSIZE - mean_g * mean_g, 1.0))
    member = prompt_of_block[:, None] == jnp.arange(GROUPS, dtype=jnp.int32)[None, :]
    mean_b = jnp.sum(jnp.where(member, mean_g[None, :], 0.0), axis=1)
    spread_b = jnp.sum(jnp.where(member, spread_g[None, :], 0.0), axis=1)
    advantage = (reward_of_block - mean_b) / spread_b
    live = jnp.arange(BLOCK, dtype=jnp.int32)[None, :] < live_rows_of_block[:, None]
    coef = jnp.where(live, -advantage[:, None] / GSIZE, 0.0).reshape(rows, 1)

    value_cotangent = (key_value_cotangent[:, 1, :].astype(F32) * coef).astype(BF)
    chosen = adapter_of_block[:, None] == slot_adapter[None, :]
    chosen = jnp.broadcast_to(chosen[:, None, :], (blocks, BLOCK, SLOTS)).reshape(rows, SLOTS)
    chosen_wide = jnp.broadcast_to(chosen[:, :, None], (rows, SLOTS, RANK)).reshape(
        rows, SLOTS * RANK
    )

    def own_slot(every):
        picked = jnp.where(chosen_wide, every, 0.0)
        return sum(picked[:, k * RANK : (k + 1) * RANK] for k in range(SLOTS))

    low = jnp.concatenate(
        [
            own_slot(dot(normed_input_rows, a_all, 1, 1)),
            own_slot(dot(value_cotangent, b_all, 1, 1)),
        ],
        axis=1,
    )
    low = low + lax.ppermute(low, "tensor", tensor_pairs(0, 1))
    low_sent = low.astype(BF)
    low = low_sent.astype(F32) + sum(
        lax.ppermute(low_sent, "tensor", tensor_pairs(s, 0)).astype(F32) for s in (1, 3, 2)
    )
    low = low.astype(BF)
    spread_low = lambda v: jnp.where(chosen_wide, jnp.tile(v, (1, SLOTS)), jnp.zeros((), BF))
    hidden_wide = spread_low(low[:, :RANK])
    narrow_wide = spread_low(low[:, RANK:])

    terms = jnp.concatenate(
        [
            LOWRANK_MULTIPLIER * dot(narrow_wide, normed_input_rows, 0, 0),
            LOWRANK_MULTIPLIER * dot(hidden_wide, value_cotangent, 0, 0),
        ],
        axis=1,
    ).astype(BF)
    terms = lax.all_to_all(terms.reshape(dp, owned, window + columns), "dp", 0, 0)
    grads = jnp.sum(terms.astype(F32), axis=0)
    grad_a, grad_b = grads[:, :window], grads[:, window:]

    total = LOWRANK_MULTIPLIER * dot(narrow_wide, a_all, 1, 0)
    weighted = jnp.concatenate(cotangents, axis=2).astype(F32) * coef[:, :, None]
    weighted = weighted.astype(BF)
    for i, slab in enumerate(slabs):
        for j in range(2):
            total = total + dot(weighted[:, j, i * columns : (i + 1) * columns], slab[j], 1, 1)
    return (total.astype(BF), grad_a, grad_b)


def solution(mesh):
    in_specs = (
        P("dp", "tensor"),
        P("dp", None, "tensor"),
        P(None, None, "tensor"),
        P("dp", "tensor"),
        P("dp", "tensor"),
        P(),
        P("dp"),
        P("dp"),
        P("dp"),
        P("dp"),
    )
    out_specs = (P("dp", "tensor"), P("dp", "tensor"), P("dp", "tensor"))
    return jax.shard_map(shards, mesh=mesh, in_specs=in_specs, out_specs=out_specs, check_vma=False)
```

time: 639 us -> 191 us (0.30)
  waiting for transfers between devices: 440 us -> 50.6 us
  blocking collectives: 146 us -> 0 us
  starting transfers between devices: 0.17 us -> 61.9 us
  matrix products: 17.7 us -> 51.3 us
  between operations: 15.8 us -> 1.07 us
  local copies, waits for them, and re-layouts: 4.96 us -> 16.4 us
    reduce_scatter x3 -> x0, waiting for transfers between devices: 440 us -> none  [the longest x1 220 us: shards(): lax.psum_scatter(owner_terms_a, 'dp', scatter_dimension=0, tiled=True)]
    psum x2 -> x0, blocking collectives: 115 us -> none  [the longest x1 64.4 us: shards(): lax.psum((jnp.sum(member * reward_of_block[:, None], axis=0), jnp.sum(mem...]
    ppermute x0 -> x18, waiting for transfers between devices: none -> 41.9 us  [the longest x7 27.3 us: shards(): slabs.append(lax.ppermute(slab, 'tensor', pairs))]
    ppermute x0 -> x18, starting transfers between devices: none -> 40.3 us  [the longest x7 26.1 us: shards(): slabs.append(lax.ppermute(slab, 'tensor', pairs))]
    dot_general x10 -> x21, matrix products: 17.7 us -> 51.3 us  [dot(): lax.dot_general(a, b, (((ca,), (cb,)), ((), ())), preferred_element_type=...]
    all_gather x1 -> x0, blocking collectives: 31.3 us -> none  [shards(): lax.all_gather(adapter_up_factors, 'dp', axis=0, tiled=True)]
    all_to_all x0 -> x2, starting transfers between devices: none -> 21.6 us  [the longest x1 11.9 us: shards(): gathered = lax.all_to_all(packed, 'dp', 0, 0)]
    all_to_all x0 -> x2, waiting for transfers between devices: none -> 8.63 us  [the longest x1 8.63 us: shards(): lax.all_to_all(terms.reshape(dp, owned, window + columns), 'dp', 0, 0)]
  transfers between devices with their start and end apart: 4 -> 20, of which waited for: 3 -> 7; matrix products, arithmetic and copies ran while one was open for 5% -> 36% of each run, Pallas kernels for 0% -> 0%
where the time goes in v1:
time: 191 us; the launch traced here: 187 us
  starting transfers between devices  61.9 us (32%)
  matrix products  51.3 us (27%)
  waiting for transfers between devices  50.6 us (26%)
  local copies, waits for them, and re-layouts  16.4 us (9%)
  other arithmetic  5.66 us (3%)
    dot_general x21, matrix products, dot(): lax.dot_general(a, b, (((ca,), (cb,)), ((), ())), preferred_element_type=...  51.3 us
    ppermute x7, waiting for transfers between devices, shards(): slabs.append(lax.ppermute(slab, 'tensor', pairs))  27.3 us
    ppermute x7, starting transfers between devices, shards(): slabs.append(lax.ppermute(slab, 'tensor', pairs))  26.1 us
    ppermute x7, waiting for transfers between devices, shards(): cotangents.append(lax.ppermute(key_value_cotangent, 'tensor', pairs))  12.4 us
    all_to_all x1, starting transfers between devices, shards(): gathered = lax.all_to_all(packed, 'dp', 0, 0)  11.9 us
    ppermute x7, starting transfers between devices, shards(): cotangents.append(lax.ppermute(key_value_cotangent, 'tensor', pairs))  9.76 us
    all_to_all x1, starting transfers between devices, shards(): lax.all_to_all(terms.reshape(dp, owned, window + columns), 'dp', 0, 0)  9.72 us
    unnamed x44, local copies, waits for them, and re-layouts  8.7 us
  transfers between devices with their start and end apart: 20, of which 7 were waited for; matrix products, arithmetic and copies ran while one was open for 36% of the time, Pallas kernels for 0%

profile of v1, /device:TPU:1, one launch (start us, length us, event | category | flops | bytes accessed | tf_op | source)
XLA Modules:
  0.0 186.8 jit_solution(5041385144290403682)
XLA Ops:
  0.7 0.8 convert_bitcast_fusion
  1.4 0.7 fusion.34
  2.2 0.8 pad_maximum_fusion.2
  2.9 1.2 broadcast_in_dim.94
  4.1 11.9 %all-to-all-start = ((bf16[32,16,1280]{2,1,0:T(8,128)(2,1)}), bf16[32,16,1280]{2,1,0:T(8,128)(2,1)S(1)}, u32[]{:S(2)}, u32[]{:S(2)}) async-start(bf16[32,16,1280]{2,1,0:T(8,128)(2,1)} %broadcast_in_dim.94), calls=%async_computation | async-start | bytes 2621440 | tf_op jit(solution)/shard_map/all_to_all | solution.py:64
  16.0 0.8 fusion.38
  16.8 1.0 collective-permute-start.10
  17.7 2.8 %collective-permute-start.9 = (bf16[512,2,128]{2,0,1:T(8,128)(2,1)S(1)}, bf16[512,2,128]{2,0,1:T(8,128)(2,1)S(1)}, u32[]{:S(2)}, u32[]{:S(2)}) collective-permute-start(bf16[512,2,128]{2,0,1:T(8,128)(2,1)S(1)} %get-tuple-element.14), channel_id=1, source_target_pairs={{0,5},{1,4},{2,7},{3,6},{4,1},{5,0},{6,3},{7,2},{8,13},{9,12},{10,... | collective-permute-start | bytes 786440 | tf_op jit(solution)/shard_map/ppermute | solution.py:52
  20.5 0.8 collective-permute-start.6
  21.3 1.4 collective-permute-start.5
  22.7 0.4 collective-permute-start.4
  23.3 3.9 %constant_dynamic-slice_fusion.6 = (bf16[2,1024,128]{2,1,0:T(8,128)(2,1)}, bf16[2,1024,128]{2,1,0:T(8,128)(2,1)}, bf16[2,1024,128]{2,1,0:T(8,128)(2,1)}, bf16[2,...) fusion(bf16[2,8192,128]{2,1,0:T(8,128)(2,1)} %param.12, ...), kind=kLoop, calls=%fused_computation.114 | loop fusion | bytes 7340060 | tf_op jit(solution)/shard_map/dynamic_slice | solution.py:53
  27.2 11.6 %collective-permute-done.4 = bf16[512,2,128]{2,0,1:T(8,128)(2,1)} collective-permute-done((bf16[512,2,128]{2,0,1:T(8,128)(2,1)S(1)}, bf16[512,2,128]{2,0,1:T(8,128)(2,1)}, u32[]{:S(2)}, u32[]{:S(2)}) %collective-permute-start.4) | collective-permute-done | bytes 262176 | tf_op jit(solution)/shard_map/ppermute | solution.py:52
  38.9 0.6 collective-permute-start.7
  39.4 1.7 constant_dynamic-update-slice_fusion.6
  41.1 2.9 %collective-permute-start.8 = (bf16[512,2,128]{2,0,1:T(8,128)(2,1)S(1)}, bf16[512,2,128]{2,0,1:T(8,128)(2,1)S(1)}, u32[]{:S(2)}, u32[]{:S(2)}) collective-permute-start(bf16[512,2,128]{2,0,1:T(8,128)(2,1)S(1)} %get-tuple-element.14), channel_id=1, source_target_pairs={{0,4},{1,5},{2,6},{3,7},{4,0},{5,1},{6,2},{7,3},{8,12},{9,13},{10,... | collective-permute-start | bytes 786440 | tf_op jit(solution)/shard_map/ppermute | solution.py:52
  44.0 1.7 constant_dynamic-update-slice_fusion.5
  45.7 0.6 collective-permute-start.11
  46.3 0.8 constant_dynamic-update-slice_fusion.4
  47.0 0.7 collective-permute-done.7
  47.8 3.0 %collective-permute-start.15 = (bf16[2,1024,128]{2,1,0:T(8,128)(2,1)}, bf16[2,1024,128]{2,1,0:T(8,128)(2,1)}, u32[]{:S(2)}, u32[]{:S(2)}) collective-permute-start(bf16[2,1024,128]{2,1,0:T(8,128)(2,1)} %get-tuple-element.8), channel_id=1, source_target_pairs={{0,4},{1,5},{2,6},{3,7},{4,0},{5,1},{6,2},{7,3},{8,12},{9,13},{10,... | collective-permute-start | bytes 1572872 | tf_op jit(solution)/shard_map/ppermute | solution.py:54
  50.7 0.8 constant_dynamic-update-slice_fusion.3
  51.5 4.6 %collective-permute-start.14 = (bf16[2,1024,128]{2,1,0:T(8,128)(2,1)}, bf16[2,1024,128]{2,1,0:T(8,128)(2,1)}, u32[]{:S(2)}, u32[]{:S(2)}) collective-permute-start(bf16[2,1024,128]{2,1,0:T(8,128)(2,1)} %get-tuple-element.9), channel_id=1, source_target_pairs={{0,7},{1,6},{2,1},{3,0},{4,3},{5,2},{6,5},{7,4},{8,15},{9,14},{10,... | collective-permute-start | bytes 1572872 | tf_op jit(solution)/shard_map/ppermute | solution.py:54
  56.0 0.8 constant_dynamic-update-slice_fusion.2
  56.8 0.7 constant_dynamic-update-slice_fusion.1
  57.6 1.9 %collective-permute-start.16 = (bf16[2,1024,128]{2,1,0:T(8,128)(2,1)}, bf16[2,1024,128]{2,1,0:T(8,128)(2,1)}, u32[]{:S(2)}, u32[]{:S(2)}) collective-permute-start(bf16[2,1024,128]{2,1,0:T(8,128)(2,1)} %get-tuple-element.13), channel_id=1, source_target_pairs={{0,5},{1,4},{2,7},{3,6},{4,1},{5,0},{6,3},{7,2},{8,13},{9,12},{10,... | collective-permute-start | bytes 1572872 | tf_op jit(solution)/shard_map/ppermute | solution.py:54
  59.5 0.8 constant_dynamic-update-slice_fusion
  61.0 0.7 bitcast_select_fusion.2
  62.3 0.4 bitcast_select_fusion.1
  62.8 0.5 copy-done.7
  63.3 0.4 multiply_convert_fusion
  63.8 20.7 %collective-permute-done.16 = bf16[2,1024,128]{2,1,0:T(8,128)(2,1)} collective-permute-done((bf16[2,1024,128]{2,1,0:T(8,128)(2,1)}, bf16[2,1024,128]{2,1,0:T(8,128)(2,1)}, u32[]{:S(2)}, u32[]{:S(2)}) %collective-permute-start.16) | collective-permute-done | bytes 524320 | tf_op jit(solution)/shard_map/ppermute | solution.py:54
  84.5 15.9 %collective-permute-start.12 = (bf16[2,1024,128]{2,1,0:T(8,128)(2,1)S(1)}, bf16[2,1024,128]{2,1,0:T(8,128)(2,1)S(1)}, u32[]{:S(2)}, u32[]{:S(2)}) collective-permute-start(bf16[2,1024,128]{2,1,0:T(8,128)(2,1)S(1)} %copy-done.11), channel_id=1, source_target_pairs={{0,3},{1,2},{2,5},{3,4},{4,7},{5,6},{6,1},{7,0},{8,11},{9,10},{10,... | collective-permute-start | bytes 1572872 | tf_op jit(solution)/shard_map/ppermute | solution.py:54
  100.4 2.7 %fusion.3 = f32[512,1024]{1,0:T(8,128)} fusion(bf16[2,1024,128]{2,1,0:T(8,128)(2,1)} %collective-permute-done.16, bf16[512,2,1024]{2,0,1:T(8,128)(2,1)S(1)} %multiply_convert_fusion), kind=kOutput, calls=%fused_computation.18 | convolution fusion | flops 134217728 | bytes 2490368 | tf_op jit(solution)/shard_map/dot_general | solution.py:23
  103.1 2.8 %fusion.4 = f32[512,1024]{1,0:T(8,128)} fusion(bf16[2,1024,128]{2,1,0:T(8,128)(2,1)} %collective-permute-done.16, bf16[512,2,1024]{2,0,1:T(8,128)(2,1)S(1)} %multiply_convert_fusion), kind=kOutput, calls=%fused_computation.20 | convolution fusion | flops 134217728 | bytes 2490368 | tf_op jit(solution)/shard_map/dot_general | solution.py:23
  105.9 6.6 %collective-permute-done.12 = bf16[2,1024,128]{2,1,0:T(8,128)(2,1)S(1)} collective-permute-done((bf16[2,1024,128]{2,1,0:T(8,128)(2,1)S(1)}, bf16[2,1024,128]{2,1,0:T(8,128)(2,1)S(1)}, u32[]{:S(2)}, u32[]{:S(2)}) %collective-permute-start.12) | collective-permute-done | bytes 524320 | tf_op jit(solution)/shard_map/ppermute | solution.py:54
  112.6 1.7 fusion.11
  114.4 1.7 fusion.12
  116.5 2.8 %fusion.9 = f32[512,1024]{1,0:T(8,128)} fusion(bf16[2,1024,128]{2,1,0:T(8,128)(2,1)} %collective-permute-done.13, bf16[512,2,1024]{2,0,1:T(8,128)(2,1)S(1)} %multiply_convert_fusion), kind=kOutput, calls=%fused_computation.30 | convolution fusion | flops 134217728 | bytes 2490368 | tf_op jit(solution)/shard_map/dot_general | solution.py:23
  119.2 2.8 %fusion.10 = f32[512,1024]{1,0:T(8,128)} fusion(bf16[2,1024,128]{2,1,0:T(8,128)(2,1)} %collective-permute-done.13, bf16[512,2,1024]{2,0,1:T(8,128)(2,1)S(1)} %multiply_convert_fusion), kind=kOutput, calls=%fused_computation.32 | convolution fusion | flops 134217728 | bytes 2490368 | tf_op jit(solution)/shard_map/dot_general | solution.py:23
  122.0 2.8 %fusion.7 = f32[512,1024]{1,0:T(8,128)} fusion(bf16[2,1024,128]{2,1,0:T(8,128)(2,1)} %collective-permute-done.14, bf16[512,2,1024]{2,0,1:T(8,128)(2,1)S(1)} %multiply_convert_fusion), kind=kOutput, calls=%fused_computation.26 | convolution fusion | flops 134217728 | bytes 2490368 | tf_op jit(solution)/shard_map/dot_general | solution.py:23
  124.8 2.7 %fusion.8 = f32[512,1024]{1,0:T(8,128)} fusion(bf16[2,1024,128]{2,1,0:T(8,128)(2,1)} %collective-permute-done.14, bf16[512,2,1024]{2,0,1:T(8,128)(2,1)S(1)} %multiply_convert_fusion), kind=kOutput, calls=%fused_computation.28 | convolution fusion | flops 134217728 | bytes 2490368 | tf_op jit(solution)/shard_map/dot_general | solution.py:23
  127.5 2.7 %fusion.5 = f32[512,1024]{1,0:T(8,128)} fusion(bf16[2,1024,128]{2,1,0:T(8,128)(2,1)} %collective-permute-done.15, bf16[512,2,1024]{2,0,1:T(8,128)(2,1)S(1)} %multiply_convert_fusion), kind=kOutput, calls=%fused_computation.22 | convolution fusion | flops 134217728 | bytes 2490368 | tf_op jit(solution)/shard_map/dot_general | solution.py:23
  130.3 2.7 %fusion.6 = f32[512,1024]{1,0:T(8,128)} fusion(bf16[2,1024,128]{2,1,0:T(8,128)(2,1)} %collective-permute-done.15, bf16[512,2,1024]{2,0,1:T(8,128)(2,1)S(1)} %multiply_convert_fusion), kind=kOutput, calls=%fused_computation.24 | convolution fusion | flops 134217728 | bytes 2490368 | tf_op jit(solution)/shard_map/dot_general | solution.py:23
  133.0 2.8 %fusion.13 = f32[512,1024]{1,0:T(8,128)} fusion(bf16[2,1024,128]{2,1,0:T(8,128)(2,1)} %collective-permute-done.11, bf16[512,2,1024]{2,0,1:T(8,128)(2,1)S(1)} %multiply_convert_fusion), kind=kOutput, calls=%fused_computation.38 | convolution fusion | flops 134217728 | bytes 2490368 | tf_op jit(solution)/shard_map/dot_general | solution.py:23
  135.8 1.7 collective-permute-start.3
  137.5 2.3 %collective-permute-start.2 = (bf16[512,128]{0,1:T(8,128)(2,1)S(1)}, bf16[512,128]{0,1:T(8,128)(2,1)S(1)}, u32[]{:S(2)}, u32[]{:S(2)}) collective-permute-start(bf16[512,128]{0,1:T(8,128)(2,1)S(1)} %add_convert_fusion.2), channel_id=1, source_target_pairs={{0,6},{1,7},{2,0},{3,1},{4,2},{5,3},{6,4},{7,5},{8,14},{9,15},{10,... | collective-permute-start | bytes 393224 | tf_op jit(solution)/shard_map/ppermute | solution.py:105
  139.9 2.8 %fusion.16 = f32[512,1024]{1,0:T(8,128)} fusion(bf16[2,8192,128]{2,1,0:T(8,128)(2,1)} %param.12, s32[]{:T(128)S(6)} %select_n.148, bf16[512,2,1024]{2,0,1:T(8,128)(2,1)S(1)} %multiply_convert_fusion), kind=kOutput, calls=%fused_computation.44 | convolution fusion | flops 134217728 | bytes 2490372 | tf_op jit(solution)/shard_map/dot_general | solution.py:23
  142.7 1.6 collective-permute-done.2
  144.2 0.7 collective-permute-done.1
  145.0 0.7 multiply_convert_fusion.1
  145.7 0.9 broadcast_select_fusion
  146.6 0.4 fusion
  147.0 1.1 pad_maximum_fusion
  148.2 9.7 %all-to-all-start.1 = ((bf16[32,16,1152]{2,1,0:T(8,128)(2,1)}), bf16[32,16,1152]{2,1,0:T(8,128)(2,1)S(1)}, u32[]{:S(2)}, u32[]{:S(2)}) async-start(bf16[32,16,1152]{2,1,0:T(8,128)(2,1)} %pad_maximum_fusion), calls=%async_computation.1 | async-start | bytes 2359296 | tf_op jit(solution)/shard_map/all_to_all | solution.py:119
  157.9 1.6 fusion.15
  159.5 3.0 %fusion.14 = f32[512,1024]{1,0:T(8,128)} fusion(bf16[2,1024,128]{2,1,0:T(8,128)(2,1)} %collective-permute-done.11, bf16[512,2,1024]{2,0,1:T(8,128)(2,1)} %copy-done.1), kind=kOutput, calls=%fused_computation.40 | convolution fusion | flops 134217728 | bytes 2490368 | tf_op jit(solution)/shard_map/dot_general | solution.py:23
  162.5 2.9 %fusion.2 = f32[512,1024]{1,0:T(8,128)} fusion(bf16[2,1024,128]{2,1,0:T(8,128)(2,1)} %collective-permute-done.17, bf16[512,2,1024]{2,0,1:T(8,128)(2,1)} %copy-done.1), kind=kOutput, calls=%fused_computation.16 | convolution fusion | flops 134217728 | bytes 2490368 | tf_op jit(solution)/shard_map/dot_general | solution.py:23
  165.4 0.7 fusion.40
  166.2 0.8 copy-done.2
  167.0 9.8 %add_convert_fusion = bf16[512,1024]{1,0:T(8,128)(2,1)} fusion(f32[512,1024]{1,0:T(8,128)} %fusion.2, f32[512,1024]{1,0:T(8,128)S(1)} %copy-done.2, f32[512,1024]{1,0:T(8,128)S(1)} %copy-done.3, f32[512,1024]{1,0:T(8,128)} %fusion.5, f32[512,1024]{1,0:T(8,128)} %fusion.6, f32[512,1024]{1,0:T(8,128)} %fusion.7, f32[512,1024]{1,0:T(8,128)} %fusion.8, ...), kind=kOutput, calls=%fused_computation.3 | convolution fusion | flops 143654912 | bytes 34996224 | tf_op jit(solution)/shard_map/dot_general | solution.py:23
  176.8 8.6 %all-to-all-done.1 = bf16[32,16,1152]{2,1,0:T(8,128)(2,1)S(1)} async-done(((bf16[32,16,1152]{2,1,0:T(8,128)(2,1)}), bf16[32,16,1152]{2,1,0:T(8,128)(2,1)S(1)}, u32[]{:S(2)}, u32[]{:S(2)}) %all-to-all-start.1) | async-done | bytes 1179680 | tf_op jit(solution)/shard_map/all_to_all | solution.py:119
  185.6 0.6 slice.297
  186.2 0.6 slice.296
  (78 shorter events, 2.4 us)
Async XLA Ops:
  0.6 60.3 %copy-start = (bf16[512,1024]{1,0:T(8,128)(2,1)S(1)}, bf16[512,1024]{1,0:T(8,128)(2,1)}, u32[]{:S(2)}) copy-start(bf16[512,1024]{1,0:T(8,128)(2,1)} %param.10) | copy-start | bytes 3145732
  0.6 15.3 %copy-start.12 = (bf16[512,2,128]{2,1,0:T(2,128)(2,1)S(1)}, bf16[512,2,128]{2,1,0:T(2,128)(2,1)}, u32[]{:S(2)}) copy-start(bf16[512,2,128]{2,1,0:T(2,128)(2,1)} %param.11) | copy-start | bytes 786436
  2.9 20.1 %copy-start.16 = (s32[8]{0:T(128)S(1)}, s32[8]{0:T(128)}, u32[]{:S(2)}) copy-start(s32[8]{0:T(128)} %param.15) | copy-start | bytes 100
  2.9 20.1 %copy-start.17 = (s32[4]{0:T(128)S(1)}, s32[4]{0:T(128)}, u32[]{:S(2)}) copy-start(s32[4]{0:T(128)} %param.16) | copy-start | bytes 52
  4.1 56.1 %all-to-all-start = ((bf16[32,16,1280]{2,1,0:T(8,128)(2,1)}), bf16[32,16,1280]{2,1,0:T(8,128)(2,1)S(1)}, u32[]{:S(2)}, u32[]{:S(2)}) async-start(bf16[32,16,1280]{2,1,0:T(8,128)(2,1)} %broadcast_in_dim.94), calls=%async_computation | async-start | bytes 2621440 | tf_op jit(solution)/shard_map/all_to_all | solution.py:64
  16.8 24.3 %copy-start.9 = (bf16[512,2,128]{2,0,1:T(8,128)(2,1)}, bf16[512,2,128]{2,0,1:T(8,128)(2,1)S(1)}, u32[]{:S(2)}) copy-start(bf16[512,2,128]{2,0,1:T(8,128)(2,1)S(1)} %get-tuple-element.14) | copy-start | bytes 786436
  16.8 40.8 %collective-permute-start.10 = (bf16[512,2,128]{2,0,1:T(8,128)(2,1)S(1)}, bf16[512,2,128]{2,0,1:T(8,128)(2,1)S(1)}, u32[]{:S(2)}, u32[]{:S(2)}) collective-permute-start(bf16[512,2,128]{2,0,1:T(8,128)(2,1)S(1)} %get-tuple-element.14), channel_id=1, source_target_pairs={{0,1},{1,0},{2,3},{3,2},{4,5},{5,4},{6,7},{7,6},{8,9},{9,8},{10,11... | collective-permute-start | bytes 786440 | tf_op jit(solution)/shard_map/ppermute | solution.py:52
  17.7 39.1 %collective-permute-start.9 = (bf16[512,2,128]{2,0,1:T(8,128)(2,1)S(1)}, bf16[512,2,128]{2,0,1:T(8,128)(2,1)S(1)}, u32[]{:S(2)}, u32[]{:S(2)}) collective-permute-start(bf16[512,2,128]{2,0,1:T(8,128)(2,1)S(1)} %get-tuple-element.14), channel_id=1, source_target_pairs={{0,5},{1,4},{2,7},{3,6},{4,1},{5,0},{6,3},{7,2},{8,13},{9,12},{10,... | collective-permute-start | bytes 786440 | tf_op jit(solution)/shard_map/ppermute | solution.py:52
  20.5 25.2 %collective-permute-start.6 = (bf16[512,2,128]{2,0,1:T(8,128)(2,1)S(1)}, bf16[512,2,128]{2,0,1:T(8,128)(2,1)S(1)}, u32[]{:S(2)}, u32[]{:S(2)}) collective-permute-start(bf16[512,2,128]{2,0,1:T(8,128)(2,1)S(1)} %get-tuple-element.14), channel_id=1, source_target_pairs={{0,6},{1,7},{2,0},{3,1},{4,2},{5,3},{6,4},{7,5},{8,14},{9,15},{10,... | collective-permute-start | bytes 786440 | tf_op jit(solution)/shard_map/ppermute | solution.py:52
  21.3 19.8 %collective-permute-start.5 = (bf16[512,2,128]{2,0,1:T(8,128)(2,1)S(1)}, bf16[512,2,128]{2,0,1:T(8,128)(2,1)}, u32[]{:S(2)}, u32[]{:S(2)}) collective-permute-start(bf16[512,2,128]{2,0,1:T(8,128)(2,1)S(1)} %get-tuple-element.14), channel_id=1, source_target_pairs={{0,3},{1,2},{2,5},{3,4},{4,7},{5,6},{6,1},{7,0},{8,11},{9,10},{10,... | collective-permute-start | bytes 786440 | tf_op jit(solution)/shard_map/ppermute | solution.py:52
  22.7 16.2 %collective-permute-start.4 = (bf16[512,2,128]{2,0,1:T(8,128)(2,1)S(1)}, bf16[512,2,128]{2,0,1:T(8,128)(2,1)}, u32[]{:S(2)}, u32[]{:S(2)}) collective-permute-start(bf16[512,2,128]{2,0,1:T(8,128)(2,1)S(1)} %get-tuple-element.14), channel_id=1, source_target_pairs={{0,2},{1,3},{2,4},{3,5},{4,6},{5,7},{6,0},{7,1},{8,10},{9,11},{10,... | collective-permute-start | bytes 786440 | tf_op jit(solution)/shard_map/ppermute | solution.py:52
  38.9 8.9 %collective-permute-start.7 = (bf16[512,2,128]{2,0,1:T(8,128)(2,1)S(1)}, bf16[512,2,128]{2,0,1:T(8,128)(2,1)S(1)}, u32[]{:S(2)}, u32[]{:S(2)}) collective-permute-start(bf16[512,2,128]{2,0,1:T(8,128)(2,1)S(1)} %get-tuple-element.14), channel_id=1, source_target_pairs={{0,7},{1,6},{2,1},{3,0},{4,3},{5,2},{6,5},{7,4},{8,15},{9,14},{10,... | collective-permute-start | bytes 786440 | tf_op jit(solution)/shard_map/ppermute | solution.py:52
  41.1 10.4 %collective-permute-start.8 = (bf16[512,2,128]{2,0,1:T(8,128)(2,1)S(1)}, bf16[512,2,128]{2,0,1:T(8,128)(2,1)S(1)}, u32[]{:S(2)}, u32[]{:S(2)}) collective-permute-start(bf16[512,2,128]{2,0,1:T(8,128)(2,1)S(1)} %get-tuple-element.14), channel_id=1, source_target_pairs={{0,4},{1,5},{2,6},{3,7},{4,0},{5,1},{6,2},{7,3},{8,12},{9,13},{10,... | collective-permute-start | bytes 786440 | tf_op jit(solution)/shard_map/ppermute | solution.py:52
  45.7 87.3 %collective-permute-start.11 = (bf16[2,1024,128]{2,1,0:T(8,128)(2,1)}, bf16[2,1024,128]{2,1,0:T(8,128)(2,1)}, u32[]{:S(2)}, u32[]{:S(2)}) collective-permute-start(bf16[2,1024,128]{2,1,0:T(8,128)(2,1)} %get-tuple-element.7), channel_id=1, source_target_pairs={{0,2},{1,3},{2,4},{3,5},{4,6},{5,7},{6,0},{7,1},{8,10},{9,11},{10,... | collective-permute-start | bytes 1572872 | tf_op jit(solution)/shard_map/ppermute | solution.py:54
  47.8 79.8 %collective-permute-start.15 = (bf16[2,1024,128]{2,1,0:T(8,128)(2,1)}, bf16[2,1024,128]{2,1,0:T(8,128)(2,1)}, u32[]{:S(2)}, u32[]{:S(2)}) collective-permute-start(bf16[2,1024,128]{2,1,0:T(8,128)(2,1)} %get-tuple-element.8), channel_id=1, source_target_pairs={{0,4},{1,5},{2,6},{3,7},{4,0},{5,1},{6,2},{7,3},{8,12},{9,13},{10,... | collective-permute-start | bytes 1572872 | tf_op jit(solution)/shard_map/ppermute | solution.py:54
  51.5 70.5 %collective-permute-start.14 = (bf16[2,1024,128]{2,1,0:T(8,128)(2,1)}, bf16[2,1024,128]{2,1,0:T(8,128)(2,1)}, u32[]{:S(2)}, u32[]{:S(2)}) collective-permute-start(bf16[2,1024,128]{2,1,0:T(8,128)(2,1)} %get-tuple-element.9), channel_id=1, source_target_pairs={{0,7},{1,6},{2,1},{3,0},{4,3},{5,2},{6,5},{7,4},{8,15},{9,14},{10,... | collective-permute-start | bytes 1572872 | tf_op jit(solution)/shard_map/ppermute | solution.py:54
  56.8 59.3 %collective-permute-start.13 = (bf16[2,1024,128]{2,1,0:T(8,128)(2,1)}, bf16[2,1024,128]{2,1,0:T(8,128)(2,1)}, u32[]{:S(2)}, u32[]{:S(2)}) collective-permute-start(bf16[2,1024,128]{2,1,0:T(8,128)(2,1)} %get-tuple-element.10), channel_id=1, source_target_pairs={{0,6},{1,7},{2,0},{3,1},{4,2},{5,3},{6,4},{7,5},{8,14},{9,15},{10,... | collective-permute-start | bytes 1572872 | tf_op jit(solution)/shard_map/ppermute | solution.py:54
  57.6 26.9 %collective-permute-start.16 = (bf16[2,1024,128]{2,1,0:T(8,128)(2,1)}, bf16[2,1024,128]{2,1,0:T(8,128)(2,1)}, u32[]{:S(2)}, u32[]{:S(2)}) collective-permute-start(bf16[2,1024,128]{2,1,0:T(8,128)(2,1)} %get-tuple-element.13), channel_id=1, source_target_pairs={{0,5},{1,4},{2,7},{3,6},{4,1},{5,0},{6,3},{7,2},{8,13},{9,12},{10,... | collective-permute-start | bytes 1572872 | tf_op jit(solution)/shard_map/ppermute | solution.py:54
  60.9 1.0 copy-start.14
  60.9 1.2 copy-start.13
  60.9 1.2 copy-start.15
  61.0 1.3 copy-start.10
  61.7 1.6 copy-start.7
  63.3 21.1 %copy-start.11 = (bf16[2,1024,128]{2,1,0:T(8,128)(2,1)S(1)}, bf16[2,1024,128]{2,1,0:T(8,128)(2,1)}, u32[]{:S(2)}) copy-start(bf16[2,1024,128]{2,1,0:T(8,128)(2,1)} %get-tuple-element.11) | copy-start | bytes 1572868
  63.7 76.1 %copy-start.1 = (bf16[512,2,1024]{2,0,1:T(8,128)(2,1)}, bf16[512,2,1024]{2,0,1:T(8,128)(2,1)S(1)}, u32[]{:S(2)}) copy-start(bf16[512,2,1024]{2,0,1:T(8,128)(2,1)S(1)} %multiply_convert_fusion) | copy-start | bytes 6291460
  84.5 28.0 %collective-permute-start.12 = (bf16[2,1024,128]{2,1,0:T(8,128)(2,1)S(1)}, bf16[2,1024,128]{2,1,0:T(8,128)(2,1)S(1)}, u32[]{:S(2)}, u32[]{:S(2)}) collective-permute-start(bf16[2,1024,128]{2,1,0:T(8,128)(2,1)S(1)} %copy-done.11), channel_id=1, source_target_pairs={{0,3},{1,2},{2,5},{3,4},{4,7},{5,6},{6,1},{7,0},{8,11},{9,10},{10,... | collective-permute-start | bytes 1572872 | tf_op jit(solution)/shard_map/ppermute | solution.py:54
  112.5 50.0 %collective-permute-start.17 = (bf16[2,1024,128]{2,1,0:T(8,128)(2,1)}, bf16[2,1024,128]{2,1,0:T(8,128)(2,1)}, u32[]{:S(2)}, u32[]{:S(2)}) collective-permute-start(bf16[2,1024,128]{2,1,0:T(8,128)(2,1)} %get-tuple-element.12), channel_id=1, source_target_pairs={{0,1},{1,0},{2,3},{3,2},{4,5},{5,4},{6,7},{7,6},{8,9},{9,8},{10,11... | collective-permute-start | bytes 1572872 | tf_op jit(solution)/shard_map/ppermute | solution.py:54
  116.1 19.6 %collective-permute-start = (f32[512,128]{0,1:T(8,128)S(1)}, f32[512,128]{0,1:T(8,128)S(1)}, u32[]{:S(2)}, u32[]{:S(2)}) collective-permute-start(f32[512,128]{0,1:T(8,128)S(1)} %pad_maximum_fusion.1), channel_id=1, source_target_pairs={{0,1},{1,0},{2,3},{3,2},{4,5},{5,4},{6,7},{7,6},{8,9},{9,8},{10,11... | collective-permute-start | bytes 786440 | tf_op jit(solution)/shard_map/ppermute | solution.py:102
  135.8 6.9 %collective-permute-start.3 = (bf16[512,128]{0,1:T(8,128)(2,1)S(1)}, bf16[512,128]{0,1:T(8,128)(2,1)S(1)}, u32[]{:S(2)}, u32[]{:S(2)}) collective-permute-start(bf16[512,128]{0,1:T(8,128)(2,1)S(1)} %add_convert_fusion.2), channel_id=1, source_target_pairs={{0,4},{1,5},{2,6},{3,7},{4,0},{5,1},{6,2},{7,3},{8,12},{9,13},{10,... | collective-permute-start | bytes 393224 | tf_op jit(solution)/shard_map/ppermute | solution.py:105
  137.5 6.7 %collective-permute-start.2 = (bf16[512,128]{0,1:T(8,128)(2,1)S(1)}, bf16[512,128]{0,1:T(8,128)(2,1)S(1)}, u32[]{:S(2)}, u32[]{:S(2)}) collective-permute-start(bf16[512,128]{0,1:T(8,128)(2,1)S(1)} %add_convert_fusion.2), channel_id=1, source_target_pairs={{0,6},{1,7},{2,0},{3,1},{4,2},{5,3},{6,4},{7,5},{8,14},{9,15},{10,... | collective-permute-start | bytes 393224 | tf_op jit(solution)/shard_map/ppermute | solution.py:105
  139.9 5.0 %collective-permute-start.1 = (bf16[512,128]{0,1:T(8,128)(2,1)S(1)}, bf16[512,128]{0,1:T(8,128)(2,1)S(1)}, u32[]{:S(2)}, u32[]{:S(2)}) collective-permute-start(bf16[512,128]{0,1:T(8,128)(2,1)S(1)} %add_convert_fusion.2), channel_id=1, source_target_pairs={{0,2},{1,3},{2,4},{3,5},{4,6},{5,7},{6,0},{7,1},{8,10},{9,11},{10,... | collective-permute-start | bytes 393224 | tf_op jit(solution)/shard_map/ppermute | solution.py:105
  148.2 37.3 %all-to-all-start.1 = ((bf16[32,16,1152]{2,1,0:T(8,128)(2,1)}), bf16[32,16,1152]{2,1,0:T(8,128)(2,1)S(1)}, u32[]{:S(2)}, u32[]{:S(2)}) async-start(bf16[32,16,1152]{2,1,0:T(8,128)(2,1)} %pad_maximum_fusion), calls=%async_computation.1 | async-start | bytes 2359296 | tf_op jit(solution)/shard_map/all_to_all | solution.py:119
  157.9 7.5 %copy-start.8 = (bf16[512,8,64]{0,2,1:T(8,128)(2,1)S(1)}, bf16[512,8,64]{0,2,1:T(8,128)(2,1)}, u32[]{:S(2)}) copy-start(bf16[512,8,64]{0,2,1:T(8,128)(2,1)} %get-tuple-element.21) | copy-start | bytes 1572868
  157.9 8.3 %copy-start.6 = (f32[512,1024]{1,0:T(8,128)S(1)}, f32[512,1024]{1,0:T(8,128)}, u32[]{:S(2)}) copy-start(f32[512,1024]{1,0:T(8,128)} %fusion.9) | copy-start | bytes 6291460
  159.5 6.6 %copy-start.4 = (f32[512,1024]{1,0:T(8,128)S(1)}, f32[512,1024]{1,0:T(8,128)}, u32[]{:S(2)}) copy-start(f32[512,1024]{1,0:T(8,128)} %fusion.11) | copy-start | bytes 6291460
  159.5 6.6 %copy-start.5 = (f32[512,1024]{1,0:T(8,128)S(1)}, f32[512,1024]{1,0:T(8,128)}, u32[]{:S(2)}) copy-start(f32[512,1024]{1,0:T(8,128)} %fusion.12) | copy-start | bytes 6291460
  162.5 3.7 %copy-start.3 = (f32[512,1024]{1,0:T(8,128)S(1)}, f32[512,1024]{1,0:T(8,128)}, u32[]{:S(2)}) copy-start(f32[512,1024]{1,0:T(8,128)} %fusion.4) | copy-start | bytes 6291460
  165.4 1.6 copy-start.2

commit v2 on v1

--- a/solution.py
+++ b/solution.py
@@ -1,6 +1,8 @@
 import jax
 import jax.numpy as jnp
 from jax import lax
+from jax.experimental import pallas as pl
+from jax.experimental.pallas import tpu as pltpu
 from jax.sharding import PartitionSpec as P
 
 BLOCK = 128
@@ -8,6 +10,7 @@
 GROUPS = 16
 SLOTS = 8
 RANK = 64
+CHIP_STEPS = (1, 3, 2)
 LOWRANK_MULTIPLIER = 2.0
 BF = jnp.bfloat16
 F32 = jnp.float32
@@ -21,6 +24,59 @@
 
 def dot(a, b, ca, cb):
     return lax.dot_general(a, b, (((ca,), (cb,)), ((), ())), preferred_element_type=F32)
+
+
+def frozen_kernel(place, same_ref, other_ref, *refs):
+    *slab_refs, narrow_ref, a_ref, coef_ref, out_ref, weighted = refs
+    chips, _, rows, columns = same_ref.shape
+
+    @pl.when(pl.program_id(0) == 0)
+    def _():
+        coef = coef_ref[...]
+        for half, ref in enumerate((same_ref, other_ref)):
+            for i in range(chips):
+                for j in range(2):
+                    k = ((half * chips + i) * 2 + j) * columns
+                    weighted[:, k : k + columns] = (ref[i, j].astype(F32) * coef).astype(BF)
+
+    slabs = [ref[j] for ref in slab_refs for j in range(2)]
+    total = dot(weighted[...], jnp.concatenate(slabs, axis=1), 1, 1)
+    total = total + LOWRANK_MULTIPLIER * dot(narrow_ref[...], a_ref[...], 1, 0)
+    out_ref[...] = total.astype(BF)
+
+
+def frozen_and_correction(te, same_core, other_core, weight, arrived, narrow, a_all, coef):
+    _, window, columns = arrived[0].shape
+    chips, _, rows, _ = same_core.shape
+    depth = narrow.shape[1]
+    tile = 256
+    steps = window // tile
+    resident = lambda shape: pl.BlockSpec(shape, lambda i, p: (0,) * len(shape))
+    return pl.pallas_call(
+        frozen_kernel,
+        grid_spec=pltpu.PrefetchScalarGridSpec(
+            num_scalar_prefetch=1,
+            grid=(steps,),
+            in_specs=[
+                resident((chips, 2, rows, columns)),
+                resident((chips, 2, rows, columns)),
+                pl.BlockSpec((2, tile, columns), lambda i, p: (0, p[0] * steps + i, 0)),
+                *[pl.BlockSpec((2, tile, columns), lambda i, p: (0, i, 0)) for _ in arrived],
+                resident((rows, depth)),
+                pl.BlockSpec((depth, tile), lambda i, p: (0, i)),
+                resident((rows, 1)),
+            ],
+            out_specs=pl.BlockSpec((rows, tile), lambda i, p: (0, i)),
+            scratch_shapes=[pltpu.VMEM((rows, 4 * chips * columns), BF)],
+        ),
+        out_shape=jax.ShapeDtypeStruct((rows, window), BF),
+        compiler_params=pltpu.CompilerParams(vmem_limit_bytes=32 * 2**20),
+        cost_estimate=pl.CostEstimate(
+            flops=2 * rows * window * (4 * chips * columns + depth),
+            bytes_accessed=8 * 2**20,
+            transcendentals=0,
+        ),
+    )(te.reshape(1), same_core, other_core, weight, *arrived, narrow, a_all, coef)
 
 
 def shards(
@@ -43,15 +99,17 @@
     te = lax.axis_index("tensor")
     chip, core = te // 2, te % 2
 
-    others = [(s, e) for s in (1, 3, 2, 0) for e in (0, 1) if (s, e) != (0, 0)]
-    cotangents = [key_value_cotangent]
-    slabs = [lax.dynamic_slice_in_dim(key_value_weight, te * window, window, 1)]
-    for s, e in others:
-        pairs = tensor_pairs(s, e)
-        target = ((chip + s) % 4) * 2 + (core + e) % 2
-        cotangents.append(lax.ppermute(key_value_cotangent, "tensor", pairs))
-        slab = lax.dynamic_slice_in_dim(key_value_weight, target * window, window, 1)
-        slabs.append(lax.ppermute(slab, "tensor", pairs))
+    def slab_for(chip_step, core_flip):
+        target = ((chip + chip_step) % 4) * 2 + (core + core_flip) % 2
+        return lax.dynamic_slice_in_dim(key_value_weight, target * window, window, 1)
+
+    def send(value, chip_step, core_flip):
+        return lax.ppermute(value, "tensor", tensor_pairs(chip_step, core_flip))
+
+    cotangent = jnp.transpose(key_value_cotangent, (1, 0, 2))
+    cotangents = [cotangent] + [send(cotangent, s, 0) for s in CHIP_STEPS]
+    slabs = {(s, 0): send(slab_for(s, 0), s, 0) for s in (1, 3)}
+    relayed = [send(slab_for(2, 0), 1, 0), send(slab_for(2, 1), 3, 1)]
 
     part_hi = lax.reduce_precision(reward_of_block, 8, 7)
     rest = reward_of_block - part_hi
@@ -62,6 +120,7 @@
     packed = jnp.concatenate([adapter_down_factors, adapter_up_factors, facts], axis=1)
     packed = jnp.broadcast_to(packed[None], (dp, *packed.shape))
     gathered = lax.all_to_all(packed, "dp", 0, 0)
+    gathered, cotangents, slabs = lax.optimization_barrier((gathered, cotangents, slabs))
     a_all = gathered[:, :, :window].reshape(SLOTS * RANK, window)
     b_all = gathered[:, :, window : window + columns].reshape(SLOTS * RANK, columns)
     facts_all = gathered[:, 0, window + columns : window + columns + 4 * blocks].astype(F32)
@@ -102,7 +161,7 @@
     low = low + lax.ppermute(low, "tensor", tensor_pairs(0, 1))
     low_sent = low.astype(BF)
     low = low_sent.astype(F32) + sum(
-        lax.ppermute(low_sent, "tensor", tensor_pairs(s, 0)).astype(F32) for s in (1, 3, 2)
+        lax.ppermute(low_sent, "tensor", tensor_pairs(s, 0)).astype(F32) for s in CHIP_STEPS
     )
     low = low.astype(BF)
     spread_low = lambda v: jnp.where(chosen_wide, jnp.tile(v, (1, SLOTS)), jnp.zeros((), BF))
@@ -116,17 +175,21 @@
         ],
         axis=1,
     ).astype(BF)
+    terms, relayed = lax.optimization_barrier((terms, relayed))
     terms = lax.all_to_all(terms.reshape(dp, owned, window + columns), "dp", 0, 0)
-    grads = jnp.sum(terms.astype(F32), axis=0)
-    grad_a, grad_b = grads[:, :window], grads[:, window:]
-
-    total = LOWRANK_MULTIPLIER * dot(narrow_wide, a_all, 1, 0)
-    weighted = jnp.concatenate(cotangents, axis=2).astype(F32) * coef[:, :, None]
-    weighted = weighted.astype(BF)
-    for i, slab in enumerate(slabs):
-        for j in range(2):
-            total = total + dot(weighted[:, j, i * columns : (i + 1) * columns], slab[j], 1, 1)
-    return (total.astype(BF), grad_a, grad_b)
+    grad_a = jnp.sum(terms[:, :, :window].astype(F32), axis=0)
+    grad_b = jnp.sum(terms[:, :, window:].astype(F32), axis=0)
+
+    same_core = jnp.stack(cotangents)
+    other_core = send(same_core, 0, 1)
+    slabs[(2, 0)] = send(relayed[0], 1, 0)
+    slabs[(2, 1)] = send(relayed[1], 3, 0)
+    slabs |= {(s, 1): send(slab_for(s, 1), s, 1) for s in (1, 3, 0)}
+    arrived = [slabs[(s, e)] for e in (0, 1) for s in (0, *CHIP_STEPS) if (s, e) != (0, 0)]
+    input_gradient = frozen_and_correction(
+        te, same_core, other_core, key_value_weight, arrived, narrow_wide, a_all, coef
+    )
+    return (input_gradient, grad_a, grad_b)
 
 
 def solution(mesh):

time: 191 us -> 137 us (0.72); the launches traced: 187 us -> 136 us
  matrix products: 51.3 us -> 3.18 us
  starting transfers between devices: 61.9 us -> 43.5 us
  Pallas kernels: 0 us -> 6.67 us
  local copies, waits for them, and re-layouts: 16.4 us -> 21.5 us
  other arithmetic: 5.66 us -> 9.1 us
    dot_general x21 -> x4, matrix products: 51.3 us -> 3.18 us  [dot(): lax.dot_general(a, b, (((ca,), (cb,)), ((), ())), preferred_element_type=...]
    ppermute x14 -> x13, starting transfers between devices: 35.9 us -> 16.6 us  [send(): return lax.ppermute(value, 'tensor', tensor_pairs(chip_step, core_flip))]
    ppermute x14 -> x13, waiting for transfers between devices: 39.7 us -> 48.3 us  [send(): return lax.ppermute(value, 'tensor', tensor_pairs(chip_step, core_flip))]
    all_to_all x1, waiting for transfers between devices: 8.63 us -> 0.01 us  [shards(): lax.all_to_all(terms.reshape(dp, owned, window + columns), 'dp', 0, 0)]
    pallas_call x0 -> x1, Pallas kernels: none -> 6.67 us  [frozen_and_correction(): pl.pallas_call(frozen_kernel, grid_spec=pltpu.PrefetchScalarGridSpec(num_...]
    optimization_barrier x0 -> x1, local copies, waits for them, and re-layouts: none -> 4.24 us  [shards(): lax.optimization_barrier((gathered, cotangents, slabs))]
    reduce_sum x1 -> x2, other arithmetic: 0.17 us -> 3.55 us  [the longest x1 2.02 us: shards(): grad_a = jnp.sum(terms[:, :, :window].astype(F32), axis=0)]
    ppermute x1, starting transfers between devices: 0.34 us -> 2.3 us  [shards(): low = low + lax.ppermute(low, 'tensor', tensor_pairs(0, 1))]
  transfers between devices with their start and end apart: 20 -> 19, of which waited for: 7 -> 7; matrix products, arithmetic and copies ran while one was open for 36% -> 6% of each run, Pallas kernels for 0% -> 5%
where the time goes in v2:
time: 137 us; the launch traced here: 136 us
  waiting for transfers between devices  50.7 us (37%)
  starting transfers between devices  43.5 us (32%)
  local copies, waits for them, and re-layouts  21.5 us (16%)
  other arithmetic  9.1 us (7%)
  Pallas kernels  6.67 us (5%)
  matrix products  3.18 us (2%)
    ppermute x13, waiting for transfers between devices, send(): return lax.ppermute(value, 'tensor', tensor_pairs(chip_step, core_flip))  48.3 us
    ppermute x13, starting transfers between devices, send(): return lax.ppermute(value, 'tensor', tensor_pairs(chip_step, core_flip))  16.6 us
    all_to_all x1, starting transfers between devices, shards(): gathered = lax.all_to_all(packed, 'dp', 0, 0)  11.9 us
    unnamed x43, local copies, waits for them, and re-layouts  10.3 us
    all_to_all x1, starting transfers between devices, shards(): lax.all_to_all(terms.reshape(dp, owned, window + columns), 'dp', 0, 0)  8.2 us
    pallas_call x1, Pallas kernels, frozen_and_correction(): pl.pallas_call(frozen_kernel, grid_spec=pltpu.PrefetchScalarGridSpec(num_...  6.67 us
    ppermute x3, starting transfers between devices, shards(): lax.ppermute(low_sent, 'tensor', tensor_pairs(s, 0)).astype(F32)  4.45 us
    optimization_barrier x1, local copies, waits for them, and re-layouts, shards(): lax.optimization_barrier((gathered, cotangents, slabs))  4.24 us
  transfers between devices with their start and end apart: 19, of which 7 were waited for; matrix products, arithmetic and copies ran while one was open for 6% of the time, Pallas kernels for 5%

profile of v2, /device:TPU:1, one launch (start us, length us, event | category | flops | bytes accessed | tf_op | source)
XLA Modules:
  0.0 135.7 jit_solution(7429763684185142844)
XLA Ops:
  0.6 0.8 fusion.18
  1.4 0.7 convert_bitcast_fusion
  2.1 0.1 fusion.13
  2.1 0.8 pad_maximum_fusion.3
  2.9 1.2 broadcast_in_dim.91
  4.1 11.9 %all-to-all-start = ((bf16[32,16,1280]{2,1,0:T(8,128)(2,1)}), bf16[32,16,1280]{2,1,0:T(8,128)(2,1)S(1)}, u32[]{:S(2)}, u32[]{:S(2)}) async-start(bf16[32,16,1280]{2,1,0:T(8,128)(2,1)} %broadcast_in_dim.91), calls=%async_computation | async-start | bytes 2621440 | tf_op jit(solution)/shard_map/all_to_all | solution.py:122
  16.1 3.6 %constant_dynamic-slice_fusion = (bf16[2,1024,128]{2,1,0:T(8,128)(2,1)}, bf16[2,1024,128]{2,1,0:T(8,128)(2,1)}, bf16[2,1024,128]{2,1,0:T(8,128)(2,1)}, bf16[2,10...) fusion(bf16[2,8192,128]{2,1,0:T(8,128)(2,1)} %refs_0_.1, ...), kind=kLoop, calls=%fused_computation.58 | loop fusion | bytes 7340060 | tf_op jit(solution)/shard_map/dynamic_slice | solution.py:104
  19.8 1.3 collective-permute-start.3
  21.1 1.4 %collective-permute-start.4 = (bf16[2,1024,128]{2,1,0:T(8,128)(2,1)S(1)}, bf16[2,1024,128]{2,1,0:T(8,128)(2,1)S(1)}, u32[]{:S(2)}, u32[]{:S(2)}) collective-permute-start(bf16[2,1024,128]{2,1,0:T(8,128)(2,1)S(1)} %get-tuple-element.32), channel_id=1, source_target_pairs={{0,6},{1,7},{2,0},{3,1},{4,2},{5,3},{6,4},{7,5},{8,14},{9,15},{10,... | collective-permute-start | bytes 1572872 | tf_op jit(solution)/shard_map/ppermute | solution.py:107
  22.6 0.1 collective-permute-start
  22.7 2.7 %collective-permute-start.1 = (bf16[2,512,128]{2,1,0:T(8,128)(2,1)S(1)}, bf16[2,512,128]{2,1,0:T(8,128)(2,1)S(1)}, u32[]{:S(2)}, u32[]{:S(2)}) collective-permute-start(bf16[2,512,128]{2,1,0:T(8,128)(2,1)S(1)} %bitcast.53), channel_id=1, source_target_pairs={{0,6},{1,7},{2,0},{3,1},{4,2},{5,3},{6,4},{7,5},{8,14},{9,15},{10,... | collective-permute-start | bytes 786440 | tf_op jit(solution)/shard_map/ppermute | solution.py:107
  25.3 0.4 collective-permute-start.2
  25.8 0.1 broadcast_bitcast_fusion
  25.9 13.3 %collective-permute-done = bf16[2,512,128]{2,1,0:T(8,128)(2,1)S(1)} collective-permute-done((bf16[2,512,128]{2,1,0:T(8,128)(2,1)S(1)}, bf16[2,512,128]{2,1,0:T(8,128)(2,1)S(1)}, u32[]{:S(2)}, u32[]{:S(2)}) %collective-permute-start) | collective-permute-done | bytes 262176 | tf_op jit(solution)/shard_map/ppermute | solution.py:107
  39.2 6.7 %collective-permute-done.2 = bf16[2,512,128]{2,1,0:T(8,128)(2,1)S(1)} collective-permute-done((bf16[2,512,128]{2,1,0:T(8,128)(2,1)S(1)}, bf16[2,512,128]{2,1,0:T(8,128)(2,1)S(1)}, u32[]{:S(2)}, u32[]{:S(2)}) %collective-permute-start.2) | collective-permute-done | bytes 262176 | tf_op jit(solution)/shard_map/ppermute | solution.py:107
  46.0 0.7 copy-done.15
  46.7 0.8 copy-done.4
  47.5 0.8 copy-done.6
  48.3 4.2 %copy.47 = bf16[32,16,1280]{0,2,1:T(8,128)(2,1)} copy(bf16[32,16,1280]{2,1,0:T(8,128)(2,1)S(1)} %all-to-all-done) | data formatting | bytes 2621440 | tf_op jit(solution)/shard_map/optimization_barrier | solution.py:123
  52.5 0.1 slice.84
  52.7 0.7 slice.121
  53.4 0.1 copy.49
  53.5 0.1 add.192
  53.6 0.1 copy.48
  53.7 0.1 convert_element_type.72
  53.8 0.1 select_reduce_fusion.1
  53.9 0.2 select_reduce_fusion.3
  54.3 1.3 convolution_select_fusion
  55.6 0.7 fusion
  56.3 0.2 slice_add_fusion
  56.6 2.3 %collective-permute-start.6 = (f32[512,128]{0,1:T(8,128)S(1)}, f32[512,128]{0,1:T(8,128)S(1)}, u32[]{:S(2)}, u32[]{:S(2)}) collective-permute-start(f32[512,128]{0,1:T(8,128)S(1)} %pad_maximum_fusion.2), channel_id=1, source_target_pairs={{0,1},{1,0},{2,3},{3,2},{4,5},{5,4},{6,7},{7,6},{8,9},{9,8},{10,11... | collective-permute-start | bytes 786440 | tf_op jit(solution)/shard_map/ppermute | solution.py:161
  58.9 1.2 collective-permute-done.6
  60.1 1.4 %collective-permute-start.7 = (bf16[512,128]{0,1:T(8,128)(2,1)S(1)}, bf16[512,128]{0,1:T(8,128)(2,1)S(1)}, u32[]{:S(2)}, u32[]{:S(2)}) collective-permute-start(bf16[512,128]{0,1:T(8,128)(2,1)S(1)} %add_convert_fusion.1), channel_id=1, source_target_pairs={{0,2},{1,3},{2,4},{3,5},{4,6},{5,7},{6,0},{7,1},{8,10},{9,11},{10,... | collective-permute-start | bytes 393224 | tf_op jit(solution)/shard_map/ppermute | solution.py:164
  61.5 1.5 %collective-permute-start.8 = (bf16[512,128]{0,1:T(8,128)(2,1)S(1)}, bf16[512,128]{0,1:T(8,128)(2,1)S(1)}, u32[]{:S(2)}, u32[]{:S(2)}) collective-permute-start(bf16[512,128]{0,1:T(8,128)(2,1)S(1)} %add_convert_fusion.1), channel_id=1, source_target_pairs={{0,6},{1,7},{2,0},{3,1},{4,2},{5,3},{6,4},{7,5},{8,14},{9,15},{10,... | collective-permute-start | bytes 393224 | tf_op jit(solution)/shard_map/ppermute | solution.py:164
  63.0 1.6 %collective-permute-start.9 = (bf16[512,128]{0,1:T(8,128)(2,1)S(1)}, bf16[512,128]{0,1:T(8,128)(2,1)S(1)}, u32[]{:S(2)}, u32[]{:S(2)}) collective-permute-start(bf16[512,128]{0,1:T(8,128)(2,1)S(1)} %add_convert_fusion.1), channel_id=1, source_target_pairs={{0,4},{1,5},{2,6},{3,7},{4,0},{5,1},{6,2},{7,3},{8,12},{9,13},{10,... | collective-permute-start | bytes 393224 | tf_op jit(solution)/shard_map/ppermute | solution.py:164
  64.5 0.4 collective-permute-start.10
  64.9 3.7 %collective-permute-start.11 = (bf16[2,1024,128]{2,1,0:T(8,128)(2,1)}, bf16[2,1024,128]{2,1,0:T(8,128)(2,1)}, u32[]{:S(2)}, u32[]{:S(2)}) collective-permute-start(bf16[2,1024,128]{2,1,0:T(8,128)(2,1)} %get-tuple-element.30), channel_id=1, source_target_pairs={{0,7},{1,6},{2,1},{3,0},{4,3},{5,2},{6,5},{7,4},{8,15},{9,14},{10,... | collective-permute-start | bytes 1572872 | tf_op jit(solution)/shard_map/ppermute | solution.py:107
  68.6 0.4 copy.50
  69.0 1.2 collective-permute-done.9
  70.3 0.2 copy.51
  70.6 0.7 multiply_convert_fusion
  71.4 0.8 copy-done.2
  72.2 0.4 fusion.1
  72.6 1.1 pad_maximum_fusion
  73.7 8.2 %collective-permute-done.10 = bf16[2,1024,128]{2,1,0:T(8,128)(2,1)} collective-permute-done((bf16[2,1024,128]{2,1,0:T(8,128)(2,1)}, bf16[2,1024,128]{2,1,0:T(8,128)(2,1)}, u32[]{:S(2)}, u32[]{:S(2)}) %collective-permute-start.10) | collective-permute-done | bytes 524320 | tf_op jit(solution)/shard_map/ppermute | solution.py:107
  81.9 8.2 %all-to-all-start.1 = ((bf16[32,16,1152]{2,1,0:T(8,128)(2,1)}), bf16[32,16,1152]{2,1,0:T(8,128)(2,1)}, u32[]{:S(2)}, u32[]{:S(2)}) async-start(bf16[32,16,1152]{2,1,0:T(8,128)(2,1)} %bitcast.22), calls=%async_computation.1 | async-start | bytes 2359296 | tf_op jit(solution)/shard_map/all_to_all | solution.py:179
  90.1 0.9 collective-permute-start.13
  91.0 1.2 pad_maximum_fusion.1.same_ref
  92.2 0.1 collective-permute-start.5
  92.3 1.2 collective-permute-start.14
  93.5 1.8 %collective-permute-start.15 = (bf16[2,1024,128]{2,1,0:T(8,128)(2,1)}, bf16[2,1024,128]{2,1,0:T(8,128)(2,1)}, u32[]{:S(2)}, u32[]{:S(2)}) collective-permute-start(bf16[2,1024,128]{2,1,0:T(8,128)(2,1)} %get-tuple-element.27), channel_id=1, source_target_pairs={{0,7},{1,6},{2,1},{3,0},{4,3},{5,2},{6,5},{7,4},{8,15},{9,14},{10,... | collective-permute-start | bytes 1572872 | tf_op jit(solution)/shard_map/ppermute | solution.py:107
  95.4 0.8 copy-done.8
  96.1 2.7 %collective-permute-start.16 = (bf16[2,1024,128]{2,1,0:T(8,128)(2,1)}, bf16[2,1024,128]{2,1,0:T(8,128)(2,1)}, u32[]{:S(2)}, u32[]{:S(2)}) collective-permute-start(bf16[2,1024,128]{2,1,0:T(8,128)(2,1)} %collective-permute-done.11), channel_id=1, source_target_pairs={{0,6},{1,7},{2,0},{3,1},{4,2},{5,3},{6,4},{7,5},{8,14},{9,15},{10,... | collective-permute-start | bytes 1572872 | tf_op jit(solution)/shard_map/ppermute | solution.py:107
  98.8 0.1 copy.53.refs_10_
  99.0 9.5 %collective-permute-done.14.refs_5_ = bf16[2,1024,128]{2,1,0:T(8,128)(2,1)} collective-permute-done((bf16[2,1024,128]{2,1,0:T(8,128)(2,1)}, bf16[2,1024,128]{2,1,0:T(8,128)(2,1)}, u32[]{:S(2)}, u32[]{:S(2)}) %collective-permute-start.14) | collective-permute-done | bytes 524320 | tf_op jit(solution)/shard_map/ppermute | solution.py:107
  108.4 10.7 %collective-permute-done.12.refs_3_ = bf16[2,1024,128]{2,1,0:T(8,128)(2,1)} collective-permute-done((bf16[2,1024,128]{2,1,0:T(8,128)(2,1)}, bf16[2,1024,128]{2,1,0:T(8,128)(2,1)}, u32[]{:S(2)}, u32[]{:S(2)}) %collective-permute-start.12) | collective-permute-done | bytes 524320 | tf_op jit(solution)/shard_map/ppermute | solution.py:107
  119.1 2.2 %copy-done.1 = bf16[2,8192,128]{2,1,0:T(8,128)(2,1)S(1)} copy-done((bf16[2,8192,128]{2,1,0:T(8,128)(2,1)S(1)}, bf16[2,8192,128]{2,1,0:T(8,128)(2,1)}, u32[]{:S(2)}) %copy-start.1) | copy-done | bytes 4194328
  121.3 1.0 copy-done.3
  122.4 1.0 copy-done.5
  123.4 1.0 copy-done.7
  124.4 1.0 copy-done.9
  125.5 6.7 %shard_map.121 = bf16[512,1024]{1,0:T(8,128)(2,1)} custom-call(s32[1]{0:T(128)} %bitcast.place, bf16[4,2,512,128]{3,2,1,0:T(8,128)(2,1)S(1)} %pad_maximum_fusion.1.same_ref, bf16[4,2,512,128]{3,2,1,0:T(8,128)(2,1)} %collective-permute-done.5.other_ref, bf16[2,8192,128]{2,1,0:T(8,128)(2,1)S(1)} %copy-done.1, bf16[2,1024,128]{2,1,0:T(8,128)(2,1)S(1)} %copy-done.5, ...), custom_call_target="tpu_custom_call" | custom-call | flops 2684354560 | bytes 8388608 | tf_op jit(solution)/shard_map/pallas_call | solution.py:55
  132.2 2.0 %convert_reduce_fusion = f32[16,1024]{1,0:T(8,128)} fusion(bf16[32,16,1152]{2,1,0:T(8,128)(2,1)} %all-to-all-done.1), kind=kLoop, calls=%fused_computation | loop fusion | flops 1032192 | bytes 1114112 | tf_op jit(solution)/shard_map/reduce_sum | solution.py:180
  134.2 1.5 %convert_reduce_fusion.1 = f32[16,128]{1,0:T(8,128)} fusion(bf16[32,16,1152]{2,1,0:T(8,128)(2,1)} %all-to-all-done.1), kind=kLoop, calls=%fused_computation.11 | loop fusion | flops 129024 | bytes 139264 | tf_op jit(solution)/shard_map/reduce_sum | solution.py:181
  (62 shorter events, 0.7 us)
Async XLA Ops:
  0.6 55.0 %copy-start = (bf16[512,1024]{1,0:T(8,128)(2,1)S(1)}, bf16[512,1024]{1,0:T(8,128)(2,1)}, u32[]{:S(2)}) copy-start(bf16[512,1024]{1,0:T(8,128)(2,1)} %param.10) | copy-start | bytes 3145732
  4.1 44.2 %all-to-all-start = ((bf16[32,16,1280]{2,1,0:T(8,128)(2,1)}), bf16[32,16,1280]{2,1,0:T(8,128)(2,1)S(1)}, u32[]{:S(2)}, u32[]{:S(2)}) async-start(bf16[32,16,1280]{2,1,0:T(8,128)(2,1)} %broadcast_in_dim.91), calls=%async_computation | async-start | bytes 2621440 | tf_op jit(solution)/shard_map/all_to_all | solution.py:122
  16.1 6.4 %copy-start.12 = (bf16[512,2,128]{2,1,0:T(2,128)(2,1)S(1)}, bf16[512,2,128]{2,1,0:T(2,128)(2,1)}, u32[]{:S(2)}) copy-start(bf16[512,2,128]{2,1,0:T(2,128)(2,1)} %param.11) | copy-start | bytes 786436
  16.1 9.6 %copy-start.19 = (s32[8]{0:T(128)S(1)}, s32[8]{0:T(128)}, u32[]{:S(2)}) copy-start(s32[8]{0:T(128)} %param.15) | copy-start | bytes 100
  16.1 9.6 %copy-start.20 = (s32[4]{0:T(128)S(1)}, s32[4]{0:T(128)}, u32[]{:S(2)}) copy-start(s32[4]{0:T(128)} %param.16) | copy-start | bytes 52
  19.8 26.2 %collective-permute-start.3 = (bf16[2,1024,128]{2,1,0:T(8,128)(2,1)S(1)}, bf16[2,1024,128]{2,1,0:T(8,128)(2,1)S(1)}, u32[]{:S(2)}, u32[]{:S(2)}) collective-permute-start(bf16[2,1024,128]{2,1,0:T(8,128)(2,1)S(1)} %get-tuple-element.33), channel_id=1, source_target_pairs={{0,2},{1,3},{2,4},{3,5},{4,6},{5,7},{6,0},{7,1},{8,10},{9,11},{10,... | collective-permute-start | bytes 1572872 | tf_op jit(solution)/shard_map/ppermute | solution.py:107
  21.1 26.4 %collective-permute-start.4 = (bf16[2,1024,128]{2,1,0:T(8,128)(2,1)S(1)}, bf16[2,1024,128]{2,1,0:T(8,128)(2,1)S(1)}, u32[]{:S(2)}, u32[]{:S(2)}) collective-permute-start(bf16[2,1024,128]{2,1,0:T(8,128)(2,1)S(1)} %get-tuple-element.32), channel_id=1, source_target_pairs={{0,6},{1,7},{2,0},{3,1},{4,2},{5,3},{6,4},{7,5},{8,14},{9,15},{10,... | collective-permute-start | bytes 1572872 | tf_op jit(solution)/shard_map/ppermute | solution.py:107
  22.5 23.4 %copy-start.10 = (bf16[512,2,128]{2,0,1:T(8,128)(2,1)}, bf16[512,2,128]{2,0,1:T(8,128)(2,1)S(1)}, u32[]{:S(2)}) copy-start(bf16[512,2,128]{2,0,1:T(8,128)(2,1)S(1)} %copy.57) | copy-start | bytes 786436
  22.6 16.6 %collective-permute-start = (bf16[2,512,128]{2,1,0:T(8,128)(2,1)S(1)}, bf16[2,512,128]{2,1,0:T(8,128)(2,1)S(1)}, u32[]{:S(2)}, u32[]{:S(2)}) collective-permute-start(bf16[2,512,128]{2,1,0:T(8,128)(2,1)S(1)} %bitcast.52), channel_id=1, source_target_pairs={{0,2},{1,3},{2,4},{3,5},{4,6},{5,7},{6,0},{7,1},{8,10},{9,11},{10,... | collective-permute-start | bytes 786440 | tf_op jit(solution)/shard_map/ppermute | solution.py:107
  22.7 16.5 %collective-permute-start.1 = (bf16[2,512,128]{2,1,0:T(8,128)(2,1)S(1)}, bf16[2,512,128]{2,1,0:T(8,128)(2,1)S(1)}, u32[]{:S(2)}, u32[]{:S(2)}) collective-permute-start(bf16[2,512,128]{2,1,0:T(8,128)(2,1)S(1)} %bitcast.53), channel_id=1, source_target_pairs={{0,6},{1,7},{2,0},{3,1},{4,2},{5,3},{6,4},{7,5},{8,14},{9,15},{10,... | collective-permute-start | bytes 786440 | tf_op jit(solution)/shard_map/ppermute | solution.py:107
  25.3 20.6 %collective-permute-start.2 = (bf16[2,512,128]{2,1,0:T(8,128)(2,1)S(1)}, bf16[2,512,128]{2,1,0:T(8,128)(2,1)S(1)}, u32[]{:S(2)}, u32[]{:S(2)}) collective-permute-start(bf16[2,512,128]{2,1,0:T(8,128)(2,1)S(1)} %bitcast.54), channel_id=1, source_target_pairs={{0,4},{1,5},{2,6},{3,7},{4,0},{5,1},{6,2},{7,3},{8,12},{9,13},{10,... | collective-permute-start | bytes 786440 | tf_op jit(solution)/shard_map/ppermute | solution.py:107
  39.2 6.7 %copy-start.13 = (bf16[2,512,128]{2,1,0:T(8,128)(2,1)}, bf16[2,512,128]{2,1,0:T(8,128)(2,1)S(1)}, u32[]{:S(2)}) copy-start(bf16[2,512,128]{2,1,0:T(8,128)(2,1)S(1)} %collective-permute-done) | copy-start | bytes 786436
  39.2 6.7 %copy-start.14 = (bf16[2,512,128]{2,1,0:T(8,128)(2,1)}, bf16[2,512,128]{2,1,0:T(8,128)(2,1)S(1)}, u32[]{:S(2)}) copy-start(bf16[2,512,128]{2,1,0:T(8,128)(2,1)S(1)} %collective-permute-done.1) | copy-start | bytes 786436
  45.9 0.7 copy-start.15
  46.6 0.8 copy-start.4
  47.5 0.8 copy-start.6
  52.5 1.4 %copy-start.17 = (s32[4]{0:T(128)S(1)}, s32[4]{0:T(128)}, u32[]{:S(2)}) copy-start(s32[4]{0:T(128)} %param.18) | copy-start | bytes 52
  52.5 1.6 %copy-start.16 = (f32[4]{0:T(128)S(1)}, f32[4]{0:T(128)}, u32[]{:S(2)}) copy-start(f32[4]{0:T(128)} %param.19) | copy-start | bytes 52
  52.5 1.6 %copy-start.18 = (s32[4]{0:T(128)S(1)}, s32[4]{0:T(128)}, u32[]{:S(2)}) copy-start(s32[4]{0:T(128)} %param.17) | copy-start | bytes 52
  56.6 3.5 %collective-permute-start.6 = (f32[512,128]{0,1:T(8,128)S(1)}, f32[512,128]{0,1:T(8,128)S(1)}, u32[]{:S(2)}, u32[]{:S(2)}) collective-permute-start(f32[512,128]{0,1:T(8,128)S(1)} %pad_maximum_fusion.2), channel_id=1, source_target_pairs={{0,1},{1,0},{2,3},{3,2},{4,5},{5,4},{6,7},{7,6},{8,9},{9,8},{10,11... | collective-permute-start | bytes 786440 | tf_op jit(solution)/shard_map/ppermute | solution.py:161
  60.1 8.9 %collective-permute-start.7 = (bf16[512,128]{0,1:T(8,128)(2,1)S(1)}, bf16[512,128]{0,1:T(8,128)(2,1)S(1)}, u32[]{:S(2)}, u32[]{:S(2)}) collective-permute-start(bf16[512,128]{0,1:T(8,128)(2,1)S(1)} %add_convert_fusion.1), channel_id=1, source_target_pairs={{0,2},{1,3},{2,4},{3,5},{4,6},{5,7},{6,0},{7,1},{8,10},{9,11},{10,... | collective-permute-start | bytes 393224 | tf_op jit(solution)/shard_map/ppermute | solution.py:164
  61.5 7.6 %collective-permute-start.8 = (bf16[512,128]{0,1:T(8,128)(2,1)S(1)}, bf16[512,128]{0,1:T(8,128)(2,1)S(1)}, u32[]{:S(2)}, u32[]{:S(2)}) collective-permute-start(bf16[512,128]{0,1:T(8,128)(2,1)S(1)} %add_convert_fusion.1), channel_id=1, source_target_pairs={{0,6},{1,7},{2,0},{3,1},{4,2},{5,3},{6,4},{7,5},{8,14},{9,15},{10,... | collective-permute-start | bytes 393224 | tf_op jit(solution)/shard_map/ppermute | solution.py:164
  63.0 7.2 %collective-permute-start.9 = (bf16[512,128]{0,1:T(8,128)(2,1)S(1)}, bf16[512,128]{0,1:T(8,128)(2,1)S(1)}, u32[]{:S(2)}, u32[]{:S(2)}) collective-permute-start(bf16[512,128]{0,1:T(8,128)(2,1)S(1)} %add_convert_fusion.1), channel_id=1, source_target_pairs={{0,4},{1,5},{2,6},{3,7},{4,0},{5,1},{6,2},{7,3},{8,12},{9,13},{10,... | collective-permute-start | bytes 393224 | tf_op jit(solution)/shard_map/ppermute | solution.py:164
  64.5 17.3 %collective-permute-start.10 = (bf16[2,1024,128]{2,1,0:T(8,128)(2,1)}, bf16[2,1024,128]{2,1,0:T(8,128)(2,1)}, u32[]{:S(2)}, u32[]{:S(2)}) collective-permute-start(bf16[2,1024,128]{2,1,0:T(8,128)(2,1)} %get-tuple-element.31), channel_id=1, source_target_pairs={{0,2},{1,3},{2,4},{3,5},{4,6},{5,7},{6,0},{7,1},{8,10},{9,11},{10,... | collective-permute-start | bytes 1572872 | tf_op jit(solution)/shard_map/ppermute | solution.py:107
  64.9 16.9 %collective-permute-start.11 = (bf16[2,1024,128]{2,1,0:T(8,128)(2,1)}, bf16[2,1024,128]{2,1,0:T(8,128)(2,1)}, u32[]{:S(2)}, u32[]{:S(2)}) collective-permute-start(bf16[2,1024,128]{2,1,0:T(8,128)(2,1)} %get-tuple-element.30), channel_id=1, source_target_pairs={{0,7},{1,6},{2,1},{3,0},{4,3},{5,2},{6,5},{7,4},{8,15},{9,14},{10,... | collective-permute-start | bytes 1572872 | tf_op jit(solution)/shard_map/ppermute | solution.py:107
  70.6 1.6 %copy-start.11 = (bf16[512,2,128]{2,0,1:T(8,128)(2,1)S(1)}, bf16[512,2,128]{2,0,1:T(8,128)(2,1)}, u32[]{:S(2)}) copy-start(bf16[512,2,128]{2,0,1:T(8,128)(2,1)} %copy-done.10) | copy-start | bytes 786436
  71.3 0.8 copy-start.2
  81.9 50.3 %all-to-all-start.1 = ((bf16[32,16,1152]{2,1,0:T(8,128)(2,1)}), bf16[32,16,1152]{2,1,0:T(8,128)(2,1)}, u32[]{:S(2)}, u32[]{:S(2)}) async-start(bf16[32,16,1152]{2,1,0:T(8,128)(2,1)} %bitcast.22), calls=%async_computation.1 | async-start | bytes 2359296 | tf_op jit(solution)/shard_map/all_to_all | solution.py:179
  90.1 5.2 %collective-permute-start.13 = (bf16[2,1024,128]{2,1,0:T(8,128)(2,1)}, bf16[2,1024,128]{2,1,0:T(8,128)(2,1)S(1)}, u32[]{:S(2)}, u32[]{:S(2)}) collective-permute-start(bf16[2,1024,128]{2,1,0:T(8,128)(2,1)} %get-tuple-element.29), channel_id=1, source_target_pairs={{0,1},{1,0},{2,3},{3,2},{4,5},{5,4},{6,7},{7,6},{8,9},{9,8},{10,11... | collective-permute-start | bytes 1572872 | tf_op jit(solution)/shard_map/ppermute | solution.py:107
  92.2 26.9 %collective-permute-start.5 = (bf16[4,2,512,128]{3,2,1,0:T(8,128)(2,1)S(1)}, bf16[4,2,512,128]{3,2,1,0:T(8,128)(2,1)}, u32[]{:S(2)}, u32[]{:S(2)}) collective-permute-start(bf16[4,2,512,128]{3,2,1,0:T(8,128)(2,1)S(1)} %pad_maximum_fusion.1.same_ref), channel_id=1, source_target_pairs={{0,1},{1,0},{2,3},{3,2},{4,5},{5,4},{6,7},{7,6},{8,9},{9,8},{10,11... | collective-permute-start | bytes 3145736 | tf_op jit(solution)/shard_map/ppermute | solution.py:107
  92.3 16.1 %collective-permute-start.14 = (bf16[2,1024,128]{2,1,0:T(8,128)(2,1)}, bf16[2,1024,128]{2,1,0:T(8,128)(2,1)}, u32[]{:S(2)}, u32[]{:S(2)}) collective-permute-start(bf16[2,1024,128]{2,1,0:T(8,128)(2,1)} %get-tuple-element.28), channel_id=1, source_target_pairs={{0,3},{1,2},{2,5},{3,4},{4,7},{5,6},{6,1},{7,0},{8,11},{9,10},{10,... | collective-permute-start | bytes 1572872 | tf_op jit(solution)/shard_map/ppermute | solution.py:107
  93.5 14.9 %collective-permute-start.15 = (bf16[2,1024,128]{2,1,0:T(8,128)(2,1)}, bf16[2,1024,128]{2,1,0:T(8,128)(2,1)}, u32[]{:S(2)}, u32[]{:S(2)}) collective-permute-start(bf16[2,1024,128]{2,1,0:T(8,128)(2,1)} %get-tuple-element.27), channel_id=1, source_target_pairs={{0,7},{1,6},{2,1},{3,0},{4,3},{5,2},{6,5},{7,4},{8,15},{9,14},{10,... | collective-permute-start | bytes 1572872 | tf_op jit(solution)/shard_map/ppermute | solution.py:107
  95.3 23.8 %collective-permute-start.12 = (bf16[2,1024,128]{2,1,0:T(8,128)(2,1)}, bf16[2,1024,128]{2,1,0:T(8,128)(2,1)}, u32[]{:S(2)}, u32[]{:S(2)}) collective-permute-start(bf16[2,1024,128]{2,1,0:T(8,128)(2,1)} %collective-permute-done.10), channel_id=1, source_target_pairs={{0,2},{1,3},{2,4},{3,5},{4,6},{5,7},{6,0},{7,1},{8,10},{9,11},{10,... | collective-permute-start | bytes 1572872 | tf_op jit(solution)/shard_map/ppermute | solution.py:107
  95.3 0.8 copy-start.8
  96.1 23.0 %collective-permute-start.16 = (bf16[2,1024,128]{2,1,0:T(8,128)(2,1)}, bf16[2,1024,128]{2,1,0:T(8,128)(2,1)}, u32[]{:S(2)}, u32[]{:S(2)}) collective-permute-start(bf16[2,1024,128]{2,1,0:T(8,128)(2,1)} %collective-permute-done.11), channel_id=1, source_target_pairs={{0,6},{1,7},{2,0},{3,1},{4,2},{5,3},{6,4},{7,5},{8,14},{9,15},{10,... | collective-permute-start | bytes 1572872 | tf_op jit(solution)/shard_map/ppermute | solution.py:107
  119.1 2.2 %copy-start.1 = (bf16[2,8192,128]{2,1,0:T(8,128)(2,1)S(1)}, bf16[2,8192,128]{2,1,0:T(8,128)(2,1)}, u32[]{:S(2)}) copy-start(bf16[2,8192,128]{2,1,0:T(8,128)(2,1)} %refs_0_.1) | copy-start | bytes 12582916
  121.3 1.0 copy-start.3
  122.4 1.0 copy-start.5
  123.4 1.0 copy-start.7
  124.4 1.0 copy-start.9

commit v3 on v1

v3 whole, which is shorter than its diff:
```python
import jax
import jax.numpy as jnp
from jax import lax
from jax.experimental import pallas as pl
from jax.experimental.pallas import tpu as pltpu
from jax.sharding import PartitionSpec as P

BLOCK = 128
GSIZE = 8
SLOTS = 8
RANK = 64
LANES = 128
CHIPS = 4
LOWRANK_MULTIPLIER = 2.0
BF = jnp.bfloat16
F32 = jnp.float32
VMEM = pl.BlockSpec(memory_space=pltpu.VMEM)
SMEM = pl.BlockSpec(memory_space=pltpu.SMEM)


def dot(a, b, ca, cb):
    return lax.dot_general(a, b, (((ca,), (cb,)), ((), ())), preferred_element_type=F32)


def call(kernel, in_specs, shapes, flops, mib):
    single = not isinstance(shapes, (list, tuple))
    shapes = [shapes] if single else list(shapes)
    return pl.pallas_call(
        kernel,
        in_specs=in_specs,
        out_specs=VMEM if single else [VMEM] * len(shapes),
        out_shape=shapes[0] if single else shapes,
        compiler_params=pltpu.CompilerParams(vmem_limit_bytes=mib * 2**20),
        cost_estimate=pl.CostEstimate(flops=flops, bytes_accessed=2**20, transcendentals=0),
    )


def tensor_send(value, chip_step, core_flip):
    pairs = [
        (y * 2 + c, (y + chip_step) % CHIPS * 2 + (c ^ core_flip))
        for y in range(CHIPS)
        for c in range(2)
    ]
    return lax.ppermute(value, "tensor", pairs)


def x_send(value, step):
    pairs = [(i, i // 4 * 4 + (i + step) % 4) for i in range(lax.axis_size("dp"))]
    return lax.ppermute(value, "dp", pairs)


def pack_kernel(prompt, reward, down_ref, up_ref, out_ref):
    shape = (down_ref.shape[0], LANES)
    row = lax.broadcasted_iota(jnp.int32, shape, 0)
    lane = lax.broadcasted_iota(jnp.int32, shape, 1)
    blocks = reward.shape[0]
    rewards = jnp.zeros(shape, F32)
    prompts = jnp.full(shape, -1.0, F32)
    for b in range(blocks):
        rewards = jnp.where(lane % blocks == b, reward[b], rewards)
        prompts = jnp.where(lane == b, prompt[b].astype(F32), prompts)
    high = rewards.astype(BF).astype(F32)
    rest = rewards - high
    middle = rest.astype(BF).astype(F32)
    part = lane // blocks
    parts = jnp.where(part == 0, high, jnp.where(part == 1, middle, rest - middle))
    parts = jnp.where(part < 3, parts, 0.0)
    facts = jnp.where(row == 0, parts, jnp.where(row == 1, prompts, 0.0)).astype(BF)
    packed = jnp.concatenate([down_ref[...], up_ref[...], facts], axis=1)
    for i in range(out_ref.shape[0]):
        out_ref[i] = packed


def factor_rows(ref, slot, start, size):
    owners = ref.shape[0] // SLOTS
    return ref[pl.ds(slot * owners, owners), :, pl.ds(start, size)].reshape(RANK, size)


def low_kernel(
    slots, live, prompt, reward, gathered_ref, x_ref, cot_ref, low_ref, weighted_ref, coef_ref
):
    window = x_ref.shape[1]
    columns = cot_ref.shape[2]
    blocks = reward.shape[0]
    facts = gathered_ref[:, :, window + columns :].astype(F32)
    row = lax.broadcasted_iota(jnp.int32, facts.shape, 1)
    parts = jnp.sum(jnp.where(row == 0, facts, 0.0), axis=1)
    prompts = jnp.sum(jnp.where(row == 1, facts, 0.0), axis=1)
    rewards = parts + pltpu.roll(parts, LANES - blocks, 1)
    rewards = rewards + pltpu.roll(parts, LANES - 2 * blocks, 1)
    place = lax.broadcasted_iota(jnp.int32, (BLOCK, 1), 0)
    whole = lambda v: jnp.sum(jnp.sum(v, axis=1, keepdims=True), axis=0, keepdims=True)
    for b in range(blocks):
        same = prompts == prompt[b].astype(F32)
        mean = whole(jnp.where(same, rewards, 0.0)) / GSIZE
        square = whole(jnp.where(same, rewards * rewards, 0.0)) / GSIZE
        spread = jnp.sqrt(jnp.maximum(square - mean * mean, 1.0))
        advantage = (reward[b] - mean) / spread
        coef = jnp.where(place < live[b], -advantage / GSIZE, 0.0)
        rows = pl.ds(b * BLOCK, BLOCK)
        weighted = (cot_ref[1, rows, :].astype(F32) * coef).astype(BF)
        low_h = dot(x_ref[rows, :], factor_rows(gathered_ref, slots[b], 0, window), 1, 1)
        low_g = dot(weighted, factor_rows(gathered_ref, slots[b], window, columns), 1, 1)
        low_ref[rows, :] = jnp.concatenate([low_h, low_g], axis=1)
        weighted_ref[rows, :] = weighted
        coef_ref[rows, :] = coef


def terms_kernel(slots, own, first, second, third, x_ref, weighted_ref, terms_ref, low_ref):
    window = x_ref.shape[1]
    columns = weighted_ref.shape[1]
    owners, owned = terms_ref.shape[0] // SLOTS, terms_ref.shape[1]
    low = own[...].astype(F32) + first[...].astype(F32)
    low = (low + second[...].astype(F32)) + third[...].astype(F32)
    low_ref[...] = low.astype(BF)
    for i in range(terms_ref.shape[0]):
        terms_ref[i] = jnp.zeros(terms_ref.shape[1:], BF)
    for b in range(x_ref.shape[0] // BLOCK):
        rows = pl.ds(b * BLOCK, BLOCK)
        low = low_ref[rows, :]
        down = LOWRANK_MULTIPLIER * dot(low, x_ref[rows, :], 0, 0)[RANK:]
        up = LOWRANK_MULTIPLIER * dot(low, weighted_ref[rows, :], 0, 0)[:RANK]
        place = pl.ds(slots[b] * owners, owners)
        terms_ref[place, :, :window] = down.astype(BF).reshape(owners, owned, window)
        terms_ref[place, :, window:] = up.astype(BF).reshape(owners, owned, columns)


def frozen_kernel(slots, quarters, *refs):
    *cot_refs, gathered_ref, low_ref, coef_ref, w0, w1, w2, w3a, w3b, out_ref, weighted = refs
    tile = w0.shape[2]
    columns = w0.shape[3]
    coef = coef_ref[...]
    at = 0
    for ref in cot_refs:
        for i in range(ref.shape[0] // 2):
            for j in range(2):
                both = ref[2 * i + j].astype(F32) * coef
                weighted[:, at : at + columns] = both.astype(BF)
                at += columns
    for r, parts in enumerate(((w0,), (w1,), (w2,), (w3a, w3b))):
        slabs = [p[i, j] for p in parts for i in range(p.shape[0]) for j in range(2)]
        total = dot(weighted[...], jnp.concatenate(slabs, axis=1), 1, 1)
        start = pl.multiple_of(quarters[r] * tile, tile)
        for b in range(total.shape[0] // BLOCK):
            rows = slice(b * BLOCK, (b + 1) * BLOCK)
            factor = factor_rows(gathered_ref, slots[b], start, tile)
            factor = jnp.concatenate([jnp.zeros_like(factor), factor], axis=0)
            extra = LOWRANK_MULTIPLIER * dot(low_ref[rows, :], factor, 1, 0)
            out_ref[rows, pl.ds(start, tile)] = (total[rows] + extra).astype(BF)


def sum_kernel(terms_ref, down_ref, up_ref):
    window = down_ref.shape[1]
    total = terms_ref[0].astype(F32)
    for i in range(1, terms_ref.shape[0]):
        total = total + terms_ref[i].astype(F32)
    down_ref[...] = total[:, :window]
    up_ref[...] = total[:, window:]


def shards(
    normed_input_rows,
    key_value_cotangent,
    key_value_weight,
    adapter_down_factors,
    adapter_up_factors,
    slot_adapter,
    adapter_of_block,
    live_rows_of_block,
    prompt_of_block,
    reward_of_block,
):
    rows, window = normed_input_rows.shape
    columns = key_value_cotangent.shape[2]
    dp = lax.axis_size("dp")
    owned = adapter_down_factors.shape[0]
    te = lax.axis_index("tensor")
    chip, core = te // 2, te % 2
    x = lax.axis_index("dp") % 4
    tile = window // 4
    shape = jax.ShapeDtypeStruct
    slots = jnp.sum(
        jnp.where(
            adapter_of_block[:, None] == slot_adapter[None, :], jnp.arange(SLOTS, dtype=jnp.int32), 0
        ),
        axis=1,
    )

    packed = call(
        pack_kernel, [SMEM, SMEM, VMEM, VMEM], shape((dp, owned, window + columns + LANES), BF), 0, 8
    )(prompt_of_block, reward_of_block, adapter_down_factors, adapter_up_factors)
    gathered = lax.all_to_all(packed, "dp", 0, 0)

    def quarter(chip_step, core_flip):
        target = ((chip + chip_step) % CHIPS) * 2 + (core + core_flip) % 2
        start = target * window + x * tile
        return lax.dynamic_slice_in_dim(key_value_weight, start, tile, 1)

    before = tensor_send(jnp.stack([quarter(1, 0), quarter(1, 1), quarter(2, 0)]), 1, 0)
    after = tensor_send(jnp.stack([quarter(3, 0), quarter(3, 1), quarter(2, 1)]), 3, 0)
    across = tensor_send(before[2], 1, 0)
    across_other = tensor_send(after[2], 3, 0)
    other = jnp.stack([quarter(0, 1), before[1], after[1], across_other])
    slabs = jnp.concatenate(
        [jnp.stack([quarter(0, 0), before[0], after[0], across]), tensor_send(other, 0, 1)]
    )
    gathered, slabs = lax.optimization_barrier((gathered, slabs))

    cotangent = jnp.transpose(key_value_cotangent, (1, 0, 2))
    low, weighted_value, coef = call(
        low_kernel,
        [SMEM] * 4 + [VMEM] * 3,
        [shape((rows, 2 * RANK), F32), shape((rows, columns), BF), shape((rows, 1), F32)],
        2 * rows * RANK * window,
        16,
    )(
        slots,
        live_rows_of_block,
        prompt_of_block,
        reward_of_block,
        gathered,
        normed_input_rows,
        cotangent,
    )
    low = (low + tensor_send(low, 0, 1)).astype(BF)
    lows = [low] + [tensor_send(low, s, 0) for s in (1, 3, 2)]
    slabs_left, slabs_right = x_send(slabs, 1), x_send(slabs, 3)

    terms, low = call(
        terms_kernel,
        [SMEM] + [VMEM] * 6,
        [shape((dp, owned, window + columns), BF), shape((rows, 2 * RANK), BF)],
        4 * rows * RANK * window,
        16,
    )(slots, *lows, normed_input_rows, weighted_value)
    terms, slabs_left, slabs_right = lax.optimization_barrier((terms, slabs_left, slabs_right))
    terms = lax.all_to_all(terms, "dp", 0, 0)

    slabs_far = (x_send(slabs_left[:4], 1), x_send(slabs_right[4:], 3))
    cot_before, cot_after = tensor_send(cotangent, 1, 0), tensor_send(cotangent, 3, 0)
    relay = [(y * 2 + c, (y + 1 + 2 * c) % CHIPS * 2 + c) for y in range(CHIPS) for c in range(2)]
    cot_across = lax.ppermute(jnp.where(core == 0, cot_before, cot_after), "tensor", relay)
    cots = jnp.concatenate([cotangent, cot_before, cot_after, cot_across])
    cots_other = tensor_send(cots, 0, 1)
    quarters = (x + jnp.array([0, 3, 1, 2], jnp.int32)) % 4
    input_gradient = pl.pallas_call(
        frozen_kernel,
        in_specs=[SMEM] * 2 + [VMEM] * 10,
        out_specs=VMEM,
        out_shape=shape((rows, window), BF),
        scratch_shapes=[pltpu.VMEM((rows, 16 * columns), BF)],
        compiler_params=pltpu.CompilerParams(vmem_limit_bytes=28 * 2**20),
        cost_estimate=pl.CostEstimate(
            flops=2 * rows * window * 18 * columns, bytes_accessed=8 * 2**20, transcendentals=0
        ),
    )(
        slots,
        quarters,
        cots,
        cots_other,
        gathered,
        low,
        coef,
        slabs,
        slabs_left,
        slabs_right,
        *slabs_far,
    )
    grad_a, grad_b = call(
        sum_kernel,
        [VMEM],
        [shape((owned, window), F32), shape((owned, columns), F32)],
        0,
        8,
    )(terms)
    return (input_gradient, grad_a, grad_b)


def solution(mesh):
    in_specs = (
        P("dp", "tensor"),
        P("dp", None, "tensor"),
        P(None, None, "tensor"),
        P("dp", "tensor"),
        P("dp", "tensor"),
        P(),
        P("dp"),
        P("dp"),
        P("dp"),
        P("dp"),
    )
    out_specs = (P("dp", "tensor"), P("dp", "tensor"), P("dp", "tensor"))
    return jax.shard_map(shards, mesh=mesh, in_specs=in_specs, out_specs=out_specs, check_vma=False)
```

time: 191 us -> 129 us (0.68); the launches traced: 187 us -> 128 us
  matrix products: 51.3 us -> 0 us
  starting transfers between devices: 61.9 us -> 47 us
  Pallas kernels: 0 us -> 10.1 us
  waiting for transfers between devices: 50.6 us -> 55.4 us
  local copies, waits for them, and re-layouts: 16.4 us -> 12.3 us
  other arithmetic: 5.66 us -> 2.62 us
    dot_general x21 -> x0, matrix products: 51.3 us -> none  [dot(): lax.dot_general(a, b, (((ca,), (cb,)), ((), ())), preferred_element_type=...]
    ppermute x18 -> x17, waiting for transfers between devices: 41.9 us -> 53.1 us  [the longest x12 28.2 us: tensor_send(): return lax.ppermute(value, 'tensor', pairs)]
    ppermute x18 -> x17, starting transfers between devices: 40.3 us -> 30 us  [the longest x12 23.8 us: tensor_send(): return lax.ppermute(value, 'tensor', pairs)]
    pallas_call x0 -> x5, Pallas kernels: none -> 10.1 us  [the longest x1 5.19 us: shards(): pl.pallas_call(frozen_kernel, in_specs=[SMEM] * 2 + [VMEM] * 10, out_spec...]
    all_to_all x1, waiting for transfers between devices: 8.63 us -> 0.01 us  [shards(): terms = lax.all_to_all(terms, 'dp', 0, 0)]
    all_to_all x1, starting transfers between devices: 9.72 us -> 5.14 us  [shards(): terms = lax.all_to_all(terms, 'dp', 0, 0)]
    dynamic_slice x1 -> x0, local copies, waits for them, and re-layouts: 3.89 us -> none  [shards(): lax.dynamic_slice_in_dim(key_value_weight, target * window, window, 1)]
    all_to_all x1, waiting for transfers between devices: 0.01 us -> 2.25 us  [shards(): gathered = lax.all_to_all(packed, 'dp', 0, 0)]
  transfers between devices with their start and end apart: 20 -> 19, of which waited for: 7 -> 14; matrix products, arithmetic and copies ran while one was open for 36% -> 8% of each run, Pallas kernels for 0% -> 6%
where the time goes in v3:
time: 129 us; the launch traced here: 128 us
  waiting for transfers between devices  55.4 us (43%)
  starting transfers between devices  47 us (36%)
  local copies, waits for them, and re-layouts  12.3 us (10%)
  Pallas kernels  10.1 us (8%)
  other arithmetic  2.62 us (2%)
    ppermute x12, waiting for transfers between devices, tensor_send(): return lax.ppermute(value, 'tensor', pairs)  28.2 us
    ppermute x12, starting transfers between devices, tensor_send(): return lax.ppermute(value, 'tensor', pairs)  23.8 us
    ppermute x4, waiting for transfers between devices, x_send(): return lax.ppermute(value, 'dp', pairs)  19.4 us
    all_to_all x1, starting transfers between devices, shards(): gathered = lax.all_to_all(packed, 'dp', 0, 0)  11.9 us
    unnamed x37, local copies, waits for them, and re-layouts  7.69 us
    ppermute x4, starting transfers between devices, x_send(): return lax.ppermute(value, 'dp', pairs)  6.05 us
    ppermute x1, waiting for transfers between devices, shards(): lax.ppermute(jnp.where(core == 0, cot_before, cot_after), 'tensor', relay)  5.5 us
    pallas_call x1, Pallas kernels, shards(): pl.pallas_call(frozen_kernel, in_specs=[SMEM] * 2 + [VMEM] * 10, out_spec...  5.19 us
  transfers between devices with their start and end apart: 19, of which 14 were waited for; matrix products, arithmetic and copies ran while one was open for 8% of the time, Pallas kernels for 6%

profile of v3, /device:TPU:1, one launch (start us, length us, event | category | flops | bytes accessed | tf_op | source)
XLA Modules:
  0.0 128.4 jit_solution(10195471329274732454)
XLA Ops:
  0.6 0.7 copy-done.7
  1.4 0.7 copy-done.8
  2.1 0.7 copy-done.9
  2.7 0.7 copy-done.11
  3.4 1.7 %shard_map.130 = bf16[32,16,1280]{2,1,0:T(8,128)(2,1)} custom-call(s32[4]{0:T(128)S(1)} %copy-done.9, f32[4]{0:T(128)S(1)} %copy-done.11, bf16[16,1024]{1,0:T(8,128)(2,1)S(1)} %copy-done.7, bf16[16,128]{1,0:T(8,128)(2,1)S(1)} %copy-done.8), custom_call_target="tpu_custom_call" | custom-call | bytes 1048576 | tf_op jit(solution)/shard_map/pallas_call | solution.py:189
  5.1 11.9 %all-to-all-start = ((bf16[32,16,1280]{2,1,0:T(8,128)(2,1)}), bf16[32,16,1280]{2,1,0:T(8,128)(2,1)S(1)}, u32[]{:S(2)}, u32[]{:S(2)}) async-start(bf16[32,16,1280]{2,1,0:T(8,128)(2,1)} %shard_map.130), calls=%async_computation | async-start | bytes 2621440 | tf_op jit(solution)/shard_map/all_to_all | solution.py:192
  17.1 1.3 %dynamic-slice_bitcast_fusion = (bf16[1,2,256,128]{3,2,1,0:T(8,128)(2,1)S(1)}, bf16[1,2,256,128]{3,2,1,0:T(8,128)(2,1)S(1)}, bf16[1,2,256,128]{3,2,1,0:T(8,128)(...) fusion(bf16[2,8192,128]{2,1,0:T(8,128)(2,1)} %param.13, ...), kind=kLoop, calls=%fused_computation.13 | loop fusion | bytes 1835036 | tf_op jit(solution)/shard_map/stack | solution.py:203
  18.5 1.4 %collective-permute-start.4 = (bf16[3,2,256,128]{3,2,1,0:T(8,128)(2,1)S(1)}, bf16[3,2,256,128]{3,2,1,0:T(8,128)(2,1)S(1)}, u32[]{:S(2)}, u32[]{:S(2)}) collective-permute-start(bf16[3,2,256,128]{3,2,1,0:T(8,128)(2,1)S(1)} %pad_maximum_fusion.2), channel_id=1, source_target_pairs={{0,2},{1,3},{2,4},{3,5},{4,6},{5,7},{6,0},{7,1},{8,10},{9,11},{10,... | collective-permute-start | bytes 1179656 | tf_op jit(solution)/shard_map/ppermute | solution.py:44
  20.0 1.5 %collective-permute-start.5 = (bf16[3,2,256,128]{3,2,1,0:T(8,128)(2,1)S(1)}, bf16[3,2,256,128]{3,2,1,0:T(8,128)(2,1)S(1)}, u32[]{:S(2)}, u32[]{:S(2)}) collective-permute-start(bf16[3,2,256,128]{3,2,1,0:T(8,128)(2,1)S(1)} %pad_maximum_fusion.3), channel_id=1, source_target_pairs={{0,6},{1,7},{2,0},{3,1},{4,2},{5,3},{6,4},{7,5},{8,14},{9,15},{10,... | collective-permute-start | bytes 1179656 | tf_op jit(solution)/shard_map/ppermute | solution.py:44
  21.5 1.6 %bitcast_dynamic-update-slice_fusion.1 = bf16[8,2,256,128]{3,2,1,0:T(8,128)(2,1)} fusion(bf16[2,8192,128]{2,1,0:T(8,128)(2,1)} %param.13, s32[]{:T(128)S(6)} %select_n.110), kind=kLoop, calls=%fused_computation.12 | loop fusion | bytes 262148
  23.1 6.6 %collective-permute-done.4 = bf16[3,2,256,128]{3,2,1,0:T(8,128)(2,1)S(1)} collective-permute-done((bf16[3,2,256,128]{3,2,1,0:T(8,128)(2,1)S(1)}, bf16[3,2,256,128]{3,2,1,0:T(8,128)(2,1)S(1)}, u32[]{:S(2)}, u32[]{:S(2)}) %collective-permute-start.4) | collective-permute-done | bytes 393248 | tf_op jit(solution)/shard_map/ppermute | solution.py:44
  29.6 0.7 fusion.1
  30.3 0.0 collective-permute-done.5
  30.3 0.7 fusion.2
  31.0 1.9 %collective-permute-start.7 = (bf16[2,256,128]{2,1,0:T(8,128)(2,1)S(1)}, bf16[2,256,128]{2,1,0:T(8,128)(2,1)S(1)}, u32[]{:S(2)}, u32[]{:S(2)}) collective-permute-start(bf16[2,256,128]{2,1,0:T(8,128)(2,1)S(1)} %get-tuple-element.38), channel_id=1, source_target_pairs={{0,6},{1,7},{2,0},{3,1},{4,2},{5,3},{6,4},{7,5},{8,14},{9,15},{10,... | collective-permute-start | bytes 393224 | tf_op jit(solution)/shard_map/ppermute | solution.py:44
  32.8 2.3 %collective-permute-done.7 = bf16[2,256,128]{2,1,0:T(8,128)(2,1)S(1)} collective-permute-done((bf16[2,256,128]{2,1,0:T(8,128)(2,1)S(1)}, bf16[2,256,128]{2,1,0:T(8,128)(2,1)S(1)}, u32[]{:S(2)}, u32[]{:S(2)}) %collective-permute-start.7) | collective-permute-done | bytes 131104 | tf_op jit(solution)/shard_map/ppermute | solution.py:44
  35.1 0.0 copy-start.12
  35.1 0.0 copy-start.13
  35.1 0.1 pad_maximum_fusion.1
  35.2 2.7 %collective-permute-start.8 = (bf16[4,2,256,128]{3,2,1,0:T(8,128)(2,1)S(1)}, bf16[4,2,256,128]{3,2,1,0:T(8,128)(2,1)S(1)}, u32[]{:S(2)}, u32[]{:S(2)}) collective-permute-start(bf16[4,2,256,128]{3,2,1,0:T(8,128)(2,1)S(1)} %pad_maximum_fusion.1), channel_id=1, source_target_pairs={{0,1},{1,0},{2,3},{3,2},{4,5},{5,4},{6,7},{7,6},{8,9},{9,8},{10,11... | collective-permute-start | bytes 1572872 | tf_op jit(solution)/shard_map/ppermute | solution.py:44
  37.9 0.8 collective-permute-start.6
  38.7 6.3 %collective-permute-done.6 = bf16[2,256,128]{2,1,0:T(8,128)(2,1)S(1)} collective-permute-done((bf16[2,256,128]{2,1,0:T(8,128)(2,1)S(1)}, bf16[2,256,128]{2,1,0:T(8,128)(2,1)S(1)}, u32[]{:S(2)}, u32[]{:S(2)}) %collective-permute-start.6) | collective-permute-done | bytes 131104 | tf_op jit(solution)/shard_map/ppermute | solution.py:44
  45.1 0.7 bitcast_dynamic-update-slice_fusion
  45.7 0.0 collective-permute-done.8
  45.7 0.8 constant_dynamic-update-slice_fusion.refs_5_
  46.6 2.2 %all-to-all-done.gathered_ref.refs_2_ = bf16[32,16,1280]{2,1,0:T(8,128)(2,1)S(1)} async-done(((bf16[32,16,1280]{2,1,0:T(8,128)(2,1)}), bf16[32,16,1280]{2,1,0:T(8,128)(2,1)S(1)}, u32[]{:S(2)}, u32[]{:S(2)}) %all-to-all-start) | async-done | bytes 1310752 | tf_op jit(solution)/shard_map/all_to_all | solution.py:192
  48.8 3.3 %collective-permute-start.14 = (bf16[8,2,256,128]{3,2,1,0:T(8,128)(2,1)}, bf16[8,2,256,128]{3,2,1,0:T(8,128)(2,1)S(1)}, u32[]{:S(2)}, u32[]{:S(2)}) collective-permute-start(bf16[8,2,256,128]{3,2,1,0:T(8,128)(2,1)} %constant_dynamic-update-slice_fusion.refs_5_), channel_id=1, source_target_pairs={{0,24},{8,0},{16,8},{24,16},{32,56},{40,32},{48,40},{56,48},{64,88... | collective-permute-start | bytes 3145736 | tf_op jit(solution)/shard_map/ppermute | solution.py:49
  52.2 0.0 collective-permute-start.13
  52.2 1.0 copy.17
  53.2 0.0 copy-start.1
  53.2 0.2 select_reduce_fusion.slots
  53.4 1.2 shard_map.131
  54.7 2.5 %collective-permute-start.9 = (f32[512,128]{1,0:T(8,128)S(1)}, f32[512,128]{1,0:T(8,128)S(1)}, u32[]{:S(2)}, u32[]{:S(2)}) collective-permute-start(f32[512,128]{1,0:T(8,128)S(1)} %get-tuple-element.16), channel_id=1, source_target_pairs={{0,1},{1,0},{2,3},{3,2},{4,5},{5,4},{6,7},{7,6},{8,9},{9,8},{10,11... | collective-permute-start | bytes 786440 | tf_op jit(solution)/shard_map/ppermute | solution.py:44
  57.2 1.2 collective-permute-done.9
  58.4 3.0 %collective-permute-start.12 = (bf16[512,128]{1,0:T(8,128)(2,1)S(1)}, bf16[512,128]{1,0:T(8,128)(2,1)S(1)}, u32[]{:S(2)}, u32[]{:S(2)}) collective-permute-start(bf16[512,128]{1,0:T(8,128)(2,1)S(1)} %add_convert_fusion.own), channel_id=1, source_target_pairs={{0,4},{1,5},{2,6},{3,7},{4,0},{5,1},{6,2},{7,3},{8,12},{9,13},{10,... | collective-permute-start | bytes 393224 | tf_op jit(solution)/shard_map/ppermute | solution.py:44
  61.4 0.8 collective-permute-start.11
  62.2 0.7 collective-permute-start.10
  62.9 1.8 %collective-permute-done.12.third = bf16[512,128]{1,0:T(8,128)(2,1)S(1)} collective-permute-done((bf16[512,128]{1,0:T(8,128)(2,1)S(1)}, bf16[512,128]{1,0:T(8,128)(2,1)S(1)}, u32[]{:S(2)}, u32[]{:S(2)}) %collective-permute-start.12) | collective-permute-done | bytes 131104 | tf_op jit(solution)/shard_map/ppermute | solution.py:44
  64.7 3.3 %collective-permute-done.11.second = bf16[512,128]{1,0:T(8,128)(2,1)S(1)} collective-permute-done((bf16[512,128]{1,0:T(8,128)(2,1)S(1)}, bf16[512,128]{1,0:T(8,128)(2,1)S(1)}, u32[]{:S(2)}, u32[]{:S(2)}) %collective-permute-start.11) | collective-permute-done | bytes 131104 | tf_op jit(solution)/shard_map/ppermute | solution.py:44
  68.0 0.0 collective-permute-done.10.first
  68.0 1.1 shard_map.132
  69.1 1.0 copy-done.2
  70.2 0.7 copy-done.5
  70.8 1.9 %collective-permute-done.14.refs_7_ = bf16[8,2,256,128]{3,2,1,0:T(8,128)(2,1)S(1)} collective-permute-done((bf16[8,2,256,128]{3,2,1,0:T(8,128)(2,1)}, bf16[8,2,256,128]{3,2,1,0:T(8,128)(2,1)S(1)}, u32[]{:S(2)}, u32[]{:S(2)}) %collective-permute-start.14) | collective-permute-done | bytes 1048608 | tf_op jit(solution)/shard_map/ppermute | solution.py:49
  72.7 3.1 %collective-permute-done.13.refs_6_ = bf16[8,2,256,128]{3,2,1,0:T(8,128)(2,1)} collective-permute-done((bf16[8,2,256,128]{3,2,1,0:T(8,128)(2,1)}, bf16[8,2,256,128]{3,2,1,0:T(8,128)(2,1)}, u32[]{:S(2)}, u32[]{:S(2)}) %collective-permute-start.13) | collective-permute-done | bytes 1048608 | tf_op jit(solution)/shard_map/ppermute | solution.py:49
  75.9 5.1 %all-to-all-start.1 = ((bf16[32,16,1152]{2,1,0:T(8,128)(2,1)}), bf16[32,16,1152]{2,1,0:T(8,128)(2,1)S(1)}, u32[]{:S(2)}, u32[]{:S(2)}) async-start(bf16[32,16,1152]{2,1,0:T(8,128)(2,1)} %copy-done.2), calls=%async_computation.1 | async-start | bytes 2359296 | tf_op jit(solution)/shard_map/all_to_all | solution.py:237
  81.0 2.1 %collective-permute-start.1 = (bf16[2,512,128]{2,1,0:T(8,128)(2,1)}, bf16[2,512,128]{2,1,0:T(8,128)(2,1)}, u32[]{:S(2)}, u32[]{:S(2)}) collective-permute-start(bf16[2,512,128]{2,1,0:T(8,128)(2,1)} %bitcast.27), channel_id=1, source_target_pairs={{0,6},{1,7},{2,0},{3,1},{4,2},{5,3},{6,4},{7,5},{8,14},{9,15},{10,... | collective-permute-start | bytes 786440 | tf_op jit(solution)/shard_map/ppermute | solution.py:44
  83.1 0.0 collective-permute-start
  83.1 3.9 %collective-permute-done.1 = bf16[2,512,128]{2,1,0:T(8,128)(2,1)} collective-permute-done((bf16[2,512,128]{2,1,0:T(8,128)(2,1)}, bf16[2,512,128]{2,1,0:T(8,128)(2,1)}, u32[]{:S(2)}, u32[]{:S(2)}) %collective-permute-start.1) | collective-permute-done | bytes 262176 | tf_op jit(solution)/shard_map/ppermute | solution.py:44
  87.0 2.9 %collective-permute-done = bf16[2,512,128]{2,1,0:T(8,128)(2,1)} collective-permute-done((bf16[2,512,128]{2,1,0:T(8,128)(2,1)}, bf16[2,512,128]{2,1,0:T(8,128)(2,1)}, u32[]{:S(2)}, u32[]{:S(2)}) %collective-permute-start) | collective-permute-done | bytes 262176 | tf_op jit(solution)/shard_map/ppermute | solution.py:44
  89.9 1.0 broadcast_select_fusion
  90.9 0.1 collective-permute-start.2
  91.0 5.5 %collective-permute-done.2 = bf16[2,512,128]{2,1,0:T(8,128)(2,1)S(1)} collective-permute-done((bf16[2,512,128]{2,1,0:T(8,128)(2,1)S(1)}, bf16[2,512,128]{2,1,0:T(8,128)(2,1)S(1)}, u32[]{:S(2)}, u32[]{:S(2)}) %collective-permute-start.2) | collective-permute-done | bytes 262176 | tf_op jit(solution)/shard_map/ppermute | solution.py:242
  96.5 1.2 pad_maximum_fusion.refs_0_
  97.7 0.0 copy-start.16
  97.8 6.5 %collective-permute-start.3 = (bf16[8,512,128]{2,1,0:T(8,128)(2,1)S(1)}, bf16[8,512,128]{2,1,0:T(8,128)(2,1)S(1)}, u32[]{:S(2)}, u32[]{:S(2)}) collective-permute-start(bf16[8,512,128]{2,1,0:T(8,128)(2,1)S(1)} %pad_maximum_fusion.refs_0_), channel_id=1, source_target_pairs={{0,1},{1,0},{2,3},{3,2},{4,5},{5,4},{6,7},{7,6},{8,9},{9,8},{10,11... | collective-permute-start | bytes 3145736 | tf_op jit(solution)/shard_map/ppermute | solution.py:44
  104.2 1.1 slice.30
  105.3 2.7 %collective-permute-start.16 = (bf16[4,2,256,128]{3,2,1,0:T(8,128)(2,1)S(1)}, bf16[4,2,256,128]{3,2,1,0:T(8,128)(2,1)S(1)}, u32[]{:S(2)}, u32[]{:S(2)}) collective-permute-start(bf16[4,2,256,128]{3,2,1,0:T(8,128)(2,1)S(1)} %slice.31), channel_id=1, source_target_pairs={{0,24},{8,0},{16,8},{24,16},{32,56},{40,32},{48,40},{56,48},{64,88... | collective-permute-start | bytes 1572872 | tf_op jit(solution)/shard_map/ppermute | solution.py:49
  108.0 0.0 collective-permute-start.15
  108.1 11.7 %collective-permute-done.16.refs_9_ = bf16[4,2,256,128]{3,2,1,0:T(8,128)(2,1)S(1)} collective-permute-done((bf16[4,2,256,128]{3,2,1,0:T(8,128)(2,1)S(1)}, bf16[4,2,256,128]{3,2,1,0:T(8,128)(2,1)S(1)}, u32[]{:S(2)}, u32[]{:S(2)}) %collective-permute-start.16) | collective-permute-done | bytes 524320 | tf_op jit(solution)/shard_map/ppermute | solution.py:49
  119.7 2.7 %collective-permute-done.15.refs_8_ = bf16[4,2,256,128]{3,2,1,0:T(8,128)(2,1)S(1)} collective-permute-done((bf16[4,2,256,128]{3,2,1,0:T(8,128)(2,1)S(1)}, bf16[4,2,256,128]{3,2,1,0:T(8,128)(2,1)S(1)}, u32[]{:S(2)}, u32[]{:S(2)}) %collective-permute-start.15) | collective-permute-done | bytes 524320 | tf_op jit(solution)/shard_map/ppermute | solution.py:49
  122.4 5.2 %shard_map.133 = bf16[512,1024]{1,0:T(8,128)(2,1)} custom-call(s32[4]{0:T(128)S(1)} %select_reduce_fusion.slots, s32[4]{0:T(128)S(1)} %and_select_fusion.quarters, bf16[8,512,128]{2,1,0:T(8,128)(2,1)S(1)} %pad_maximum_fusion.refs_0_, bf16[8,512,128]{2,1,0:T(8,128)(2,1)S(1)} %collective-permute-done.3.refs_1_, ...), custom_call_target="tpu_custom_call" | custom-call | flops 2415919104 | bytes 8388608 | tf_op jit(solution)/shard_map/pallas_call | solution.py:246
  127.6 0.0 all-to-all-done.1.terms_ref
  127.6 0.8 shard_map.134
  (30 shorter events, 0.2 us)
Async XLA Ops:
  0.6 0.8 copy-start.7
  1.4 0.7 copy-start.8
  2.1 0.7 copy-start.9
  2.7 0.7 copy-start.11
  5.1 43.7 %all-to-all-start = ((bf16[32,16,1280]{2,1,0:T(8,128)(2,1)}), bf16[32,16,1280]{2,1,0:T(8,128)(2,1)S(1)}, u32[]{:S(2)}, u32[]{:S(2)}) async-start(bf16[32,16,1280]{2,1,0:T(8,128)(2,1)} %shard_map.130), calls=%async_computation | async-start | bytes 2621440 | tf_op jit(solution)/shard_map/all_to_all | solution.py:192
  18.5 11.1 %collective-permute-start.4 = (bf16[3,2,256,128]{3,2,1,0:T(8,128)(2,1)S(1)}, bf16[3,2,256,128]{3,2,1,0:T(8,128)(2,1)S(1)}, u32[]{:S(2)}, u32[]{:S(2)}) collective-permute-start(bf16[3,2,256,128]{3,2,1,0:T(8,128)(2,1)S(1)} %pad_maximum_fusion.2), channel_id=1, source_target_pairs={{0,2},{1,3},{2,4},{3,5},{4,6},{5,7},{6,0},{7,1},{8,10},{9,11},{10,... | collective-permute-start | bytes 1179656 | tf_op jit(solution)/shard_map/ppermute | solution.py:44
  20.0 10.3 %collective-permute-start.5 = (bf16[3,2,256,128]{3,2,1,0:T(8,128)(2,1)S(1)}, bf16[3,2,256,128]{3,2,1,0:T(8,128)(2,1)S(1)}, u32[]{:S(2)}, u32[]{:S(2)}) collective-permute-start(bf16[3,2,256,128]{3,2,1,0:T(8,128)(2,1)S(1)} %pad_maximum_fusion.3), channel_id=1, source_target_pairs={{0,6},{1,7},{2,0},{3,1},{4,2},{5,3},{6,4},{7,5},{8,14},{9,15},{10,... | collective-permute-start | bytes 1179656 | tf_op jit(solution)/shard_map/ppermute | solution.py:44
  31.0 4.1 %collective-permute-start.7 = (bf16[2,256,128]{2,1,0:T(8,128)(2,1)S(1)}, bf16[2,256,128]{2,1,0:T(8,128)(2,1)S(1)}, u32[]{:S(2)}, u32[]{:S(2)}) collective-permute-start(bf16[2,256,128]{2,1,0:T(8,128)(2,1)S(1)} %get-tuple-element.38), channel_id=1, source_target_pairs={{0,6},{1,7},{2,0},{3,1},{4,2},{5,3},{6,4},{7,5},{8,14},{9,15},{10,... | collective-permute-start | bytes 393224 | tf_op jit(solution)/shard_map/ppermute | solution.py:44
  35.1 18.1 %copy-start.14 = (s32[8]{0:T(128)S(1)}, s32[8]{0:T(128)}, u32[]{:S(2)}) copy-start(s32[8]{0:T(128)} %param.16) | copy-start | bytes 100
  35.1 18.1 %copy-start.15 = (s32[4]{0:T(128)S(1)}, s32[4]{0:T(128)}, u32[]{:S(2)}) copy-start(s32[4]{0:T(128)} %param.17) | copy-start | bytes 52
  35.1 18.3 %copy-start = (bf16[512,1024]{1,0:T(8,128)(2,1)S(1)}, bf16[512,1024]{1,0:T(8,128)(2,1)}, u32[]{:S(2)}) copy-start(bf16[512,1024]{1,0:T(8,128)(2,1)} %x_ref.3) | copy-start | bytes 3145732
  35.1 18.3 %copy-start.10 = (s32[4]{0:T(128)S(1)}, s32[4]{0:T(128)}, u32[]{:S(2)}) copy-start(s32[4]{0:T(128)} %prompt.3) | copy-start | bytes 52
  35.1 18.3 %copy-start.12 = (f32[4]{0:T(128)S(1)}, f32[4]{0:T(128)}, u32[]{:S(2)}) copy-start(f32[4]{0:T(128)} %reward.3) | copy-start | bytes 52
  35.1 18.3 %copy-start.13 = (s32[4]{0:T(128)S(1)}, s32[4]{0:T(128)}, u32[]{:S(2)}) copy-start(s32[4]{0:T(128)} %live.1) | copy-start | bytes 52
  35.2 10.5 %collective-permute-start.8 = (bf16[4,2,256,128]{3,2,1,0:T(8,128)(2,1)S(1)}, bf16[4,2,256,128]{3,2,1,0:T(8,128)(2,1)S(1)}, u32[]{:S(2)}, u32[]{:S(2)}) collective-permute-start(bf16[4,2,256,128]{3,2,1,0:T(8,128)(2,1)S(1)} %pad_maximum_fusion.1), channel_id=1, source_target_pairs={{0,1},{1,0},{2,3},{3,2},{4,5},{5,4},{6,7},{7,6},{8,9},{9,8},{10,11... | collective-permute-start | bytes 1572872 | tf_op jit(solution)/shard_map/ppermute | solution.py:44
  37.9 7.1 %collective-permute-start.6 = (bf16[2,256,128]{2,1,0:T(8,128)(2,1)S(1)}, bf16[2,256,128]{2,1,0:T(8,128)(2,1)S(1)}, u32[]{:S(2)}, u32[]{:S(2)}) collective-permute-start(bf16[2,256,128]{2,1,0:T(8,128)(2,1)S(1)} %get-tuple-element.35), channel_id=1, source_target_pairs={{0,2},{1,3},{2,4},{3,5},{4,6},{5,7},{6,0},{7,1},{8,10},{9,11},{10,... | collective-permute-start | bytes 393224 | tf_op jit(solution)/shard_map/ppermute | solution.py:44
  48.8 23.9 %collective-permute-start.14 = (bf16[8,2,256,128]{3,2,1,0:T(8,128)(2,1)}, bf16[8,2,256,128]{3,2,1,0:T(8,128)(2,1)S(1)}, u32[]{:S(2)}, u32[]{:S(2)}) collective-permute-start(bf16[8,2,256,128]{3,2,1,0:T(8,128)(2,1)} %constant_dynamic-update-slice_fusion.refs_5_), channel_id=1, source_target_pairs={{0,24},{8,0},{16,8},{24,16},{32,56},{40,32},{48,40},{56,48},{64,88... | collective-permute-start | bytes 3145736 | tf_op jit(solution)/shard_map/ppermute | solution.py:49
  52.2 23.7 %collective-permute-start.13 = (bf16[8,2,256,128]{3,2,1,0:T(8,128)(2,1)}, bf16[8,2,256,128]{3,2,1,0:T(8,128)(2,1)}, u32[]{:S(2)}, u32[]{:S(2)}) collective-permute-start(bf16[8,2,256,128]{3,2,1,0:T(8,128)(2,1)} %constant_dynamic-update-slice_fusion.refs_5_), channel_id=1, source_target_pairs={{0,8},{8,16},{16,24},{24,0},{32,40},{40,48},{48,56},{56,32},{64,72... | collective-permute-start | bytes 3145736 | tf_op jit(solution)/shard_map/ppermute | solution.py:49
  53.2 1.5 %copy-start.1 = (bf16[512,2,128]{2,0,1:T(8,128)(2,1)}, bf16[512,2,128]{2,0,1:T(8,128)(2,1)S(1)}, u32[]{:S(2)}) copy-start(bf16[512,2,128]{2,0,1:T(8,128)(2,1)S(1)} %copy.17) | copy-start | bytes 786436
  54.7 13.3 %copy-start.3 = (f32[512,1]{1,0:T(8,128)}, f32[512,1]{1,0:T(8,128)S(1)}, u32[]{:S(2)}) copy-start(f32[512,1]{1,0:T(8,128)S(1)} %get-tuple-element.19.refs_4_) | copy-start | bytes 6148
  54.7 3.7 %collective-permute-start.9 = (f32[512,128]{1,0:T(8,128)S(1)}, f32[512,128]{1,0:T(8,128)S(1)}, u32[]{:S(2)}, u32[]{:S(2)}) collective-permute-start(f32[512,128]{1,0:T(8,128)S(1)} %get-tuple-element.16), channel_id=1, source_target_pairs={{0,1},{1,0},{2,3},{3,2},{4,5},{5,4},{6,7},{7,6},{8,9},{9,8},{10,11... | collective-permute-start | bytes 786440 | tf_op jit(solution)/shard_map/ppermute | solution.py:44
  58.4 6.3 %collective-permute-start.12 = (bf16[512,128]{1,0:T(8,128)(2,1)S(1)}, bf16[512,128]{1,0:T(8,128)(2,1)S(1)}, u32[]{:S(2)}, u32[]{:S(2)}) collective-permute-start(bf16[512,128]{1,0:T(8,128)(2,1)S(1)} %add_convert_fusion.own), channel_id=1, source_target_pairs={{0,4},{1,5},{2,6},{3,7},{4,0},{5,1},{6,2},{7,3},{8,12},{9,13},{10,... | collective-permute-start | bytes 393224 | tf_op jit(solution)/shard_map/ppermute | solution.py:44
  61.4 6.6 %collective-permute-start.11 = (bf16[512,128]{1,0:T(8,128)(2,1)S(1)}, bf16[512,128]{1,0:T(8,128)(2,1)S(1)}, u32[]{:S(2)}, u32[]{:S(2)}) collective-permute-start(bf16[512,128]{1,0:T(8,128)(2,1)S(1)} %add_convert_fusion.own), channel_id=1, source_target_pairs={{0,6},{1,7},{2,0},{3,1},{4,2},{5,3},{6,4},{7,5},{8,14},{9,15},{10,... | collective-permute-start | bytes 393224 | tf_op jit(solution)/shard_map/ppermute | solution.py:44
  62.2 5.8 %collective-permute-start.10 = (bf16[512,128]{1,0:T(8,128)(2,1)S(1)}, bf16[512,128]{1,0:T(8,128)(2,1)S(1)}, u32[]{:S(2)}, u32[]{:S(2)}) collective-permute-start(bf16[512,128]{1,0:T(8,128)(2,1)S(1)} %add_convert_fusion.own), channel_id=1, source_target_pairs={{0,2},{1,3},{2,4},{3,5},{4,6},{5,7},{6,0},{7,1},{8,10},{9,11},{10,... | collective-permute-start | bytes 393224 | tf_op jit(solution)/shard_map/ppermute | solution.py:44
  69.1 1.0 copy-start.2
  70.2 0.7 copy-start.5
  75.9 51.8 %all-to-all-start.1 = ((bf16[32,16,1152]{2,1,0:T(8,128)(2,1)}), bf16[32,16,1152]{2,1,0:T(8,128)(2,1)S(1)}, u32[]{:S(2)}, u32[]{:S(2)}) async-start(bf16[32,16,1152]{2,1,0:T(8,128)(2,1)} %copy-done.2), calls=%async_computation.1 | async-start | bytes 2359296 | tf_op jit(solution)/shard_map/all_to_all | solution.py:237
  81.0 6.0 %collective-permute-start.1 = (bf16[2,512,128]{2,1,0:T(8,128)(2,1)}, bf16[2,512,128]{2,1,0:T(8,128)(2,1)}, u32[]{:S(2)}, u32[]{:S(2)}) collective-permute-start(bf16[2,512,128]{2,1,0:T(8,128)(2,1)} %bitcast.27), channel_id=1, source_target_pairs={{0,6},{1,7},{2,0},{3,1},{4,2},{5,3},{6,4},{7,5},{8,14},{9,15},{10,... | collective-permute-start | bytes 786440 | tf_op jit(solution)/shard_map/ppermute | solution.py:44
  83.1 6.8 %collective-permute-start = (bf16[2,512,128]{2,1,0:T(8,128)(2,1)}, bf16[2,512,128]{2,1,0:T(8,128)(2,1)}, u32[]{:S(2)}, u32[]{:S(2)}) collective-permute-start(bf16[2,512,128]{2,1,0:T(8,128)(2,1)} %bitcast.28), channel_id=1, source_target_pairs={{0,2},{1,3},{2,4},{3,5},{4,6},{5,7},{6,0},{7,1},{8,10},{9,11},{10,... | collective-permute-start | bytes 786440 | tf_op jit(solution)/shard_map/ppermute | solution.py:44
  90.9 5.6 %collective-permute-start.2 = (bf16[2,512,128]{2,1,0:T(8,128)(2,1)S(1)}, bf16[2,512,128]{2,1,0:T(8,128)(2,1)S(1)}, u32[]{:S(2)}, u32[]{:S(2)}) collective-permute-start(bf16[2,512,128]{2,1,0:T(8,128)(2,1)S(1)} %broadcast_select_fusion), channel_id=1, source_target_pairs={{0,2},{1,7},{2,4},{3,1},{4,6},{5,3},{6,0},{7,5},{8,10},{9,15},{10,... | collective-permute-start | bytes 786440 | tf_op jit(solution)/shard_map/ppermute | solution.py:242
  97.7 10.3 %copy-start.16 = (s32[4]{0:T(128)S(1)}, s32[4]{0:T(128)}, u32[]{:S(2)}) copy-start(s32[4]{0:T(128)} %constant.106.clone) | copy-start | bytes 52
  97.7 24.7 %copy-start.4 = (f32[512,1]{1,0:T(8,128)S(1)}, f32[512,1]{1,0:T(8,128)}, u32[]{:S(2)}) copy-start(f32[512,1]{1,0:T(8,128)} %copy-done.3) | copy-start | bytes 6148
  97.7 24.7 %copy-start.6 = (bf16[512,128]{1,0:T(8,128)(2,1)S(1)}, bf16[512,128]{1,0:T(8,128)(2,1)}, u32[]{:S(2)}) copy-start(bf16[512,128]{1,0:T(8,128)(2,1)} %copy-done.5) | copy-start | bytes 393220
  97.8 10.3 %collective-permute-start.3 = (bf16[8,512,128]{2,1,0:T(8,128)(2,1)S(1)}, bf16[8,512,128]{2,1,0:T(8,128)(2,1)S(1)}, u32[]{:S(2)}, u32[]{:S(2)}) collective-permute-start(bf16[8,512,128]{2,1,0:T(8,128)(2,1)S(1)} %pad_maximum_fusion.refs_0_), channel_id=1, source_target_pairs={{0,1},{1,0},{2,3},{3,2},{4,5},{5,4},{6,7},{7,6},{8,9},{9,8},{10,11... | collective-permute-start | bytes 3145736 | tf_op jit(solution)/shard_map/ppermute | solution.py:44
  105.3 14.4 %collective-permute-start.16 = (bf16[4,2,256,128]{3,2,1,0:T(8,128)(2,1)S(1)}, bf16[4,2,256,128]{3,2,1,0:T(8,128)(2,1)S(1)}, u32[]{:S(2)}, u32[]{:S(2)}) collective-permute-start(bf16[4,2,256,128]{3,2,1,0:T(8,128)(2,1)S(1)} %slice.31), channel_id=1, source_target_pairs={{0,24},{8,0},{16,8},{24,16},{32,56},{40,32},{48,40},{56,48},{64,88... | collective-permute-start | bytes 1572872 | tf_op jit(solution)/shard_map/ppermute | solution.py:49
  108.0 14.4 %collective-permute-start.15 = (bf16[4,2,256,128]{3,2,1,0:T(8,128)(2,1)S(1)}, bf16[4,2,256,128]{3,2,1,0:T(8,128)(2,1)S(1)}, u32[]{:S(2)}, u32[]{:S(2)}) collective-permute-start(bf16[4,2,256,128]{3,2,1,0:T(8,128)(2,1)S(1)} %slice.30), channel_id=1, source_target_pairs={{0,8},{8,16},{16,24},{24,0},{32,40},{40,48},{48,56},{56,32},{64,72... | collective-permute-start | bytes 1572872 | tf_op jit(solution)/shard_map/ppermute | solution.py:49

commit v4 on v3

--- a/solution.py
+++ b/solution.py
@@ -11,6 +11,7 @@
 RANK = 64
 LANES = 128
 CHIPS = 4
+FULL_VMEM = 60 * 2**20
 LOWRANK_MULTIPLIER = 2.0
 BF = jnp.bfloat16
 F32 = jnp.float32
@@ -53,12 +54,13 @@
     shape = (down_ref.shape[0], LANES)
     row = lax.broadcasted_iota(jnp.int32, shape, 0)
     lane = lax.broadcasted_iota(jnp.int32, shape, 1)
-    blocks = reward.shape[0]
+    blocks = reward.shape[1]
     rewards = jnp.zeros(shape, F32)
     prompts = jnp.full(shape, -1.0, F32)
     for b in range(blocks):
-        rewards = jnp.where(lane % blocks == b, reward[b], rewards)
-        prompts = jnp.where(lane == b, prompt[b].astype(F32), prompts)
+        one = (slice(0, 1), slice(b, b + 1))
+        rewards = jnp.where(lane % blocks == b, reward[one], rewards)
+        prompts = jnp.where(lane == b, prompt[one].astype(F32), prompts)
     high = rewards.astype(BF).astype(F32)
     rest = rewards - high
     middle = rest.astype(BF).astype(F32)
@@ -69,6 +71,57 @@
     packed = jnp.concatenate([down_ref[...], up_ref[...], facts], axis=1)
     for i in range(out_ref.shape[0]):
         out_ref[i] = packed
+
+
+def streamed(kernel, blocks, out):
+    whole = lambda shape: pl.BlockSpec(shape, lambda i: (0,) * len(shape))
+    return pl.pallas_call(
+        kernel,
+        grid=(1,),
+        in_specs=[whole(shape) for shape in blocks],
+        out_specs=whole(out),
+        out_shape=jax.ShapeDtypeStruct(out, BF),
+        compiler_params=pltpu.CompilerParams(vmem_limit_bytes=FULL_VMEM),
+    )
+
+
+def payload_kernel(places, *refs):
+    *slabs, cot_ref, next_ref, next_other, prev_ref, prev_other, mine_ref, other_ref = refs
+    tile, rows = slabs[0].shape[1], cot_ref.shape[1]
+    key, value = (cot_ref.at[0],), (cot_ref.at[1],)
+    slab = lambda i: (slabs[i].at[0], slabs[i].at[1])
+    orders = (
+        (next_ref, (slab(0), slab(2), key, value)),
+        (next_other, (slab(1),)),
+        (prev_ref, (slab(3), key, value, slab(5))),
+        (prev_other, (slab(4),)),
+        (mine_ref, (slab(6),)),
+        (other_ref, (slab(7),)),
+    )
+    for out_ref, units in orders:
+        at = 0
+        for piece in (p for unit in units for p in unit):
+            out_ref[at : at + piece.shape[0]] = piece[...]
+            at += piece.shape[0]
+
+
+def payloads(places, weight, cotangent, tile):
+    columns = weight.shape[2]
+    slab = [
+        pl.BlockSpec((2, tile, columns), lambda g, p, i=i: (0, p[i], 0)) for i in range(8)
+    ]
+    sizes = [n * 2 * tile for n in (4, 1, 4, 1, 1, 1)]
+    return pl.pallas_call(
+        payload_kernel,
+        grid_spec=pltpu.PrefetchScalarGridSpec(
+            num_scalar_prefetch=1,
+            grid=(1,),
+            in_specs=[*slab, pl.BlockSpec(cotangent.shape, lambda g, p: (0, 0, 0))],
+            out_specs=[pl.BlockSpec((n, columns), lambda g, p: (0, 0)) for n in sizes],
+        ),
+        out_shape=[jax.ShapeDtypeStruct((n, columns), BF) for n in sizes],
+        compiler_params=pltpu.CompilerParams(vmem_limit_bytes=FULL_VMEM),
+    )(places, *[weight] * 8, cotangent)
 
 
 def factor_rows(ref, slot, start, size):
@@ -126,27 +179,31 @@
 
 
 def frozen_kernel(slots, quarters, *refs):
-    *cot_refs, gathered_ref, low_ref, coef_ref, w0, w1, w2, w3a, w3b, out_ref, weighted = refs
-    tile = w0.shape[2]
-    columns = w0.shape[3]
+    own, before, after, hop_next, hop_prev, swapped, *refs = refs
+    gathered_ref, low_ref, coef_ref, w0, w1, w2, w3a, w3b, out_ref, weighted = refs
+    rows, columns = own.shape[1:]
+    tile = rows // 2
     coef = coef_ref[...]
-    at = 0
-    for ref in cot_refs:
-        for i in range(ref.shape[0] // 2):
-            for j in range(2):
-                both = ref[2 * i + j].astype(F32) * coef
-                weighted[:, at : at + columns] = both.astype(BF)
-                at += columns
+    pieces = [own.at[0], own.at[1]]
+    pieces += [before.at[pl.ds(i * rows, rows)] for i in (2, 3)]
+    pieces += [after.at[pl.ds(i * rows, rows)] for i in (1, 2)]
+    pieces += [hop_next.at[pl.ds(rows, rows)], swapped.at[pl.ds(7 * rows, rows)]]
+    pieces += [swapped.at[pl.ds(i * rows, rows)] for i in range(7)]
+    pieces += [hop_prev.at[pl.ds(0, rows)]]
+    for i, piece in enumerate(pieces):
+        weighted[:, i * columns : (i + 1) * columns] = (piece[...].astype(F32) * coef).astype(BF)
     for r, parts in enumerate(((w0,), (w1,), (w2,), (w3a, w3b))):
-        slabs = [p[i, j] for p in parts for i in range(p.shape[0]) for j in range(2)]
+        slabs = [
+            p[i * tile : (i + 1) * tile] for p in parts for i in range(p.shape[0] // tile)
+        ]
         total = dot(weighted[...], jnp.concatenate(slabs, axis=1), 1, 1)
         start = pl.multiple_of(quarters[r] * tile, tile)
-        for b in range(total.shape[0] // BLOCK):
-            rows = slice(b * BLOCK, (b + 1) * BLOCK)
+        for b in range(rows // BLOCK):
+            block = slice(b * BLOCK, (b + 1) * BLOCK)
             factor = factor_rows(gathered_ref, slots[b], start, tile)
             factor = jnp.concatenate([jnp.zeros_like(factor), factor], axis=0)
-            extra = LOWRANK_MULTIPLIER * dot(low_ref[rows, :], factor, 1, 0)
-            out_ref[rows, pl.ds(start, tile)] = (total[rows] + extra).astype(BF)
+            extra = LOWRANK_MULTIPLIER * dot(low_ref[block, :], factor, 1, 0)
+            out_ref[block, pl.ds(start, tile)] = (total[block] + extra).astype(BF)
 
 
 def sum_kernel(terms_ref, down_ref, up_ref):
@@ -186,27 +243,47 @@
         axis=1,
     )
 
-    packed = call(
-        pack_kernel, [SMEM, SMEM, VMEM, VMEM], shape((dp, owned, window + columns + LANES), BF), 0, 8
-    )(prompt_of_block, reward_of_block, adapter_down_factors, adapter_up_factors)
+    packed = streamed(
+        pack_kernel,
+        [(1, 4), (1, 4), (owned, window), (owned, columns)],
+        (dp, owned, window + columns + LANES),
+    )(
+        prompt_of_block.reshape(1, -1),
+        reward_of_block.reshape(1, -1),
+        adapter_down_factors,
+        adapter_up_factors,
+    )
     gathered = lax.all_to_all(packed, "dp", 0, 0)
 
-    def quarter(chip_step, core_flip):
-        target = ((chip + chip_step) % CHIPS) * 2 + (core + core_flip) % 2
-        start = target * window + x * tile
-        return lax.dynamic_slice_in_dim(key_value_weight, start, tile, 1)
-
-    before = tensor_send(jnp.stack([quarter(1, 0), quarter(1, 1), quarter(2, 0)]), 1, 0)
-    after = tensor_send(jnp.stack([quarter(3, 0), quarter(3, 1), quarter(2, 1)]), 3, 0)
-    across = tensor_send(before[2], 1, 0)
-    across_other = tensor_send(after[2], 3, 0)
-    other = jnp.stack([quarter(0, 1), before[1], after[1], across_other])
+    cotangent = jnp.transpose(key_value_cotangent, (1, 0, 2))
+    steps = jnp.array([[1, 0], [1, 1], [2, 0], [3, 0], [3, 1], [2, 1], [0, 0], [0, 1]], jnp.int32)
+    targets = (chip + steps[:, 0]) % CHIPS * 2 + (core + steps[:, 1]) % 2
+    to_next, next_other, to_prev, prev_other, mine, other = payloads(
+        targets * 4 + x, key_value_weight, cotangent, tile
+    )
+    before, after = tensor_send(to_next, 1, 0), tensor_send(to_prev, 3, 0)
+    before_other, after_other = tensor_send(next_other, 1, 1), tensor_send(prev_other, 3, 1)
+    partner = tensor_send(other, 0, 1)
+    unit = 2 * tile
+    part = lambda v, start, stop: v[start * unit : stop * unit]
+    hop_next, hop_prev = lax.optimization_barrier((part(before, 1, 3), part(after, 2, 4)))
+    hop_next, hop_prev = tensor_send(hop_next, 1, 0), tensor_send(hop_prev, 3, 1)
     slabs = jnp.concatenate(
-        [jnp.stack([quarter(0, 0), before[0], after[0], across]), tensor_send(other, 0, 1)]
-    )
-    gathered, slabs = lax.optimization_barrier((gathered, slabs))
-
-    cotangent = jnp.transpose(key_value_cotangent, (1, 0, 2))
+        [
+            mine,
+            part(before, 0, 1),
+            part(after, 0, 1),
+            part(hop_next, 0, 1),
+            partner,
+            before_other,
+            after_other,
+            part(hop_prev, 1, 2),
+        ]
+    )
+    gathered, slabs, hop_next, hop_prev = lax.optimization_barrier(
+        (gathered, slabs, hop_next, hop_prev)
+    )
+
     low, weighted_value, coef = call(
         low_kernel,
         [SMEM] * 4 + [VMEM] * 3,
@@ -235,37 +312,40 @@
     )(slots, *lows, normed_input_rows, weighted_value)
     terms, slabs_left, slabs_right = lax.optimization_barrier((terms, slabs_left, slabs_right))
     terms = lax.all_to_all(terms, "dp", 0, 0)
-
-    slabs_far = (x_send(slabs_left[:4], 1), x_send(slabs_right[4:], 3))
-    cot_before, cot_after = tensor_send(cotangent, 1, 0), tensor_send(cotangent, 3, 0)
-    relay = [(y * 2 + c, (y + 1 + 2 * c) % CHIPS * 2 + c) for y in range(CHIPS) for c in range(2)]
-    cot_across = lax.ppermute(jnp.where(core == 0, cot_before, cot_after), "tensor", relay)
-    cots = jnp.concatenate([cotangent, cot_before, cot_after, cot_across])
-    cots_other = tensor_send(cots, 0, 1)
+    swapped = jnp.concatenate(
+        [
+            cotangent.reshape(2 * rows, columns),
+            part(before, 2, 4),
+            part(after, 1, 3),
+            part(hop_next, 1, 2),
+            part(hop_prev, 0, 1),
+        ]
+    )
+    swapped = tensor_send(swapped, 0, 1)
+
+    half = slabs.shape[0] // 2
+    slabs_far = (x_send(slabs_left[:half], 1), x_send(slabs_right[half:], 3))
     quarters = (x + jnp.array([0, 3, 1, 2], jnp.int32)) % 4
+    streams = [
+        cotangent, before, after, hop_next, hop_prev, swapped, gathered, low, coef,
+        slabs, slabs_left, slabs_right, *slabs_far,
+    ]
+    whole = lambda dims: pl.BlockSpec(dims, lambda i, *_: (0,) * len(dims))
     input_gradient = pl.pallas_call(
         frozen_kernel,
-        in_specs=[SMEM] * 2 + [VMEM] * 10,
-        out_specs=VMEM,
+        grid_spec=pltpu.PrefetchScalarGridSpec(
+            num_scalar_prefetch=2,
+            grid=(1,),
+            in_specs=[whole(v.shape) for v in streams],
+            out_specs=whole((rows, window)),
+            scratch_shapes=[pltpu.VMEM((rows, 16 * columns), BF)],
+        ),
         out_shape=shape((rows, window), BF),
-        scratch_shapes=[pltpu.VMEM((rows, 16 * columns), BF)],
-        compiler_params=pltpu.CompilerParams(vmem_limit_bytes=28 * 2**20),
+        compiler_params=pltpu.CompilerParams(vmem_limit_bytes=FULL_VMEM),
         cost_estimate=pl.CostEstimate(
             flops=2 * rows * window * 18 * columns, bytes_accessed=8 * 2**20, transcendentals=0
         ),
-    )(
-        slots,
-        quarters,
-        cots,
-        cots_other,
-        gathered,
-        low,
-        coef,
-        slabs,
-        slabs_left,
-        slabs_right,
-        *slabs_far,
-    )
+    )(slots, quarters, *streams)
     grad_a, grad_b = call(
         sum_kernel,
         [VMEM],

time: 129 us -> 124 us (0.961)
  waiting for transfers between devices: 55.4 us -> 42.3 us
  Pallas kernels: 10.1 us -> 16.3 us
  local copies, waits for them, and re-layouts: 12.3 us -> 16 us
  other arithmetic: 2.62 us -> 1.26 us
    ppermute x12, waiting for transfers between devices: 28.2 us -> 12.7 us  [tensor_send(): return lax.ppermute(value, 'tensor', pairs)]
    ppermute x4, waiting for transfers between devices: 19.4 us -> 29.6 us  [x_send(): return lax.ppermute(value, 'dp', pairs)]
    pallas_call x2 -> x3, Pallas kernels: 6.91 us -> 13.1 us  [the longest x1 7.8 us: shards(): pl.pallas_call(frozen_kernel, grid_spec=pltpu.PrefetchScalarGridSpec(num_...]
    ppermute x1 -> x0, waiting for transfers between devices: 5.5 us -> none  [shards(): lax.ppermute(jnp.where(core == 0, cot_before, cot_after), 'tensor', relay)]
    unnamed x37 -> x60, local copies, waits for them, and re-layouts: 7.69 us -> 12.5 us
    all_to_all x1, waiting for transfers between devices: 2.25 us -> 0.01 us  [shards(): gathered = lax.all_to_all(packed, 'dp', 0, 0)]
    all_to_all x1, starting transfers between devices: 5.14 us -> 6.9 us  [shards(): terms = lax.all_to_all(terms, 'dp', 0, 0)]
    another operation x1 -> x0, local copies, waits for them, and re-layouts: 1.33 us -> none  [shards(): other = jnp.stack([quarter(0, 1), before[1], after[1], across_other])]
  transfers between devices with their start and end apart: 19 -> 18, of which waited for: 14 -> 9; matrix products, arithmetic and copies ran while one was open for 8% -> 11% of each run, Pallas kernels for 6% -> 11%
where the time goes in v4:
time: 124 us; the launch traced here: 123 us
  starting transfers between devices  46.8 us (38%)
  waiting for transfers between devices  42.3 us (34%)
  Pallas kernels  16.3 us (13%)
  local copies, waits for them, and re-layouts  16 us (13%)
  other arithmetic  1.26 us (1%)
    ppermute x4, waiting for transfers between devices, x_send(): return lax.ppermute(value, 'dp', pairs)  29.6 us
    ppermute x12, starting transfers between devices, tensor_send(): return lax.ppermute(value, 'tensor', pairs)  22.6 us
    ppermute x12, waiting for transfers between devices, tensor_send(): return lax.ppermute(value, 'tensor', pairs)  12.7 us
    unnamed x60, local copies, waits for them, and re-layouts  12.5 us
    all_to_all x1, starting transfers between devices, shards(): gathered = lax.all_to_all(packed, 'dp', 0, 0)  12 us
    pallas_call x1, Pallas kernels, shards(): pl.pallas_call(frozen_kernel, grid_spec=pltpu.PrefetchScalarGridSpec(num_...  7.8 us
    all_to_all x1, starting transfers between devices, shards(): terms = lax.all_to_all(terms, 'dp', 0, 0)  6.9 us
    ppermute x4, starting transfers between devices, x_send(): return lax.ppermute(value, 'dp', pairs)  5.25 us
  transfers between devices with their start and end apart: 18, of which 9 were waited for; matrix products, arithmetic and copies ran while one was open for 11% of the time, Pallas kernels for 11%

profile of v4, /device:TPU:1, one launch (start us, length us, event | category | flops | bytes accessed | tf_op | source)
XLA Modules:
  0.0 123.4 jit_solution(5063656076585261866)
XLA Ops:
  0.6 2.0 %shard_map.140 = bf16[32,16,1280]{2,1,0:T(8,128)(2,1)} custom-call(s32[1,4]{1,0:T(1,128)} %bitcast.18, f32[1,4]{1,0:T(1,128)} %bitcast.19, bf16[16,1024]{1,0:T(8,128)(2,1)} %down_ref.1, bf16[16,128]{1,0:T(8,128)(2,1)} %up_ref.1), custom_call_target="tpu_custom_call" | custom-call | tf_op jit(solution)/shard_map/pallas_call | solution.py:246
  2.6 12.0 %all-to-all-start = ((bf16[32,16,1280]{2,1,0:T(8,128)(2,1)}), bf16[32,16,1280]{2,1,0:T(8,128)(2,1)S(1)}, u32[]{:S(2)}, u32[]{:S(2)}) async-start(bf16[32,16,1280]{2,1,0:T(8,128)(2,1)} %shard_map.140), calls=%async_computation | async-start | bytes 2621440 | tf_op jit(solution)/shard_map/all_to_all | solution.py:256
  14.7 0.7 copy.19
  15.4 0.5 multiply_add_fusion.places
  15.9 3.3 %shard_map.139 = (bf16[2048,128]{1,0:T(8,128)(2,1)}, bf16[512,128]{1,0:T(8,128)(2,1)}, bf16[2048,128]{1,0:T(8,128)(2,1)}, bf16[512,128]{1,0:T(8,128)(2,1)}, bf16...) custom-call(s32[8]{0:T(128)} %multiply_add_fusion.places, bf16[2,8192,128]{2,1,0:T(8,128)(2,1)} %refs_7_.1, ...), custom_call_target="tpu_custom_call" | custom-call | tf_op jit(solution)/shard_map/pallas_call | solution.py:114
  19.3 1.3 %collective-permute-start = (bf16[2048,128]{1,0:T(8,128)(2,1)}, bf16[2048,128]{1,0:T(8,128)(2,1)S(1)}, u32[]{:S(2)}, u32[]{:S(2)}) collective-permute-start(bf16[2048,128]{1,0:T(8,128)(2,1)} %get-tuple-element.25), channel_id=1, source_target_pairs={{0,2},{1,3},{2,4},{3,5},{4,6},{5,7},{6,0},{7,1},{8,10},{9,11},{10,... | collective-permute-start | bytes 1572872 | tf_op jit(solution)/shard_map/ppermute | solution.py:45
  20.6 1.5 %collective-permute-start.1 = (bf16[2048,128]{1,0:T(8,128)(2,1)}, bf16[2048,128]{1,0:T(8,128)(2,1)S(1)}, u32[]{:S(2)}, u32[]{:S(2)}) collective-permute-start(bf16[2048,128]{1,0:T(8,128)(2,1)} %get-tuple-element.26), channel_id=1, source_target_pairs={{0,6},{1,7},{2,0},{3,1},{4,2},{5,3},{6,4},{7,5},{8,14},{9,15},{10,... | collective-permute-start | bytes 1572872 | tf_op jit(solution)/shard_map/ppermute | solution.py:45
  22.1 1.4 %collective-permute-start.3 = (bf16[512,128]{1,0:T(8,128)(2,1)}, bf16[512,128]{1,0:T(8,128)(2,1)S(1)}, u32[]{:S(2)}, u32[]{:S(2)}) collective-permute-start(bf16[512,128]{1,0:T(8,128)(2,1)} %get-tuple-element.29), channel_id=1, source_target_pairs={{0,1},{1,0},{2,3},{3,2},{4,5},{5,4},{6,7},{7,6},{8,9},{9,8},{10,11... | collective-permute-start | bytes 393224 | tf_op jit(solution)/shard_map/ppermute | solution.py:45
  23.4 0.0 collective-permute-start.4
  23.4 3.0 %collective-permute-start.5 = (bf16[512,128]{1,0:T(8,128)(2,1)}, bf16[512,128]{1,0:T(8,128)(2,1)S(1)}, u32[]{:S(2)}, u32[]{:S(2)}) collective-permute-start(bf16[512,128]{1,0:T(8,128)(2,1)} %get-tuple-element.31), channel_id=1, source_target_pairs={{0,7},{1,6},{2,1},{3,0},{4,3},{5,2},{6,5},{7,4},{8,15},{9,14},{10,... | collective-permute-start | bytes 393224 | tf_op jit(solution)/shard_map/ppermute | solution.py:45
  26.4 1.6 %constant_dynamic-update-slice_fusion.3 = bf16[4096,128]{1,0:T(8,128)(2,1)} fusion(bf16[512,128]{1,0:T(8,128)(2,1)} %get-tuple-element.27), kind=kLoop, calls=%fused_computation.12 | loop fusion | bytes 262144
  28.0 0.7 constant_dynamic-update-slice_fusion.4
  28.7 4.6 %collective-permute-done.refs_1_ = bf16[2048,128]{1,0:T(8,128)(2,1)S(1)} collective-permute-done((bf16[2048,128]{1,0:T(8,128)(2,1)}, bf16[2048,128]{1,0:T(8,128)(2,1)S(1)}, u32[]{:S(2)}, u32[]{:S(2)}) %collective-permute-start) | collective-permute-done | bytes 524320 | tf_op jit(solution)/shard_map/ppermute | solution.py:45
  33.3 0.8 slice_dynamic-update-slice_fusion.1
  34.1 0.0 collective-permute-done.1.refs_2_
  34.1 0.0 copy-start.2
  34.1 0.0 copy-start.7
  34.1 0.0 copy-start.8
  34.1 0.0 copy-start.9
  34.1 0.7 slice_dynamic-update-slice_fusion
  34.9 0.1 collective-permute-start.2
  35.0 5.9 %collective-permute-start.6 = (bf16[1024,128]{1,0:T(8,128)(2,1)S(1)}, bf16[1024,128]{1,0:T(8,128)(2,1)S(1)}, u32[]{:S(2)}, u32[]{:S(2)}) collective-permute-start(bf16[1024,128]{1,0:T(8,128)(2,1)S(1)} %get-tuple-element.32), channel_id=1, source_target_pairs={{0,7},{1,6},{2,1},{3,0},{4,3},{5,2},{6,5},{7,4},{8,15},{9,14},{10,... | collective-permute-start | bytes 786440 | tf_op jit(solution)/shard_map/ppermute | solution.py:45
  40.9 0.7 slice_dynamic-update-slice_fusion.5
  41.6 0.7 slice_dynamic-update-slice_fusion.4
  42.2 0.0 collective-permute-done.2.refs_3_
  42.2 0.7 slice_dynamic-update-slice_fusion.3
  43.0 0.7 constant_dynamic-update-slice_fusion.2
  43.6 0.0 collective-permute-done.4
  43.6 0.7 constant_dynamic-update-slice_fusion.1
  44.3 0.7 constant_dynamic-update-slice_fusion
  44.9 1.8 %collective-permute-done.6.refs_4_ = bf16[1024,128]{1,0:T(8,128)(2,1)S(1)} collective-permute-done((bf16[1024,128]{1,0:T(8,128)(2,1)S(1)}, bf16[1024,128]{1,0:T(8,128)(2,1)S(1)}, u32[]{:S(2)}, u32[]{:S(2)}) %collective-permute-start.6) | collective-permute-done | bytes 262176 | tf_op jit(solution)/shard_map/ppermute | solution.py:45
  46.7 0.7 copy-done.14
  47.4 0.7 slice_dynamic-update-slice_fusion.2.refs_9_
  48.1 0.0 all-to-all-done.gathered_ref.refs_6_
  48.1 2.4 %collective-permute-start.13 = (bf16[4096,128]{1,0:T(8,128)(2,1)}, bf16[4096,128]{1,0:T(8,128)(2,1)}, u32[]{:S(2)}, u32[]{:S(2)}) collective-permute-start(bf16[4096,128]{1,0:T(8,128)(2,1)} %slice_dynamic-update-slice_fusion.2.refs_9_), channel_id=1, source_target_pairs={{0,24},{8,0},{16,8},{24,16},{32,56},{40,32},{48,40},{56,48},{64,88... | collective-permute-start | bytes 3145736 | tf_op jit(solution)/shard_map/ppermute | solution.py:50
  50.6 0.2 select_reduce_fusion.slots
  50.8 0.0 copy-start.6
  50.8 1.2 %shard_map.141 = (f32[512,128]{1,0:T(8,128)S(1)}, bf16[512,128]{1,0:T(8,128)(2,1)S(1)}, f32[512,1]{1,0:T(8,128)S(1)}) custom-call(s32[4]{0:T(128)S(1)} %select_reduce_fusion.slots, s32[4]{0:T(128)S(1)} %copy-done.9, s32[4]{0:T(128)S(1)} %copy-done.7, f32[4]{0:T(128)S(1)} %copy-done.8, bf16[32,16,1280]{2,1,0:T(8,128)(2,1)S(1)} %all-to-all-done.gathered_ref.refs_6_, ...), custom_call_target="tpu_custom_call" | custom-call | flops 67108864 | bytes 1048576 | tf_op jit(solution)/shard_map/pallas_call | solution.py:287
  52.0 2.0 %collective-permute-start.8 = (f32[512,128]{1,0:T(8,128)S(1)}, f32[512,128]{1,0:T(8,128)S(1)}, u32[]{:S(2)}, u32[]{:S(2)}) collective-permute-start(f32[512,128]{1,0:T(8,128)S(1)} %get-tuple-element.36), channel_id=1, source_target_pairs={{0,1},{1,0},{2,3},{3,2},{4,5},{5,4},{6,7},{7,6},{8,9},{9,8},{10,11... | collective-permute-start | bytes 786440 | tf_op jit(solution)/shard_map/ppermute | solution.py:45
  54.0 1.2 collective-permute-done.8
  55.2 2.9 %collective-permute-start.11 = (bf16[512,128]{1,0:T(8,128)(2,1)S(1)}, bf16[512,128]{1,0:T(8,128)(2,1)S(1)}, u32[]{:S(2)}, u32[]{:S(2)}) collective-permute-start(bf16[512,128]{1,0:T(8,128)(2,1)S(1)} %add_convert_fusion.own), channel_id=1, source_target_pairs={{0,4},{1,5},{2,6},{3,7},{4,0},{5,1},{6,2},{7,3},{8,12},{9,13},{10,... | collective-permute-start | bytes 393224 | tf_op jit(solution)/shard_map/ppermute | solution.py:45
  58.1 0.8 collective-permute-start.10
  58.9 0.7 collective-permute-start.9
  59.6 2.0 %collective-permute-done.11.third = bf16[512,128]{1,0:T(8,128)(2,1)S(1)} collective-permute-done((bf16[512,128]{1,0:T(8,128)(2,1)S(1)}, bf16[512,128]{1,0:T(8,128)(2,1)S(1)}, u32[]{:S(2)}, u32[]{:S(2)}) %collective-permute-start.11) | collective-permute-done | bytes 131104 | tf_op jit(solution)/shard_map/ppermute | solution.py:45
  61.5 3.1 %collective-permute-done.10.second = bf16[512,128]{1,0:T(8,128)(2,1)S(1)} collective-permute-done((bf16[512,128]{1,0:T(8,128)(2,1)S(1)}, bf16[512,128]{1,0:T(8,128)(2,1)S(1)}, u32[]{:S(2)}, u32[]{:S(2)}) %collective-permute-start.10) | collective-permute-done | bytes 131104 | tf_op jit(solution)/shard_map/ppermute | solution.py:45
  64.7 1.1 shard_map.142
  65.8 1.0 copy-done.3
  66.8 0.6 copy-done.5
  67.5 4.2 %collective-permute-done.13.refs_11_ = bf16[4096,128]{1,0:T(8,128)(2,1)} collective-permute-done((bf16[4096,128]{1,0:T(8,128)(2,1)}, bf16[4096,128]{1,0:T(8,128)(2,1)}, u32[]{:S(2)}, u32[]{:S(2)}) %collective-permute-start.13) | collective-permute-done | bytes 1048608 | tf_op jit(solution)/shard_map/ppermute | solution.py:50
  71.7 3.1 %collective-permute-done.12.refs_10_ = bf16[4096,128]{1,0:T(8,128)(2,1)} collective-permute-done((bf16[4096,128]{1,0:T(8,128)(2,1)}, bf16[4096,128]{1,0:T(8,128)(2,1)}, u32[]{:S(2)}, u32[]{:S(2)}) %collective-permute-start.12) | collective-permute-done | bytes 1048608 | tf_op jit(solution)/shard_map/ppermute | solution.py:50
  74.8 6.9 %all-to-all-start.1 = ((bf16[32,16,1152]{2,1,0:T(8,128)(2,1)}), bf16[32,16,1152]{2,1,0:T(8,128)(2,1)S(1)}, u32[]{:S(2)}, u32[]{:S(2)}) async-start(bf16[32,16,1152]{2,1,0:T(8,128)(2,1)} %copy-done.3), calls=%async_computation.1 | async-start | bytes 2359296 | tf_op jit(solution)/shard_map/all_to_all | solution.py:314
  81.7 0.0 copy-start.23
  81.8 0.7 slice_dynamic-update-slice_fusion.7
  82.4 0.7 slice_dynamic-update-slice_fusion.6
  83.1 3.1 %collective-permute-start.7 = (bf16[4096,128]{1,0:T(8,128)(2,1)}, bf16[4096,128]{1,0:T(8,128)(2,1)S(1)}, u32[]{:S(2)}, u32[]{:S(2)}) collective-permute-start(bf16[4096,128]{1,0:T(8,128)(2,1)} %slice_dynamic-update-slice_fusion.6), channel_id=1, source_target_pairs={{0,1},{1,0},{2,3},{3,2},{4,5},{5,4},{6,7},{7,6},{8,9},{9,8},{10,11... | collective-permute-start | bytes 3145736 | tf_op jit(solution)/shard_map/ppermute | solution.py:45
  86.2 1.1 slice.54
  87.3 1.1 slice.55
  88.3 2.8 %collective-permute-start.15 = (bf16[2048,128]{1,0:T(8,128)(2,1)S(1)}, bf16[2048,128]{1,0:T(8,128)(2,1)S(1)}, u32[]{:S(2)}, u32[]{:S(2)}) collective-permute-start(bf16[2048,128]{1,0:T(8,128)(2,1)S(1)} %slice.55), channel_id=1, source_target_pairs={{0,24},{8,0},{16,8},{24,16},{32,56},{40,32},{48,40},{56,48},{64,88... | collective-permute-start | bytes 1572872 | tf_op jit(solution)/shard_map/ppermute | solution.py:50
  91.2 0.5 and_select_fusion.2.quarters
  91.7 18.5 %collective-permute-done.15.refs_13_ = bf16[2048,128]{1,0:T(8,128)(2,1)S(1)} collective-permute-done((bf16[2048,128]{1,0:T(8,128)(2,1)S(1)}, bf16[2048,128]{1,0:T(8,128)(2,1)S(1)}, u32[]{:S(2)}, u32[]{:S(2)}) %collective-permute-start.15) | collective-permute-done | bytes 524320 | tf_op jit(solution)/shard_map/ppermute | solution.py:50
  110.2 3.8 %collective-permute-done.14.refs_12_ = bf16[2048,128]{1,0:T(8,128)(2,1)S(1)} collective-permute-done((bf16[2048,128]{1,0:T(8,128)(2,1)S(1)}, bf16[2048,128]{1,0:T(8,128)(2,1)S(1)}, u32[]{:S(2)}, u32[]{:S(2)}) %collective-permute-start.14) | collective-permute-done | bytes 524320 | tf_op jit(solution)/shard_map/ppermute | solution.py:50
  114.0 0.8 copy-done.17
  114.8 7.8 %shard_map.143 = bf16[512,1024]{1,0:T(8,128)(2,1)} custom-call(s32[4]{0:T(128)} %copy-done.6, s32[4]{0:T(128)} %and_select_fusion.2.quarters, bf16[2,512,128]{2,1,0:T(8,128)(2,1)} %bitcast.15, bf16[2048,128]{1,0:T(8,128)(2,1)} %copy-done.10, bf16[2048,128]{1,0:T(8,128)(2,1)} %copy-done.11, bf16[1024,128]{1,0:T(8,128)(2,1)} %copy-done.13, ...), custom_call_target="tpu_custom_call" | custom-call | flops 2415919104 | bytes 8388608 | tf_op jit(solution)/shard_map/pallas_call | solution.py:334
  122.6 0.8 shard_map.144
  (46 shorter events, 0.1 us)
Async XLA Ops:
  2.6 12.0 %copy-start.18 = (bf16[512,2,128]{2,1,0:T(2,128)(2,1)S(1)}, bf16[512,2,128]{2,1,0:T(2,128)(2,1)}, u32[]{:S(2)}) copy-start(bf16[512,2,128]{2,1,0:T(2,128)(2,1)} %param.13) | copy-start | bytes 786436
  2.6 12.8 %copy-start.19 = (s32[8,1]{0,1:T(1,128)S(1)}, s32[8,1]{0,1:T(1,128)}, u32[]{:S(2)}) copy-start(s32[8,1]{0,1:T(1,128)} %constant.80) | copy-start | bytes 100
  2.6 12.8 %copy-start.20 = (s32[8,1]{0,1:T(1,128)S(1)}, s32[8,1]{0,1:T(1,128)}, u32[]{:S(2)}) copy-start(s32[8,1]{0,1:T(1,128)} %constant.79) | copy-start | bytes 100
  2.6 45.5 %all-to-all-start = ((bf16[32,16,1280]{2,1,0:T(8,128)(2,1)}), bf16[32,16,1280]{2,1,0:T(8,128)(2,1)S(1)}, u32[]{:S(2)}, u32[]{:S(2)}) async-start(bf16[32,16,1280]{2,1,0:T(8,128)(2,1)} %shard_map.140), calls=%async_computation | async-start | bytes 2621440 | tf_op jit(solution)/shard_map/all_to_all | solution.py:256
  15.9 12.0 %copy-start.1 = (bf16[512,2,128]{2,0,1:T(8,128)(2,1)S(1)}, bf16[512,2,128]{2,0,1:T(8,128)(2,1)}, u32[]{:S(2)}) copy-start(bf16[512,2,128]{2,0,1:T(8,128)(2,1)} %copy.19) | copy-start | bytes 786436
  19.3 14.0 %collective-permute-start = (bf16[2048,128]{1,0:T(8,128)(2,1)}, bf16[2048,128]{1,0:T(8,128)(2,1)S(1)}, u32[]{:S(2)}, u32[]{:S(2)}) collective-permute-start(bf16[2048,128]{1,0:T(8,128)(2,1)} %get-tuple-element.25), channel_id=1, source_target_pairs={{0,2},{1,3},{2,4},{3,5},{4,6},{5,7},{6,0},{7,1},{8,10},{9,11},{10,... | collective-permute-start | bytes 1572872 | tf_op jit(solution)/shard_map/ppermute | solution.py:45
  20.6 13.5 %collective-permute-start.1 = (bf16[2048,128]{1,0:T(8,128)(2,1)}, bf16[2048,128]{1,0:T(8,128)(2,1)S(1)}, u32[]{:S(2)}, u32[]{:S(2)}) collective-permute-start(bf16[2048,128]{1,0:T(8,128)(2,1)} %get-tuple-element.26), channel_id=1, source_target_pairs={{0,6},{1,7},{2,0},{3,1},{4,2},{5,3},{6,4},{7,5},{8,14},{9,15},{10,... | collective-permute-start | bytes 1572872 | tf_op jit(solution)/shard_map/ppermute | solution.py:45
  22.1 20.9 %collective-permute-start.3 = (bf16[512,128]{1,0:T(8,128)(2,1)}, bf16[512,128]{1,0:T(8,128)(2,1)S(1)}, u32[]{:S(2)}, u32[]{:S(2)}) collective-permute-start(bf16[512,128]{1,0:T(8,128)(2,1)} %get-tuple-element.29), channel_id=1, source_target_pairs={{0,1},{1,0},{2,3},{3,2},{4,5},{5,4},{6,7},{7,6},{8,9},{9,8},{10,11... | collective-permute-start | bytes 393224 | tf_op jit(solution)/shard_map/ppermute | solution.py:45
  23.4 20.2 %collective-permute-start.4 = (bf16[512,128]{1,0:T(8,128)(2,1)}, bf16[512,128]{1,0:T(8,128)(2,1)S(1)}, u32[]{:S(2)}, u32[]{:S(2)}) collective-permute-start(bf16[512,128]{1,0:T(8,128)(2,1)} %get-tuple-element.30), channel_id=1, source_target_pairs={{0,3},{1,2},{2,5},{3,4},{4,7},{5,6},{6,1},{7,0},{8,11},{9,10},{10,... | collective-permute-start | bytes 393224 | tf_op jit(solution)/shard_map/ppermute | solution.py:45
  23.4 20.8 %collective-permute-start.5 = (bf16[512,128]{1,0:T(8,128)(2,1)}, bf16[512,128]{1,0:T(8,128)(2,1)S(1)}, u32[]{:S(2)}, u32[]{:S(2)}) collective-permute-start(bf16[512,128]{1,0:T(8,128)(2,1)} %get-tuple-element.31), channel_id=1, source_target_pairs={{0,7},{1,6},{2,1},{3,0},{4,3},{5,2},{6,5},{7,4},{8,15},{9,14},{10,... | collective-permute-start | bytes 393224 | tf_op jit(solution)/shard_map/ppermute | solution.py:45
  33.3 9.0 %copy-start.10 = (bf16[2048,128]{1,0:T(8,128)(2,1)}, bf16[2048,128]{1,0:T(8,128)(2,1)S(1)}, u32[]{:S(2)}) copy-start(bf16[2048,128]{1,0:T(8,128)(2,1)S(1)} %collective-permute-done.refs_1_) | copy-start | bytes 1572868
  34.1 10.9 %copy-start.11 = (bf16[2048,128]{1,0:T(8,128)(2,1)}, bf16[2048,128]{1,0:T(8,128)(2,1)S(1)}, u32[]{:S(2)}) copy-start(bf16[2048,128]{1,0:T(8,128)(2,1)S(1)} %collective-permute-done.1.refs_2_) | copy-start | bytes 1572868
  34.1 16.5 %copy-start.21 = (s32[8]{0:T(128)S(1)}, s32[8]{0:T(128)}, u32[]{:S(2)}) copy-start(s32[8]{0:T(128)} %param.17) | copy-start | bytes 100
  34.1 16.5 %copy-start.22 = (s32[4]{0:T(128)S(1)}, s32[4]{0:T(128)}, u32[]{:S(2)}) copy-start(s32[4]{0:T(128)} %param.18) | copy-start | bytes 52
  34.1 16.7 %copy-start.2 = (bf16[512,1024]{1,0:T(8,128)(2,1)S(1)}, bf16[512,1024]{1,0:T(8,128)(2,1)}, u32[]{:S(2)}) copy-start(bf16[512,1024]{1,0:T(8,128)(2,1)} %x_ref.3) | copy-start | bytes 3145732
  34.1 16.6 %copy-start.7 = (s32[4]{0:T(128)S(1)}, s32[4]{0:T(128)}, u32[]{:S(2)}) copy-start(s32[4]{0:T(128)} %prompt.1) | copy-start | bytes 52
  34.1 16.6 %copy-start.8 = (f32[4]{0:T(128)S(1)}, f32[4]{0:T(128)}, u32[]{:S(2)}) copy-start(f32[4]{0:T(128)} %reward.1) | copy-start | bytes 52
  34.1 16.6 %copy-start.9 = (s32[4]{0:T(128)S(1)}, s32[4]{0:T(128)}, u32[]{:S(2)}) copy-start(s32[4]{0:T(128)} %live.1) | copy-start | bytes 52
  34.9 7.4 %collective-permute-start.2 = (bf16[1024,128]{1,0:T(8,128)(2,1)S(1)}, bf16[1024,128]{1,0:T(8,128)(2,1)S(1)}, u32[]{:S(2)}, u32[]{:S(2)}) collective-permute-start(bf16[1024,128]{1,0:T(8,128)(2,1)S(1)} %get-tuple-element.28), channel_id=1, source_target_pairs={{0,2},{1,3},{2,4},{3,5},{4,6},{5,7},{6,0},{7,1},{8,10},{9,11},{10,... | collective-permute-start | bytes 786440 | tf_op jit(solution)/shard_map/ppermute | solution.py:45
  35.0 11.7 %collective-permute-start.6 = (bf16[1024,128]{1,0:T(8,128)(2,1)S(1)}, bf16[1024,128]{1,0:T(8,128)(2,1)S(1)}, u32[]{:S(2)}, u32[]{:S(2)}) collective-permute-start(bf16[1024,128]{1,0:T(8,128)(2,1)S(1)} %get-tuple-element.32), channel_id=1, source_target_pairs={{0,7},{1,6},{2,1},{3,0},{4,3},{5,2},{6,5},{7,4},{8,15},{9,14},{10,... | collective-permute-start | bytes 786440 | tf_op jit(solution)/shard_map/ppermute | solution.py:45
  42.2 39.5 %copy-start.13 = (bf16[1024,128]{1,0:T(8,128)(2,1)}, bf16[1024,128]{1,0:T(8,128)(2,1)S(1)}, u32[]{:S(2)}) copy-start(bf16[1024,128]{1,0:T(8,128)(2,1)S(1)} %collective-permute-done.2.refs_3_) | copy-start | bytes 786436
  46.7 0.7 copy-start.14
  48.1 3.9 %copy-start = (bf16[32,16,1280]{2,1,0:T(8,128)(2,1)}, bf16[32,16,1280]{2,1,0:T(8,128)(2,1)S(1)}, u32[]{:S(2)}) copy-start(bf16[32,16,1280]{2,1,0:T(8,128)(2,1)S(1)} %all-to-all-done.gathered_ref.refs_6_) | copy-start | bytes 3932164
  48.1 23.6 %collective-permute-start.13 = (bf16[4096,128]{1,0:T(8,128)(2,1)}, bf16[4096,128]{1,0:T(8,128)(2,1)}, u32[]{:S(2)}, u32[]{:S(2)}) collective-permute-start(bf16[4096,128]{1,0:T(8,128)(2,1)} %slice_dynamic-update-slice_fusion.2.refs_9_), channel_id=1, source_target_pairs={{0,24},{8,0},{16,8},{24,16},{32,56},{40,32},{48,40},{56,48},{64,88... | collective-permute-start | bytes 3145736 | tf_op jit(solution)/shard_map/ppermute | solution.py:50
  50.5 24.3 %collective-permute-start.12 = (bf16[4096,128]{1,0:T(8,128)(2,1)}, bf16[4096,128]{1,0:T(8,128)(2,1)}, u32[]{:S(2)}, u32[]{:S(2)}) collective-permute-start(bf16[4096,128]{1,0:T(8,128)(2,1)} %slice_dynamic-update-slice_fusion.2.refs_9_), channel_id=1, source_target_pairs={{0,8},{8,16},{16,24},{24,0},{32,40},{40,48},{48,56},{56,32},{64,72... | collective-permute-start | bytes 3145736 | tf_op jit(solution)/shard_map/ppermute | solution.py:50
  50.8 13.9 %copy-start.6 = (s32[4]{0:T(128)}, s32[4]{0:T(128)S(1)}, u32[]{:S(2)}) copy-start(s32[4]{0:T(128)S(1)} %select_reduce_fusion.slots) | copy-start | bytes 52
  52.0 12.6 %copy-start.4 = (f32[512,1]{1,0:T(8,128)}, f32[512,1]{1,0:T(8,128)S(1)}, u32[]{:S(2)}) copy-start(f32[512,1]{1,0:T(8,128)S(1)} %get-tuple-element.39.refs_8_) | copy-start | bytes 6148
  52.0 3.1 %collective-permute-start.8 = (f32[512,128]{1,0:T(8,128)S(1)}, f32[512,128]{1,0:T(8,128)S(1)}, u32[]{:S(2)}, u32[]{:S(2)}) collective-permute-start(f32[512,128]{1,0:T(8,128)S(1)} %get-tuple-element.36), channel_id=1, source_target_pairs={{0,1},{1,0},{2,3},{3,2},{4,5},{5,4},{6,7},{7,6},{8,9},{9,8},{10,11... | collective-permute-start | bytes 786440 | tf_op jit(solution)/shard_map/ppermute | solution.py:45
  55.2 6.3 %collective-permute-start.11 = (bf16[512,128]{1,0:T(8,128)(2,1)S(1)}, bf16[512,128]{1,0:T(8,128)(2,1)S(1)}, u32[]{:S(2)}, u32[]{:S(2)}) collective-permute-start(bf16[512,128]{1,0:T(8,128)(2,1)S(1)} %add_convert_fusion.own), channel_id=1, source_target_pairs={{0,4},{1,5},{2,6},{3,7},{4,0},{5,1},{6,2},{7,3},{8,12},{9,13},{10,... | collective-permute-start | bytes 393224 | tf_op jit(solution)/shard_map/ppermute | solution.py:45
  58.1 6.6 %collective-permute-start.10 = (bf16[512,128]{1,0:T(8,128)(2,1)S(1)}, bf16[512,128]{1,0:T(8,128)(2,1)S(1)}, u32[]{:S(2)}, u32[]{:S(2)}) collective-permute-start(bf16[512,128]{1,0:T(8,128)(2,1)S(1)} %add_convert_fusion.own), channel_id=1, source_target_pairs={{0,6},{1,7},{2,0},{3,1},{4,2},{5,3},{6,4},{7,5},{8,14},{9,15},{10,... | collective-permute-start | bytes 393224 | tf_op jit(solution)/shard_map/ppermute | solution.py:45
  58.9 5.8 %collective-permute-start.9 = (bf16[512,128]{1,0:T(8,128)(2,1)S(1)}, bf16[512,128]{1,0:T(8,128)(2,1)S(1)}, u32[]{:S(2)}, u32[]{:S(2)}) collective-permute-start(bf16[512,128]{1,0:T(8,128)(2,1)S(1)} %add_convert_fusion.own), channel_id=1, source_target_pairs={{0,2},{1,3},{2,4},{3,5},{4,6},{5,7},{6,0},{7,1},{8,10},{9,11},{10,... | collective-permute-start | bytes 393224 | tf_op jit(solution)/shard_map/ppermute | solution.py:45
  65.8 1.0 copy-start.3
  66.8 0.7 copy-start.5
  74.8 7.6 %copy-start.15 = (bf16[1024,128]{1,0:T(8,128)(2,1)S(1)}, bf16[1024,128]{1,0:T(8,128)(2,1)}, u32[]{:S(2)}) copy-start(bf16[1024,128]{1,0:T(8,128)(2,1)} %copy-done.14) | copy-start | bytes 786436
  74.8 47.8 %all-to-all-start.1 = ((bf16[32,16,1152]{2,1,0:T(8,128)(2,1)}), bf16[32,16,1152]{2,1,0:T(8,128)(2,1)S(1)}, u32[]{:S(2)}, u32[]{:S(2)}) async-start(bf16[32,16,1152]{2,1,0:T(8,128)(2,1)} %copy-done.3), calls=%async_computation.1 | async-start | bytes 2359296 | tf_op jit(solution)/shard_map/all_to_all | solution.py:314
  81.7 9.4 %copy-start.23 = (s32[4]{0:T(128)S(1)}, s32[4]{0:T(128)}, u32[]{:S(2)}) copy-start(s32[4]{0:T(128)} %constant.72.clone) | copy-start | bytes 52
  83.1 8.6 %collective-permute-start.7 = (bf16[4096,128]{1,0:T(8,128)(2,1)}, bf16[4096,128]{1,0:T(8,128)(2,1)S(1)}, u32[]{:S(2)}, u32[]{:S(2)}) collective-permute-start(bf16[4096,128]{1,0:T(8,128)(2,1)} %slice_dynamic-update-slice_fusion.6), channel_id=1, source_target_pairs={{0,1},{1,0},{2,3},{3,2},{4,5},{5,4},{6,7},{7,6},{8,9},{9,8},{10,11... | collective-permute-start | bytes 3145736 | tf_op jit(solution)/shard_map/ppermute | solution.py:45
  88.3 21.8 %collective-permute-start.15 = (bf16[2048,128]{1,0:T(8,128)(2,1)S(1)}, bf16[2048,128]{1,0:T(8,128)(2,1)S(1)}, u32[]{:S(2)}, u32[]{:S(2)}) collective-permute-start(bf16[2048,128]{1,0:T(8,128)(2,1)S(1)} %slice.55), channel_id=1, source_target_pairs={{0,24},{8,0},{16,8},{24,16},{32,56},{40,32},{48,40},{56,48},{64,88... | collective-permute-start | bytes 1572872 | tf_op jit(solution)/shard_map/ppermute | solution.py:50
  91.1 22.8 %collective-permute-start.14 = (bf16[2048,128]{1,0:T(8,128)(2,1)S(1)}, bf16[2048,128]{1,0:T(8,128)(2,1)S(1)}, u32[]{:S(2)}, u32[]{:S(2)}) collective-permute-start(bf16[2048,128]{1,0:T(8,128)(2,1)S(1)} %slice.54), channel_id=1, source_target_pairs={{0,8},{8,16},{16,24},{24,0},{32,40},{40,48},{48,56},{56,32},{64,72... | collective-permute-start | bytes 1572872 | tf_op jit(solution)/shard_map/ppermute | solution.py:50
  91.7 22.3 %copy-start.12 = (bf16[4096,128]{1,0:T(8,128)(2,1)}, bf16[4096,128]{1,0:T(8,128)(2,1)S(1)}, u32[]{:S(2)}) copy-start(bf16[4096,128]{1,0:T(8,128)(2,1)S(1)} %collective-permute-done.7.refs_5_) | copy-start | bytes 3145732
  110.2 3.8 %copy-start.16 = (bf16[2048,128]{1,0:T(8,128)(2,1)}, bf16[2048,128]{1,0:T(8,128)(2,1)S(1)}, u32[]{:S(2)}) copy-start(bf16[2048,128]{1,0:T(8,128)(2,1)S(1)} %collective-permute-done.15.refs_13_) | copy-start | bytes 1572868
  114.0 0.8 copy-start.17

commit v5 on v4

--- a/solution.py
+++ b/solution.py
@@ -1,3 +1,5 @@
+import functools
+
 import jax
 import jax.numpy as jnp
 from jax import lax
@@ -85,43 +87,58 @@
     )
 
 
+def assemble_kernel(cuts, *refs):
+    *pieces, out_ref = refs
+    at = 0
+    for piece, (start, stop) in zip(pieces, cuts, strict=True):
+        out_ref[at : at + stop - start] = piece[start:stop]
+        at += stop - start
+
+
+def assemble(*pieces):
+    arrays = [p[0] for p in pieces]
+    cuts = [p[1:] for p in pieces]
+    columns = arrays[0].shape[1]
+    total = sum(stop - start for start, stop in cuts)
+    whole = lambda shape: pl.BlockSpec(shape, lambda i: (0,) * len(shape))
+    return pl.pallas_call(
+        functools.partial(assemble_kernel, cuts),
+        grid=(1,),
+        in_specs=[whole(v.shape) for v in arrays],
+        out_specs=whole((total, columns)),
+        out_shape=jax.ShapeDtypeStruct((total, columns), BF),
+        compiler_params=pltpu.CompilerParams(vmem_limit_bytes=24 * 2**20),
+    )(*arrays)
+
+
 def payload_kernel(places, *refs):
-    *slabs, cot_ref, next_ref, next_other, prev_ref, prev_other, mine_ref, other_ref = refs
-    tile, rows = slabs[0].shape[1], cot_ref.shape[1]
-    key, value = (cot_ref.at[0],), (cot_ref.at[1],)
-    slab = lambda i: (slabs[i].at[0], slabs[i].at[1])
-    orders = (
-        (next_ref, (slab(0), slab(2), key, value)),
-        (next_other, (slab(1),)),
-        (prev_ref, (slab(3), key, value, slab(5))),
-        (prev_other, (slab(4),)),
-        (mine_ref, (slab(6),)),
-        (other_ref, (slab(7),)),
-    )
-    for out_ref, units in orders:
+    slabs, outs = refs[:8], refs[8:]
+    tile = slabs[0].shape[1]
+    for out_ref, units in zip(outs, ((0, 2), (1,), (3, 5), (4,), (6,), (7,)), strict=True):
         at = 0
-        for piece in (p for unit in units for p in unit):
-            out_ref[at : at + piece.shape[0]] = piece[...]
-            at += piece.shape[0]
-
-
-def payloads(places, weight, cotangent, tile):
+        for i in units:
+            for j in range(2):
+                out_ref[at : at + tile] = slabs[i][j]
+                at += tile
+
+
+def payloads(places, weight, tile):
     columns = weight.shape[2]
     slab = [
         pl.BlockSpec((2, tile, columns), lambda g, p, i=i: (0, p[i], 0)) for i in range(8)
     ]
-    sizes = [n * 2 * tile for n in (4, 1, 4, 1, 1, 1)]
+    sizes = [n * 2 * tile for n in (2, 1, 2, 1, 1, 1)]
     return pl.pallas_call(
         payload_kernel,
         grid_spec=pltpu.PrefetchScalarGridSpec(
             num_scalar_prefetch=1,
             grid=(1,),
-            in_specs=[*slab, pl.BlockSpec(cotangent.shape, lambda g, p: (0, 0, 0))],
+            in_specs=slab,
             out_specs=[pl.BlockSpec((n, columns), lambda g, p: (0, 0)) for n in sizes],
         ),
         out_shape=[jax.ShapeDtypeStruct((n, columns), BF) for n in sizes],
         compiler_params=pltpu.CompilerParams(vmem_limit_bytes=FULL_VMEM),
-    )(places, *[weight] * 8, cotangent)
+    )(places, *[weight] * 8)
 
 
 def factor_rows(ref, slot, start, size):
@@ -159,12 +176,11 @@
         coef_ref[rows, :] = coef
 
 
-def terms_kernel(slots, own, first, second, third, x_ref, weighted_ref, terms_ref, low_ref):
+def terms_kernel(slots, own, received, x_ref, weighted_ref, terms_ref, low_ref):
     window = x_ref.shape[1]
     columns = weighted_ref.shape[1]
     owners, owned = terms_ref.shape[0] // SLOTS, terms_ref.shape[1]
-    low = own[...].astype(F32) + first[...].astype(F32)
-    low = (low + second[...].astype(F32)) + third[...].astype(F32)
+    low = own[...].astype(F32) + received[...].astype(F32)
     low_ref[...] = low.astype(BF)
     for i in range(terms_ref.shape[0]):
         terms_ref[i] = jnp.zeros(terms_ref.shape[1:], BF)
@@ -178,32 +194,76 @@
         terms_ref[place, :, window:] = up.astype(BF).reshape(owners, owned, columns)
 
 
-def frozen_kernel(slots, quarters, *refs):
-    own, before, after, hop_next, hop_prev, swapped, *refs = refs
-    gathered_ref, low_ref, coef_ref, w0, w1, w2, w3a, w3b, out_ref, weighted = refs
-    rows, columns = own.shape[1:]
+def quarter(weighted, parts, low_ref, gathered_ref, slots, start, tile):
+    slabs = [p[i * tile : (i + 1) * tile] for p in parts for i in range(p.shape[0] // tile)]
+    total = dot(weighted[...], jnp.concatenate(slabs, axis=1), 1, 1)
+    extra = []
+    for b in range(total.shape[0] // BLOCK):
+        factor = factor_rows(gathered_ref, slots[b], start, tile)
+        factor = jnp.concatenate([jnp.zeros_like(factor), factor], axis=0)
+        low = low_ref[b * BLOCK : (b + 1) * BLOCK, :]
+        extra.append(LOWRANK_MULTIPLIER * dot(low, factor, 1, 0))
+    return (total + jnp.concatenate(extra, axis=0)).astype(BF)
+
+
+def near_kernel(slots, quarters, cots, others, gathered_ref, low_ref, coef_ref, *refs):
+    *slabs, out_ref, weighted = refs
+    rows, columns = coef_ref.shape[0], cots.shape[1]
     tile = rows // 2
     coef = coef_ref[...]
-    pieces = [own.at[0], own.at[1]]
-    pieces += [before.at[pl.ds(i * rows, rows)] for i in (2, 3)]
-    pieces += [after.at[pl.ds(i * rows, rows)] for i in (1, 2)]
-    pieces += [hop_next.at[pl.ds(rows, rows)], swapped.at[pl.ds(7 * rows, rows)]]
-    pieces += [swapped.at[pl.ds(i * rows, rows)] for i in range(7)]
-    pieces += [hop_prev.at[pl.ds(0, rows)]]
-    for i, piece in enumerate(pieces):
-        weighted[:, i * columns : (i + 1) * columns] = (piece[...].astype(F32) * coef).astype(BF)
-    for r, parts in enumerate(((w0,), (w1,), (w2,), (w3a, w3b))):
-        slabs = [
-            p[i * tile : (i + 1) * tile] for p in parts for i in range(p.shape[0] // tile)
-        ]
-        total = dot(weighted[...], jnp.concatenate(slabs, axis=1), 1, 1)
+    count = cots.shape[0] // rows
+    for i in range(2 * count):
+        piece = (cots, others)[i // count][i % count * rows : (i % count + 1) * rows]
+        weighted[:, i * columns : (i + 1) * columns] = (piece.astype(F32) * coef).astype(BF)
+    for r, part in enumerate(slabs):
         start = pl.multiple_of(quarters[r] * tile, tile)
-        for b in range(rows // BLOCK):
-            block = slice(b * BLOCK, (b + 1) * BLOCK)
-            factor = factor_rows(gathered_ref, slots[b], start, tile)
-            factor = jnp.concatenate([jnp.zeros_like(factor), factor], axis=0)
-            extra = LOWRANK_MULTIPLIER * dot(low_ref[block, :], factor, 1, 0)
-            out_ref[block, pl.ds(start, tile)] = (total[block] + extra).astype(BF)
+        out_ref[:, pl.ds(start, tile)] = quarter(
+            weighted, (part,), low_ref, gathered_ref, slots, start, tile
+        )
+
+
+def far_kernel(slots, quarters, near_ref, weighted, gathered_ref, low_ref, first, second, out_ref):
+    tile = out_ref.shape[1]
+    out_ref[...] = quarter(weighted, (first, second), low_ref, gathered_ref, slots, 0, tile)
+
+
+def frozen_and_correction(slots, quarters, cots, adapter, near, far, window):
+    gathered, low, coef = adapter
+    rows, columns, tile = coef.shape[0], cots[0].shape[1], window // 4
+    depth = 2 * cots[0].shape[0] // rows * columns
+    shape = jax.ShapeDtypeStruct
+    whole = lambda dims: pl.BlockSpec(dims, lambda i, *_: (0,) * len(dims))
+    streams = [*cots, gathered, low, coef, *near]
+    partial, weighted = pl.pallas_call(
+        near_kernel,
+        grid_spec=pltpu.PrefetchScalarGridSpec(
+            num_scalar_prefetch=2,
+            grid=(1,),
+            in_specs=[whole(v.shape) for v in streams],
+            out_specs=[whole((rows, window)), whole((rows, depth))],
+        ),
+        out_shape=[shape((rows, window), BF), shape((rows, depth), BF)],
+        compiler_params=pltpu.CompilerParams(vmem_limit_bytes=FULL_VMEM),
+    )(slots, quarters, *streams)
+    owners, owned = gathered.shape[:2]
+    return pl.pallas_call(
+        far_kernel,
+        grid_spec=pltpu.PrefetchScalarGridSpec(
+            num_scalar_prefetch=2,
+            grid=(1,),
+            in_specs=[
+                pl.BlockSpec(memory_space=pl.ANY),
+                whole(weighted.shape),
+                pl.BlockSpec((owners, owned, tile), lambda i, s, q: (0, 0, q[3])),
+                whole(low.shape),
+                *[whole(v.shape) for v in far],
+            ],
+            out_specs=pl.BlockSpec((rows, tile), lambda i, s, q: (0, q[3])),
+        ),
+        out_shape=shape((rows, window), BF),
+        input_output_aliases={2: 0},
+        compiler_params=pltpu.CompilerParams(vmem_limit_bytes=FULL_VMEM),
+    )(slots, quarters, partial, weighted, gathered, low, *far)
 
 
 def sum_kernel(terms_ref, down_ref, up_ref):
@@ -259,30 +319,18 @@
     steps = jnp.array([[1, 0], [1, 1], [2, 0], [3, 0], [3, 1], [2, 1], [0, 0], [0, 1]], jnp.int32)
     targets = (chip + steps[:, 0]) % CHIPS * 2 + (core + steps[:, 1]) % 2
     to_next, next_other, to_prev, prev_other, mine, other = payloads(
-        targets * 4 + x, key_value_weight, cotangent, tile
+        targets * 4 + x, key_value_weight, tile
     )
     before, after = tensor_send(to_next, 1, 0), tensor_send(to_prev, 3, 0)
     before_other, after_other = tensor_send(next_other, 1, 1), tensor_send(prev_other, 3, 1)
     partner = tensor_send(other, 0, 1)
     unit = 2 * tile
-    part = lambda v, start, stop: v[start * unit : stop * unit]
-    hop_next, hop_prev = lax.optimization_barrier((part(before, 1, 3), part(after, 2, 4)))
+    hop_next, hop_prev = lax.optimization_barrier((before[unit:], after[unit:]))
     hop_next, hop_prev = tensor_send(hop_next, 1, 0), tensor_send(hop_prev, 3, 1)
-    slabs = jnp.concatenate(
-        [
-            mine,
-            part(before, 0, 1),
-            part(after, 0, 1),
-            part(hop_next, 0, 1),
-            partner,
-            before_other,
-            after_other,
-            part(hop_prev, 1, 2),
-        ]
-    )
-    gathered, slabs, hop_next, hop_prev = lax.optimization_barrier(
-        (gathered, slabs, hop_next, hop_prev)
-    )
+    pieces = mine, before, after, hop_next, partner, before_other, after_other, hop_prev
+    slabs = assemble(*[(piece, 0, unit) for piece in pieces])
+    flat = cotangent.reshape(2 * rows, columns)
+    gathered, slabs, flat = lax.optimization_barrier((gathered, slabs, flat))
 
     low, weighted_value, coef = call(
         low_kernel,
@@ -300,52 +348,48 @@
         cotangent,
     )
     low = (low + tensor_send(low, 0, 1)).astype(BF)
-    lows = [low] + [tensor_send(low, s, 0) for s in (1, 3, 2)]
+    for swap in (1, 3):
+        pairs = [(y * 2 + c, (y ^ swap) * 2 + c) for y in range(CHIPS) for c in range(2)]
+        sent = low
+        received = lax.ppermute(sent, "tensor", pairs)
+        if swap == 1:
+            low = (sent.astype(F32) + received.astype(F32)).astype(BF)
     slabs_left, slabs_right = x_send(slabs, 1), x_send(slabs, 3)
+    cot_before, cot_after = tensor_send(flat, 1, 0), tensor_send(flat, 3, 0)
 
     terms, low = call(
         terms_kernel,
-        [SMEM] + [VMEM] * 6,
+        [SMEM] + [VMEM] * 4,
         [shape((dp, owned, window + columns), BF), shape((rows, 2 * RANK), BF)],
         4 * rows * RANK * window,
         16,
-    )(slots, *lows, normed_input_rows, weighted_value)
-    terms, slabs_left, slabs_right = lax.optimization_barrier((terms, slabs_left, slabs_right))
+    )(slots, sent, received, normed_input_rows, weighted_value)
+    cot_next = tensor_send(cot_before[:rows], 1, 0)
+    cot_prev = tensor_send(cot_after[rows:], 3, 0)
+    cots = assemble(
+        (flat, 0, 2 * rows),
+        (cot_before, 0, 2 * rows),
+        (cot_after, 0, 2 * rows),
+        (cot_next, 0, rows),
+        (cot_prev, 0, rows),
+    )
+    cots_other = tensor_send(cots, 0, 1)
+    terms, slabs_left, slabs_right, cots, cots_other = lax.optimization_barrier(
+        (terms, slabs_left, slabs_right, cots, cots_other)
+    )
     terms = lax.all_to_all(terms, "dp", 0, 0)
-    swapped = jnp.concatenate(
-        [
-            cotangent.reshape(2 * rows, columns),
-            part(before, 2, 4),
-            part(after, 1, 3),
-            part(hop_next, 1, 2),
-            part(hop_prev, 0, 1),
-        ]
-    )
-    swapped = tensor_send(swapped, 0, 1)
-
     half = slabs.shape[0] // 2
     slabs_far = (x_send(slabs_left[:half], 1), x_send(slabs_right[half:], 3))
     quarters = (x + jnp.array([0, 3, 1, 2], jnp.int32)) % 4
-    streams = [
-        cotangent, before, after, hop_next, hop_prev, swapped, gathered, low, coef,
-        slabs, slabs_left, slabs_right, *slabs_far,
-    ]
-    whole = lambda dims: pl.BlockSpec(dims, lambda i, *_: (0,) * len(dims))
-    input_gradient = pl.pallas_call(
-        frozen_kernel,
-        grid_spec=pltpu.PrefetchScalarGridSpec(
-            num_scalar_prefetch=2,
-            grid=(1,),
-            in_specs=[whole(v.shape) for v in streams],
-            out_specs=whole((rows, window)),
-            scratch_shapes=[pltpu.VMEM((rows, 16 * columns), BF)],
-        ),
-        out_shape=shape((rows, window), BF),
-        compiler_params=pltpu.CompilerParams(vmem_limit_bytes=FULL_VMEM),
-        cost_estimate=pl.CostEstimate(
-            flops=2 * rows * window * 18 * columns, bytes_accessed=8 * 2**20, transcendentals=0
-        ),
-    )(slots, quarters, *streams)
+    input_gradient = frozen_and_correction(
+        slots,
+        quarters,
+        (cots, cots_other),
+        (gathered, low, coef),
+        (slabs, slabs_left, slabs_right),
+        slabs_far,
+        window,
+    )
     grad_a, grad_b = call(
         sum_kernel,
         [VMEM],

time: 124 us -> 125 us (level)
  local copies, waits for them, and re-layouts: 16 us -> 6.42 us
  Pallas kernels: 16.3 us -> 20.2 us
  starting transfers between devices: 46.8 us -> 49.6 us
  waiting for transfers between devices: 42.3 us -> 44.8 us
    ppermute x4, waiting for transfers between devices: 29.6 us -> 14.8 us  [x_send(): return lax.ppermute(value, 'dp', pairs)]
    ppermute x0 -> x2, waiting for transfers between devices: none -> 10.2 us  [shards(): received = lax.ppermute(sent, 'tensor', pairs)]
    all_to_all x1, waiting for transfers between devices: 0.01 us -> 8.83 us  [shards(): gathered = lax.all_to_all(packed, 'dp', 0, 0)]
    unnamed x60 -> x51, local copies, waits for them, and re-layouts: 12.5 us -> 5.5 us
    pallas_call x2 -> x5, Pallas kernels: 8.93 us -> 13.1 us  [the longest x1 6.69 us: frozen_and_correction(): pl.pallas_call(near_kernel, grid_spec=pltpu.PrefetchScalarGridSpec(num_sc...]
    ppermute x12 -> x13, starting transfers between devices: 22.6 us -> 25 us  [tensor_send(): return lax.ppermute(value, 'tensor', pairs)]
    ppermute x12 -> x13, waiting for transfers between devices: 12.7 us -> 11 us  [tensor_send(): return lax.ppermute(value, 'tensor', pairs)]
    concatenate x2 -> x0, local copies, waits for them, and re-layouts: 1.32 us -> none  [the longest x1 0.66 us: shards(): jnp.concatenate([cotangent.reshape(2 * rows, columns), part(before, 2, 4)...]
  transfers between devices with their start and end apart: 18 -> 21, of which waited for: 9 -> 10; matrix products, arithmetic and copies ran while one was open for 11% -> 2% of each run, Pallas kernels for 11% -> 14%
where the time goes in v5:
time: 125 us; the launch traced here: 123 us
  starting transfers between devices  49.6 us (40%)
  waiting for transfers between devices  44.8 us (36%)
  Pallas kernels  20.2 us (16%)
  local copies, waits for them, and re-layouts  6.42 us (5%)
  other arithmetic  1.29 us (1%)
    ppermute x13, starting transfers between devices, tensor_send(): return lax.ppermute(value, 'tensor', pairs)  25 us
    ppermute x4, waiting for transfers between devices, x_send(): return lax.ppermute(value, 'dp', pairs)  14.8 us
    all_to_all x1, starting transfers between devices, shards(): gathered = lax.all_to_all(packed, 'dp', 0, 0)  12 us
    ppermute x13, waiting for transfers between devices, tensor_send(): return lax.ppermute(value, 'tensor', pairs)  11 us
    ppermute x2, waiting for transfers between devices, shards(): received = lax.ppermute(sent, 'tensor', pairs)  10.2 us
    all_to_all x1, waiting for transfers between devices, shards(): gathered = lax.all_to_all(packed, 'dp', 0, 0)  8.83 us
    pallas_call x1, Pallas kernels, frozen_and_correction(): pl.pallas_call(near_kernel, grid_spec=pltpu.PrefetchScalarGridSpec(num_sc...  6.69 us
    ppermute x4, starting transfers between devices, x_send(): return lax.ppermute(value, 'dp', pairs)  6.5 us
  transfers between devices with their start and end apart: 21, of which 10 were waited for; matrix products, arithmetic and copies ran while one was open for 2% of the time, Pallas kernels for 14%

profile of v5, /device:TPU:1, one launch (start us, length us, event | category | flops | bytes accessed | tf_op | source)
XLA Modules:
  0.0 123.3 jit_solution(12182825518721645626)
XLA Ops:
  0.6 2.0 %shard_map.139 = bf16[32,16,1280]{2,1,0:T(8,128)(2,1)} custom-call(s32[1,4]{1,0:T(1,128)} %bitcast.19, f32[1,4]{1,0:T(1,128)} %bitcast.20, bf16[16,1024]{1,0:T(8,128)(2,1)} %down_ref.1, bf16[16,128]{1,0:T(8,128)(2,1)} %up_ref.1), custom_call_target="tpu_custom_call" | custom-call | tf_op jit(solution)/shard_map/pallas_call | solution.py:306
  2.6 12.0 %all-to-all-start = ((bf16[32,16,1280]{2,1,0:T(8,128)(2,1)}), bf16[32,16,1280]{2,1,0:T(8,128)(2,1)S(1)}, u32[]{:S(2)}, u32[]{:S(2)}) async-start(bf16[32,16,1280]{2,1,0:T(8,128)(2,1)} %shard_map.139), calls=%async_computation | async-start | bytes 2621440 | tf_op jit(solution)/shard_map/all_to_all | solution.py:316
  14.7 0.5 multiply_add_fusion.places
  15.2 3.1 %shard_map.140 = (bf16[1024,128]{1,0:T(8,128)(2,1)}, bf16[512,128]{1,0:T(8,128)(2,1)}, bf16[1024,128]{1,0:T(8,128)(2,1)}, bf16[512,128]{1,0:T(8,128)(2,1)}, bf16...) custom-call(s32[8]{0:T(128)} %multiply_add_fusion.places, bf16[2,8192,128]{2,1,0:T(8,128)(2,1)} %refs_7_.1, ...), custom_call_target="tpu_custom_call" | custom-call | tf_op jit(solution)/shard_map/pallas_call | solution.py:131
  18.3 1.3 %collective-permute-start = (bf16[1024,128]{1,0:T(8,128)(2,1)}, bf16[1024,128]{1,0:T(8,128)(2,1)S(1)}, u32[]{:S(2)}, u32[]{:S(2)}) collective-permute-start(bf16[1024,128]{1,0:T(8,128)(2,1)} %get-tuple-element.29), channel_id=1, source_target_pairs={{0,2},{1,3},{2,4},{3,5},{4,6},{5,7},{6,0},{7,1},{8,10},{9,11},{10,... | collective-permute-start | bytes 786440 | tf_op jit(solution)/shard_map/ppermute | solution.py:47
  19.6 1.5 %collective-permute-start.1 = (bf16[1024,128]{1,0:T(8,128)(2,1)}, bf16[1024,128]{1,0:T(8,128)(2,1)S(1)}, u32[]{:S(2)}, u32[]{:S(2)}) collective-permute-start(bf16[1024,128]{1,0:T(8,128)(2,1)} %get-tuple-element.30), channel_id=1, source_target_pairs={{0,6},{1,7},{2,0},{3,1},{4,2},{5,3},{6,4},{7,5},{8,14},{9,15},{10,... | collective-permute-start | bytes 786440 | tf_op jit(solution)/shard_map/ppermute | solution.py:47
  21.1 1.4 %collective-permute-start.3 = (bf16[512,128]{1,0:T(8,128)(2,1)}, bf16[512,128]{1,0:T(8,128)(2,1)S(1)}, u32[]{:S(2)}, u32[]{:S(2)}) collective-permute-start(bf16[512,128]{1,0:T(8,128)(2,1)} %get-tuple-element.32), channel_id=1, source_target_pairs={{0,1},{1,0},{2,3},{3,2},{4,5},{5,4},{6,7},{7,6},{8,9},{9,8},{10,11... | collective-permute-start | bytes 393224 | tf_op jit(solution)/shard_map/ppermute | solution.py:47
  22.5 0.0 collective-permute-start.4
  22.5 3.0 %collective-permute-start.5 = (bf16[512,128]{1,0:T(8,128)(2,1)}, bf16[512,128]{1,0:T(8,128)(2,1)S(1)}, u32[]{:S(2)}, u32[]{:S(2)}) collective-permute-start(bf16[512,128]{1,0:T(8,128)(2,1)} %get-tuple-element.34), channel_id=1, source_target_pairs={{0,7},{1,6},{2,1},{3,0},{4,3},{5,2},{6,5},{7,4},{8,15},{9,14},{10,... | collective-permute-start | bytes 393224 | tf_op jit(solution)/shard_map/ppermute | solution.py:47
  25.4 1.3 %collective-permute-done.refs_1_ = bf16[1024,128]{1,0:T(8,128)(2,1)S(1)} collective-permute-done((bf16[1024,128]{1,0:T(8,128)(2,1)}, bf16[1024,128]{1,0:T(8,128)(2,1)S(1)}, u32[]{:S(2)}, u32[]{:S(2)}) %collective-permute-start) | collective-permute-done | bytes 262176 | tf_op jit(solution)/shard_map/ppermute | solution.py:47
  26.7 0.0 collective-permute-done.1.refs_2_
  26.7 1.0 collective-permute-start.2
  27.7 5.1 %collective-permute-start.6 = (bf16[512,128]{1,0:T(8,128)(2,1)S(1)}, bf16[512,128]{1,0:T(8,128)(2,1)S(1)}, u32[]{:S(2)}, u32[]{:S(2)}) collective-permute-start(bf16[512,128]{1,0:T(8,128)(2,1)S(1)} %slice.33), channel_id=1, source_target_pairs={{0,7},{1,6},{2,1},{3,0},{4,3},{5,2},{6,5},{7,4},{8,15},{9,14},{10,... | collective-permute-start | bytes 393224 | tf_op jit(solution)/shard_map/ppermute | solution.py:47
  32.9 0.0 copy-start.4
  32.9 0.0 collective-permute-done.3.refs_4_
  32.9 0.0 collective-permute-done.4.refs_5_
  32.9 0.0 collective-permute-done.5.refs_6_
  32.9 0.0 collective-permute-done.2.refs_3_
  32.9 3.7 %collective-permute-done.6.refs_7_ = bf16[512,128]{1,0:T(8,128)(2,1)S(1)} collective-permute-done((bf16[512,128]{1,0:T(8,128)(2,1)S(1)}, bf16[512,128]{1,0:T(8,128)(2,1)S(1)}, u32[]{:S(2)}, u32[]{:S(2)}) %collective-permute-start.6) | collective-permute-done | bytes 131104 | tf_op jit(solution)/shard_map/ppermute | solution.py:47
  36.6 0.9 copy-done.8
  37.6 0.1 shard_map.141.refs_0_
  37.6 8.8 %all-to-all-done.gathered_ref = bf16[32,16,1280]{2,1,0:T(8,128)(2,1)S(1)} async-done(((bf16[32,16,1280]{2,1,0:T(8,128)(2,1)}), bf16[32,16,1280]{2,1,0:T(8,128)(2,1)S(1)}, u32[]{:S(2)}, u32[]{:S(2)}) %all-to-all-start) | async-done | bytes 1310752 | tf_op jit(solution)/shard_map/all_to_all | solution.py:316
  46.5 0.0 copy-start.1
  46.5 2.8 %collective-permute-start.13 = (bf16[1024,128]{1,0:T(8,128)(2,1)S(1)}, bf16[1024,128]{1,0:T(8,128)(2,1)S(1)}, u32[]{:S(2)}, u32[]{:S(2)}) collective-permute-start(bf16[1024,128]{1,0:T(8,128)(2,1)S(1)} %bitcast.15), channel_id=1, source_target_pairs={{0,6},{1,7},{2,0},{3,1},{4,2},{5,3},{6,4},{7,5},{8,14},{9,15},{10,... | collective-permute-start | bytes 786440 | tf_op jit(solution)/shard_map/ppermute | solution.py:47
  49.3 0.0 collective-permute-start.12
  49.3 3.3 %collective-permute-done.13.refs_2_ = bf16[1024,128]{1,0:T(8,128)(2,1)S(1)} collective-permute-done((bf16[1024,128]{1,0:T(8,128)(2,1)S(1)}, bf16[1024,128]{1,0:T(8,128)(2,1)S(1)}, u32[]{:S(2)}, u32[]{:S(2)}) %collective-permute-start.13) | collective-permute-done | bytes 262176 | tf_op jit(solution)/shard_map/ppermute | solution.py:47
  52.6 3.2 %collective-permute-start.15 = (bf16[512,128]{1,0:T(8,128)(2,1)S(1)}, bf16[512,128]{1,0:T(8,128)(2,1)S(1)}, u32[]{:S(2)}, u32[]{:S(2)}) collective-permute-start(bf16[512,128]{1,0:T(8,128)(2,1)S(1)} %slice.35), channel_id=1, source_target_pairs={{0,6},{1,7},{2,0},{3,1},{4,2},{5,3},{6,4},{7,5},{8,14},{9,15},{10,... | collective-permute-start | bytes 393224 | tf_op jit(solution)/shard_map/ppermute | solution.py:47
  55.8 0.0 collective-permute-done.12.refs_1_
  55.9 0.1 collective-permute-start.14
  55.9 3.8 %collective-permute-start.11 = (bf16[4096,128]{1,0:T(8,128)(2,1)S(1)}, bf16[4096,128]{1,0:T(8,128)(2,1)S(1)}, u32[]{:S(2)}, u32[]{:S(2)}) collective-permute-start(bf16[4096,128]{1,0:T(8,128)(2,1)S(1)} %shard_map.141.refs_0_), channel_id=1, source_target_pairs={{0,24},{8,0},{16,8},{24,16},{32,56},{40,32},{48,40},{56,48},{64,88... | collective-permute-start | bytes 3145736 | tf_op jit(solution)/shard_map/ppermute | solution.py:52
  59.8 0.0 collective-permute-start.10
  59.8 0.0 collective-permute-done.15.refs_4_
  59.8 1.2 collective-permute-done.14.refs_3_
  61.0 0.9 copy-done.5
  61.9 0.1 shard_map.144.cots
  62.0 5.4 %collective-permute-start.16 = (bf16[4096,128]{1,0:T(8,128)(2,1)S(1)}, bf16[4096,128]{1,0:T(8,128)(2,1)S(1)}, u32[]{:S(2)}, u32[]{:S(2)}) collective-permute-start(bf16[4096,128]{1,0:T(8,128)(2,1)S(1)} %shard_map.144.cots), channel_id=1, source_target_pairs={{0,1},{1,0},{2,3},{3,2},{4,5},{5,4},{6,7},{7,6},{8,9},{9,8},{10,11... | collective-permute-start | bytes 3145736 | tf_op jit(solution)/shard_map/ppermute | solution.py:47
  67.4 0.2 select_reduce_fusion.slots
  67.6 1.2 %shard_map.142 = (f32[512,128]{1,0:T(8,128)S(1)}, bf16[512,128]{1,0:T(8,128)(2,1)S(1)}, f32[512,1]{1,0:T(8,128)S(1)}) custom-call(s32[4]{0:T(128)S(1)} %select_reduce_fusion.slots, s32[4]{0:T(128)S(1)} %copy-done.12, s32[4]{0:T(128)S(1)} %copy-done.10, f32[4]{0:T(128)S(1)} %copy-done.11, bf16[32,16,1280]{2,1,0:T(8,128)(2,1)S(1)} %all-to-all-done.gathered_ref, ...), custom_call_target="tpu_custom_call" | custom-call | flops 67108864 | bytes 1048576 | tf_op jit(solution)/shard_map/pallas_call | solution.py:335
  68.9 0.3 collective-permute-start.7
  69.2 1.5 %collective-permute-done.7 = f32[512,128]{1,0:T(8,128)S(1)} collective-permute-done((f32[512,128]{1,0:T(8,128)S(1)}, f32[512,128]{1,0:T(8,128)S(1)}, u32[]{:S(2)}, u32[]{:S(2)}) %collective-permute-start.7) | collective-permute-done | bytes 262176 | tf_op jit(solution)/shard_map/ppermute | solution.py:47
  70.7 0.1 collective-permute-start.8
  70.8 4.9 %collective-permute-done.8 = bf16[512,128]{1,0:T(8,128)(2,1)S(1)} collective-permute-done((bf16[512,128]{1,0:T(8,128)(2,1)S(1)}, bf16[512,128]{1,0:T(8,128)(2,1)S(1)}, u32[]{:S(2)}, u32[]{:S(2)}) %collective-permute-start.8) | collective-permute-done | bytes 131104 | tf_op jit(solution)/shard_map/ppermute | solution.py:354
  75.8 0.2 collective-permute-start.9
  76.0 5.3 %collective-permute-done.9.received = bf16[512,128]{1,0:T(8,128)(2,1)S(1)} collective-permute-done((bf16[512,128]{1,0:T(8,128)(2,1)S(1)}, bf16[512,128]{1,0:T(8,128)(2,1)S(1)}, u32[]{:S(2)}, u32[]{:S(2)}) %collective-permute-start.9) | collective-permute-done | bytes 131104 | tf_op jit(solution)/shard_map/ppermute | solution.py:354
  81.2 2.1 %shard_map.143 = (bf16[32,16,1152]{2,1,0:T(8,128)(2,1)}, bf16[512,128]{1,0:T(8,128)(2,1)S(1)}) custom-call(s32[4]{0:T(128)S(1)} %select_reduce_fusion.slots, bf16[512,128]{1,0:T(8,128)(2,1)S(1)} %add_convert_fusion.own, bf16[512,128]{1,0:T(8,128)(2,1)S(1)} %collective-permute-done.9.received, bf16[512,1024]{1,0:T(8,128)(2,1)S(1)} %copy-done.1, ...), custom_call_target="tpu_custom_call" | custom-call | flops 134217728 | bytes 1048576 | tf_op jit(solution)/shard_map/pallas_call | solution.py:360
  83.4 0.6 copy-done.6
  84.0 0.0 collective-permute-done.11.refs_2_
  84.0 0.0 collective-permute-done.10.refs_1_
  84.0 0.0 collective-permute-done.16.others
  84.0 1.1 copy-done.14
  85.1 1.0 copy-done.16
  86.1 5.8 %all-to-all-start.1 = ((bf16[32,16,1152]{2,1,0:T(8,128)(2,1)}), bf16[32,16,1152]{2,1,0:T(8,128)(2,1)S(1)}, u32[]{:S(2)}, u32[]{:S(2)}) async-start(bf16[32,16,1152]{2,1,0:T(8,128)(2,1)} %get-tuple-element.50), calls=%async_computation.1 | async-start | bytes 2359296 | tf_op jit(solution)/shard_map/all_to_all | solution.py:380
  91.9 0.0 copy-start.24
  92.0 0.8 slice.30
  92.9 1.2 collective-permute-start.17
  94.1 1.4 %collective-permute-start.18 = (bf16[2048,128]{1,0:T(8,128)(2,1)S(1)}, bf16[2048,128]{1,0:T(8,128)(2,1)S(1)}, u32[]{:S(2)}, u32[]{:S(2)}) collective-permute-start(bf16[2048,128]{1,0:T(8,128)(2,1)S(1)} %slice.31), channel_id=1, source_target_pairs={{0,24},{8,0},{16,8},{24,16},{32,56},{40,32},{48,40},{56,48},{64,88... | collective-permute-start | bytes 1572872 | tf_op jit(solution)/shard_map/ppermute | solution.py:52
  95.5 0.5 and_select_fusion.2.quarters
  96.1 6.7 %shard_map.145 = (bf16[512,1024]{1,0:T(8,128)(2,1)}, bf16[512,2048]{1,0:T(8,128)(2,1)}) custom-call(s32[4]{0:T(128)} %copy-done.9, s32[4]{0:T(128)} %and_select_fusion.2.quarters, bf16[4096,128]{1,0:T(8,128)(2,1)} %copy-done.3, bf16[4096,128]{1,0:T(8,128)(2,1)} %copy-done.16, bf16[32,16,1280]{2,1,0:T(8,128)(2,1)} %copy-done, bf16[512,128]{1,0:T(8,128)(2,1)} %copy-done.6, ...), custom_call_target="tpu_custom_call" | custom-call | tf_op jit(solution)/shard_map/pallas_call | solution.py:237
  102.7 11.5 %collective-permute-done.17.first = bf16[2048,128]{1,0:T(8,128)(2,1)S(1)} collective-permute-done((bf16[2048,128]{1,0:T(8,128)(2,1)}, bf16[2048,128]{1,0:T(8,128)(2,1)S(1)}, u32[]{:S(2)}, u32[]{:S(2)}) %collective-permute-start.17) | collective-permute-done | bytes 524320 | tf_op jit(solution)/shard_map/ppermute | solution.py:52
  114.3 3.3 %collective-permute-done.18.second = bf16[2048,128]{1,0:T(8,128)(2,1)S(1)} collective-permute-done((bf16[2048,128]{1,0:T(8,128)(2,1)S(1)}, bf16[2048,128]{1,0:T(8,128)(2,1)S(1)}, u32[]{:S(2)}, u32[]{:S(2)}) %collective-permute-start.18) | collective-permute-done | bytes 524320 | tf_op jit(solution)/shard_map/ppermute | solution.py:52
  117.5 0.8 copy-done.18
  118.3 4.2 %shard_map.146 = bf16[512,1024]{1,0:T(8,128)(2,1)} custom-call(s32[4]{0:T(128)} %copy-done.9, s32[4]{0:T(128)} %and_select_fusion.2.quarters, bf16[512,1024]{1,0:T(8,128)(2,1)} %get-tuple-element.48.near_ref, bf16[512,2048]{1,0:T(8,128)(2,1)} %get-tuple-element.49.weighted, bf16[32,16,1280]{2,1,0:T(8,128)(2,1)} %copy-done, ...), custom_call_target="tpu_custom_call", output_to_operand_aliasing={{}: (2, {})} | custom-call | tf_op jit(solution)/shard_map/pallas_call | solution.py:249
  122.5 0.0 all-to-all-done.1.terms_ref
  122.5 0.8 shard_map.147
  (49 shorter events, 0.3 us)
Async XLA Ops:
  2.6 12.0 %copy-start.20 = (s32[8,1]{0,1:T(1,128)S(1)}, s32[8,1]{0,1:T(1,128)}, u32[]{:S(2)}) copy-start(s32[8,1]{0,1:T(1,128)} %constant.80) | copy-start | bytes 100
  2.6 12.0 %copy-start.21 = (s32[8,1]{0,1:T(1,128)S(1)}, s32[8,1]{0,1:T(1,128)}, u32[]{:S(2)}) copy-start(s32[8,1]{0,1:T(1,128)} %constant.79) | copy-start | bytes 100
  2.6 43.8 %all-to-all-start = ((bf16[32,16,1280]{2,1,0:T(8,128)(2,1)}), bf16[32,16,1280]{2,1,0:T(8,128)(2,1)S(1)}, u32[]{:S(2)}, u32[]{:S(2)}) async-start(bf16[32,16,1280]{2,1,0:T(8,128)(2,1)} %shard_map.139), calls=%async_computation | async-start | bytes 2621440 | tf_op jit(solution)/shard_map/all_to_all | solution.py:316
  15.2 17.6 %copy-start.19 = (bf16[512,2,128]{2,1,0:T(2,128)(2,1)S(1)}, bf16[512,2,128]{2,1,0:T(2,128)(2,1)}, u32[]{:S(2)}) copy-start(bf16[512,2,128]{2,1,0:T(2,128)(2,1)} %param.13) | copy-start | bytes 786436
  18.3 8.4 %collective-permute-start = (bf16[1024,128]{1,0:T(8,128)(2,1)}, bf16[1024,128]{1,0:T(8,128)(2,1)S(1)}, u32[]{:S(2)}, u32[]{:S(2)}) collective-permute-start(bf16[1024,128]{1,0:T(8,128)(2,1)} %get-tuple-element.29), channel_id=1, source_target_pairs={{0,2},{1,3},{2,4},{3,5},{4,6},{5,7},{6,0},{7,1},{8,10},{9,11},{10,... | collective-permute-start | bytes 786440 | tf_op jit(solution)/shard_map/ppermute | solution.py:47
  19.6 7.1 %collective-permute-start.1 = (bf16[1024,128]{1,0:T(8,128)(2,1)}, bf16[1024,128]{1,0:T(8,128)(2,1)S(1)}, u32[]{:S(2)}, u32[]{:S(2)}) collective-permute-start(bf16[1024,128]{1,0:T(8,128)(2,1)} %get-tuple-element.30), channel_id=1, source_target_pairs={{0,6},{1,7},{2,0},{3,1},{4,2},{5,3},{6,4},{7,5},{8,14},{9,15},{10,... | collective-permute-start | bytes 786440 | tf_op jit(solution)/shard_map/ppermute | solution.py:47
  21.1 11.8 %collective-permute-start.3 = (bf16[512,128]{1,0:T(8,128)(2,1)}, bf16[512,128]{1,0:T(8,128)(2,1)S(1)}, u32[]{:S(2)}, u32[]{:S(2)}) collective-permute-start(bf16[512,128]{1,0:T(8,128)(2,1)} %get-tuple-element.32), channel_id=1, source_target_pairs={{0,1},{1,0},{2,3},{3,2},{4,5},{5,4},{6,7},{7,6},{8,9},{9,8},{10,11... | collective-permute-start | bytes 393224 | tf_op jit(solution)/shard_map/ppermute | solution.py:47
  22.5 10.4 %collective-permute-start.4 = (bf16[512,128]{1,0:T(8,128)(2,1)}, bf16[512,128]{1,0:T(8,128)(2,1)S(1)}, u32[]{:S(2)}, u32[]{:S(2)}) collective-permute-start(bf16[512,128]{1,0:T(8,128)(2,1)} %get-tuple-element.33), channel_id=1, source_target_pairs={{0,3},{1,2},{2,5},{3,4},{4,7},{5,6},{6,1},{7,0},{8,11},{9,10},{10,... | collective-permute-start | bytes 393224 | tf_op jit(solution)/shard_map/ppermute | solution.py:47
  22.5 10.4 %collective-permute-start.5 = (bf16[512,128]{1,0:T(8,128)(2,1)}, bf16[512,128]{1,0:T(8,128)(2,1)S(1)}, u32[]{:S(2)}, u32[]{:S(2)}) collective-permute-start(bf16[512,128]{1,0:T(8,128)(2,1)} %get-tuple-element.34), channel_id=1, source_target_pairs={{0,7},{1,6},{2,1},{3,0},{4,3},{5,2},{6,5},{7,4},{8,15},{9,14},{10,... | collective-permute-start | bytes 393224 | tf_op jit(solution)/shard_map/ppermute | solution.py:47
  26.7 6.2 %collective-permute-start.2 = (bf16[512,128]{1,0:T(8,128)(2,1)S(1)}, bf16[512,128]{1,0:T(8,128)(2,1)S(1)}, u32[]{:S(2)}, u32[]{:S(2)}) collective-permute-start(bf16[512,128]{1,0:T(8,128)(2,1)S(1)} %slice.32), channel_id=1, source_target_pairs={{0,2},{1,3},{2,4},{3,5},{4,6},{5,7},{6,0},{7,1},{8,10},{9,11},{10,... | collective-permute-start | bytes 393224 | tf_op jit(solution)/shard_map/ppermute | solution.py:47
  27.7 8.9 %collective-permute-start.6 = (bf16[512,128]{1,0:T(8,128)(2,1)S(1)}, bf16[512,128]{1,0:T(8,128)(2,1)S(1)}, u32[]{:S(2)}, u32[]{:S(2)}) collective-permute-start(bf16[512,128]{1,0:T(8,128)(2,1)S(1)} %slice.33), channel_id=1, source_target_pairs={{0,7},{1,6},{2,1},{3,0},{4,3},{5,2},{6,5},{7,4},{8,15},{9,14},{10,... | collective-permute-start | bytes 393224 | tf_op jit(solution)/shard_map/ppermute | solution.py:47
  32.9 19.8 %copy-start.4 = (bf16[512,2,128]{2,0,1:T(8,128)(2,1)}, bf16[512,2,128]{2,0,1:T(8,128)(2,1)S(1)}, u32[]{:S(2)}) copy-start(bf16[512,2,128]{2,0,1:T(8,128)(2,1)S(1)} %copy.20) | copy-start | bytes 786436
  36.6 0.9 copy-start.8
  37.5 29.8 %copy-start.22 = (s32[8]{0:T(128)S(1)}, s32[8]{0:T(128)}, u32[]{:S(2)}) copy-start(s32[8]{0:T(128)} %param.17) | copy-start | bytes 100
  37.5 29.8 %copy-start.23 = (s32[4]{0:T(128)S(1)}, s32[4]{0:T(128)}, u32[]{:S(2)}) copy-start(s32[4]{0:T(128)} %param.18) | copy-start | bytes 52
  37.6 24.4 %copy-start.2 = (bf16[4096,128]{1,0:T(8,128)(2,1)}, bf16[4096,128]{1,0:T(8,128)(2,1)S(1)}, u32[]{:S(2)}) copy-start(bf16[4096,128]{1,0:T(8,128)(2,1)S(1)} %shard_map.141.refs_0_) | copy-start | bytes 3145732
  46.5 21.1 %copy-start = (bf16[32,16,1280]{2,1,0:T(8,128)(2,1)}, bf16[32,16,1280]{2,1,0:T(8,128)(2,1)S(1)}, u32[]{:S(2)}) copy-start(bf16[32,16,1280]{2,1,0:T(8,128)(2,1)S(1)} %all-to-all-done.gathered_ref) | copy-start | bytes 3932164
  46.5 21.1 %copy-start.10 = (s32[4]{0:T(128)S(1)}, s32[4]{0:T(128)}, u32[]{:S(2)}) copy-start(s32[4]{0:T(128)} %prompt.1) | copy-start | bytes 52
  46.5 21.1 %copy-start.11 = (f32[4]{0:T(128)S(1)}, f32[4]{0:T(128)}, u32[]{:S(2)}) copy-start(f32[4]{0:T(128)} %reward.1) | copy-start | bytes 52
  46.5 21.1 %copy-start.12 = (s32[4]{0:T(128)S(1)}, s32[4]{0:T(128)}, u32[]{:S(2)}) copy-start(s32[4]{0:T(128)} %live.1) | copy-start | bytes 52
  46.5 21.1 %copy-start.1 = (bf16[512,1024]{1,0:T(8,128)(2,1)S(1)}, bf16[512,1024]{1,0:T(8,128)(2,1)}, u32[]{:S(2)}) copy-start(bf16[512,1024]{1,0:T(8,128)(2,1)} %x_ref.3) | copy-start | bytes 3145732
  46.5 6.1 %collective-permute-start.13 = (bf16[1024,128]{1,0:T(8,128)(2,1)S(1)}, bf16[1024,128]{1,0:T(8,128)(2,1)S(1)}, u32[]{:S(2)}, u32[]{:S(2)}) collective-permute-start(bf16[1024,128]{1,0:T(8,128)(2,1)S(1)} %bitcast.15), channel_id=1, source_target_pairs={{0,6},{1,7},{2,0},{3,1},{4,2},{5,3},{6,4},{7,5},{8,14},{9,15},{10,... | collective-permute-start | bytes 786440 | tf_op jit(solution)/shard_map/ppermute | solution.py:47
  49.3 6.5 %collective-permute-start.12 = (bf16[1024,128]{1,0:T(8,128)(2,1)S(1)}, bf16[1024,128]{1,0:T(8,128)(2,1)S(1)}, u32[]{:S(2)}, u32[]{:S(2)}) collective-permute-start(bf16[1024,128]{1,0:T(8,128)(2,1)S(1)} %bitcast.16), channel_id=1, source_target_pairs={{0,2},{1,3},{2,4},{3,5},{4,6},{5,7},{6,0},{7,1},{8,10},{9,11},{10,... | collective-permute-start | bytes 786440 | tf_op jit(solution)/shard_map/ppermute | solution.py:47
  52.6 7.1 %collective-permute-start.15 = (bf16[512,128]{1,0:T(8,128)(2,1)S(1)}, bf16[512,128]{1,0:T(8,128)(2,1)S(1)}, u32[]{:S(2)}, u32[]{:S(2)}) collective-permute-start(bf16[512,128]{1,0:T(8,128)(2,1)S(1)} %slice.35), channel_id=1, source_target_pairs={{0,6},{1,7},{2,0},{3,1},{4,2},{5,3},{6,4},{7,5},{8,14},{9,15},{10,... | collective-permute-start | bytes 393224 | tf_op jit(solution)/shard_map/ppermute | solution.py:47
  55.9 5.1 %collective-permute-start.14 = (bf16[512,128]{1,0:T(8,128)(2,1)S(1)}, bf16[512,128]{1,0:T(8,128)(2,1)S(1)}, u32[]{:S(2)}, u32[]{:S(2)}) collective-permute-start(bf16[512,128]{1,0:T(8,128)(2,1)S(1)} %slice.34), channel_id=1, source_target_pairs={{0,2},{1,3},{2,4},{3,5},{4,6},{5,7},{6,0},{7,1},{8,10},{9,11},{10,... | collective-permute-start | bytes 393224 | tf_op jit(solution)/shard_map/ppermute | solution.py:47
  55.9 28.1 %collective-permute-start.11 = (bf16[4096,128]{1,0:T(8,128)(2,1)S(1)}, bf16[4096,128]{1,0:T(8,128)(2,1)S(1)}, u32[]{:S(2)}, u32[]{:S(2)}) collective-permute-start(bf16[4096,128]{1,0:T(8,128)(2,1)S(1)} %shard_map.141.refs_0_), channel_id=1, source_target_pairs={{0,24},{8,0},{16,8},{24,16},{32,56},{40,32},{48,40},{56,48},{64,88... | collective-permute-start | bytes 3145736 | tf_op jit(solution)/shard_map/ppermute | solution.py:52
  59.8 24.3 %collective-permute-start.10 = (bf16[4096,128]{1,0:T(8,128)(2,1)S(1)}, bf16[4096,128]{1,0:T(8,128)(2,1)S(1)}, u32[]{:S(2)}, u32[]{:S(2)}) collective-permute-start(bf16[4096,128]{1,0:T(8,128)(2,1)S(1)} %shard_map.141.refs_0_), channel_id=1, source_target_pairs={{0,8},{8,16},{16,24},{24,0},{32,40},{40,48},{48,56},{56,32},{64,72... | collective-permute-start | bytes 3145736 | tf_op jit(solution)/shard_map/ppermute | solution.py:52
  61.0 1.0 copy-start.5
  62.0 6.9 %copy-start.3 = (bf16[4096,128]{1,0:T(8,128)(2,1)}, bf16[4096,128]{1,0:T(8,128)(2,1)S(1)}, u32[]{:S(2)}) copy-start(bf16[4096,128]{1,0:T(8,128)(2,1)S(1)} %shard_map.144.cots) | copy-start | bytes 3145732
  62.0 22.0 %collective-permute-start.16 = (bf16[4096,128]{1,0:T(8,128)(2,1)S(1)}, bf16[4096,128]{1,0:T(8,128)(2,1)S(1)}, u32[]{:S(2)}, u32[]{:S(2)}) collective-permute-start(bf16[4096,128]{1,0:T(8,128)(2,1)S(1)} %shard_map.144.cots), channel_id=1, source_target_pairs={{0,1},{1,0},{2,3},{3,2},{4,5},{5,4},{6,7},{7,6},{8,9},{9,8},{10,11... | collective-permute-start | bytes 3145736 | tf_op jit(solution)/shard_map/ppermute | solution.py:47
  67.6 13.7 %copy-start.9 = (s32[4]{0:T(128)}, s32[4]{0:T(128)S(1)}, u32[]{:S(2)}) copy-start(s32[4]{0:T(128)S(1)} %select_reduce_fusion.slots) | copy-start | bytes 52
  68.9 12.3 %copy-start.7 = (f32[512,1]{1,0:T(8,128)}, f32[512,1]{1,0:T(8,128)S(1)}, u32[]{:S(2)}) copy-start(f32[512,1]{1,0:T(8,128)S(1)} %get-tuple-element.45.coef_ref) | copy-start | bytes 6148
  68.9 1.8 %collective-permute-start.7 = (f32[512,128]{1,0:T(8,128)S(1)}, f32[512,128]{1,0:T(8,128)S(1)}, u32[]{:S(2)}, u32[]{:S(2)}) collective-permute-start(f32[512,128]{1,0:T(8,128)S(1)} %get-tuple-element.37), channel_id=1, source_target_pairs={{0,1},{1,0},{2,3},{3,2},{4,5},{5,4},{6,7},{7,6},{8,9},{9,8},{10,11... | collective-permute-start | bytes 786440 | tf_op jit(solution)/shard_map/ppermute | solution.py:47
  70.7 5.0 %collective-permute-start.8 = (bf16[512,128]{1,0:T(8,128)(2,1)S(1)}, bf16[512,128]{1,0:T(8,128)(2,1)S(1)}, u32[]{:S(2)}, u32[]{:S(2)}) collective-permute-start(bf16[512,128]{1,0:T(8,128)(2,1)S(1)} %add_convert_fusion.1), channel_id=1, source_target_pairs={{0,2},{1,3},{2,0},{3,1},{4,6},{5,7},{6,4},{7,5},{8,10},{9,11},{10,... | collective-permute-start | bytes 393224 | tf_op jit(solution)/shard_map/ppermute | solution.py:354
  75.8 5.4 %collective-permute-start.9 = (bf16[512,128]{1,0:T(8,128)(2,1)S(1)}, bf16[512,128]{1,0:T(8,128)(2,1)S(1)}, u32[]{:S(2)}, u32[]{:S(2)}) collective-permute-start(bf16[512,128]{1,0:T(8,128)(2,1)S(1)} %add_convert_fusion.own), channel_id=1, source_target_pairs={{0,6},{1,7},{2,4},{3,5},{4,2},{5,3},{6,0},{7,1},{8,14},{9,15},{10,... | collective-permute-start | bytes 393224 | tf_op jit(solution)/shard_map/ppermute | solution.py:354
  83.4 0.6 copy-start.6
  84.0 8.0 %copy-start.13 = (bf16[4096,128]{1,0:T(8,128)(2,1)}, bf16[4096,128]{1,0:T(8,128)(2,1)S(1)}, u32[]{:S(2)}) copy-start(bf16[4096,128]{1,0:T(8,128)(2,1)S(1)} %collective-permute-done.11.refs_2_) | copy-start | bytes 3145732
  84.0 1.1 copy-start.14
  85.1 1.0 copy-start.16
  86.1 5.9 %copy-start.15 = (bf16[4096,128]{1,0:T(8,128)(2,1)S(1)}, bf16[4096,128]{1,0:T(8,128)(2,1)}, u32[]{:S(2)}) copy-start(bf16[4096,128]{1,0:T(8,128)(2,1)} %copy-done.14) | copy-start | bytes 3145732
  86.1 36.3 %all-to-all-start.1 = ((bf16[32,16,1152]{2,1,0:T(8,128)(2,1)}), bf16[32,16,1152]{2,1,0:T(8,128)(2,1)S(1)}, u32[]{:S(2)}, u32[]{:S(2)}) async-start(bf16[32,16,1152]{2,1,0:T(8,128)(2,1)} %get-tuple-element.50), calls=%async_computation.1 | async-start | bytes 2359296 | tf_op jit(solution)/shard_map/all_to_all | solution.py:380
  91.9 3.6 %copy-start.24 = (s32[4]{0:T(128)S(1)}, s32[4]{0:T(128)}, u32[]{:S(2)}) copy-start(s32[4]{0:T(128)} %constant.72.clone) | copy-start | bytes 52
  92.9 21.4 %collective-permute-start.17 = (bf16[2048,128]{1,0:T(8,128)(2,1)}, bf16[2048,128]{1,0:T(8,128)(2,1)S(1)}, u32[]{:S(2)}, u32[]{:S(2)}) collective-permute-start(bf16[2048,128]{1,0:T(8,128)(2,1)} %slice.30), channel_id=1, source_target_pairs={{0,8},{8,16},{16,24},{24,0},{32,40},{40,48},{48,56},{56,32},{64,72... | collective-permute-start | bytes 1572872 | tf_op jit(solution)/shard_map/ppermute | solution.py:52
  94.1 23.4 %collective-permute-start.18 = (bf16[2048,128]{1,0:T(8,128)(2,1)S(1)}, bf16[2048,128]{1,0:T(8,128)(2,1)S(1)}, u32[]{:S(2)}, u32[]{:S(2)}) collective-permute-start(bf16[2048,128]{1,0:T(8,128)(2,1)S(1)} %slice.31), channel_id=1, source_target_pairs={{0,24},{8,0},{16,8},{24,16},{32,56},{40,32},{48,40},{56,48},{64,88... | collective-permute-start | bytes 1572872 | tf_op jit(solution)/shard_map/ppermute | solution.py:52
  114.3 3.3 %copy-start.17 = (bf16[2048,128]{1,0:T(8,128)(2,1)}, bf16[2048,128]{1,0:T(8,128)(2,1)S(1)}, u32[]{:S(2)}) copy-start(bf16[2048,128]{1,0:T(8,128)(2,1)S(1)} %collective-permute-done.17.first) | copy-start | bytes 1572868
  117.5 0.8 copy-start.18

commit v6 on v5

--- a/solution.py
+++ b/solution.py
@@ -141,18 +141,23 @@
     )(places, *[weight] * 8)
 
 
-def factor_rows(ref, slot, start, size):
-    owners = ref.shape[0] // SLOTS
-    return ref[pl.ds(slot * owners, owners), :, pl.ds(start, size)].reshape(RANK, size)
+def factor_rows(table_ref, slot, start, size):
+    return table_ref[pl.ds(pl.multiple_of(slot * RANK, RANK), RANK), pl.ds(start, size)]
 
 
 def low_kernel(
-    slots, live, prompt, reward, gathered_ref, x_ref, cot_ref, low_ref, weighted_ref, coef_ref
+    slots, live, prompt, reward, own, before, after, far_first, far_second, x_ref, cot_ref, *outs
 ):
+    low_ref, weighted_ref, coef_ref, table_ref = outs
     window = x_ref.shape[1]
     columns = cot_ref.shape[2]
     blocks = reward.shape[0]
-    facts = gathered_ref[:, :, window + columns :].astype(F32)
+    owned, half = own.shape[1], far_first.shape[0]
+    for k in range(SLOTS):
+        far = far_first[k] if k < half else far_second[k - half]
+        for i, piece in enumerate((own[k], before[k], after[k], far)):
+            table_ref[k * RANK + i * owned : k * RANK + (i + 1) * owned] = piece
+    facts = table_ref[:, window + columns :].astype(F32).reshape(-1, owned, LANES)
     row = lax.broadcasted_iota(jnp.int32, facts.shape, 1)
     parts = jnp.sum(jnp.where(row == 0, facts, 0.0), axis=1)
     prompts = jnp.sum(jnp.where(row == 1, facts, 0.0), axis=1)
@@ -169,18 +174,20 @@
         coef = jnp.where(place < live[b], -advantage / GSIZE, 0.0)
         rows = pl.ds(b * BLOCK, BLOCK)
         weighted = (cot_ref[1, rows, :].astype(F32) * coef).astype(BF)
-        low_h = dot(x_ref[rows, :], factor_rows(gathered_ref, slots[b], 0, window), 1, 1)
-        low_g = dot(weighted, factor_rows(gathered_ref, slots[b], window, columns), 1, 1)
+        low_h = dot(x_ref[rows, :], factor_rows(table_ref, slots[b], 0, window), 1, 1)
+        low_g = dot(weighted, factor_rows(table_ref, slots[b], window, columns), 1, 1)
         low_ref[rows, :] = jnp.concatenate([low_h, low_g], axis=1)
         weighted_ref[rows, :] = weighted
         coef_ref[rows, :] = coef
 
 
-def terms_kernel(slots, own, received, x_ref, weighted_ref, terms_ref, low_ref):
+def terms_kernel(
+    slots, order, own, first, second, third, x_ref, weighted_ref, terms_ref, low_ref
+):
     window = x_ref.shape[1]
-    columns = weighted_ref.shape[1]
-    owners, owned = terms_ref.shape[0] // SLOTS, terms_ref.shape[1]
-    low = own[...].astype(F32) + received[...].astype(F32)
+    owned, owners = terms_ref.shape[1], terms_ref.shape[0] // SLOTS
+    low = own[...].astype(F32) + first[...].astype(F32)
+    low = (low + second[...].astype(F32)) + third[...].astype(F32)
     low_ref[...] = low.astype(BF)
     for i in range(terms_ref.shape[0]):
         terms_ref[i] = jnp.zeros(terms_ref.shape[1:], BF)
@@ -189,24 +196,26 @@
         low = low_ref[rows, :]
         down = LOWRANK_MULTIPLIER * dot(low, x_ref[rows, :], 0, 0)[RANK:]
         up = LOWRANK_MULTIPLIER * dot(low, weighted_ref[rows, :], 0, 0)[:RANK]
-        place = pl.ds(slots[b] * owners, owners)
-        terms_ref[place, :, :window] = down.astype(BF).reshape(owners, owned, window)
-        terms_ref[place, :, window:] = up.astype(BF).reshape(owners, owned, columns)
-
-
-def quarter(weighted, parts, low_ref, gathered_ref, slots, start, tile):
+        for i in range(owners):
+            place = slots[b] * owners + order[i]
+            cut = slice(i * owned, (i + 1) * owned)
+            terms_ref[place, :, :window] = down[cut].astype(BF)
+            terms_ref[place, :, window:] = up[cut].astype(BF)
+
+
+def quarter(weighted, parts, low_ref, table_ref, slots, start, tile):
     slabs = [p[i * tile : (i + 1) * tile] for p in parts for i in range(p.shape[0] // tile)]
     total = dot(weighted[...], jnp.concatenate(slabs, axis=1), 1, 1)
     extra = []
     for b in range(total.shape[0] // BLOCK):
-        factor = factor_rows(gathered_ref, slots[b], start, tile)
+        factor = factor_rows(table_ref, slots[b], start, tile)
         factor = jnp.concatenate([jnp.zeros_like(factor), factor], axis=0)
         low = low_ref[b * BLOCK : (b + 1) * BLOCK, :]
         extra.append(LOWRANK_MULTIPLIER * dot(low, factor, 1, 0))
     return (total + jnp.concatenate(extra, axis=0)).astype(BF)
 
 
-def near_kernel(slots, quarters, cots, others, gathered_ref, low_ref, coef_ref, *refs):
+def near_kernel(slots, quarters, cots, others, table_ref, low_ref, coef_ref, *refs):
     *slabs, out_ref, weighted = refs
     rows, columns = coef_ref.shape[0], cots.shape[1]
     tile = rows // 2
@@ -218,22 +227,22 @@
     for r, part in enumerate(slabs):
         start = pl.multiple_of(quarters[r] * tile, tile)
         out_ref[:, pl.ds(start, tile)] = quarter(
-            weighted, (part,), low_ref, gathered_ref, slots, start, tile
+            weighted, (part,), low_ref, table_ref, slots, start, tile
         )
 
 
-def far_kernel(slots, quarters, near_ref, weighted, gathered_ref, low_ref, first, second, out_ref):
+def far_kernel(slots, quarters, near_ref, weighted, table_ref, low_ref, first, second, out_ref):
     tile = out_ref.shape[1]
-    out_ref[...] = quarter(weighted, (first, second), low_ref, gathered_ref, slots, 0, tile)
+    out_ref[...] = quarter(weighted, (first, second), low_ref, table_ref, slots, 0, tile)
 
 
 def frozen_and_correction(slots, quarters, cots, adapter, near, far, window):
-    gathered, low, coef = adapter
+    table, low, coef = adapter
     rows, columns, tile = coef.shape[0], cots[0].shape[1], window // 4
     depth = 2 * cots[0].shape[0] // rows * columns
     shape = jax.ShapeDtypeStruct
     whole = lambda dims: pl.BlockSpec(dims, lambda i, *_: (0,) * len(dims))
-    streams = [*cots, gathered, low, coef, *near]
+    streams = [*cots, table, low, coef, *near]
     partial, weighted = pl.pallas_call(
         near_kernel,
         grid_spec=pltpu.PrefetchScalarGridSpec(
@@ -245,7 +254,6 @@
         out_shape=[shape((rows, window), BF), shape((rows, depth), BF)],
         compiler_params=pltpu.CompilerParams(vmem_limit_bytes=FULL_VMEM),
     )(slots, quarters, *streams)
-    owners, owned = gathered.shape[:2]
     return pl.pallas_call(
         far_kernel,
         grid_spec=pltpu.PrefetchScalarGridSpec(
@@ -254,7 +262,7 @@
             in_specs=[
                 pl.BlockSpec(memory_space=pl.ANY),
                 whole(weighted.shape),
-                pl.BlockSpec((owners, owned, tile), lambda i, s, q: (0, 0, q[3])),
+                pl.BlockSpec((table.shape[0], tile), lambda i, s, q: (0, q[3])),
                 whole(low.shape),
                 *[whole(v.shape) for v in far],
             ],
@@ -263,7 +271,7 @@
         out_shape=shape((rows, window), BF),
         input_output_aliases={2: 0},
         compiler_params=pltpu.CompilerParams(vmem_limit_bytes=FULL_VMEM),
-    )(slots, quarters, partial, weighted, gathered, low, *far)
+    )(slots, quarters, partial, weighted, table, low, *far)
 
 
 def sum_kernel(terms_ref, down_ref, up_ref):
@@ -306,14 +314,15 @@
     packed = streamed(
         pack_kernel,
         [(1, 4), (1, 4), (owned, window), (owned, columns)],
-        (dp, owned, window + columns + LANES),
+        (dp // 4, owned, window + columns + LANES),
     )(
         prompt_of_block.reshape(1, -1),
         reward_of_block.reshape(1, -1),
         adapter_down_factors,
         adapter_up_factors,
     )
-    gathered = lax.all_to_all(packed, "dp", 0, 0)
+    along_z = [[z * 4 + i for z in range(dp // 4)] for i in range(4)]
+    own_x = lax.all_to_all(packed, "dp", 0, 0, axis_index_groups=along_z)
 
     cotangent = jnp.transpose(key_value_cotangent, (1, 0, 2))
     steps = jnp.array([[1, 0], [1, 1], [2, 0], [3, 0], [3, 1], [2, 1], [0, 0], [0, 1]], jnp.int32)
@@ -321,21 +330,40 @@
     to_next, next_other, to_prev, prev_other, mine, other = payloads(
         targets * 4 + x, key_value_weight, tile
     )
-    before, after = tensor_send(to_next, 1, 0), tensor_send(to_prev, 3, 0)
-    before_other, after_other = tensor_send(next_other, 1, 1), tensor_send(prev_other, 3, 1)
-    partner = tensor_send(other, 0, 1)
     unit = 2 * tile
-    hop_next, hop_prev = lax.optimization_barrier((before[unit:], after[unit:]))
-    hop_next, hop_prev = tensor_send(hop_next, 1, 0), tensor_send(hop_prev, 3, 1)
-    pieces = mine, before, after, hop_next, partner, before_other, after_other, hop_prev
-    slabs = assemble(*[(piece, 0, unit) for piece in pieces])
+    chain = (
+        tensor_send(to_next, 1, 0),
+        tensor_send(to_prev, 3, 0),
+        tensor_send(next_other, 1, 1),
+        tensor_send(prev_other, 3, 1),
+        tensor_send(other, 0, 1),
+    )
+    own_x, chain = lax.optimization_barrier((own_x, chain))
+    before, after, before_other, after_other, partner = chain
+    before_x, after_x = x_send(own_x, 1), x_send(own_x, 3)
+    hop_next = tensor_send(before[unit:], 1, 0)
+    hop_prev = tensor_send(after[unit:], 3, 1)
+    split = dp // 8
+    far_x = x_send(before_x[:split], 1), x_send(after_x[split:], 3)
+    gathered = own_x, before_x, after_x, *far_x
+    gathered, hop_next, hop_prev = lax.optimization_barrier((gathered, hop_next, hop_prev))
     flat = cotangent.reshape(2 * rows, columns)
-    gathered, slabs, flat = lax.optimization_barrier((gathered, slabs, flat))
-
-    low, weighted_value, coef = call(
+    slabs = assemble(
+        *[(piece, 0, unit) for piece in (mine, before, after, hop_next)],
+        *[(piece, 0, unit) for piece in (partner, before_other, after_other)],
+        (hop_prev, 0, unit),
+    )
+    quarters = (x + jnp.array([0, 3, 1, 2], jnp.int32)) % 4
+
+    low, weighted_value, coef, table = call(
         low_kernel,
-        [SMEM] * 4 + [VMEM] * 3,
-        [shape((rows, 2 * RANK), F32), shape((rows, columns), BF), shape((rows, 1), F32)],
+        [SMEM] * 4 + [VMEM] * 7,
+        [
+            shape((rows, 2 * RANK), F32),
+            shape((rows, columns), BF),
+            shape((rows, 1), F32),
+            shape((SLOTS * RANK, window + columns + LANES), BF),
+        ],
         2 * rows * RANK * window,
         16,
     )(
@@ -343,27 +371,26 @@
         live_rows_of_block,
         prompt_of_block,
         reward_of_block,
-        gathered,
+        *gathered,
         normed_input_rows,
         cotangent,
     )
     low = (low + tensor_send(low, 0, 1)).astype(BF)
-    for swap in (1, 3):
-        pairs = [(y * 2 + c, (y ^ swap) * 2 + c) for y in range(CHIPS) for c in range(2)]
-        sent = low
-        received = lax.ppermute(sent, "tensor", pairs)
-        if swap == 1:
-            low = (sent.astype(F32) + received.astype(F32)).astype(BF)
+    lows = [low] + [tensor_send(low, s, 0) for s in (1, 3, 2)]
     slabs_left, slabs_right = x_send(slabs, 1), x_send(slabs, 3)
-    cot_before, cot_after = tensor_send(flat, 1, 0), tensor_send(flat, 3, 0)
 
     terms, low = call(
         terms_kernel,
-        [SMEM] + [VMEM] * 4,
+        [SMEM] * 2 + [VMEM] * 6,
         [shape((dp, owned, window + columns), BF), shape((rows, 2 * RANK), BF)],
         4 * rows * RANK * window,
         16,
-    )(slots, sent, received, normed_input_rows, weighted_value)
+    )(slots, quarters, *lows, normed_input_rows, weighted_value)
+    terms, slabs_left, slabs_right = lax.optimization_barrier((terms, slabs_left, slabs_right))
+    terms = lax.all_to_all(terms, "dp", 0, 0)
+    half = slabs.shape[0] // 2
+    slabs_far = (x_send(slabs_left[:half], 1), x_send(slabs_right[half:], 3))
+    cot_before, cot_after = tensor_send(flat, 1, 0), tensor_send(flat, 3, 0)
     cot_next = tensor_send(cot_before[:rows], 1, 0)
     cot_prev = tensor_send(cot_after[rows:], 3, 0)
     cots = assemble(
@@ -374,18 +401,11 @@
         (cot_prev, 0, rows),
     )
     cots_other = tensor_send(cots, 0, 1)
-    terms, slabs_left, slabs_right, cots, cots_other = lax.optimization_barrier(
-        (terms, slabs_left, slabs_right, cots, cots_other)
-    )
-    terms = lax.all_to_all(terms, "dp", 0, 0)
-    half = slabs.shape[0] // 2
-    slabs_far = (x_send(slabs_left[:half], 1), x_send(slabs_right[half:], 3))
-    quarters = (x + jnp.array([0, 3, 1, 2], jnp.int32)) % 4
     input_gradient = frozen_and_correction(
         slots,
         quarters,
         (cots, cots_other),
-        (gathered, low, coef),
+        (table, low, coef),
         (slabs, slabs_left, slabs_right),
         slabs_far,
         window,

time: 125 us -> 131 us (1.048); the launches traced: 123 us -> 131 us
  waiting for transfers between devices: 44.8 us -> 54.6 us
  local copies, waits for them, and re-layouts: 6.42 us -> 4.82 us
    ppermute x13 -> x16, waiting for transfers between devices: 11 us -> 30.5 us  [tensor_send(): return lax.ppermute(value, 'tensor', pairs)]
    ppermute x2 -> x0, waiting for transfers between devices: 10.2 us -> none  [shards(): received = lax.ppermute(sent, 'tensor', pairs)]
    ppermute x4 -> x8, waiting for transfers between devices: 14.8 us -> 24.1 us  [x_send(): return lax.ppermute(value, 'dp', pairs)]
    all_to_all x1, waiting for transfers between devices: 8.83 us -> 0.01 us  [shards(): own_x = lax.all_to_all(packed, 'dp', 0, 0, axis_index_groups=along_z)]
    ppermute x4 -> x8, starting transfers between devices: 6.5 us -> 11.8 us  [x_send(): return lax.ppermute(value, 'dp', pairs)]
    ppermute x13 -> x16, starting transfers between devices: 25 us -> 20.8 us  [tensor_send(): return lax.ppermute(value, 'tensor', pairs)]
    all_to_all x1, starting transfers between devices: 12 us -> 9.01 us  [shards(): own_x = lax.all_to_all(packed, 'dp', 0, 0, axis_index_groups=along_z)]
    all_to_all x1, starting transfers between devices: 5.79 us -> 7.39 us  [shards(): terms = lax.all_to_all(terms, 'dp', 0, 0)]
  transfers between devices with their start and end apart: 21 -> 26, of which waited for: 10 -> 15; matrix products, arithmetic and copies ran while one was open for 2% -> 1% of each run, Pallas kernels for 14% -> 14%
where the time goes in v6:
time: 131 us
  waiting for transfers between devices  54.6 us (42%)
  starting transfers between devices  49.1 us (37%)
  Pallas kernels  20.1 us (15%)
  local copies, waits for them, and re-layouts  4.82 us (4%)
  other arithmetic  1.42 us (1%)
    ppermute x16, waiting for transfers between devices, tensor_send(): return lax.ppermute(value, 'tensor', pairs)  30.5 us
    ppermute x8, waiting for transfers between devices, x_send(): return lax.ppermute(value, 'dp', pairs)  24.1 us
    ppermute x16, starting transfers between devices, tensor_send(): return lax.ppermute(value, 'tensor', pairs)  20.8 us
    ppermute x8, starting transfers between devices, x_send(): return lax.ppermute(value, 'dp', pairs)  11.8 us
    all_to_all x1, starting transfers between devices, shards(): own_x = lax.all_to_all(packed, 'dp', 0, 0, axis_index_groups=along_z)  9.01 us
    all_to_all x1, starting transfers between devices, shards(): terms = lax.all_to_all(terms, 'dp', 0, 0)  7.39 us
    pallas_call x1, Pallas kernels, frozen_and_correction(): pl.pallas_call(near_kernel, grid_spec=pltpu.PrefetchScalarGridSpec(num_sc...  7.03 us
    unnamed x43, local copies, waits for them, and re-layouts  4.68 us
  transfers between devices with their start and end apart: 26, of which 15 were waited for; matrix products, arithmetic and copies ran while one was open for 1% of the time, Pallas kernels for 14%

profile of v6, /device:TPU:1, one launch (start us, length us, event | category | flops | bytes accessed | tf_op | source)
XLA Modules:
  0.0 131.0 jit_solution(381470347028821686)
XLA Ops:
  0.6 1.6 %shard_map.140 = bf16[8,16,1280]{2,1,0:T(8,128)(2,1)} custom-call(s32[1,4]{1,0:T(1,128)} %bitcast.19, f32[1,4]{1,0:T(1,128)} %bitcast.20, bf16[16,1024]{1,0:T(8,128)(2,1)} %down_ref.1, bf16[16,128]{1,0:T(8,128)(2,1)} %up_ref.1), custom_call_target="tpu_custom_call" | custom-call | tf_op jit(solution)/shard_map/pallas_call | solution.py:314
  2.2 9.0 %all-to-all-start = ((bf16[8,16,1280]{2,1,0:T(8,128)(2,1)}), bf16[8,16,1280]{2,1,0:T(8,128)(2,1)S(1)}, u32[]{:S(2)}, u32[]{:S(2)}) async-start(bf16[8,16,1280]{2,1,0:T(8,128)(2,1)} %shard_map.140), calls=%async_computation | async-start | bytes 655360 | tf_op jit(solution)/shard_map/all_to_all | solution.py:325
  11.3 1.2 multiply_add_fusion.places
  12.4 3.0 %shard_map.141 = (bf16[1024,128]{1,0:T(8,128)(2,1)}, bf16[512,128]{1,0:T(8,128)(2,1)}, bf16[1024,128]{1,0:T(8,128)(2,1)}, bf16[512,128]{1,0:T(8,128)(2,1)}, bf16...) custom-call(s32[8]{0:T(128)} %multiply_add_fusion.places, bf16[2,8192,128]{2,1,0:T(8,128)(2,1)} %refs_7_.1, ...), custom_call_target="tpu_custom_call" | custom-call | tf_op jit(solution)/shard_map/pallas_call | solution.py:131
  15.4 1.3 collective-permute-start.5
  16.7 1.5 %collective-permute-start.6 = (bf16[1024,128]{1,0:T(8,128)(2,1)}, bf16[1024,128]{1,0:T(8,128)(2,1)S(1)}, u32[]{:S(2)}, u32[]{:S(2)}) collective-permute-start(bf16[1024,128]{1,0:T(8,128)(2,1)} %get-tuple-element.36), channel_id=1, source_target_pairs={{0,6},{1,7},{2,0},{3,1},{4,2},{5,3},{6,4},{7,5},{8,14},{9,15},{10,... | collective-permute-start | bytes 786440 | tf_op jit(solution)/shard_map/ppermute | solution.py:47
  18.2 1.4 %collective-permute-start.7 = (bf16[512,128]{1,0:T(8,128)(2,1)}, bf16[512,128]{1,0:T(8,128)(2,1)S(1)}, u32[]{:S(2)}, u32[]{:S(2)}) collective-permute-start(bf16[512,128]{1,0:T(8,128)(2,1)} %get-tuple-element.37), channel_id=1, source_target_pairs={{0,3},{1,2},{2,5},{3,4},{4,7},{5,6},{6,1},{7,0},{8,11},{9,10},{10,... | collective-permute-start | bytes 393224 | tf_op jit(solution)/shard_map/ppermute | solution.py:47
  19.6 1.6 %collective-permute-start.8 = (bf16[512,128]{1,0:T(8,128)(2,1)}, bf16[512,128]{1,0:T(8,128)(2,1)S(1)}, u32[]{:S(2)}, u32[]{:S(2)}) collective-permute-start(bf16[512,128]{1,0:T(8,128)(2,1)} %get-tuple-element.38), channel_id=1, source_target_pairs={{0,7},{1,6},{2,1},{3,0},{4,3},{5,2},{6,5},{7,4},{8,15},{9,14},{10,... | collective-permute-start | bytes 393224 | tf_op jit(solution)/shard_map/ppermute | solution.py:47
  21.2 1.4 %collective-permute-start.9 = (bf16[512,128]{1,0:T(8,128)(2,1)}, bf16[512,128]{1,0:T(8,128)(2,1)S(1)}, u32[]{:S(2)}, u32[]{:S(2)}) collective-permute-start(bf16[512,128]{1,0:T(8,128)(2,1)} %get-tuple-element.39), channel_id=1, source_target_pairs={{0,1},{1,0},{2,3},{3,2},{4,5},{5,4},{6,7},{7,6},{8,9},{9,8},{10,11... | collective-permute-start | bytes 393224 | tf_op jit(solution)/shard_map/ppermute | solution.py:47
  22.6 5.2 %collective-permute-done.7.refs_5_ = bf16[512,128]{1,0:T(8,128)(2,1)S(1)} collective-permute-done((bf16[512,128]{1,0:T(8,128)(2,1)}, bf16[512,128]{1,0:T(8,128)(2,1)S(1)}, u32[]{:S(2)}, u32[]{:S(2)}) %collective-permute-start.7) | collective-permute-done | bytes 131104 | tf_op jit(solution)/shard_map/ppermute | solution.py:47
  27.7 0.0 collective-permute-done.8.refs_6_
  27.7 0.0 collective-permute-done.9.refs_4_
  27.8 2.6 %collective-permute-start.11 = (bf16[8,16,1280]{2,1,0:T(8,128)(2,1)S(1)}, bf16[8,16,1280]{2,1,0:T(8,128)(2,1)S(1)}, u32[]{:S(2)}, u32[]{:S(2)}) collective-permute-start(bf16[8,16,1280]{2,1,0:T(8,128)(2,1)S(1)} %all-to-all-done.own), channel_id=1, source_target_pairs={{0,24},{8,0},{16,8},{24,16},{32,56},{40,32},{48,40},{56,48},{64,88... | collective-permute-start | bytes 983048 | tf_op jit(solution)/shard_map/ppermute | solution.py:52
  30.3 0.0 collective-permute-start.10
  30.3 7.0 %collective-permute-done.11.after = bf16[8,16,1280]{2,1,0:T(8,128)(2,1)S(1)} collective-permute-done((bf16[8,16,1280]{2,1,0:T(8,128)(2,1)S(1)}, bf16[8,16,1280]{2,1,0:T(8,128)(2,1)S(1)}, u32[]{:S(2)}, u32[]{:S(2)}) %collective-permute-start.11) | collective-permute-done | bytes 327712 | tf_op jit(solution)/shard_map/ppermute | solution.py:52
  37.4 3.5 %collective-permute-start.13 = (bf16[4,16,1280]{2,1,0:T(8,128)(2,1)S(1)}, bf16[4,16,1280]{2,1,0:T(8,128)(2,1)S(1)}, u32[]{:S(2)}, u32[]{:S(2)}) collective-permute-start(bf16[4,16,1280]{2,1,0:T(8,128)(2,1)S(1)} %slice.43), channel_id=1, source_target_pairs={{0,24},{8,0},{16,8},{24,16},{32,56},{40,32},{48,40},{56,48},{64,88... | collective-permute-start | bytes 491528 | tf_op jit(solution)/shard_map/ppermute | solution.py:52
  40.9 0.1 collective-permute-start.12
  41.0 0.0 copy-start.17
  41.1 3.3 %collective-permute-start.15 = (bf16[512,128]{1,0:T(8,128)(2,1)S(1)}, bf16[512,128]{1,0:T(8,128)(2,1)S(1)}, u32[]{:S(2)}, u32[]{:S(2)}) collective-permute-start(bf16[512,128]{1,0:T(8,128)(2,1)S(1)} %slice.37), channel_id=1, source_target_pairs={{0,7},{1,6},{2,1},{3,0},{4,3},{5,2},{6,5},{7,4},{8,15},{9,14},{10,... | collective-permute-start | bytes 393224 | tf_op jit(solution)/shard_map/ppermute | solution.py:47
  44.4 3.0 %collective-permute-done.15.refs_7_ = bf16[512,128]{1,0:T(8,128)(2,1)S(1)} collective-permute-done((bf16[512,128]{1,0:T(8,128)(2,1)S(1)}, bf16[512,128]{1,0:T(8,128)(2,1)S(1)}, u32[]{:S(2)}, u32[]{:S(2)}) %collective-permute-start.15) | collective-permute-done | bytes 131104 | tf_op jit(solution)/shard_map/ppermute | solution.py:47
  47.4 3.3 %collective-permute-done.14.refs_3_ = bf16[512,128]{1,0:T(8,128)(2,1)S(1)} collective-permute-done((bf16[512,128]{1,0:T(8,128)(2,1)S(1)}, bf16[512,128]{1,0:T(8,128)(2,1)S(1)}, u32[]{:S(2)}, u32[]{:S(2)}) %collective-permute-start.14) | collective-permute-done | bytes 131104 | tf_op jit(solution)/shard_map/ppermute | solution.py:47
  50.6 0.9 copy-done.6
  51.6 0.0 copy-start.10
  51.6 0.0 copy-start.11
  51.6 0.1 shard_map.144.refs_0_
  51.7 3.2 %collective-permute-start.21 = (bf16[4096,128]{1,0:T(8,128)(2,1)S(1)}, bf16[4096,128]{1,0:T(8,128)(2,1)S(1)}, u32[]{:S(2)}, u32[]{:S(2)}) collective-permute-start(bf16[4096,128]{1,0:T(8,128)(2,1)S(1)} %shard_map.144.refs_0_), channel_id=1, source_target_pairs={{0,24},{8,0},{16,8},{24,16},{32,56},{40,32},{48,40},{56,48},{64,88... | collective-permute-start | bytes 3145736 | tf_op jit(solution)/shard_map/ppermute | solution.py:52
  54.8 0.0 collective-permute-start.20
  54.9 0.2 select_reduce_fusion.slots
  55.1 0.0 copy-start.20
  55.1 1.3 %shard_map.142 = (f32[512,128]{1,0:T(8,128)S(1)}, bf16[512,128]{1,0:T(8,128)(2,1)S(1)}, f32[512,1]{1,0:T(8,128)S(1)}, bf16[512,1280]{1,0:T(8,128)(2,1)S(1)}) custom-call(s32[4]{0:T(128)S(1)} %select_reduce_fusion.slots, s32[4]{0:T(128)S(1)} %copy-done.11, s32[4]{0:T(128)S(1)} %copy-done.9, f32[4]{0:T(128)S(1)} %copy-done.10, ...), custom_call_target="tpu_custom_call" | custom-call | flops 67108864 | bytes 1048576 | tf_op jit(solution)/shard_map/pallas_call | solution.py:358
  56.5 1.1 copy-done
  57.6 1.0 collective-permute-start.16
  58.5 1.2 collective-permute-done.16
  59.7 0.3 collective-permute-start.19
  60.0 1.2 collective-permute-start.18
  61.2 0.4 collective-permute-start.17
  61.6 0.0 copy-start.8
  61.6 4.6 %collective-permute-done.19.third = bf16[512,128]{1,0:T(8,128)(2,1)S(1)} collective-permute-done((bf16[512,128]{1,0:T(8,128)(2,1)S(1)}, bf16[512,128]{1,0:T(8,128)(2,1)S(1)}, u32[]{:S(2)}, u32[]{:S(2)}) %collective-permute-start.19) | collective-permute-done | bytes 131104 | tf_op jit(solution)/shard_map/ppermute | solution.py:47
  66.2 0.4 collective-permute-done.18.second
  66.6 3.1 %collective-permute-done.17.first = bf16[512,128]{1,0:T(8,128)(2,1)S(1)} collective-permute-done((bf16[512,128]{1,0:T(8,128)(2,1)S(1)}, bf16[512,128]{1,0:T(8,128)(2,1)S(1)}, u32[]{:S(2)}, u32[]{:S(2)}) %collective-permute-start.17) | collective-permute-done | bytes 131104 | tf_op jit(solution)/shard_map/ppermute | solution.py:47
  69.7 2.2 %shard_map.143 = (bf16[32,16,1152]{2,1,0:T(8,128)(2,1)}, bf16[512,128]{1,0:T(8,128)(2,1)S(1)}) custom-call(s32[4]{0:T(128)S(1)} %select_reduce_fusion.slots, s32[4]{0:T(128)S(1)} %and_select_fusion.2.order.quarters, bf16[512,128]{1,0:T(8,128)(2,1)S(1)} %add_convert_fusion.own, bf16[512,128]{1,0:T(8,128)(2,1)S(1)} %collective-permute-done.17.first, ...), custom_call_target="tpu_custom_call" | custom-call | flops 134217728 | bytes 1048576 | tf_op jit(solution)/shard_map/pallas_call | solution.py:382
  71.8 0.6 copy-done.4
  72.5 4.2 %collective-permute-done.21.refs_2_ = bf16[4096,128]{1,0:T(8,128)(2,1)S(1)} collective-permute-done((bf16[4096,128]{1,0:T(8,128)(2,1)S(1)}, bf16[4096,128]{1,0:T(8,128)(2,1)S(1)}, u32[]{:S(2)}, u32[]{:S(2)}) %collective-permute-start.21) | collective-permute-done | bytes 1048608 | tf_op jit(solution)/shard_map/ppermute | solution.py:52
  76.6 3.1 %collective-permute-done.20.refs_1_ = bf16[4096,128]{1,0:T(8,128)(2,1)S(1)} collective-permute-done((bf16[4096,128]{1,0:T(8,128)(2,1)S(1)}, bf16[4096,128]{1,0:T(8,128)(2,1)S(1)}, u32[]{:S(2)}, u32[]{:S(2)}) %collective-permute-start.20) | collective-permute-done | bytes 1048608 | tf_op jit(solution)/shard_map/ppermute | solution.py:52
  79.7 1.0 copy-done.14
  80.8 7.4 %all-to-all-start.1 = ((bf16[32,16,1152]{2,1,0:T(8,128)(2,1)}), bf16[32,16,1152]{2,1,0:T(8,128)(2,1)S(1)}, u32[]{:S(2)}, u32[]{:S(2)}) async-start(bf16[32,16,1152]{2,1,0:T(8,128)(2,1)} %get-tuple-element.64), calls=%async_computation.1 | async-start | bytes 2359296 | tf_op jit(solution)/shard_map/all_to_all | solution.py:390
  88.2 0.7 collective-permute-start.1
  88.9 0.8 collective-permute-start
  89.7 4.5 %collective-permute-done.1.refs_2_ = bf16[1024,128]{1,0:T(8,128)(2,1)S(1)} collective-permute-done((bf16[1024,128]{1,0:T(8,128)(2,1)S(1)}, bf16[1024,128]{1,0:T(8,128)(2,1)S(1)}, u32[]{:S(2)}, u32[]{:S(2)}) %collective-permute-start.1) | collective-permute-done | bytes 262176 | tf_op jit(solution)/shard_map/ppermute | solution.py:47
  94.2 2.2 %collective-permute-start.3 = (bf16[512,128]{1,0:T(8,128)(2,1)S(1)}, bf16[512,128]{1,0:T(8,128)(2,1)S(1)}, u32[]{:S(2)}, u32[]{:S(2)}) collective-permute-start(bf16[512,128]{1,0:T(8,128)(2,1)S(1)} %slice.41), channel_id=1, source_target_pairs={{0,6},{1,7},{2,0},{3,1},{4,2},{5,3},{6,4},{7,5},{8,14},{9,15},{10,... | collective-permute-start | bytes 393224 | tf_op jit(solution)/shard_map/ppermute | solution.py:47
  96.5 0.1 collective-permute-start.2
  96.6 1.8 %collective-permute-done.3.refs_4_ = bf16[512,128]{1,0:T(8,128)(2,1)S(1)} collective-permute-done((bf16[512,128]{1,0:T(8,128)(2,1)S(1)}, bf16[512,128]{1,0:T(8,128)(2,1)S(1)}, u32[]{:S(2)}, u32[]{:S(2)}) %collective-permute-start.3) | collective-permute-done | bytes 131104 | tf_op jit(solution)/shard_map/ppermute | solution.py:47
  98.4 3.4 %collective-permute-done.2.refs_3_ = bf16[512,128]{1,0:T(8,128)(2,1)S(1)} collective-permute-done((bf16[512,128]{1,0:T(8,128)(2,1)S(1)}, bf16[512,128]{1,0:T(8,128)(2,1)S(1)}, u32[]{:S(2)}, u32[]{:S(2)}) %collective-permute-start.2) | collective-permute-done | bytes 131104 | tf_op jit(solution)/shard_map/ppermute | solution.py:47
  101.8 0.1 shard_map.139.cots
  101.9 3.7 %collective-permute-start.4 = (bf16[4096,128]{1,0:T(8,128)(2,1)S(1)}, bf16[4096,128]{1,0:T(8,128)(2,1)S(1)}, u32[]{:S(2)}, u32[]{:S(2)}) collective-permute-start(bf16[4096,128]{1,0:T(8,128)(2,1)S(1)} %shard_map.139.cots), channel_id=1, source_target_pairs={{0,1},{1,0},{2,3},{3,2},{4,5},{5,4},{6,7},{7,6},{8,9},{9,8},{10,11... | collective-permute-start | bytes 3145736 | tf_op jit(solution)/shard_map/ppermute | solution.py:47
  105.7 2.5 %collective-permute-start.23 = (bf16[2048,128]{1,0:T(8,128)(2,1)S(1)}, bf16[2048,128]{1,0:T(8,128)(2,1)}, u32[]{:S(2)}, u32[]{:S(2)}) collective-permute-start(bf16[2048,128]{1,0:T(8,128)(2,1)S(1)} %slice.39), channel_id=1, source_target_pairs={{0,24},{8,0},{16,8},{24,16},{32,56},{40,32},{48,40},{56,48},{64,88... | collective-permute-start | bytes 1572872 | tf_op jit(solution)/shard_map/ppermute | solution.py:52
  108.2 0.0 collective-permute-start.22
  108.2 0.0 collective-permute-done.4.others
  108.2 0.9 copy-done.16
  109.2 7.0 %shard_map.145 = (bf16[512,1024]{1,0:T(8,128)(2,1)}, bf16[512,2048]{1,0:T(8,128)(2,1)}) custom-call(s32[4]{0:T(128)} %copy-done.7, s32[4]{0:T(128)} %copy-done.8, bf16[4096,128]{1,0:T(8,128)(2,1)} %copy-done.3, bf16[4096,128]{1,0:T(8,128)(2,1)} %copy-done.16, bf16[512,1280]{1,0:T(8,128)(2,1)} %copy-done, bf16[512,128]{1,0:T(8,128)(2,1)} %copy-done.4, ...), custom_call_target="tpu_custom_call" | custom-call | tf_op jit(solution)/shard_map/pallas_call | solution.py:246
  116.2 7.0 %collective-permute-done.23.second = bf16[2048,128]{1,0:T(8,128)(2,1)} collective-permute-done((bf16[2048,128]{1,0:T(8,128)(2,1)S(1)}, bf16[2048,128]{1,0:T(8,128)(2,1)}, u32[]{:S(2)}, u32[]{:S(2)}) %collective-permute-start.23) | collective-permute-done | bytes 524320 | tf_op jit(solution)/shard_map/ppermute | solution.py:52
  123.2 2.8 %collective-permute-done.22.first = bf16[2048,128]{1,0:T(8,128)(2,1)} collective-permute-done((bf16[2048,128]{1,0:T(8,128)(2,1)S(1)}, bf16[2048,128]{1,0:T(8,128)(2,1)}, u32[]{:S(2)}, u32[]{:S(2)}) %collective-permute-start.22) | collective-permute-done | bytes 524320 | tf_op jit(solution)/shard_map/ppermute | solution.py:52
  126.0 4.2 %shard_map.146 = bf16[512,1024]{1,0:T(8,128)(2,1)} custom-call(s32[4]{0:T(128)} %copy-done.7, s32[4]{0:T(128)} %copy-done.8, bf16[512,1024]{1,0:T(8,128)(2,1)} %get-tuple-element.62.near_ref, bf16[512,2048]{1,0:T(8,128)(2,1)} %get-tuple-element.63.weighted, bf16[512,1280]{1,0:T(8,128)(2,1)} %copy-done, ...), custom_call_target="tpu_custom_call", output_to_operand_aliasing={{}: (2, {})} | custom-call | tf_op jit(solution)/shard_map/pallas_call | solution.py:257
  130.2 0.8 shard_map.147
  (52 shorter events, 0.3 us)
Async XLA Ops:
  2.2 25.5 %all-to-all-start = ((bf16[8,16,1280]{2,1,0:T(8,128)(2,1)}), bf16[8,16,1280]{2,1,0:T(8,128)(2,1)S(1)}, u32[]{:S(2)}, u32[]{:S(2)}) async-start(bf16[8,16,1280]{2,1,0:T(8,128)(2,1)} %shard_map.140), calls=%async_computation | async-start | bytes 655360 | tf_op jit(solution)/shard_map/all_to_all | solution.py:325
  15.4 12.4 %collective-permute-start.5 = (bf16[1024,128]{1,0:T(8,128)(2,1)}, bf16[1024,128]{1,0:T(8,128)(2,1)S(1)}, u32[]{:S(2)}, u32[]{:S(2)}) collective-permute-start(bf16[1024,128]{1,0:T(8,128)(2,1)} %get-tuple-element.35), channel_id=1, source_target_pairs={{0,2},{1,3},{2,4},{3,5},{4,6},{5,7},{6,0},{7,1},{8,10},{9,11},{10,... | collective-permute-start | bytes 786440 | tf_op jit(solution)/shard_map/ppermute | solution.py:47
  16.7 11.1 %collective-permute-start.6 = (bf16[1024,128]{1,0:T(8,128)(2,1)}, bf16[1024,128]{1,0:T(8,128)(2,1)S(1)}, u32[]{:S(2)}, u32[]{:S(2)}) collective-permute-start(bf16[1024,128]{1,0:T(8,128)(2,1)} %get-tuple-element.36), channel_id=1, source_target_pairs={{0,6},{1,7},{2,0},{3,1},{4,2},{5,3},{6,4},{7,5},{8,14},{9,15},{10,... | collective-permute-start | bytes 786440 | tf_op jit(solution)/shard_map/ppermute | solution.py:47
  18.2 9.5 %collective-permute-start.7 = (bf16[512,128]{1,0:T(8,128)(2,1)}, bf16[512,128]{1,0:T(8,128)(2,1)S(1)}, u32[]{:S(2)}, u32[]{:S(2)}) collective-permute-start(bf16[512,128]{1,0:T(8,128)(2,1)} %get-tuple-element.37), channel_id=1, source_target_pairs={{0,3},{1,2},{2,5},{3,4},{4,7},{5,6},{6,1},{7,0},{8,11},{9,10},{10,... | collective-permute-start | bytes 393224 | tf_op jit(solution)/shard_map/ppermute | solution.py:47
  19.6 8.2 %collective-permute-start.8 = (bf16[512,128]{1,0:T(8,128)(2,1)}, bf16[512,128]{1,0:T(8,128)(2,1)S(1)}, u32[]{:S(2)}, u32[]{:S(2)}) collective-permute-start(bf16[512,128]{1,0:T(8,128)(2,1)} %get-tuple-element.38), channel_id=1, source_target_pairs={{0,7},{1,6},{2,1},{3,0},{4,3},{5,2},{6,5},{7,4},{8,15},{9,14},{10,... | collective-permute-start | bytes 393224 | tf_op jit(solution)/shard_map/ppermute | solution.py:47
  21.2 6.6 %collective-permute-start.9 = (bf16[512,128]{1,0:T(8,128)(2,1)}, bf16[512,128]{1,0:T(8,128)(2,1)S(1)}, u32[]{:S(2)}, u32[]{:S(2)}) collective-permute-start(bf16[512,128]{1,0:T(8,128)(2,1)} %get-tuple-element.39), channel_id=1, source_target_pairs={{0,1},{1,0},{2,3},{3,2},{4,5},{5,4},{6,7},{7,6},{8,9},{9,8},{10,11... | collective-permute-start | bytes 393224 | tf_op jit(solution)/shard_map/ppermute | solution.py:47
  27.8 9.6 %collective-permute-start.11 = (bf16[8,16,1280]{2,1,0:T(8,128)(2,1)S(1)}, bf16[8,16,1280]{2,1,0:T(8,128)(2,1)S(1)}, u32[]{:S(2)}, u32[]{:S(2)}) collective-permute-start(bf16[8,16,1280]{2,1,0:T(8,128)(2,1)S(1)} %all-to-all-done.own), channel_id=1, source_target_pairs={{0,24},{8,0},{16,8},{24,16},{32,56},{40,32},{48,40},{56,48},{64,88... | collective-permute-start | bytes 983048 | tf_op jit(solution)/shard_map/ppermute | solution.py:52
  30.3 10.6 %collective-permute-start.10 = (bf16[8,16,1280]{2,1,0:T(8,128)(2,1)S(1)}, bf16[8,16,1280]{2,1,0:T(8,128)(2,1)S(1)}, u32[]{:S(2)}, u32[]{:S(2)}) collective-permute-start(bf16[8,16,1280]{2,1,0:T(8,128)(2,1)S(1)} %all-to-all-done.own), channel_id=1, source_target_pairs={{0,8},{8,16},{16,24},{24,0},{32,40},{40,48},{48,56},{56,32},{64,72... | collective-permute-start | bytes 983048 | tf_op jit(solution)/shard_map/ppermute | solution.py:52
  37.4 13.2 %collective-permute-start.13 = (bf16[4,16,1280]{2,1,0:T(8,128)(2,1)S(1)}, bf16[4,16,1280]{2,1,0:T(8,128)(2,1)S(1)}, u32[]{:S(2)}, u32[]{:S(2)}) collective-permute-start(bf16[4,16,1280]{2,1,0:T(8,128)(2,1)S(1)} %slice.43), channel_id=1, source_target_pairs={{0,24},{8,0},{16,8},{24,16},{32,56},{40,32},{48,40},{56,48},{64,88... | collective-permute-start | bytes 491528 | tf_op jit(solution)/shard_map/ppermute | solution.py:52
  40.9 9.7 %collective-permute-start.12 = (bf16[4,16,1280]{2,1,0:T(8,128)(2,1)S(1)}, bf16[4,16,1280]{2,1,0:T(8,128)(2,1)S(1)}, u32[]{:S(2)}, u32[]{:S(2)}) collective-permute-start(bf16[4,16,1280]{2,1,0:T(8,128)(2,1)S(1)} %slice.42), channel_id=1, source_target_pairs={{0,8},{8,16},{16,24},{24,0},{32,40},{40,48},{48,56},{56,32},{64,72... | collective-permute-start | bytes 491528 | tf_op jit(solution)/shard_map/ppermute | solution.py:52
  41.0 13.8 %copy-start.17 = (bf16[512,2,128]{2,1,0:T(2,128)(2,1)S(1)}, bf16[512,2,128]{2,1,0:T(2,128)(2,1)}, u32[]{:S(2)}) copy-start(bf16[512,2,128]{2,1,0:T(2,128)(2,1)} %param.13) | copy-start | bytes 786436
  41.1 6.3 %collective-permute-start.15 = (bf16[512,128]{1,0:T(8,128)(2,1)S(1)}, bf16[512,128]{1,0:T(8,128)(2,1)S(1)}, u32[]{:S(2)}, u32[]{:S(2)}) collective-permute-start(bf16[512,128]{1,0:T(8,128)(2,1)S(1)} %slice.37), channel_id=1, source_target_pairs={{0,7},{1,6},{2,1},{3,0},{4,3},{5,2},{6,5},{7,4},{8,15},{9,14},{10,... | collective-permute-start | bytes 393224 | tf_op jit(solution)/shard_map/ppermute | solution.py:47
  44.4 6.3 %collective-permute-start.14 = (bf16[512,128]{1,0:T(8,128)(2,1)S(1)}, bf16[512,128]{1,0:T(8,128)(2,1)S(1)}, u32[]{:S(2)}, u32[]{:S(2)}) collective-permute-start(bf16[512,128]{1,0:T(8,128)(2,1)S(1)} %slice.36), channel_id=1, source_target_pairs={{0,2},{1,3},{2,4},{3,5},{4,6},{5,7},{6,0},{7,1},{8,10},{9,11},{10,... | collective-permute-start | bytes 393224 | tf_op jit(solution)/shard_map/ppermute | solution.py:47
  50.6 0.9 copy-start.6
  51.5 3.3 %copy-start.18 = (s32[8]{0:T(128)S(1)}, s32[8]{0:T(128)}, u32[]{:S(2)}) copy-start(s32[8]{0:T(128)} %param.17) | copy-start | bytes 100
  51.6 3.3 %copy-start.19 = (s32[4]{0:T(128)S(1)}, s32[4]{0:T(128)}, u32[]{:S(2)}) copy-start(s32[4]{0:T(128)} %param.18) | copy-start | bytes 52
  51.6 3.5 %copy-start.1 = (bf16[512,1024]{1,0:T(8,128)(2,1)S(1)}, bf16[512,1024]{1,0:T(8,128)(2,1)}, u32[]{:S(2)}) copy-start(bf16[512,1024]{1,0:T(8,128)(2,1)} %x_ref.3) | copy-start | bytes 3145732
  51.6 3.5 %copy-start.9 = (s32[4]{0:T(128)S(1)}, s32[4]{0:T(128)}, u32[]{:S(2)}) copy-start(s32[4]{0:T(128)} %prompt.1) | copy-start | bytes 52
  51.6 3.6 %copy-start.10 = (f32[4]{0:T(128)S(1)}, f32[4]{0:T(128)}, u32[]{:S(2)}) copy-start(f32[4]{0:T(128)} %reward.1) | copy-start | bytes 52
  51.6 3.6 %copy-start.11 = (s32[4]{0:T(128)S(1)}, s32[4]{0:T(128)}, u32[]{:S(2)}) copy-start(s32[4]{0:T(128)} %live.1) | copy-start | bytes 52
  51.7 4.8 %copy-start.2 = (bf16[4096,128]{1,0:T(8,128)(2,1)}, bf16[4096,128]{1,0:T(8,128)(2,1)S(1)}, u32[]{:S(2)}) copy-start(bf16[4096,128]{1,0:T(8,128)(2,1)S(1)} %shard_map.144.refs_0_) | copy-start | bytes 3145732
  51.7 25.0 %collective-permute-start.21 = (bf16[4096,128]{1,0:T(8,128)(2,1)S(1)}, bf16[4096,128]{1,0:T(8,128)(2,1)S(1)}, u32[]{:S(2)}, u32[]{:S(2)}) collective-permute-start(bf16[4096,128]{1,0:T(8,128)(2,1)S(1)} %shard_map.144.refs_0_), channel_id=1, source_target_pairs={{0,24},{8,0},{16,8},{24,16},{32,56},{40,32},{48,40},{56,48},{64,88... | collective-permute-start | bytes 3145736 | tf_op jit(solution)/shard_map/ppermute | solution.py:52
  54.8 24.9 %collective-permute-start.20 = (bf16[4096,128]{1,0:T(8,128)(2,1)S(1)}, bf16[4096,128]{1,0:T(8,128)(2,1)S(1)}, u32[]{:S(2)}, u32[]{:S(2)}) collective-permute-start(bf16[4096,128]{1,0:T(8,128)(2,1)S(1)} %shard_map.144.refs_0_), channel_id=1, source_target_pairs={{0,8},{8,16},{16,24},{24,0},{32,40},{40,48},{48,56},{56,32},{64,72... | collective-permute-start | bytes 3145736 | tf_op jit(solution)/shard_map/ppermute | solution.py:52
  55.1 14.6 %copy-start.7 = (s32[4]{0:T(128)}, s32[4]{0:T(128)S(1)}, u32[]{:S(2)}) copy-start(s32[4]{0:T(128)S(1)} %select_reduce_fusion.slots) | copy-start | bytes 52
  55.1 6.4 %copy-start.20 = (s32[4]{0:T(128)S(1)}, s32[4]{0:T(128)}, u32[]{:S(2)}) copy-start(s32[4]{0:T(128)} %constant.72.clone) | copy-start | bytes 52
  56.5 1.1 copy-start
  57.6 22.2 %copy-start.5 = (f32[512,1]{1,0:T(8,128)}, f32[512,1]{1,0:T(8,128)S(1)}, u32[]{:S(2)}) copy-start(f32[512,1]{1,0:T(8,128)S(1)} %get-tuple-element.52.coef_ref) | copy-start | bytes 6148
  57.6 2.1 %collective-permute-start.16 = (f32[512,128]{1,0:T(8,128)S(1)}, f32[512,128]{1,0:T(8,128)S(1)}, u32[]{:S(2)}, u32[]{:S(2)}) collective-permute-start(f32[512,128]{1,0:T(8,128)S(1)} %get-tuple-element.49), channel_id=1, source_target_pairs={{0,1},{1,0},{2,3},{3,2},{4,5},{5,4},{6,7},{7,6},{8,9},{9,8},{10,11... | collective-permute-start | bytes 786440 | tf_op jit(solution)/shard_map/ppermute | solution.py:47
  59.7 6.5 %collective-permute-start.19 = (bf16[512,128]{1,0:T(8,128)(2,1)S(1)}, bf16[512,128]{1,0:T(8,128)(2,1)S(1)}, u32[]{:S(2)}, u32[]{:S(2)}) collective-permute-start(bf16[512,128]{1,0:T(8,128)(2,1)S(1)} %add_convert_fusion.own), channel_id=1, source_target_pairs={{0,4},{1,5},{2,6},{3,7},{4,0},{5,1},{6,2},{7,3},{8,12},{9,13},{10,... | collective-permute-start | bytes 393224 | tf_op jit(solution)/shard_map/ppermute | solution.py:47
  60.0 6.6 %collective-permute-start.18 = (bf16[512,128]{1,0:T(8,128)(2,1)S(1)}, bf16[512,128]{1,0:T(8,128)(2,1)S(1)}, u32[]{:S(2)}, u32[]{:S(2)}) collective-permute-start(bf16[512,128]{1,0:T(8,128)(2,1)S(1)} %add_convert_fusion.own), channel_id=1, source_target_pairs={{0,6},{1,7},{2,0},{3,1},{4,2},{5,3},{6,4},{7,5},{8,14},{9,15},{10,... | collective-permute-start | bytes 393224 | tf_op jit(solution)/shard_map/ppermute | solution.py:47
  61.2 8.5 %collective-permute-start.17 = (bf16[512,128]{1,0:T(8,128)(2,1)S(1)}, bf16[512,128]{1,0:T(8,128)(2,1)S(1)}, u32[]{:S(2)}, u32[]{:S(2)}) collective-permute-start(bf16[512,128]{1,0:T(8,128)(2,1)S(1)} %add_convert_fusion.own), channel_id=1, source_target_pairs={{0,2},{1,3},{2,4},{3,5},{4,6},{5,7},{6,0},{7,1},{8,10},{9,11},{10,... | collective-permute-start | bytes 393224 | tf_op jit(solution)/shard_map/ppermute | solution.py:47
  61.6 19.2 %copy-start.8 = (s32[4]{0:T(128)}, s32[4]{0:T(128)S(1)}, u32[]{:S(2)}) copy-start(s32[4]{0:T(128)S(1)} %and_select_fusion.2.order.quarters) | copy-start | bytes 52
  71.8 0.6 copy-start.4
  76.6 3.1 %copy-start.12 = (bf16[4096,128]{1,0:T(8,128)(2,1)}, bf16[4096,128]{1,0:T(8,128)(2,1)S(1)}, u32[]{:S(2)}) copy-start(bf16[4096,128]{1,0:T(8,128)(2,1)S(1)} %collective-permute-done.21.refs_2_) | copy-start | bytes 3145732
  79.7 1.0 copy-start.14
  80.8 49.4 %all-to-all-start.1 = ((bf16[32,16,1152]{2,1,0:T(8,128)(2,1)}), bf16[32,16,1152]{2,1,0:T(8,128)(2,1)S(1)}, u32[]{:S(2)}, u32[]{:S(2)}) async-start(bf16[32,16,1152]{2,1,0:T(8,128)(2,1)} %get-tuple-element.64), calls=%async_computation.1 | async-start | bytes 2359296 | tf_op jit(solution)/shard_map/all_to_all | solution.py:390
  88.2 17.5 %copy-start.15 = (bf16[4096,128]{1,0:T(8,128)(2,1)S(1)}, bf16[4096,128]{1,0:T(8,128)(2,1)}, u32[]{:S(2)}) copy-start(bf16[4096,128]{1,0:T(8,128)(2,1)} %copy-done.14) | copy-start | bytes 3145732
  88.2 6.0 %collective-permute-start.1 = (bf16[1024,128]{1,0:T(8,128)(2,1)S(1)}, bf16[1024,128]{1,0:T(8,128)(2,1)S(1)}, u32[]{:S(2)}, u32[]{:S(2)}) collective-permute-start(bf16[1024,128]{1,0:T(8,128)(2,1)S(1)} %bitcast.16), channel_id=1, source_target_pairs={{0,6},{1,7},{2,0},{3,1},{4,2},{5,3},{6,4},{7,5},{8,14},{9,15},{10,... | collective-permute-start | bytes 786440 | tf_op jit(solution)/shard_map/ppermute | solution.py:47
  88.9 7.6 %collective-permute-start = (bf16[1024,128]{1,0:T(8,128)(2,1)S(1)}, bf16[1024,128]{1,0:T(8,128)(2,1)S(1)}, u32[]{:S(2)}, u32[]{:S(2)}) collective-permute-start(bf16[1024,128]{1,0:T(8,128)(2,1)S(1)} %bitcast.17), channel_id=1, source_target_pairs={{0,2},{1,3},{2,4},{3,5},{4,6},{5,7},{6,0},{7,1},{8,10},{9,11},{10,... | collective-permute-start | bytes 786440 | tf_op jit(solution)/shard_map/ppermute | solution.py:47
  94.2 4.2 %collective-permute-start.3 = (bf16[512,128]{1,0:T(8,128)(2,1)S(1)}, bf16[512,128]{1,0:T(8,128)(2,1)S(1)}, u32[]{:S(2)}, u32[]{:S(2)}) collective-permute-start(bf16[512,128]{1,0:T(8,128)(2,1)S(1)} %slice.41), channel_id=1, source_target_pairs={{0,6},{1,7},{2,0},{3,1},{4,2},{5,3},{6,4},{7,5},{8,14},{9,15},{10,... | collective-permute-start | bytes 393224 | tf_op jit(solution)/shard_map/ppermute | solution.py:47
  96.5 9.2 %copy-start.13 = (bf16[4096,128]{1,0:T(8,128)(2,1)S(1)}, bf16[4096,128]{1,0:T(8,128)(2,1)}, u32[]{:S(2)}) copy-start(bf16[4096,128]{1,0:T(8,128)(2,1)} %copy-done.12) | copy-start | bytes 3145732
  96.5 5.3 %collective-permute-start.2 = (bf16[512,128]{1,0:T(8,128)(2,1)S(1)}, bf16[512,128]{1,0:T(8,128)(2,1)S(1)}, u32[]{:S(2)}, u32[]{:S(2)}) collective-permute-start(bf16[512,128]{1,0:T(8,128)(2,1)S(1)} %slice.40), channel_id=1, source_target_pairs={{0,2},{1,3},{2,4},{3,5},{4,6},{5,7},{6,0},{7,1},{8,10},{9,11},{10,... | collective-permute-start | bytes 393224 | tf_op jit(solution)/shard_map/ppermute | solution.py:47
  101.9 7.3 %copy-start.3 = (bf16[4096,128]{1,0:T(8,128)(2,1)}, bf16[4096,128]{1,0:T(8,128)(2,1)S(1)}, u32[]{:S(2)}) copy-start(bf16[4096,128]{1,0:T(8,128)(2,1)S(1)} %shard_map.139.cots) | copy-start | bytes 3145732
  101.9 6.4 %collective-permute-start.4 = (bf16[4096,128]{1,0:T(8,128)(2,1)S(1)}, bf16[4096,128]{1,0:T(8,128)(2,1)S(1)}, u32[]{:S(2)}, u32[]{:S(2)}) collective-permute-start(bf16[4096,128]{1,0:T(8,128)(2,1)S(1)} %shard_map.139.cots), channel_id=1, source_target_pairs={{0,1},{1,0},{2,3},{3,2},{4,5},{5,4},{6,7},{7,6},{8,9},{9,8},{10,11... | collective-permute-start | bytes 3145736 | tf_op jit(solution)/shard_map/ppermute | solution.py:47
  105.7 17.5 %collective-permute-start.23 = (bf16[2048,128]{1,0:T(8,128)(2,1)S(1)}, bf16[2048,128]{1,0:T(8,128)(2,1)}, u32[]{:S(2)}, u32[]{:S(2)}) collective-permute-start(bf16[2048,128]{1,0:T(8,128)(2,1)S(1)} %slice.39), channel_id=1, source_target_pairs={{0,24},{8,0},{16,8},{24,16},{32,56},{40,32},{48,40},{56,48},{64,88... | collective-permute-start | bytes 1572872 | tf_op jit(solution)/shard_map/ppermute | solution.py:52
  108.2 17.8 %collective-permute-start.22 = (bf16[2048,128]{1,0:T(8,128)(2,1)S(1)}, bf16[2048,128]{1,0:T(8,128)(2,1)}, u32[]{:S(2)}, u32[]{:S(2)}) collective-permute-start(bf16[2048,128]{1,0:T(8,128)(2,1)S(1)} %slice.38), channel_id=1, source_target_pairs={{0,8},{8,16},{16,24},{24,0},{32,40},{40,48},{48,56},{56,32},{64,72... | collective-permute-start | bytes 1572872 | tf_op jit(solution)/shard_map/ppermute | solution.py:52
  108.2 1.0 copy-start.16

commit v7 on v5

--- a/solution.py
+++ b/solution.py
@@ -112,33 +112,42 @@
 
 
 def payload_kernel(places, *refs):
-    slabs, outs = refs[:8], refs[8:]
-    tile = slabs[0].shape[1]
-    for out_ref, units in zip(outs, ((0, 2), (1,), (3, 5), (4,), (6,), (7,)), strict=True):
+    *slabs, cot_ref, next_ref, next_other, prev_ref, prev_other, mine_ref, other_ref = refs
+    tile, rows = slabs[0].shape[1], cot_ref.shape[1]
+    key, value = (cot_ref.at[0],), (cot_ref.at[1],)
+    slab = lambda i: (slabs[i].at[0], slabs[i].at[1])
+    orders = (
+        (next_ref, (slab(0), slab(2), key, value)),
+        (next_other, (slab(1),)),
+        (prev_ref, (slab(3), key, value, slab(5))),
+        (prev_other, (slab(4),)),
+        (mine_ref, (slab(6),)),
+        (other_ref, (slab(7),)),
+    )
+    for out_ref, units in orders:
         at = 0
-        for i in units:
-            for j in range(2):
-                out_ref[at : at + tile] = slabs[i][j]
-                at += tile
-
-
-def payloads(places, weight, tile):
+        for piece in (p for unit in units for p in unit):
+            out_ref[at : at + piece.shape[0]] = piece[...]
+            at += piece.shape[0]
+
+
+def payloads(places, weight, cotangent, tile):
     columns = weight.shape[2]
     slab = [
         pl.BlockSpec((2, tile, columns), lambda g, p, i=i: (0, p[i], 0)) for i in range(8)
     ]
-    sizes = [n * 2 * tile for n in (2, 1, 2, 1, 1, 1)]
+    sizes = [n * 2 * tile for n in (4, 1, 4, 1, 1, 1)]
     return pl.pallas_call(
         payload_kernel,
         grid_spec=pltpu.PrefetchScalarGridSpec(
             num_scalar_prefetch=1,
             grid=(1,),
-            in_specs=slab,
+            in_specs=[*slab, pl.BlockSpec(cotangent.shape, lambda g, p: (0, 0, 0))],
             out_specs=[pl.BlockSpec((n, columns), lambda g, p: (0, 0)) for n in sizes],
         ),
         out_shape=[jax.ShapeDtypeStruct((n, columns), BF) for n in sizes],
         compiler_params=pltpu.CompilerParams(vmem_limit_bytes=FULL_VMEM),
-    )(places, *[weight] * 8)
+    )(places, *[weight] * 8, cotangent)
 
 
 def factor_rows(ref, slot, start, size):
@@ -176,11 +185,12 @@
         coef_ref[rows, :] = coef
 
 
-def terms_kernel(slots, own, received, x_ref, weighted_ref, terms_ref, low_ref):
+def terms_kernel(slots, own, first, second, third, x_ref, weighted_ref, terms_ref, low_ref):
     window = x_ref.shape[1]
     columns = weighted_ref.shape[1]
     owners, owned = terms_ref.shape[0] // SLOTS, terms_ref.shape[1]
-    low = own[...].astype(F32) + received[...].astype(F32)
+    low = own[...].astype(F32) + first[...].astype(F32)
+    low = (low + second[...].astype(F32)) + third[...].astype(F32)
     low_ref[...] = low.astype(BF)
     for i in range(terms_ref.shape[0]):
         terms_ref[i] = jnp.zeros(terms_ref.shape[1:], BF)
@@ -213,7 +223,8 @@
     coef = coef_ref[...]
     count = cots.shape[0] // rows
     for i in range(2 * count):
-        piece = (cots, others)[i // count][i % count * rows : (i % count + 1) * rows]
+        source = (cots, others)[(i // count + (i % count == count - 1)) % 2]
+        piece = source[i % count * rows : (i % count + 1) * rows]
         weighted[:, i * columns : (i + 1) * columns] = (piece.astype(F32) * coef).astype(BF)
     for r, part in enumerate(slabs):
         start = pl.multiple_of(quarters[r] * tile, tile)
@@ -319,18 +330,27 @@
     steps = jnp.array([[1, 0], [1, 1], [2, 0], [3, 0], [3, 1], [2, 1], [0, 0], [0, 1]], jnp.int32)
     targets = (chip + steps[:, 0]) % CHIPS * 2 + (core + steps[:, 1]) % 2
     to_next, next_other, to_prev, prev_other, mine, other = payloads(
-        targets * 4 + x, key_value_weight, tile
+        targets * 4 + x, key_value_weight, cotangent, tile
     )
     before, after = tensor_send(to_next, 1, 0), tensor_send(to_prev, 3, 0)
     before_other, after_other = tensor_send(next_other, 1, 1), tensor_send(prev_other, 3, 1)
     partner = tensor_send(other, 0, 1)
     unit = 2 * tile
-    hop_next, hop_prev = lax.optimization_barrier((before[unit:], after[unit:]))
+    hop_next, hop_prev = lax.optimization_barrier((before[unit : 3 * unit], after[2 * unit :]))
     hop_next, hop_prev = tensor_send(hop_next, 1, 0), tensor_send(hop_prev, 3, 1)
-    pieces = mine, before, after, hop_next, partner, before_other, after_other, hop_prev
-    slabs = assemble(*[(piece, 0, unit) for piece in pieces])
-    flat = cotangent.reshape(2 * rows, columns)
-    gathered, slabs, flat = lax.optimization_barrier((gathered, slabs, flat))
+    slabs = assemble(
+        *[(piece, 0, unit) for piece in (mine, before, after, hop_next)],
+        *[(piece, 0, unit) for piece in (partner, before_other, after_other)],
+        (hop_prev, unit, 2 * unit),
+    )
+    cots = assemble(
+        (cotangent.reshape(2 * rows, columns), 0, 2 * rows),
+        (before, 2 * unit, 4 * unit),
+        (after, unit, 3 * unit),
+        (hop_next, unit, 2 * unit),
+        (hop_prev, 0, unit),
+    )
+    gathered, slabs, cots = lax.optimization_barrier((gathered, slabs, cots))
 
     low, weighted_value, coef = call(
         low_kernel,
@@ -348,31 +368,16 @@
         cotangent,
     )
     low = (low + tensor_send(low, 0, 1)).astype(BF)
-    for swap in (1, 3):
-        pairs = [(y * 2 + c, (y ^ swap) * 2 + c) for y in range(CHIPS) for c in range(2)]
-        sent = low
-        received = lax.ppermute(sent, "tensor", pairs)
-        if swap == 1:
-            low = (sent.astype(F32) + received.astype(F32)).astype(BF)
+    lows = [low] + [tensor_send(low, s, 0) for s in (1, 3, 2)]
     slabs_left, slabs_right = x_send(slabs, 1), x_send(slabs, 3)
-    cot_before, cot_after = tensor_send(flat, 1, 0), tensor_send(flat, 3, 0)
 
     terms, low = call(
         terms_kernel,
-        [SMEM] + [VMEM] * 4,
+        [SMEM] + [VMEM] * 6,
         [shape((dp, owned, window + columns), BF), shape((rows, 2 * RANK), BF)],
         4 * rows * RANK * window,
         16,
-    )(slots, sent, received, normed_input_rows, weighted_value)
-    cot_next = tensor_send(cot_before[:rows], 1, 0)
-    cot_prev = tensor_send(cot_after[rows:], 3, 0)
-    cots = assemble(
-        (flat, 0, 2 * rows),
-        (cot_before, 0, 2 * rows),
-        (cot_after, 0, 2 * rows),
-        (cot_next, 0, rows),
-        (cot_prev, 0, rows),
-    )
+    )(slots, *lows, normed_input_rows, weighted_value)
     cots_other = tensor_send(cots, 0, 1)
     terms, slabs_left, slabs_right, cots, cots_other = lax.optimization_barrier(
         (terms, slabs_left, slabs_right, cots, cots_other)

time: 125 us -> 117 us (0.936)
  starting transfers between devices: 49.6 us -> 40.5 us
  waiting for transfers between devices: 44.8 us -> 46.3 us
    ppermute x13 -> x12, waiting for transfers between devices: 11 us -> 24.5 us  [tensor_send(): return lax.ppermute(value, 'tensor', pairs)]
    ppermute x2 -> x0, waiting for transfers between devices: 10.2 us -> none  [shards(): received = lax.ppermute(sent, 'tensor', pairs)]
    all_to_all x1, waiting for transfers between devices: 8.83 us -> 0.01 us  [shards(): gathered = lax.all_to_all(packed, 'dp', 0, 0)]
    ppermute x13 -> x12, starting transfers between devices: 25 us -> 16.6 us  [tensor_send(): return lax.ppermute(value, 'tensor', pairs)]
    ppermute x4, waiting for transfers between devices: 14.8 us -> 21.7 us  [x_send(): return lax.ppermute(value, 'dp', pairs)]
    slice x2, local copies, waits for them, and re-layouts: 0.88 us -> 2.16 us  [shards(): slabs_far = (x_send(slabs_left[:half], 1), x_send(slabs_right[half:], 3))]
    unnamed x51 -> x43, local copies, waits for them, and re-layouts: 5.5 us -> 5.22 us
  transfers between devices with their start and end apart: 21 -> 18, of which waited for: 10 -> 11; matrix products, arithmetic and copies ran while one was open for 2% -> 4% of each run, Pallas kernels for 14% -> 14%
where the time goes in v7:
time: 117 us; the launch traced here: 116 us
  waiting for transfers between devices  46.3 us (40%)
  starting transfers between devices  40.5 us (35%)
  Pallas kernels  19.4 us (17%)
  local copies, waits for them, and re-layouts  7.41 us (6%)
  other arithmetic  1.26 us (1%)
    ppermute x12, waiting for transfers between devices, tensor_send(): return lax.ppermute(value, 'tensor', pairs)  24.5 us
    ppermute x4, waiting for transfers between devices, x_send(): return lax.ppermute(value, 'dp', pairs)  21.7 us
    ppermute x12, starting transfers between devices, tensor_send(): return lax.ppermute(value, 'tensor', pairs)  16.6 us
    all_to_all x1, starting transfers between devices, shards(): gathered = lax.all_to_all(packed, 'dp', 0, 0)  12 us
    pallas_call x1, Pallas kernels, frozen_and_correction(): pl.pallas_call(near_kernel, grid_spec=pltpu.PrefetchScalarGridSpec(num_sc...  6.69 us
    all_to_all x1, starting transfers between devices, shards(): terms = lax.all_to_all(terms, 'dp', 0, 0)  6.34 us
    ppermute x4, starting transfers between devices, x_send(): return lax.ppermute(value, 'dp', pairs)  5.59 us
    unnamed x43, local copies, waits for them, and re-layouts  5.22 us
  transfers between devices with their start and end apart: 18, of which 11 were waited for; matrix products, arithmetic and copies ran while one was open for 4% of the time, Pallas kernels for 14%

profile of v7, /device:TPU:1, one launch (start us, length us, event | category | flops | bytes accessed | tf_op | source)
XLA Modules:
  0.0 115.8 jit_solution(4066939844470949088)
XLA Ops:
  0.6 2.0 %shard_map.139 = bf16[32,16,1280]{2,1,0:T(8,128)(2,1)} custom-call(s32[1,4]{1,0:T(1,128)} %bitcast.17, f32[1,4]{1,0:T(1,128)} %bitcast.18, bf16[16,1024]{1,0:T(8,128)(2,1)} %down_ref.1, bf16[16,128]{1,0:T(8,128)(2,1)} %up_ref.1), custom_call_target="tpu_custom_call" | custom-call | tf_op jit(solution)/shard_map/pallas_call | solution.py:317
  2.6 12.0 %all-to-all-start = ((bf16[32,16,1280]{2,1,0:T(8,128)(2,1)}), bf16[32,16,1280]{2,1,0:T(8,128)(2,1)S(1)}, u32[]{:S(2)}, u32[]{:S(2)}) async-start(bf16[32,16,1280]{2,1,0:T(8,128)(2,1)} %shard_map.139), calls=%async_computation | async-start | bytes 2621440 | tf_op jit(solution)/shard_map/all_to_all | solution.py:327
  14.7 0.7 copy.20
  15.4 0.5 multiply_add_fusion.places
  15.9 3.3 %shard_map.140 = (bf16[2048,128]{1,0:T(8,128)(2,1)}, bf16[512,128]{1,0:T(8,128)(2,1)}, bf16[2048,128]{1,0:T(8,128)(2,1)}, bf16[512,128]{1,0:T(8,128)(2,1)}, bf16...) custom-call(s32[8]{0:T(128)} %multiply_add_fusion.places, bf16[2,8192,128]{2,1,0:T(8,128)(2,1)} %refs_7_.1, ...), custom_call_target="tpu_custom_call" | custom-call | tf_op jit(solution)/shard_map/pallas_call | solution.py:140
  19.3 1.3 %collective-permute-start = (bf16[2048,128]{1,0:T(8,128)(2,1)}, bf16[2048,128]{1,0:T(8,128)(2,1)S(1)}, u32[]{:S(2)}, u32[]{:S(2)}) collective-permute-start(bf16[2048,128]{1,0:T(8,128)(2,1)} %get-tuple-element.29), channel_id=1, source_target_pairs={{0,2},{1,3},{2,4},{3,5},{4,6},{5,7},{6,0},{7,1},{8,10},{9,11},{10,... | collective-permute-start | bytes 1572872 | tf_op jit(solution)/shard_map/ppermute | solution.py:47
  20.5 1.5 %collective-permute-start.1 = (bf16[2048,128]{1,0:T(8,128)(2,1)}, bf16[2048,128]{1,0:T(8,128)(2,1)S(1)}, u32[]{:S(2)}, u32[]{:S(2)}) collective-permute-start(bf16[2048,128]{1,0:T(8,128)(2,1)} %get-tuple-element.30), channel_id=1, source_target_pairs={{0,6},{1,7},{2,0},{3,1},{4,2},{5,3},{6,4},{7,5},{8,14},{9,15},{10,... | collective-permute-start | bytes 1572872 | tf_op jit(solution)/shard_map/ppermute | solution.py:47
  22.1 11.2 %collective-permute-done.refs_1_ = bf16[2048,128]{1,0:T(8,128)(2,1)S(1)} collective-permute-done((bf16[2048,128]{1,0:T(8,128)(2,1)}, bf16[2048,128]{1,0:T(8,128)(2,1)S(1)}, u32[]{:S(2)}, u32[]{:S(2)}) %collective-permute-start) | collective-permute-done | bytes 524320 | tf_op jit(solution)/shard_map/ppermute | solution.py:47
  33.3 0.0 collective-permute-done.1.refs_2_
  33.3 1.0 collective-permute-start.2
  34.3 3.7 %collective-permute-start.6 = (bf16[1024,128]{1,0:T(8,128)(2,1)S(1)}, bf16[1024,128]{1,0:T(8,128)(2,1)S(1)}, u32[]{:S(2)}, u32[]{:S(2)}) collective-permute-start(bf16[1024,128]{1,0:T(8,128)(2,1)S(1)} %slice.25), channel_id=1, source_target_pairs={{0,7},{1,6},{2,1},{3,0},{4,3},{5,2},{6,5},{7,4},{8,15},{9,14},{10,... | collective-permute-start | bytes 786440 | tf_op jit(solution)/shard_map/ppermute | solution.py:47
  38.1 0.0 collective-permute-start.3
  38.1 0.5 collective-permute-start.4
  38.5 2.5 %collective-permute-start.5 = (bf16[512,128]{1,0:T(8,128)(2,1)}, bf16[512,128]{1,0:T(8,128)(2,1)S(1)}, u32[]{:S(2)}, u32[]{:S(2)}) collective-permute-start(bf16[512,128]{1,0:T(8,128)(2,1)} %get-tuple-element.34), channel_id=1, source_target_pairs={{0,7},{1,6},{2,1},{3,0},{4,3},{5,2},{6,5},{7,4},{8,15},{9,14},{10,... | collective-permute-start | bytes 393224 | tf_op jit(solution)/shard_map/ppermute | solution.py:47
  41.0 0.0 collective-permute-done.2.refs_3_
  41.0 3.6 %collective-permute-done.6.refs_7_.refs_4_ = bf16[1024,128]{1,0:T(8,128)(2,1)S(1)} collective-permute-done((bf16[1024,128]{1,0:T(8,128)(2,1)S(1)}, bf16[1024,128]{1,0:T(8,128)(2,1)S(1)}, u32[]{:S(2)}, u32[]{:S(2)}) %collective-permute-start.6) | collective-permute-done | bytes 262176 | tf_op jit(solution)/shard_map/ppermute | solution.py:47
  44.7 0.1 shard_map.142.cots
  44.7 0.0 copy-start.4
  44.7 1.0 copy-done.4
  45.7 0.0 collective-permute-done.3.refs_4_
  45.7 0.0 collective-permute-done.4.refs_5_
  45.8 1.7 %collective-permute-done.5.refs_6_ = bf16[512,128]{1,0:T(8,128)(2,1)S(1)} collective-permute-done((bf16[512,128]{1,0:T(8,128)(2,1)}, bf16[512,128]{1,0:T(8,128)(2,1)S(1)}, u32[]{:S(2)}, u32[]{:S(2)}) %collective-permute-start.5) | collective-permute-done | bytes 131104 | tf_op jit(solution)/shard_map/ppermute | solution.py:47
  47.5 0.0 copy-done.8
  47.5 0.0 copy-start.10
  47.5 0.0 copy-start.11
  47.5 0.0 copy-start.12
  47.5 0.1 shard_map.141.refs_0_
  47.6 1.0 copy-done.3
  48.6 0.0 all-to-all-done.gathered_ref
  48.6 0.6 collective-permute-start.13
  49.2 2.8 %collective-permute-start.12 = (bf16[4096,128]{1,0:T(8,128)(2,1)}, bf16[4096,128]{1,0:T(8,128)(2,1)}, u32[]{:S(2)}, u32[]{:S(2)}) collective-permute-start(bf16[4096,128]{1,0:T(8,128)(2,1)} %copy-done.3), channel_id=1, source_target_pairs={{0,24},{8,0},{16,8},{24,16},{32,56},{40,32},{48,40},{56,48},{64,88... | collective-permute-start | bytes 3145736 | tf_op jit(solution)/shard_map/ppermute | solution.py:52
  52.0 0.0 collective-permute-start.11
  52.0 0.2 select_reduce_fusion.slots
  52.2 0.0 copy-start.9
  52.2 1.2 %shard_map.143 = (f32[512,128]{1,0:T(8,128)S(1)}, bf16[512,128]{1,0:T(8,128)(2,1)S(1)}, f32[512,1]{1,0:T(8,128)S(1)}) custom-call(s32[4]{0:T(128)S(1)} %select_reduce_fusion.slots, s32[4]{0:T(128)S(1)} %copy-done.12, s32[4]{0:T(128)S(1)} %copy-done.10, f32[4]{0:T(128)S(1)} %copy-done.11, bf16[32,16,1280]{2,1,0:T(8,128)(2,1)S(1)} %all-to-all-done.gathered_ref, ...), custom_call_target="tpu_custom_call" | custom-call | flops 67108864 | bytes 1048576 | tf_op jit(solution)/shard_map/pallas_call | solution.py:355
  53.5 0.4 collective-permute-start.7
  53.9 1.3 %collective-permute-done.7 = f32[512,128]{1,0:T(8,128)S(1)} collective-permute-done((f32[512,128]{1,0:T(8,128)S(1)}, f32[512,128]{1,0:T(8,128)S(1)}, u32[]{:S(2)}, u32[]{:S(2)}) %collective-permute-start.7) | collective-permute-done | bytes 262176 | tf_op jit(solution)/shard_map/ppermute | solution.py:47
  55.2 3.0 %collective-permute-start.10 = (bf16[512,128]{1,0:T(8,128)(2,1)S(1)}, bf16[512,128]{1,0:T(8,128)(2,1)S(1)}, u32[]{:S(2)}, u32[]{:S(2)}) collective-permute-start(bf16[512,128]{1,0:T(8,128)(2,1)S(1)} %add_convert_fusion.own), channel_id=1, source_target_pairs={{0,4},{1,5},{2,6},{3,7},{4,0},{5,1},{6,2},{7,3},{8,12},{9,13},{10,... | collective-permute-start | bytes 393224 | tf_op jit(solution)/shard_map/ppermute | solution.py:47
  58.2 0.8 collective-permute-start.9
  58.9 2.6 %collective-permute-done.10.third = bf16[512,128]{1,0:T(8,128)(2,1)S(1)} collective-permute-done((bf16[512,128]{1,0:T(8,128)(2,1)S(1)}, bf16[512,128]{1,0:T(8,128)(2,1)S(1)}, u32[]{:S(2)}, u32[]{:S(2)}) %collective-permute-start.10) | collective-permute-done | bytes 131104 | tf_op jit(solution)/shard_map/ppermute | solution.py:47
  61.6 1.4 %collective-permute-start.8 = (bf16[512,128]{1,0:T(8,128)(2,1)S(1)}, bf16[512,128]{1,0:T(8,128)(2,1)S(1)}, u32[]{:S(2)}, u32[]{:S(2)}) collective-permute-start(bf16[512,128]{1,0:T(8,128)(2,1)S(1)} %add_convert_fusion.own), channel_id=1, source_target_pairs={{0,2},{1,3},{2,4},{3,5},{4,6},{5,7},{6,0},{7,1},{8,10},{9,11},{10,... | collective-permute-start | bytes 393224 | tf_op jit(solution)/shard_map/ppermute | solution.py:47
  63.0 1.8 %collective-permute-done.9.second = bf16[512,128]{1,0:T(8,128)(2,1)S(1)} collective-permute-done((bf16[512,128]{1,0:T(8,128)(2,1)S(1)}, bf16[512,128]{1,0:T(8,128)(2,1)S(1)}, u32[]{:S(2)}, u32[]{:S(2)}) %collective-permute-start.9) | collective-permute-done | bytes 131104 | tf_op jit(solution)/shard_map/ppermute | solution.py:47
  64.8 2.2 %collective-permute-done.8.first = bf16[512,128]{1,0:T(8,128)(2,1)S(1)} collective-permute-done((bf16[512,128]{1,0:T(8,128)(2,1)S(1)}, bf16[512,128]{1,0:T(8,128)(2,1)S(1)}, u32[]{:S(2)}, u32[]{:S(2)}) %collective-permute-start.8) | collective-permute-done | bytes 131104 | tf_op jit(solution)/shard_map/ppermute | solution.py:47
  67.1 1.1 shard_map.144
  68.2 1.0 copy-done.5
  69.2 0.6 copy-done.6
  69.9 0.0 collective-permute-done.13.others
  69.9 5.0 %collective-permute-done.12.refs_2_ = bf16[4096,128]{1,0:T(8,128)(2,1)} collective-permute-done((bf16[4096,128]{1,0:T(8,128)(2,1)}, bf16[4096,128]{1,0:T(8,128)(2,1)}, u32[]{:S(2)}, u32[]{:S(2)}) %collective-permute-start.12) | collective-permute-done | bytes 1048608 | tf_op jit(solution)/shard_map/ppermute | solution.py:52
  74.9 3.1 %collective-permute-done.11.refs_1_ = bf16[4096,128]{1,0:T(8,128)(2,1)} collective-permute-done((bf16[4096,128]{1,0:T(8,128)(2,1)}, bf16[4096,128]{1,0:T(8,128)(2,1)}, u32[]{:S(2)}, u32[]{:S(2)}) %collective-permute-start.11) | collective-permute-done | bytes 1048608 | tf_op jit(solution)/shard_map/ppermute | solution.py:52
  78.0 6.3 %all-to-all-start.1 = ((bf16[32,16,1152]{2,1,0:T(8,128)(2,1)}), bf16[32,16,1152]{2,1,0:T(8,128)(2,1)S(1)}, u32[]{:S(2)}, u32[]{:S(2)}) async-start(bf16[32,16,1152]{2,1,0:T(8,128)(2,1)} %copy-done.5), calls=%async_computation.1 | async-start | bytes 2359296 | tf_op jit(solution)/shard_map/all_to_all | solution.py:385
  84.3 0.0 copy-start.20
  84.4 1.1 slice.23
  85.4 1.1 slice.22
  86.5 1.3 %collective-permute-start.14 = (bf16[2048,128]{1,0:T(8,128)(2,1)S(1)}, bf16[2048,128]{1,0:T(8,128)(2,1)S(1)}, u32[]{:S(2)}, u32[]{:S(2)}) collective-permute-start(bf16[2048,128]{1,0:T(8,128)(2,1)S(1)} %slice.22), channel_id=1, source_target_pairs={{0,8},{8,16},{16,24},{24,0},{32,40},{40,48},{48,56},{56,32},{64,72... | collective-permute-start | bytes 1572872 | tf_op jit(solution)/shard_map/ppermute | solution.py:52
  87.8 1.4 %collective-permute-start.15 = (bf16[2048,128]{1,0:T(8,128)(2,1)S(1)}, bf16[2048,128]{1,0:T(8,128)(2,1)S(1)}, u32[]{:S(2)}, u32[]{:S(2)}) collective-permute-start(bf16[2048,128]{1,0:T(8,128)(2,1)S(1)} %slice.23), channel_id=1, source_target_pairs={{0,24},{8,0},{16,8},{24,16},{32,56},{40,32},{48,40},{56,48},{64,88... | collective-permute-start | bytes 1572872 | tf_op jit(solution)/shard_map/ppermute | solution.py:52
  89.3 0.5 and_select_fusion.2.quarters
  89.8 6.7 %shard_map.145 = (bf16[512,1024]{1,0:T(8,128)(2,1)}, bf16[512,2048]{1,0:T(8,128)(2,1)}) custom-call(s32[4]{0:T(128)} %copy-done.9, s32[4]{0:T(128)} %and_select_fusion.2.quarters, bf16[4096,128]{1,0:T(8,128)(2,1)} %copy-done.4, bf16[4096,128]{1,0:T(8,128)(2,1)} %collective-permute-done.13.others, bf16[32,16,1280]{2,1,0:T(8,128)(2,1)} %copy-done, ...), custom_call_target="tpu_custom_call" | custom-call | tf_op jit(solution)/shard_map/pallas_call | solution.py:248
  96.5 12.8 %collective-permute-done.14.first = bf16[2048,128]{1,0:T(8,128)(2,1)S(1)} collective-permute-done((bf16[2048,128]{1,0:T(8,128)(2,1)S(1)}, bf16[2048,128]{1,0:T(8,128)(2,1)S(1)}, u32[]{:S(2)}, u32[]{:S(2)}) %collective-permute-start.14) | collective-permute-done | bytes 524320 | tf_op jit(solution)/shard_map/ppermute | solution.py:52
  109.3 0.8 collective-permute-done.15.second
  110.1 0.0 copy-done.13
  110.1 0.8 copy-done.14
  110.9 4.2 %shard_map.146 = bf16[512,1024]{1,0:T(8,128)(2,1)} custom-call(s32[4]{0:T(128)} %copy-done.9, s32[4]{0:T(128)} %and_select_fusion.2.quarters, bf16[512,1024]{1,0:T(8,128)(2,1)} %get-tuple-element.48.near_ref, bf16[512,2048]{1,0:T(8,128)(2,1)} %get-tuple-element.49.weighted, bf16[32,16,1280]{2,1,0:T(8,128)(2,1)} %copy-done, ...), custom_call_target="tpu_custom_call", output_to_operand_aliasing={{}: (2, {})} | custom-call | tf_op jit(solution)/shard_map/pallas_call | solution.py:260
  115.0 0.0 all-to-all-done.1.terms_ref
  115.0 0.8 shard_map.147
  (32 shorter events, 0.1 us)
Async XLA Ops:
  2.6 12.0 %copy-start.15 = (bf16[512,2,128]{2,1,0:T(2,128)(2,1)S(1)}, bf16[512,2,128]{2,1,0:T(2,128)(2,1)}, u32[]{:S(2)}) copy-start(bf16[512,2,128]{2,1,0:T(2,128)(2,1)} %param.13) | copy-start | bytes 786436
  2.6 12.8 %copy-start.16 = (s32[8,1]{0,1:T(1,128)S(1)}, s32[8,1]{0,1:T(1,128)}, u32[]{:S(2)}) copy-start(s32[8,1]{0,1:T(1,128)} %constant.80) | copy-start | bytes 100
  2.6 12.8 %copy-start.17 = (s32[8,1]{0,1:T(1,128)S(1)}, s32[8,1]{0,1:T(1,128)}, u32[]{:S(2)}) copy-start(s32[8,1]{0,1:T(1,128)} %constant.79) | copy-start | bytes 100
  2.6 46.0 %all-to-all-start = ((bf16[32,16,1280]{2,1,0:T(8,128)(2,1)}), bf16[32,16,1280]{2,1,0:T(8,128)(2,1)S(1)}, u32[]{:S(2)}, u32[]{:S(2)}) async-start(bf16[32,16,1280]{2,1,0:T(8,128)(2,1)} %shard_map.139), calls=%async_computation | async-start | bytes 2621440 | tf_op jit(solution)/shard_map/all_to_all | solution.py:327
  15.9 28.7 %copy-start.1 = (bf16[512,2,128]{2,0,1:T(8,128)(2,1)S(1)}, bf16[512,2,128]{2,0,1:T(8,128)(2,1)}, u32[]{:S(2)}) copy-start(bf16[512,2,128]{2,0,1:T(8,128)(2,1)} %copy.20) | copy-start | bytes 786436
  19.3 14.0 %collective-permute-start = (bf16[2048,128]{1,0:T(8,128)(2,1)}, bf16[2048,128]{1,0:T(8,128)(2,1)S(1)}, u32[]{:S(2)}, u32[]{:S(2)}) collective-permute-start(bf16[2048,128]{1,0:T(8,128)(2,1)} %get-tuple-element.29), channel_id=1, source_target_pairs={{0,2},{1,3},{2,4},{3,5},{4,6},{5,7},{6,0},{7,1},{8,10},{9,11},{10,... | collective-permute-start | bytes 1572872 | tf_op jit(solution)/shard_map/ppermute | solution.py:47
  20.5 12.7 %collective-permute-start.1 = (bf16[2048,128]{1,0:T(8,128)(2,1)}, bf16[2048,128]{1,0:T(8,128)(2,1)S(1)}, u32[]{:S(2)}, u32[]{:S(2)}) collective-permute-start(bf16[2048,128]{1,0:T(8,128)(2,1)} %get-tuple-element.30), channel_id=1, source_target_pairs={{0,6},{1,7},{2,0},{3,1},{4,2},{5,3},{6,4},{7,5},{8,14},{9,15},{10,... | collective-permute-start | bytes 1572872 | tf_op jit(solution)/shard_map/ppermute | solution.py:47
  33.3 7.7 %collective-permute-start.2 = (bf16[1024,128]{1,0:T(8,128)(2,1)S(1)}, bf16[1024,128]{1,0:T(8,128)(2,1)S(1)}, u32[]{:S(2)}, u32[]{:S(2)}) collective-permute-start(bf16[1024,128]{1,0:T(8,128)(2,1)S(1)} %slice.24), channel_id=1, source_target_pairs={{0,2},{1,3},{2,4},{3,5},{4,6},{5,7},{6,0},{7,1},{8,10},{9,11},{10,... | collective-permute-start | bytes 786440 | tf_op jit(solution)/shard_map/ppermute | solution.py:47
  34.3 10.3 %collective-permute-start.6 = (bf16[1024,128]{1,0:T(8,128)(2,1)S(1)}, bf16[1024,128]{1,0:T(8,128)(2,1)S(1)}, u32[]{:S(2)}, u32[]{:S(2)}) collective-permute-start(bf16[1024,128]{1,0:T(8,128)(2,1)S(1)} %slice.25), channel_id=1, source_target_pairs={{0,7},{1,6},{2,1},{3,0},{4,3},{5,2},{6,5},{7,4},{8,15},{9,14},{10,... | collective-permute-start | bytes 786440 | tf_op jit(solution)/shard_map/ppermute | solution.py:47
  38.1 7.7 %collective-permute-start.3 = (bf16[512,128]{1,0:T(8,128)(2,1)}, bf16[512,128]{1,0:T(8,128)(2,1)S(1)}, u32[]{:S(2)}, u32[]{:S(2)}) collective-permute-start(bf16[512,128]{1,0:T(8,128)(2,1)} %get-tuple-element.32), channel_id=1, source_target_pairs={{0,1},{1,0},{2,3},{3,2},{4,5},{5,4},{6,7},{7,6},{8,9},{9,8},{10,11... | collective-permute-start | bytes 393224 | tf_op jit(solution)/shard_map/ppermute | solution.py:47
  38.1 7.7 %collective-permute-start.4 = (bf16[512,128]{1,0:T(8,128)(2,1)}, bf16[512,128]{1,0:T(8,128)(2,1)S(1)}, u32[]{:S(2)}, u32[]{:S(2)}) collective-permute-start(bf16[512,128]{1,0:T(8,128)(2,1)} %get-tuple-element.33), channel_id=1, source_target_pairs={{0,3},{1,2},{2,5},{3,4},{4,7},{5,6},{6,1},{7,0},{8,11},{9,10},{10,... | collective-permute-start | bytes 393224 | tf_op jit(solution)/shard_map/ppermute | solution.py:47
  38.5 8.9 %collective-permute-start.5 = (bf16[512,128]{1,0:T(8,128)(2,1)}, bf16[512,128]{1,0:T(8,128)(2,1)S(1)}, u32[]{:S(2)}, u32[]{:S(2)}) collective-permute-start(bf16[512,128]{1,0:T(8,128)(2,1)} %get-tuple-element.34), channel_id=1, source_target_pairs={{0,7},{1,6},{2,1},{3,0},{4,3},{5,2},{6,5},{7,4},{8,15},{9,14},{10,... | collective-permute-start | bytes 393224 | tf_op jit(solution)/shard_map/ppermute | solution.py:47
  44.7 2.8 %copy-start.8 = (bf16[512,128]{1,0:T(8,128)(2,1)S(1)}, bf16[512,128]{1,0:T(8,128)(2,1)}, u32[]{:S(2)}) copy-start(bf16[512,128]{1,0:T(8,128)(2,1)} %get-tuple-element.28.refs_0_) | copy-start | bytes 393220
  44.7 1.0 copy-start.4
  47.5 4.5 %copy-start.18 = (s32[8]{0:T(128)S(1)}, s32[8]{0:T(128)}, u32[]{:S(2)}) copy-start(s32[8]{0:T(128)} %param.17) | copy-start | bytes 100
  47.5 4.6 %copy-start.19 = (s32[4]{0:T(128)S(1)}, s32[4]{0:T(128)}, u32[]{:S(2)}) copy-start(s32[4]{0:T(128)} %param.18) | copy-start | bytes 52
  47.5 4.7 %copy-start.2 = (bf16[512,1024]{1,0:T(8,128)(2,1)S(1)}, bf16[512,1024]{1,0:T(8,128)(2,1)}, u32[]{:S(2)}) copy-start(bf16[512,1024]{1,0:T(8,128)(2,1)} %x_ref.3) | copy-start | bytes 3145732
  47.5 4.7 %copy-start.10 = (s32[4]{0:T(128)S(1)}, s32[4]{0:T(128)}, u32[]{:S(2)}) copy-start(s32[4]{0:T(128)} %prompt.1) | copy-start | bytes 52
  47.5 4.7 %copy-start.11 = (f32[4]{0:T(128)S(1)}, f32[4]{0:T(128)}, u32[]{:S(2)}) copy-start(f32[4]{0:T(128)} %reward.1) | copy-start | bytes 52
  47.5 4.7 %copy-start.12 = (s32[4]{0:T(128)S(1)}, s32[4]{0:T(128)}, u32[]{:S(2)}) copy-start(s32[4]{0:T(128)} %live.1) | copy-start | bytes 52
  47.6 1.0 copy-start.3
  48.6 4.9 %copy-start = (bf16[32,16,1280]{2,1,0:T(8,128)(2,1)}, bf16[32,16,1280]{2,1,0:T(8,128)(2,1)S(1)}, u32[]{:S(2)}) copy-start(bf16[32,16,1280]{2,1,0:T(8,128)(2,1)S(1)} %all-to-all-done.gathered_ref) | copy-start | bytes 3932164
  48.6 21.3 %collective-permute-start.13 = (bf16[4096,128]{1,0:T(8,128)(2,1)}, bf16[4096,128]{1,0:T(8,128)(2,1)}, u32[]{:S(2)}, u32[]{:S(2)}) collective-permute-start(bf16[4096,128]{1,0:T(8,128)(2,1)} %copy-done.4), channel_id=1, source_target_pairs={{0,1},{1,0},{2,3},{3,2},{4,5},{5,4},{6,7},{7,6},{8,9},{9,8},{10,11... | collective-permute-start | bytes 3145736 | tf_op jit(solution)/shard_map/ppermute | solution.py:47
  49.2 25.7 %collective-permute-start.12 = (bf16[4096,128]{1,0:T(8,128)(2,1)}, bf16[4096,128]{1,0:T(8,128)(2,1)}, u32[]{:S(2)}, u32[]{:S(2)}) collective-permute-start(bf16[4096,128]{1,0:T(8,128)(2,1)} %copy-done.3), channel_id=1, source_target_pairs={{0,24},{8,0},{16,8},{24,16},{32,56},{40,32},{48,40},{56,48},{64,88... | collective-permute-start | bytes 3145736 | tf_op jit(solution)/shard_map/ppermute | solution.py:52
  52.0 26.0 %collective-permute-start.11 = (bf16[4096,128]{1,0:T(8,128)(2,1)}, bf16[4096,128]{1,0:T(8,128)(2,1)}, u32[]{:S(2)}, u32[]{:S(2)}) collective-permute-start(bf16[4096,128]{1,0:T(8,128)(2,1)} %copy-done.3), channel_id=1, source_target_pairs={{0,8},{8,16},{16,24},{24,0},{32,40},{40,48},{48,56},{56,32},{64,72... | collective-permute-start | bytes 3145736 | tf_op jit(solution)/shard_map/ppermute | solution.py:52
  52.2 14.8 %copy-start.9 = (s32[4]{0:T(128)}, s32[4]{0:T(128)S(1)}, u32[]{:S(2)}) copy-start(s32[4]{0:T(128)S(1)} %select_reduce_fusion.slots) | copy-start | bytes 52
  53.5 13.6 %copy-start.7 = (f32[512,1]{1,0:T(8,128)}, f32[512,1]{1,0:T(8,128)S(1)}, u32[]{:S(2)}) copy-start(f32[512,1]{1,0:T(8,128)S(1)} %get-tuple-element.45.coef_ref) | copy-start | bytes 6148
  53.5 1.6 %collective-permute-start.7 = (f32[512,128]{1,0:T(8,128)S(1)}, f32[512,128]{1,0:T(8,128)S(1)}, u32[]{:S(2)}, u32[]{:S(2)}) collective-permute-start(f32[512,128]{1,0:T(8,128)S(1)} %get-tuple-element.37), channel_id=1, source_target_pairs={{0,1},{1,0},{2,3},{3,2},{4,5},{5,4},{6,7},{7,6},{8,9},{9,8},{10,11... | collective-permute-start | bytes 786440 | tf_op jit(solution)/shard_map/ppermute | solution.py:47
  55.2 6.4 %collective-permute-start.10 = (bf16[512,128]{1,0:T(8,128)(2,1)S(1)}, bf16[512,128]{1,0:T(8,128)(2,1)S(1)}, u32[]{:S(2)}, u32[]{:S(2)}) collective-permute-start(bf16[512,128]{1,0:T(8,128)(2,1)S(1)} %add_convert_fusion.own), channel_id=1, source_target_pairs={{0,4},{1,5},{2,6},{3,7},{4,0},{5,1},{6,2},{7,3},{8,12},{9,13},{10,... | collective-permute-start | bytes 393224 | tf_op jit(solution)/shard_map/ppermute | solution.py:47
  58.2 6.7 %collective-permute-start.9 = (bf16[512,128]{1,0:T(8,128)(2,1)S(1)}, bf16[512,128]{1,0:T(8,128)(2,1)S(1)}, u32[]{:S(2)}, u32[]{:S(2)}) collective-permute-start(bf16[512,128]{1,0:T(8,128)(2,1)S(1)} %add_convert_fusion.own), channel_id=1, source_target_pairs={{0,6},{1,7},{2,0},{3,1},{4,2},{5,3},{6,4},{7,5},{8,14},{9,15},{10,... | collective-permute-start | bytes 393224 | tf_op jit(solution)/shard_map/ppermute | solution.py:47
  61.6 5.5 %collective-permute-start.8 = (bf16[512,128]{1,0:T(8,128)(2,1)S(1)}, bf16[512,128]{1,0:T(8,128)(2,1)S(1)}, u32[]{:S(2)}, u32[]{:S(2)}) collective-permute-start(bf16[512,128]{1,0:T(8,128)(2,1)S(1)} %add_convert_fusion.own), channel_id=1, source_target_pairs={{0,2},{1,3},{2,4},{3,5},{4,6},{5,7},{6,0},{7,1},{8,10},{9,11},{10,... | collective-permute-start | bytes 393224 | tf_op jit(solution)/shard_map/ppermute | solution.py:47
  68.2 1.0 copy-start.5
  69.2 0.6 copy-start.6
  78.0 37.0 %all-to-all-start.1 = ((bf16[32,16,1152]{2,1,0:T(8,128)(2,1)}), bf16[32,16,1152]{2,1,0:T(8,128)(2,1)S(1)}, u32[]{:S(2)}, u32[]{:S(2)}) async-start(bf16[32,16,1152]{2,1,0:T(8,128)(2,1)} %copy-done.5), calls=%async_computation.1 | async-start | bytes 2359296 | tf_op jit(solution)/shard_map/all_to_all | solution.py:385
  84.3 4.9 %copy-start.20 = (s32[4]{0:T(128)S(1)}, s32[4]{0:T(128)}, u32[]{:S(2)}) copy-start(s32[4]{0:T(128)} %constant.72.clone) | copy-start | bytes 52
  86.5 22.7 %collective-permute-start.14 = (bf16[2048,128]{1,0:T(8,128)(2,1)S(1)}, bf16[2048,128]{1,0:T(8,128)(2,1)S(1)}, u32[]{:S(2)}, u32[]{:S(2)}) collective-permute-start(bf16[2048,128]{1,0:T(8,128)(2,1)S(1)} %slice.22), channel_id=1, source_target_pairs={{0,8},{8,16},{16,24},{24,0},{32,40},{40,48},{48,56},{56,32},{64,72... | collective-permute-start | bytes 1572872 | tf_op jit(solution)/shard_map/ppermute | solution.py:52
  87.8 22.2 %collective-permute-start.15 = (bf16[2048,128]{1,0:T(8,128)(2,1)S(1)}, bf16[2048,128]{1,0:T(8,128)(2,1)S(1)}, u32[]{:S(2)}, u32[]{:S(2)}) collective-permute-start(bf16[2048,128]{1,0:T(8,128)(2,1)S(1)} %slice.23), channel_id=1, source_target_pairs={{0,24},{8,0},{16,8},{24,16},{32,56},{40,32},{48,40},{56,48},{64,88... | collective-permute-start | bytes 1572872 | tf_op jit(solution)/shard_map/ppermute | solution.py:52
  109.3 0.8 copy-start.13
  110.1 0.8 copy-start.14

commit v8 on v7

--- a/solution.py
+++ b/solution.py
@@ -233,9 +233,11 @@
         )
 
 
-def far_kernel(slots, quarters, near_ref, weighted, gathered_ref, low_ref, first, second, out_ref):
+def far_kernel(slots, quarters, near_ref, weighted, gathered_ref, low_ref, *refs):
+    *parts, out_ref = refs
     tile = out_ref.shape[1]
-    out_ref[...] = quarter(weighted, (first, second), low_ref, gathered_ref, slots, 0, tile)
+    parts = [ref.at[pl.ds(0, 2 * tile)] for ref in parts]
+    out_ref[...] = quarter(weighted, parts, low_ref, gathered_ref, slots, 0, tile)
 
 
 def frozen_and_correction(slots, quarters, cots, adapter, near, far, window):
@@ -254,7 +256,7 @@
             out_specs=[whole((rows, window)), whole((rows, depth))],
         ),
         out_shape=[shape((rows, window), BF), shape((rows, depth), BF)],
-        compiler_params=pltpu.CompilerParams(vmem_limit_bytes=FULL_VMEM),
+        compiler_params=pltpu.CompilerParams(vmem_limit_bytes=FULL_VMEM // 2),
     )(slots, quarters, *streams)
     owners, owned = gathered.shape[:2]
     return pl.pallas_call(
@@ -273,7 +275,7 @@
         ),
         out_shape=shape((rows, window), BF),
         input_output_aliases={2: 0},
-        compiler_params=pltpu.CompilerParams(vmem_limit_bytes=FULL_VMEM),
+        compiler_params=pltpu.CompilerParams(vmem_limit_bytes=FULL_VMEM // 2),
     )(slots, quarters, partial, weighted, gathered, low, *far)
 
 
@@ -350,7 +352,20 @@
         (hop_next, unit, 2 * unit),
         (hop_prev, 0, unit),
     )
-    gathered, slabs, cots = lax.optimization_barrier((gathered, slabs, cots))
+    gathered, slabs, cots, weight = lax.optimization_barrier(
+        (gathered, slabs, cots, key_value_weight)
+    )
+
+    def across(chip_step, core_flip):
+        target = (chip + chip_step) % CHIPS * 2 + (core + core_flip) % 2
+        start = target * window + (x + 2) % 4 * tile
+        return lax.dynamic_slice_in_dim(weight, start, tile, 1).reshape(unit, columns)
+
+    late = [
+        jnp.concatenate([across(1, 0), across(2, 0)]),
+        jnp.concatenate([across(3, 0), across(2, 1)]),
+        *[across(*step) for step in ((1, 1), (3, 1), (0, 1), (0, 0))],
+    ]
 
     low, weighted_value, coef = call(
         low_kernel,
@@ -379,12 +394,19 @@
         16,
     )(slots, *lows, normed_input_rows, weighted_value)
     cots_other = tensor_send(cots, 0, 1)
-    terms, slabs_left, slabs_right, cots, cots_other = lax.optimization_barrier(
-        (terms, slabs_left, slabs_right, cots, cots_other)
+    terms, slabs_left, slabs_right, cots, cots_other, late = lax.optimization_barrier(
+        (terms, slabs_left, slabs_right, cots, cots_other, late)
     )
     terms = lax.all_to_all(terms, "dp", 0, 0)
-    half = slabs.shape[0] // 2
-    slabs_far = (x_send(slabs_left[:half], 1), x_send(slabs_right[half:], 3))
+    routes = (1, 0), (3, 0), (1, 1), (3, 1), (0, 1)
+    before, after, before_other, after_other, partner = [
+        tensor_send(v, *route) for v, route in zip(late[:5], routes, strict=True)
+    ]
+    hop_next, hop_prev = lax.optimization_barrier((before[unit:], after[unit:]))
+    slabs_far = [
+        late[5], before, after, tensor_send(hop_next, 1, 0),
+        partner, before_other, after_other, tensor_send(hop_prev, 3, 1),
+    ]
     quarters = (x + jnp.array([0, 3, 1, 2], jnp.int32)) % 4
     input_gradient = frozen_and_correction(
         slots,

time: 117 us -> 117 us (level)
  the two profiles are of different devices: /device:TPU:1 before, /device:TPU:2 now
where the time goes in v8:
time: 117 us; the launch traced here: 116 us
  starting transfers between devices  46.6 us (40%)
  waiting for transfers between devices  39.9 us (34%)
  Pallas kernels  16.2 us (14%)
  local copies, waits for them, and re-layouts  11.5 us (10%)
    ppermute x19, waiting for transfers between devices, tensor_send(): return lax.ppermute(value, 'tensor', pairs)  26.4 us
    ppermute x19, starting transfers between devices, tensor_send(): return lax.ppermute(value, 'tensor', pairs)  23.4 us
    all_to_all x1, starting transfers between devices, shards(): gathered = lax.all_to_all(packed, 'dp', 0, 0)  11.8 us
    all_to_all x1, starting transfers between devices, shards(): terms = lax.all_to_all(terms, 'dp', 0, 0)  9.46 us
    unnamed x45, local copies, waits for them, and re-layouts  9.43 us
    all_to_all x1, waiting for transfers between devices, shards(): terms = lax.all_to_all(terms, 'dp', 0, 0)  8.35 us
    pallas_call x1, Pallas kernels, frozen_and_correction(): pl.pallas_call(near_kernel, grid_spec=pltpu.PrefetchScalarGridSpec(num_sc...  5.47 us
    ppermute x2, waiting for transfers between devices, x_send(): return lax.ppermute(value, 'dp', pairs)  5.19 us
  transfers between devices with their start and end apart: 23, of which 12 were waited for; matrix products, arithmetic and copies ran while one was open for 3% of the time, Pallas kernels for 12%

profile of v8, /device:TPU:2, one launch (start us, length us, event | category | flops | bytes accessed | tf_op | source)
XLA Modules:
  0.0 116.0 jit_solution(4201193990253525341)
XLA Ops:
  0.6 2.0 %shard_map.139 = bf16[32,16,1280]{2,1,0:T(8,128)(2,1)} custom-call(s32[1,4]{1,0:T(1,128)} %bitcast.26, f32[1,4]{1,0:T(1,128)} %bitcast.27, bf16[16,1024]{1,0:T(8,128)(2,1)} %down_ref.1, bf16[16,128]{1,0:T(8,128)(2,1)} %up_ref.1), custom_call_target="tpu_custom_call" | custom-call | tf_op jit(solution)/shard_map/pallas_call | solution.py:319
  2.6 11.8 %all-to-all-start = ((bf16[32,16,1280]{2,1,0:T(8,128)(2,1)}), bf16[32,16,1280]{2,1,0:T(8,128)(2,1)S(1)}, u32[]{:S(2)}, u32[]{:S(2)}) async-start(bf16[32,16,1280]{2,1,0:T(8,128)(2,1)} %shard_map.139), calls=%async_computation | async-start | bytes 2621440 | tf_op jit(solution)/shard_map/all_to_all | solution.py:329
  14.4 0.7 copy.20
  15.2 0.5 multiply_add_fusion.places
  15.7 3.3 %shard_map.140 = (bf16[2048,128]{1,0:T(8,128)(2,1)}, bf16[512,128]{1,0:T(8,128)(2,1)}, bf16[2048,128]{1,0:T(8,128)(2,1)}, bf16[512,128]{1,0:T(8,128)(2,1)}, bf16...) custom-call(s32[8]{0:T(128)} %multiply_add_fusion.places, bf16[2,8192,128]{2,1,0:T(8,128)(2,1)} %refs_7_.1, ...), custom_call_target="tpu_custom_call" | custom-call | tf_op jit(solution)/shard_map/pallas_call | solution.py:140
  19.0 1.6 %collective-permute-start = (bf16[2048,128]{1,0:T(8,128)(2,1)}, bf16[2048,128]{1,0:T(8,128)(2,1)S(1)}, u32[]{:S(2)}, u32[]{:S(2)}) collective-permute-start(bf16[2048,128]{1,0:T(8,128)(2,1)} %get-tuple-element.38), channel_id=1, source_target_pairs={{0,2},{1,3},{2,4},{3,5},{4,6},{5,7},{6,0},{7,1},{8,10},{9,11},{10,... | collective-permute-start | bytes 1572872 | tf_op jit(solution)/shard_map/ppermute | solution.py:47
  20.6 1.7 %collective-permute-start.1 = (bf16[2048,128]{1,0:T(8,128)(2,1)}, bf16[2048,128]{1,0:T(8,128)(2,1)S(1)}, u32[]{:S(2)}, u32[]{:S(2)}) collective-permute-start(bf16[2048,128]{1,0:T(8,128)(2,1)} %get-tuple-element.39), channel_id=1, source_target_pairs={{0,6},{1,7},{2,0},{3,1},{4,2},{5,3},{6,4},{7,5},{8,14},{9,15},{10,... | collective-permute-start | bytes 1572872 | tf_op jit(solution)/shard_map/ppermute | solution.py:47
  22.2 11.3 %collective-permute-done.refs_1_ = bf16[2048,128]{1,0:T(8,128)(2,1)S(1)} collective-permute-done((bf16[2048,128]{1,0:T(8,128)(2,1)}, bf16[2048,128]{1,0:T(8,128)(2,1)S(1)}, u32[]{:S(2)}, u32[]{:S(2)}) %collective-permute-start) | collective-permute-done | bytes 524320 | tf_op jit(solution)/shard_map/ppermute | solution.py:47
  33.6 0.0 collective-permute-done.1.refs_2_
  33.6 1.6 %collective-permute-start.2 = (bf16[1024,128]{1,0:T(8,128)(2,1)S(1)}, bf16[1024,128]{1,0:T(8,128)(2,1)S(1)}, u32[]{:S(2)}, u32[]{:S(2)}) collective-permute-start(bf16[1024,128]{1,0:T(8,128)(2,1)S(1)} %slice.24), channel_id=1, source_target_pairs={{0,2},{1,3},{2,4},{3,5},{4,6},{5,7},{6,0},{7,1},{8,10},{9,11},{10,... | collective-permute-start | bytes 786440 | tf_op jit(solution)/shard_map/ppermute | solution.py:47
  35.3 1.8 %collective-permute-start.3 = (bf16[512,128]{1,0:T(8,128)(2,1)}, bf16[512,128]{1,0:T(8,128)(2,1)S(1)}, u32[]{:S(2)}, u32[]{:S(2)}) collective-permute-start(bf16[512,128]{1,0:T(8,128)(2,1)} %get-tuple-element.41), channel_id=1, source_target_pairs={{0,1},{1,0},{2,3},{3,2},{4,5},{5,4},{6,7},{7,6},{8,9},{9,8},{10,11... | collective-permute-start | bytes 393224 | tf_op jit(solution)/shard_map/ppermute | solution.py:47
  37.1 3.0 %collective-permute-start.5 = (bf16[512,128]{1,0:T(8,128)(2,1)}, bf16[512,128]{1,0:T(8,128)(2,1)S(1)}, u32[]{:S(2)}, u32[]{:S(2)}) collective-permute-start(bf16[512,128]{1,0:T(8,128)(2,1)} %get-tuple-element.43), channel_id=1, source_target_pairs={{0,7},{1,6},{2,1},{3,0},{4,3},{5,2},{6,5},{7,4},{8,15},{9,14},{10,... | collective-permute-start | bytes 393224 | tf_op jit(solution)/shard_map/ppermute | solution.py:47
  40.0 1.5 %collective-permute-done.2.refs_3_ = bf16[1024,128]{1,0:T(8,128)(2,1)S(1)} collective-permute-done((bf16[1024,128]{1,0:T(8,128)(2,1)S(1)}, bf16[1024,128]{1,0:T(8,128)(2,1)S(1)}, u32[]{:S(2)}, u32[]{:S(2)}) %collective-permute-start.2) | collective-permute-done | bytes 262176 | tf_op jit(solution)/shard_map/ppermute | solution.py:47
  41.6 2.3 %collective-permute-done.6.refs_7_.refs_4_ = bf16[1024,128]{1,0:T(8,128)(2,1)S(1)} collective-permute-done((bf16[1024,128]{1,0:T(8,128)(2,1)S(1)}, bf16[1024,128]{1,0:T(8,128)(2,1)S(1)}, u32[]{:S(2)}, u32[]{:S(2)}) %collective-permute-start.6) | collective-permute-done | bytes 262176 | tf_op jit(solution)/shard_map/ppermute | solution.py:47
  43.9 0.1 shard_map.142.cots
  44.0 0.0 copy-start.4
  44.0 1.0 copy-done.4
  44.9 0.0 collective-permute-done.4.refs_5_
  44.9 1.6 %collective-permute-done.5.refs_6_ = bf16[512,128]{1,0:T(8,128)(2,1)S(1)} collective-permute-done((bf16[512,128]{1,0:T(8,128)(2,1)}, bf16[512,128]{1,0:T(8,128)(2,1)S(1)}, u32[]{:S(2)}, u32[]{:S(2)}) %collective-permute-start.5) | collective-permute-done | bytes 131104 | tf_op jit(solution)/shard_map/ppermute | solution.py:47
  46.6 0.0 copy-start.13
  46.6 0.0 copy-start.14
  46.6 0.0 copy-start.15
  46.6 0.1 shard_map.141.refs_0_
  46.7 1.0 copy-done.2
  47.7 0.0 all-to-all-done.gathered_ref
  47.7 0.0 collective-permute-start.13
  47.7 0.5 collective-permute-start.12
  48.2 1.5 %collective-permute-start.11 = (bf16[4096,128]{1,0:T(8,128)(2,1)}, bf16[4096,128]{1,0:T(8,128)(2,1)}, u32[]{:S(2)}, u32[]{:S(2)}) collective-permute-start(bf16[4096,128]{1,0:T(8,128)(2,1)} %copy-done.2), channel_id=1, source_target_pairs={{0,8},{8,16},{16,24},{24,0},{32,40},{40,48},{48,56},{56,32},{64,72... | collective-permute-start | bytes 3145736 | tf_op jit(solution)/shard_map/ppermute | solution.py:52
  49.7 0.2 select_reduce_fusion.slots
  49.9 1.2 %shard_map.143 = (f32[512,128]{1,0:T(8,128)S(1)}, bf16[512,128]{1,0:T(8,128)(2,1)S(1)}, f32[512,1]{1,0:T(8,128)S(1)}) custom-call(s32[4]{0:T(128)S(1)} %select_reduce_fusion.slots, s32[4]{0:T(128)S(1)} %copy-done.15, s32[4]{0:T(128)S(1)} %copy-done.13, f32[4]{0:T(128)S(1)} %copy-done.14, bf16[32,16,1280]{2,1,0:T(8,128)(2,1)S(1)} %all-to-all-done.gathered_ref, ...), custom_call_target="tpu_custom_call" | custom-call | flops 67108864 | bytes 1048576 | tf_op jit(solution)/shard_map/pallas_call | solution.py:370
  51.2 0.7 copy-done.10
  51.9 0.1 collective-permute-start.7
  51.9 1.5 %collective-permute-done.7 = f32[512,128]{1,0:T(8,128)S(1)} collective-permute-done((f32[512,128]{1,0:T(8,128)S(1)}, f32[512,128]{1,0:T(8,128)S(1)}, u32[]{:S(2)}, u32[]{:S(2)}) %collective-permute-start.7) | collective-permute-done | bytes 262176 | tf_op jit(solution)/shard_map/ppermute | solution.py:47
  53.4 3.1 %collective-permute-start.10 = (bf16[512,128]{1,0:T(8,128)(2,1)S(1)}, bf16[512,128]{1,0:T(8,128)(2,1)S(1)}, u32[]{:S(2)}, u32[]{:S(2)}) collective-permute-start(bf16[512,128]{1,0:T(8,128)(2,1)S(1)} %add_convert_fusion.own), channel_id=1, source_target_pairs={{0,4},{1,5},{2,6},{3,7},{4,0},{5,1},{6,2},{7,3},{8,12},{9,13},{10,... | collective-permute-start | bytes 393224 | tf_op jit(solution)/shard_map/ppermute | solution.py:47
  56.6 1.2 %collective-permute-start.9 = (bf16[512,128]{1,0:T(8,128)(2,1)S(1)}, bf16[512,128]{1,0:T(8,128)(2,1)S(1)}, u32[]{:S(2)}, u32[]{:S(2)}) collective-permute-start(bf16[512,128]{1,0:T(8,128)(2,1)S(1)} %add_convert_fusion.own), channel_id=1, source_target_pairs={{0,6},{1,7},{2,0},{3,1},{4,2},{5,3},{6,4},{7,5},{8,14},{9,15},{10,... | collective-permute-start | bytes 393224 | tf_op jit(solution)/shard_map/ppermute | solution.py:47
  57.8 2.8 %collective-permute-done.10.third = bf16[512,128]{1,0:T(8,128)(2,1)S(1)} collective-permute-done((bf16[512,128]{1,0:T(8,128)(2,1)S(1)}, bf16[512,128]{1,0:T(8,128)(2,1)S(1)}, u32[]{:S(2)}, u32[]{:S(2)}) %collective-permute-start.10) | collective-permute-done | bytes 131104 | tf_op jit(solution)/shard_map/ppermute | solution.py:47
  60.6 2.4 %collective-permute-start.8 = (bf16[512,128]{1,0:T(8,128)(2,1)S(1)}, bf16[512,128]{1,0:T(8,128)(2,1)S(1)}, u32[]{:S(2)}, u32[]{:S(2)}) collective-permute-start(bf16[512,128]{1,0:T(8,128)(2,1)S(1)} %add_convert_fusion.own), channel_id=1, source_target_pairs={{0,2},{1,3},{2,4},{3,5},{4,6},{5,7},{6,0},{7,1},{8,10},{9,11},{10,... | collective-permute-start | bytes 393224 | tf_op jit(solution)/shard_map/ppermute | solution.py:47
  63.0 2.1 %constant_dynamic-slice_fusion = (bf16[2,256,128]{2,1,0:T(8,128)(2,1)}, bf16[2,256,128]{2,1,0:T(8,128)(2,1)}, bf16[2,256,128]{2,1,0:T(8,128)(2,1)S(1)}, bf16[2,2...) fusion(bf16[2,8192,128]{2,1,0:T(8,128)(2,1)} %refs_7_.1, ...), kind=kLoop, calls=%fused_computation.10 | loop fusion | bytes 2097184 | tf_op jit(solution)/shard_map/dynamic_slice | solution.py:362
  65.1 0.0 collective-permute-done.9.second
  65.1 2.1 %collective-permute-done.8.first = bf16[512,128]{1,0:T(8,128)(2,1)S(1)} collective-permute-done((bf16[512,128]{1,0:T(8,128)(2,1)S(1)}, bf16[512,128]{1,0:T(8,128)(2,1)S(1)}, u32[]{:S(2)}, u32[]{:S(2)}) %collective-permute-start.8) | collective-permute-done | bytes 131104 | tf_op jit(solution)/shard_map/ppermute | solution.py:47
  67.2 1.1 shard_map.144
  68.3 1.1 copy-done.6
  69.4 0.6 copy-done.8
  70.0 0.0 collective-permute-done.13.others
  70.0 3.7 %collective-permute-done.12.refs_2_ = bf16[4096,128]{1,0:T(8,128)(2,1)} collective-permute-done((bf16[4096,128]{1,0:T(8,128)(2,1)}, bf16[4096,128]{1,0:T(8,128)(2,1)}, u32[]{:S(2)}, u32[]{:S(2)}) %collective-permute-start.12) | collective-permute-done | bytes 1048608 | tf_op jit(solution)/shard_map/ppermute | solution.py:52
  73.7 1.5 %collective-permute-done.11.refs_1_ = bf16[4096,128]{1,0:T(8,128)(2,1)} collective-permute-done((bf16[4096,128]{1,0:T(8,128)(2,1)}, bf16[4096,128]{1,0:T(8,128)(2,1)}, u32[]{:S(2)}, u32[]{:S(2)}) %collective-permute-start.11) | collective-permute-done | bytes 1048608 | tf_op jit(solution)/shard_map/ppermute | solution.py:52
  75.2 9.5 %all-to-all-start.1 = ((bf16[32,16,1152]{2,1,0:T(8,128)(2,1)}), bf16[32,16,1152]{2,1,0:T(8,128)(2,1)S(1)}, u32[]{:S(2)}, u32[]{:S(2)}) async-start(bf16[32,16,1152]{2,1,0:T(8,128)(2,1)} %copy-done.6), calls=%async_computation.1 | async-start | bytes 2359296 | tf_op jit(solution)/shard_map/all_to_all | solution.py:400
  84.7 1.4 %collective-permute-start.14 = (bf16[1024,128]{1,0:T(8,128)(2,1)S(1)}, bf16[1024,128]{1,0:T(8,128)(2,1)S(1)}, u32[]{:S(2)}, u32[]{:S(2)}) collective-permute-start(bf16[1024,128]{1,0:T(8,128)(2,1)S(1)} %get-tuple-element.61), channel_id=1, source_target_pairs={{0,2},{1,3},{2,4},{3,5},{4,6},{5,7},{6,0},{7,1},{8,10},{9,11},{10,... | collective-permute-start | bytes 786440 | tf_op jit(solution)/shard_map/ppermute | solution.py:47
  86.1 1.9 %collective-permute-start.15 = (bf16[1024,128]{1,0:T(8,128)(2,1)S(1)}, bf16[1024,128]{1,0:T(8,128)(2,1)S(1)}, u32[]{:S(2)}, u32[]{:S(2)}) collective-permute-start(bf16[1024,128]{1,0:T(8,128)(2,1)S(1)} %get-tuple-element.62), channel_id=1, source_target_pairs={{0,6},{1,7},{2,0},{3,1},{4,2},{5,3},{6,4},{7,5},{8,14},{9,15},{10,... | collective-permute-start | bytes 786440 | tf_op jit(solution)/shard_map/ppermute | solution.py:47
  88.0 0.0 collective-permute-start.17
  88.0 0.2 collective-permute-start.18
  88.2 2.7 %collective-permute-start.19 = (bf16[512,128]{1,0:T(8,128)(2,1)S(1)}, bf16[512,128]{1,0:T(8,128)(2,1)S(1)}, u32[]{:S(2)}, u32[]{:S(2)}) collective-permute-start(bf16[512,128]{1,0:T(8,128)(2,1)S(1)} %bitcast.32), channel_id=1, source_target_pairs={{0,7},{1,6},{2,1},{3,0},{4,3},{5,2},{6,5},{7,4},{8,15},{9,14},{10,... | collective-permute-start | bytes 393224 | tf_op jit(solution)/shard_map/ppermute | solution.py:47
  91.0 2.9 %collective-permute-done.14.refs_1_ = bf16[1024,128]{1,0:T(8,128)(2,1)S(1)} collective-permute-done((bf16[1024,128]{1,0:T(8,128)(2,1)S(1)}, bf16[1024,128]{1,0:T(8,128)(2,1)S(1)}, u32[]{:S(2)}, u32[]{:S(2)}) %collective-permute-start.14) | collective-permute-done | bytes 262176 | tf_op jit(solution)/shard_map/ppermute | solution.py:47
  93.9 0.3 collective-permute-done.15.refs_2_
  94.2 0.7 collective-permute-start.16
  94.9 0.0 collective-permute-start.20
  94.9 1.2 %copy-done.3 = bf16[4096,128]{1,0:T(8,128)(2,1)S(1)} copy-done((bf16[4096,128]{1,0:T(8,128)(2,1)S(1)}, bf16[4096,128]{1,0:T(8,128)(2,1)}, u32[]{:S(2)}) %copy-start.3) | copy-done | bytes 1048600
  96.1 1.2 %copy-done.5 = bf16[4096,128]{1,0:T(8,128)(2,1)S(1)} copy-done((bf16[4096,128]{1,0:T(8,128)(2,1)S(1)}, bf16[4096,128]{1,0:T(8,128)(2,1)}, u32[]{:S(2)}) %copy-start.5) | copy-done | bytes 1048600
  97.4 0.9 copy-done.9
  98.3 0.9 copy-done.11
  99.2 5.5 %shard_map.145 = (bf16[512,1024]{1,0:T(8,128)(2,1)}, bf16[512,2048]{1,0:T(8,128)(2,1)S(1)}) custom-call(s32[4]{0:T(128)S(1)} %select_reduce_fusion.slots, s32[4]{0:T(128)S(1)} %and_select_fusion.2.quarters, bf16[4096,128]{1,0:T(8,128)(2,1)S(1)} %copy-done.5, bf16[4096,128]{1,0:T(8,128)(2,1)} %collective-permute-done.13.others, ...), custom_call_target="tpu_custom_call" | custom-call | tf_op jit(solution)/shard_map/pallas_call | solution.py:250
  104.7 2.1 %shard_map.146 = bf16[512,1024]{1,0:T(8,128)(2,1)} custom-call(s32[4]{0:T(128)S(1)} %select_reduce_fusion.slots, s32[4]{0:T(128)S(1)} %and_select_fusion.2.quarters, bf16[512,1024]{1,0:T(8,128)(2,1)} %get-tuple-element.58.near_ref, bf16[512,2048]{1,0:T(8,128)(2,1)S(1)} %get-tuple-element.59.weighted, ...), custom_call_target="tpu_custom_call", output_to_operand_aliasing={{}: (2, {})} | custom-call | tf_op jit(solution)/shard_map/pallas_call | solution.py:262
  106.8 8.4 %all-to-all-done.1.terms_ref = bf16[32,16,1152]{2,1,0:T(8,128)(2,1)S(1)} async-done(((bf16[32,16,1152]{2,1,0:T(8,128)(2,1)}), bf16[32,16,1152]{2,1,0:T(8,128)(2,1)S(1)}, u32[]{:S(2)}, u32[]{:S(2)}) %all-to-all-start.1) | async-done | bytes 1179680 | tf_op jit(solution)/shard_map/all_to_all | solution.py:400
  115.2 0.8 shard_map.147
  (46 shorter events, 0.2 us)
Async XLA Ops:
  2.6 11.8 %copy-start.16 = (bf16[512,2,128]{2,1,0:T(2,128)(2,1)S(1)}, bf16[512,2,128]{2,1,0:T(2,128)(2,1)}, u32[]{:S(2)}) copy-start(bf16[512,2,128]{2,1,0:T(2,128)(2,1)} %param.13) | copy-start | bytes 786436
  2.6 12.5 %copy-start.17 = (s32[8,1]{0,1:T(1,128)S(1)}, s32[8,1]{0,1:T(1,128)}, u32[]{:S(2)}) copy-start(s32[8,1]{0,1:T(1,128)} %constant.150) | copy-start | bytes 100
  2.6 12.5 %copy-start.18 = (s32[8,1]{0,1:T(1,128)S(1)}, s32[8,1]{0,1:T(1,128)}, u32[]{:S(2)}) copy-start(s32[8,1]{0,1:T(1,128)} %constant.149) | copy-start | bytes 100
  2.6 45.0 %all-to-all-start = ((bf16[32,16,1280]{2,1,0:T(8,128)(2,1)}), bf16[32,16,1280]{2,1,0:T(8,128)(2,1)S(1)}, u32[]{:S(2)}, u32[]{:S(2)}) async-start(bf16[32,16,1280]{2,1,0:T(8,128)(2,1)} %shard_map.139), calls=%async_computation | async-start | bytes 2621440 | tf_op jit(solution)/shard_map/all_to_all | solution.py:329
  15.7 28.2 %copy-start = (bf16[512,2,128]{2,0,1:T(8,128)(2,1)S(1)}, bf16[512,2,128]{2,0,1:T(8,128)(2,1)}, u32[]{:S(2)}) copy-start(bf16[512,2,128]{2,0,1:T(8,128)(2,1)} %copy.20) | copy-start | bytes 786436
  19.0 14.6 %collective-permute-start = (bf16[2048,128]{1,0:T(8,128)(2,1)}, bf16[2048,128]{1,0:T(8,128)(2,1)S(1)}, u32[]{:S(2)}, u32[]{:S(2)}) collective-permute-start(bf16[2048,128]{1,0:T(8,128)(2,1)} %get-tuple-element.38), channel_id=1, source_target_pairs={{0,2},{1,3},{2,4},{3,5},{4,6},{5,7},{6,0},{7,1},{8,10},{9,11},{10,... | collective-permute-start | bytes 1572872 | tf_op jit(solution)/shard_map/ppermute | solution.py:47
  20.6 13.0 %collective-permute-start.1 = (bf16[2048,128]{1,0:T(8,128)(2,1)}, bf16[2048,128]{1,0:T(8,128)(2,1)S(1)}, u32[]{:S(2)}, u32[]{:S(2)}) collective-permute-start(bf16[2048,128]{1,0:T(8,128)(2,1)} %get-tuple-element.39), channel_id=1, source_target_pairs={{0,6},{1,7},{2,0},{3,1},{4,2},{5,3},{6,4},{7,5},{8,14},{9,15},{10,... | collective-permute-start | bytes 1572872 | tf_op jit(solution)/shard_map/ppermute | solution.py:47
  33.6 7.9 %collective-permute-start.2 = (bf16[1024,128]{1,0:T(8,128)(2,1)S(1)}, bf16[1024,128]{1,0:T(8,128)(2,1)S(1)}, u32[]{:S(2)}, u32[]{:S(2)}) collective-permute-start(bf16[1024,128]{1,0:T(8,128)(2,1)S(1)} %slice.24), channel_id=1, source_target_pairs={{0,2},{1,3},{2,4},{3,5},{4,6},{5,7},{6,0},{7,1},{8,10},{9,11},{10,... | collective-permute-start | bytes 786440 | tf_op jit(solution)/shard_map/ppermute | solution.py:47
  35.3 8.6 %collective-permute-start.6 = (bf16[1024,128]{1,0:T(8,128)(2,1)S(1)}, bf16[1024,128]{1,0:T(8,128)(2,1)S(1)}, u32[]{:S(2)}, u32[]{:S(2)}) collective-permute-start(bf16[1024,128]{1,0:T(8,128)(2,1)S(1)} %slice.25), channel_id=1, source_target_pairs={{0,7},{1,6},{2,1},{3,0},{4,3},{5,2},{6,5},{7,4},{8,15},{9,14},{10,... | collective-permute-start | bytes 786440 | tf_op jit(solution)/shard_map/ppermute | solution.py:47
  35.3 9.7 %collective-permute-start.3 = (bf16[512,128]{1,0:T(8,128)(2,1)}, bf16[512,128]{1,0:T(8,128)(2,1)S(1)}, u32[]{:S(2)}, u32[]{:S(2)}) collective-permute-start(bf16[512,128]{1,0:T(8,128)(2,1)} %get-tuple-element.41), channel_id=1, source_target_pairs={{0,1},{1,0},{2,3},{3,2},{4,5},{5,4},{6,7},{7,6},{8,9},{9,8},{10,11... | collective-permute-start | bytes 393224 | tf_op jit(solution)/shard_map/ppermute | solution.py:47
  37.1 7.9 %collective-permute-start.4 = (bf16[512,128]{1,0:T(8,128)(2,1)}, bf16[512,128]{1,0:T(8,128)(2,1)S(1)}, u32[]{:S(2)}, u32[]{:S(2)}) collective-permute-start(bf16[512,128]{1,0:T(8,128)(2,1)} %get-tuple-element.42), channel_id=1, source_target_pairs={{0,3},{1,2},{2,5},{3,4},{4,7},{5,6},{6,1},{7,0},{8,11},{9,10},{10,... | collective-permute-start | bytes 393224 | tf_op jit(solution)/shard_map/ppermute | solution.py:47
  37.1 9.5 %collective-permute-start.5 = (bf16[512,128]{1,0:T(8,128)(2,1)}, bf16[512,128]{1,0:T(8,128)(2,1)S(1)}, u32[]{:S(2)}, u32[]{:S(2)}) collective-permute-start(bf16[512,128]{1,0:T(8,128)(2,1)} %get-tuple-element.43), channel_id=1, source_target_pairs={{0,7},{1,6},{2,1},{3,0},{4,3},{5,2},{6,5},{7,4},{8,15},{9,14},{10,... | collective-permute-start | bytes 393224 | tf_op jit(solution)/shard_map/ppermute | solution.py:47
  43.9 2.6 %copy-start.12 = (bf16[512,128]{1,0:T(8,128)(2,1)S(1)}, bf16[512,128]{1,0:T(8,128)(2,1)}, u32[]{:S(2)}) copy-start(bf16[512,128]{1,0:T(8,128)(2,1)} %get-tuple-element.37.refs_0_) | copy-start | bytes 393220
  44.0 1.0 copy-start.4
  46.5 3.2 %copy-start.19 = (s32[8]{0:T(128)S(1)}, s32[8]{0:T(128)}, u32[]{:S(2)}) copy-start(s32[8]{0:T(128)} %param.17) | copy-start | bytes 100
  46.5 3.2 %copy-start.20 = (s32[4]{0:T(128)S(1)}, s32[4]{0:T(128)}, u32[]{:S(2)}) copy-start(s32[4]{0:T(128)} %param.18) | copy-start | bytes 52
  46.5 3.3 %copy-start.1 = (bf16[512,1024]{1,0:T(8,128)(2,1)S(1)}, bf16[512,1024]{1,0:T(8,128)(2,1)}, u32[]{:S(2)}) copy-start(bf16[512,1024]{1,0:T(8,128)(2,1)} %x_ref.3) | copy-start | bytes 3145732
  46.6 3.3 %copy-start.13 = (s32[4]{0:T(128)S(1)}, s32[4]{0:T(128)}, u32[]{:S(2)}) copy-start(s32[4]{0:T(128)} %prompt.1) | copy-start | bytes 52
  46.6 3.3 %copy-start.14 = (f32[4]{0:T(128)S(1)}, f32[4]{0:T(128)}, u32[]{:S(2)}) copy-start(f32[4]{0:T(128)} %reward.1) | copy-start | bytes 52
  46.6 3.3 %copy-start.15 = (s32[4]{0:T(128)S(1)}, s32[4]{0:T(128)}, u32[]{:S(2)}) copy-start(s32[4]{0:T(128)} %live.1) | copy-start | bytes 52
  46.7 1.0 copy-start.2
  47.7 22.3 %collective-permute-start.13 = (bf16[4096,128]{1,0:T(8,128)(2,1)}, bf16[4096,128]{1,0:T(8,128)(2,1)}, u32[]{:S(2)}, u32[]{:S(2)}) collective-permute-start(bf16[4096,128]{1,0:T(8,128)(2,1)} %copy-done.4), channel_id=1, source_target_pairs={{0,1},{1,0},{2,3},{3,2},{4,5},{5,4},{6,7},{7,6},{8,9},{9,8},{10,11... | collective-permute-start | bytes 3145736 | tf_op jit(solution)/shard_map/ppermute | solution.py:47
  47.7 26.0 %collective-permute-start.12 = (bf16[4096,128]{1,0:T(8,128)(2,1)}, bf16[4096,128]{1,0:T(8,128)(2,1)}, u32[]{:S(2)}, u32[]{:S(2)}) collective-permute-start(bf16[4096,128]{1,0:T(8,128)(2,1)} %copy-done.2), channel_id=1, source_target_pairs={{0,24},{8,0},{16,8},{24,16},{32,56},{40,32},{48,40},{56,48},{64,88... | collective-permute-start | bytes 3145736 | tf_op jit(solution)/shard_map/ppermute | solution.py:52
  48.2 27.0 %collective-permute-start.11 = (bf16[4096,128]{1,0:T(8,128)(2,1)}, bf16[4096,128]{1,0:T(8,128)(2,1)}, u32[]{:S(2)}, u32[]{:S(2)}) collective-permute-start(bf16[4096,128]{1,0:T(8,128)(2,1)} %copy-done.2), channel_id=1, source_target_pairs={{0,8},{8,16},{16,24},{24,0},{32,40},{40,48},{48,56},{56,32},{64,72... | collective-permute-start | bytes 3145736 | tf_op jit(solution)/shard_map/ppermute | solution.py:52
  51.2 0.7 copy-start.10
  51.9 1.5 %collective-permute-start.7 = (f32[512,128]{1,0:T(8,128)S(1)}, f32[512,128]{1,0:T(8,128)S(1)}, u32[]{:S(2)}, u32[]{:S(2)}) collective-permute-start(f32[512,128]{1,0:T(8,128)S(1)} %get-tuple-element.46), channel_id=1, source_target_pairs={{0,1},{1,0},{2,3},{3,2},{4,5},{5,4},{6,7},{7,6},{8,9},{9,8},{10,11... | collective-permute-start | bytes 786440 | tf_op jit(solution)/shard_map/ppermute | solution.py:47
  53.4 7.1 %collective-permute-start.10 = (bf16[512,128]{1,0:T(8,128)(2,1)S(1)}, bf16[512,128]{1,0:T(8,128)(2,1)S(1)}, u32[]{:S(2)}, u32[]{:S(2)}) collective-permute-start(bf16[512,128]{1,0:T(8,128)(2,1)S(1)} %add_convert_fusion.own), channel_id=1, source_target_pairs={{0,4},{1,5},{2,6},{3,7},{4,0},{5,1},{6,2},{7,3},{8,12},{9,13},{10,... | collective-permute-start | bytes 393224 | tf_op jit(solution)/shard_map/ppermute | solution.py:47
  56.6 8.5 %collective-permute-start.9 = (bf16[512,128]{1,0:T(8,128)(2,1)S(1)}, bf16[512,128]{1,0:T(8,128)(2,1)S(1)}, u32[]{:S(2)}, u32[]{:S(2)}) collective-permute-start(bf16[512,128]{1,0:T(8,128)(2,1)S(1)} %add_convert_fusion.own), channel_id=1, source_target_pairs={{0,6},{1,7},{2,0},{3,1},{4,2},{5,3},{6,4},{7,5},{8,14},{9,15},{10,... | collective-permute-start | bytes 393224 | tf_op jit(solution)/shard_map/ppermute | solution.py:47
  60.6 6.6 %collective-permute-start.8 = (bf16[512,128]{1,0:T(8,128)(2,1)S(1)}, bf16[512,128]{1,0:T(8,128)(2,1)S(1)}, u32[]{:S(2)}, u32[]{:S(2)}) collective-permute-start(bf16[512,128]{1,0:T(8,128)(2,1)S(1)} %add_convert_fusion.own), channel_id=1, source_target_pairs={{0,2},{1,3},{2,4},{3,5},{4,6},{5,7},{6,0},{7,1},{8,10},{9,11},{10,... | collective-permute-start | bytes 393224 | tf_op jit(solution)/shard_map/ppermute | solution.py:47
  68.3 1.1 copy-start.6
  69.4 0.6 copy-start.8
  75.2 19.7 %copy-start.21 = (s32[4]{0:T(128)S(1)}, s32[4]{0:T(128)}, u32[]{:S(2)}) copy-start(s32[4]{0:T(128)} %constant.142.clone) | copy-start | bytes 52
  75.2 40.0 %all-to-all-start.1 = ((bf16[32,16,1152]{2,1,0:T(8,128)(2,1)}), bf16[32,16,1152]{2,1,0:T(8,128)(2,1)S(1)}, u32[]{:S(2)}, u32[]{:S(2)}) async-start(bf16[32,16,1152]{2,1,0:T(8,128)(2,1)} %copy-done.6), calls=%async_computation.1 | async-start | bytes 2359296 | tf_op jit(solution)/shard_map/all_to_all | solution.py:400
  84.7 9.2 %collective-permute-start.14 = (bf16[1024,128]{1,0:T(8,128)(2,1)S(1)}, bf16[1024,128]{1,0:T(8,128)(2,1)S(1)}, u32[]{:S(2)}, u32[]{:S(2)}) collective-permute-start(bf16[1024,128]{1,0:T(8,128)(2,1)S(1)} %get-tuple-element.61), channel_id=1, source_target_pairs={{0,2},{1,3},{2,4},{3,5},{4,6},{5,7},{6,0},{7,1},{8,10},{9,11},{10,... | collective-permute-start | bytes 786440 | tf_op jit(solution)/shard_map/ppermute | solution.py:47
  86.1 8.1 %collective-permute-start.15 = (bf16[1024,128]{1,0:T(8,128)(2,1)S(1)}, bf16[1024,128]{1,0:T(8,128)(2,1)S(1)}, u32[]{:S(2)}, u32[]{:S(2)}) collective-permute-start(bf16[1024,128]{1,0:T(8,128)(2,1)S(1)} %get-tuple-element.62), channel_id=1, source_target_pairs={{0,6},{1,7},{2,0},{3,1},{4,2},{5,3},{6,4},{7,5},{8,14},{9,15},{10,... | collective-permute-start | bytes 786440 | tf_op jit(solution)/shard_map/ppermute | solution.py:47
  88.0 16.7 %collective-permute-start.17 = (bf16[512,128]{1,0:T(8,128)(2,1)}, bf16[512,128]{1,0:T(8,128)(2,1)S(1)}, u32[]{:S(2)}, u32[]{:S(2)}) collective-permute-start(bf16[512,128]{1,0:T(8,128)(2,1)} %bitcast.34), channel_id=1, source_target_pairs={{0,1},{1,0},{2,3},{3,2},{4,5},{5,4},{6,7},{7,6},{8,9},{9,8},{10,11... | collective-permute-start | bytes 393224 | tf_op jit(solution)/shard_map/ppermute | solution.py:47
  88.0 16.7 %collective-permute-start.18 = (bf16[512,128]{1,0:T(8,128)(2,1)S(1)}, bf16[512,128]{1,0:T(8,128)(2,1)S(1)}, u32[]{:S(2)}, u32[]{:S(2)}) collective-permute-start(bf16[512,128]{1,0:T(8,128)(2,1)S(1)} %bitcast.33), channel_id=1, source_target_pairs={{0,3},{1,2},{2,5},{3,4},{4,7},{5,6},{6,1},{7,0},{8,11},{9,10},{10,... | collective-permute-start | bytes 393224 | tf_op jit(solution)/shard_map/ppermute | solution.py:47
  88.2 16.4 %collective-permute-start.19 = (bf16[512,128]{1,0:T(8,128)(2,1)S(1)}, bf16[512,128]{1,0:T(8,128)(2,1)S(1)}, u32[]{:S(2)}, u32[]{:S(2)}) collective-permute-start(bf16[512,128]{1,0:T(8,128)(2,1)S(1)} %bitcast.32), channel_id=1, source_target_pairs={{0,7},{1,6},{2,1},{3,0},{4,3},{5,2},{6,5},{7,4},{8,15},{9,14},{10,... | collective-permute-start | bytes 393224 | tf_op jit(solution)/shard_map/ppermute | solution.py:47
  94.2 10.5 %collective-permute-start.16 = (bf16[512,128]{1,0:T(8,128)(2,1)S(1)}, bf16[512,128]{1,0:T(8,128)(2,1)S(1)}, u32[]{:S(2)}, u32[]{:S(2)}) collective-permute-start(bf16[512,128]{1,0:T(8,128)(2,1)S(1)} %slice.26), channel_id=1, source_target_pairs={{0,2},{1,3},{2,4},{3,5},{4,6},{5,7},{6,0},{7,1},{8,10},{9,11},{10,... | collective-permute-start | bytes 393224 | tf_op jit(solution)/shard_map/ppermute | solution.py:47
  94.9 9.8 %collective-permute-start.20 = (bf16[512,128]{1,0:T(8,128)(2,1)S(1)}, bf16[512,128]{1,0:T(8,128)(2,1)S(1)}, u32[]{:S(2)}, u32[]{:S(2)}) collective-permute-start(bf16[512,128]{1,0:T(8,128)(2,1)S(1)} %slice.27), channel_id=1, source_target_pairs={{0,7},{1,6},{2,1},{3,0},{4,3},{5,2},{6,5},{7,4},{8,15},{9,14},{10,... | collective-permute-start | bytes 393224 | tf_op jit(solution)/shard_map/ppermute | solution.py:47
  94.9 1.2 %copy-start.3 = (bf16[4096,128]{1,0:T(8,128)(2,1)S(1)}, bf16[4096,128]{1,0:T(8,128)(2,1)}, u32[]{:S(2)}) copy-start(bf16[4096,128]{1,0:T(8,128)(2,1)} %copy-done.2) | copy-start | bytes 3145732
  96.1 1.2 %copy-start.5 = (bf16[4096,128]{1,0:T(8,128)(2,1)S(1)}, bf16[4096,128]{1,0:T(8,128)(2,1)}, u32[]{:S(2)}) copy-start(bf16[4096,128]{1,0:T(8,128)(2,1)} %copy-done.4) | copy-start | bytes 3145732
  97.4 0.9 copy-start.9
  98.3 0.9 copy-start.11
  99.2 5.5 %copy-start.7 = (bf16[2,256,128]{2,1,0:T(8,128)(2,1)S(1)}, bf16[2,256,128]{2,1,0:T(8,128)(2,1)}, u32[]{:S(2)}) copy-start(bf16[2,256,128]{2,1,0:T(8,128)(2,1)} %get-tuple-element.71) | copy-start | bytes 393220

commit v9 on v8

--- a/solution.py
+++ b/solution.py
@@ -226,10 +226,10 @@
         source = (cots, others)[(i // count + (i % count == count - 1)) % 2]
         piece = source[i % count * rows : (i % count + 1) * rows]
         weighted[:, i * columns : (i + 1) * columns] = (piece.astype(F32) * coef).astype(BF)
-    for r, part in enumerate(slabs):
+    for r, pair in enumerate(zip(slabs[::2], slabs[1::2], strict=True)):
         start = pl.multiple_of(quarters[r] * tile, tile)
         out_ref[:, pl.ds(start, tile)] = quarter(
-            weighted, (part,), low_ref, gathered_ref, slots, start, tile
+            weighted, pair, low_ref, gathered_ref, slots, start, tile
         )
 
 
@@ -340,8 +340,8 @@
     unit = 2 * tile
     hop_next, hop_prev = lax.optimization_barrier((before[unit : 3 * unit], after[2 * unit :]))
     hop_next, hop_prev = tensor_send(hop_next, 1, 0), tensor_send(hop_prev, 3, 1)
-    slabs = assemble(
-        *[(piece, 0, unit) for piece in (mine, before, after, hop_next)],
+    same_slabs = assemble(*[(piece, 0, unit) for piece in (mine, before, after, hop_next)])
+    other_slabs = assemble(
         *[(piece, 0, unit) for piece in (partner, before_other, after_other)],
         (hop_prev, unit, 2 * unit),
     )
@@ -352,8 +352,8 @@
         (hop_next, unit, 2 * unit),
         (hop_prev, 0, unit),
     )
-    gathered, slabs, cots, weight = lax.optimization_barrier(
-        (gathered, slabs, cots, key_value_weight)
+    gathered, same_slabs, other_slabs, cots, weight = lax.optimization_barrier(
+        (gathered, same_slabs, other_slabs, cots, key_value_weight)
     )
 
     def across(chip_step, core_flip):
@@ -384,7 +384,7 @@
     )
     low = (low + tensor_send(low, 0, 1)).astype(BF)
     lows = [low] + [tensor_send(low, s, 0) for s in (1, 3, 2)]
-    slabs_left, slabs_right = x_send(slabs, 1), x_send(slabs, 3)
+    same_left, same_right = x_send(same_slabs, 1), x_send(same_slabs, 3)
 
     terms, low = call(
         terms_kernel,
@@ -394,9 +394,10 @@
         16,
     )(slots, *lows, normed_input_rows, weighted_value)
     cots_other = tensor_send(cots, 0, 1)
-    terms, slabs_left, slabs_right, cots, cots_other, late = lax.optimization_barrier(
-        (terms, slabs_left, slabs_right, cots, cots_other, late)
-    )
+    terms, same_left, same_right, other_slabs, cots, cots_other, late = lax.optimization_barrier(
+        (terms, same_left, same_right, other_slabs, cots, cots_other, late)
+    )
+    other_left, other_right = x_send(other_slabs, 1), x_send(other_slabs, 3)
     terms = lax.all_to_all(terms, "dp", 0, 0)
     routes = (1, 0), (3, 0), (1, 1), (3, 1), (0, 1)
     before, after, before_other, after_other, partner = [
@@ -413,7 +414,7 @@
         quarters,
         (cots, cots_other),
         (gathered, low, coef),
-        (slabs, slabs_left, slabs_right),
+        (same_slabs, other_slabs, same_left, other_left, same_right, other_right),
         slabs_far,
         window,
     )

time: 117 us -> 119 us (1.017)
  the two profiles are of different devices: /device:TPU:2 before, /device:TPU:1 now
where the time goes in v9:
time: 119 us
  starting transfers between devices  60.1 us (51%)
  waiting for transfers between devices  27.9 us (23%)
  Pallas kernels  15.6 us (13%)
  local copies, waits for them, and re-layouts  12.4 us (10%)
  other arithmetic  1.61 us (1%)
    ppermute x19, starting transfers between devices, tensor_send(): return lax.ppermute(value, 'tensor', pairs)  34.8 us
    ppermute x19, waiting for transfers between devices, tensor_send(): return lax.ppermute(value, 'tensor', pairs)  18.8 us
    all_to_all x1, starting transfers between devices, shards(): gathered = lax.all_to_all(packed, 'dp', 0, 0)  12 us
    unnamed x55, local copies, waits for them, and re-layouts  10.2 us
    ppermute x4, waiting for transfers between devices, x_send(): return lax.ppermute(value, 'dp', pairs)  9.09 us
    all_to_all x1, starting transfers between devices, shards(): terms = lax.all_to_all(terms, 'dp', 0, 0)  8.01 us
    ppermute x4, starting transfers between devices, x_send(): return lax.ppermute(value, 'dp', pairs)  5.36 us
    pallas_call x1, Pallas kernels, frozen_and_correction(): pl.pallas_call(near_kernel, grid_spec=pltpu.PrefetchScalarGridSpec(num_sc...  5.07 us
  transfers between devices with their start and end apart: 25, of which 8 were waited for; matrix products, arithmetic and copies ran while one was open for 4% of the time, Pallas kernels for 11%

profile of v9, /device:TPU:1, one launch (start us, length us, event | category | flops | bytes accessed | tf_op | source)
XLA Modules:
  0.0 118.6 jit_solution(13179947093851989356)
XLA Ops:
  0.6 2.0 %shard_map.139 = bf16[32,16,1280]{2,1,0:T(8,128)(2,1)} custom-call(s32[1,4]{1,0:T(1,128)} %bitcast.26, f32[1,4]{1,0:T(1,128)} %bitcast.27, bf16[16,1024]{1,0:T(8,128)(2,1)} %down_ref.1, bf16[16,128]{1,0:T(8,128)(2,1)} %up_ref.1), custom_call_target="tpu_custom_call" | custom-call | tf_op jit(solution)/shard_map/pallas_call | solution.py:319
  2.6 12.0 %all-to-all-start = ((bf16[32,16,1280]{2,1,0:T(8,128)(2,1)}), bf16[32,16,1280]{2,1,0:T(8,128)(2,1)S(1)}, u32[]{:S(2)}, u32[]{:S(2)}) async-start(bf16[32,16,1280]{2,1,0:T(8,128)(2,1)} %shard_map.139), calls=%async_computation | async-start | bytes 2621440 | tf_op jit(solution)/shard_map/all_to_all | solution.py:329
  14.7 0.7 copy.20
  15.4 0.5 multiply_add_fusion.places
  15.9 3.2 %shard_map.140 = (bf16[2048,128]{1,0:T(8,128)(2,1)}, bf16[512,128]{1,0:T(8,128)(2,1)}, bf16[2048,128]{1,0:T(8,128)(2,1)}, bf16[512,128]{1,0:T(8,128)(2,1)}, bf16...) custom-call(s32[8]{0:T(128)} %multiply_add_fusion.places, bf16[2,8192,128]{2,1,0:T(8,128)(2,1)} %refs_7_.1, ...), custom_call_target="tpu_custom_call" | custom-call | tf_op jit(solution)/shard_map/pallas_call | solution.py:140
  19.1 1.3 %collective-permute-start = (bf16[2048,128]{1,0:T(8,128)(2,1)}, bf16[2048,128]{1,0:T(8,128)(2,1)S(1)}, u32[]{:S(2)}, u32[]{:S(2)}) collective-permute-start(bf16[2048,128]{1,0:T(8,128)(2,1)} %get-tuple-element.40), channel_id=1, source_target_pairs={{0,2},{1,3},{2,4},{3,5},{4,6},{5,7},{6,0},{7,1},{8,10},{9,11},{10,... | collective-permute-start | bytes 1572872 | tf_op jit(solution)/shard_map/ppermute | solution.py:47
  20.4 1.5 %collective-permute-start.1 = (bf16[2048,128]{1,0:T(8,128)(2,1)}, bf16[2048,128]{1,0:T(8,128)(2,1)S(1)}, u32[]{:S(2)}, u32[]{:S(2)}) collective-permute-start(bf16[2048,128]{1,0:T(8,128)(2,1)} %get-tuple-element.41), channel_id=1, source_target_pairs={{0,6},{1,7},{2,0},{3,1},{4,2},{5,3},{6,4},{7,5},{8,14},{9,15},{10,... | collective-permute-start | bytes 1572872 | tf_op jit(solution)/shard_map/ppermute | solution.py:47
  21.9 11.2 %collective-permute-done.refs_1_ = bf16[2048,128]{1,0:T(8,128)(2,1)S(1)} collective-permute-done((bf16[2048,128]{1,0:T(8,128)(2,1)}, bf16[2048,128]{1,0:T(8,128)(2,1)S(1)}, u32[]{:S(2)}, u32[]{:S(2)}) %collective-permute-start) | collective-permute-done | bytes 524320 | tf_op jit(solution)/shard_map/ppermute | solution.py:47
  33.2 1.0 collective-permute-start.2
  34.2 3.7 %collective-permute-start.6 = (bf16[1024,128]{1,0:T(8,128)(2,1)S(1)}, bf16[1024,128]{1,0:T(8,128)(2,1)S(1)}, u32[]{:S(2)}, u32[]{:S(2)}) collective-permute-start(bf16[1024,128]{1,0:T(8,128)(2,1)S(1)} %slice.25), channel_id=1, source_target_pairs={{0,7},{1,6},{2,1},{3,0},{4,3},{5,2},{6,5},{7,4},{8,15},{9,14},{10,... | collective-permute-start | bytes 786440 | tf_op jit(solution)/shard_map/ppermute | solution.py:47
  37.9 0.5 collective-permute-start.4
  38.4 2.5 %collective-permute-start.5 = (bf16[512,128]{1,0:T(8,128)(2,1)}, bf16[512,128]{1,0:T(8,128)(2,1)S(1)}, u32[]{:S(2)}, u32[]{:S(2)}) collective-permute-start(bf16[512,128]{1,0:T(8,128)(2,1)} %get-tuple-element.45), channel_id=1, source_target_pairs={{0,7},{1,6},{2,1},{3,0},{4,3},{5,2},{6,5},{7,4},{8,15},{9,14},{10,... | collective-permute-start | bytes 393224 | tf_op jit(solution)/shard_map/ppermute | solution.py:47
  40.9 0.0 collective-permute-done.2.refs_3_
  40.9 0.9 copy-done.15
  41.9 2.7 %collective-permute-done.6.refs_3_.refs_4_ = bf16[1024,128]{1,0:T(8,128)(2,1)S(1)} collective-permute-done((bf16[1024,128]{1,0:T(8,128)(2,1)S(1)}, bf16[1024,128]{1,0:T(8,128)(2,1)S(1)}, u32[]{:S(2)}, u32[]{:S(2)}) %collective-permute-start.6) | collective-permute-done | bytes 262176 | tf_op jit(solution)/shard_map/ppermute | solution.py:47
  44.5 0.0 copy-start.17
  44.6 0.0 copy-start.18
  44.6 0.1 shard_map.143.cots
  44.7 0.0 copy-start.2
  44.7 1.0 copy-done.2
  45.6 0.0 collective-permute-done.3.refs_0_
  45.6 0.0 collective-permute-done.4.refs_1_
  45.6 1.7 %collective-permute-done.5.refs_2_ = bf16[512,128]{1,0:T(8,128)(2,1)S(1)} collective-permute-done((bf16[512,128]{1,0:T(8,128)(2,1)}, bf16[512,128]{1,0:T(8,128)(2,1)S(1)}, u32[]{:S(2)}, u32[]{:S(2)}) %collective-permute-start.5) | collective-permute-done | bytes 131104 | tf_op jit(solution)/shard_map/ppermute | solution.py:47
  47.4 0.8 copy-done.4
  48.2 1.0 collective-permute-start.13
  49.2 0.2 select_reduce_fusion.slots
  49.4 1.2 %shard_map.144 = (f32[512,128]{1,0:T(8,128)S(1)}, bf16[512,128]{1,0:T(8,128)(2,1)S(1)}, f32[512,1]{1,0:T(8,128)S(1)}) custom-call(s32[4]{0:T(128)S(1)} %select_reduce_fusion.slots, s32[4]{0:T(128)S(1)} %copy-done.18, s32[4]{0:T(128)S(1)} %copy-done.16, f32[4]{0:T(128)S(1)} %copy-done.17, bf16[32,16,1280]{2,1,0:T(8,128)(2,1)S(1)} %all-to-all-done.gathered_ref, ...), custom_call_target="tpu_custom_call" | custom-call | flops 67108864 | bytes 1048576 | tf_op jit(solution)/shard_map/pallas_call | solution.py:370
  50.6 0.7 copy-done.13
  51.3 0.0 collective-permute-start.7
  51.4 2.8 %collective-permute-start.12 = (bf16[2048,128]{1,0:T(8,128)(2,1)S(1)}, bf16[2048,128]{1,0:T(8,128)(2,1)}, u32[]{:S(2)}, u32[]{:S(2)}) collective-permute-start(bf16[2048,128]{1,0:T(8,128)(2,1)S(1)} %shard_map.141.refs_0_), channel_id=1, source_target_pairs={{0,24},{8,0},{16,8},{24,16},{32,56},{40,32},{48,40},{56,48},{64,88... | collective-permute-start | bytes 1572872 | tf_op jit(solution)/shard_map/ppermute | solution.py:52
  54.2 0.0 collective-permute-start.11
  54.2 3.0 %collective-permute-start.10 = (bf16[512,128]{1,0:T(8,128)(2,1)S(1)}, bf16[512,128]{1,0:T(8,128)(2,1)S(1)}, u32[]{:S(2)}, u32[]{:S(2)}) collective-permute-start(bf16[512,128]{1,0:T(8,128)(2,1)S(1)} %add_convert_fusion.own), channel_id=1, source_target_pairs={{0,4},{1,5},{2,6},{3,7},{4,0},{5,1},{6,2},{7,3},{8,12},{9,13},{10,... | collective-permute-start | bytes 393224 | tf_op jit(solution)/shard_map/ppermute | solution.py:47
  57.2 0.8 collective-permute-start.9
  58.0 2.1 %collective-permute-done.10.third = bf16[512,128]{1,0:T(8,128)(2,1)S(1)} collective-permute-done((bf16[512,128]{1,0:T(8,128)(2,1)S(1)}, bf16[512,128]{1,0:T(8,128)(2,1)S(1)}, u32[]{:S(2)}, u32[]{:S(2)}) %collective-permute-start.10) | collective-permute-done | bytes 131104 | tf_op jit(solution)/shard_map/ppermute | solution.py:47
  60.1 1.4 %collective-permute-start.8 = (bf16[512,128]{1,0:T(8,128)(2,1)S(1)}, bf16[512,128]{1,0:T(8,128)(2,1)S(1)}, u32[]{:S(2)}, u32[]{:S(2)}) collective-permute-start(bf16[512,128]{1,0:T(8,128)(2,1)S(1)} %add_convert_fusion.own), channel_id=1, source_target_pairs={{0,2},{1,3},{2,4},{3,5},{4,6},{5,7},{6,0},{7,1},{8,10},{9,11},{10,... | collective-permute-start | bytes 393224 | tf_op jit(solution)/shard_map/ppermute | solution.py:47
  61.5 2.1 %constant_dynamic-slice_fusion = (bf16[2,256,128]{2,1,0:T(8,128)(2,1)}, bf16[2,256,128]{2,1,0:T(8,128)(2,1)}, bf16[2,256,128]{2,1,0:T(8,128)(2,1)}, bf16[2,256,1...) fusion(bf16[2,8192,128]{2,1,0:T(8,128)(2,1)} %refs_7_.1, ...), kind=kLoop, calls=%fused_computation.10 | loop fusion | bytes 2097184 | tf_op jit(solution)/shard_map/dynamic_slice | solution.py:362
  63.6 0.9 pad_maximum_fusion
  64.5 0.0 collective-permute-done.9.second
  64.5 1.1 collective-permute-done.8.first
  65.6 1.1 shard_map.145
  66.7 0.6 copy-done.11
  67.4 0.0 collective-permute-done.12.refs_4_
  67.4 0.8 collective-permute-done.11.refs_2_
  68.2 0.2 copy-done.9
  68.4 8.0 %all-to-all-start.1 = ((bf16[32,16,1152]{2,1,0:T(8,128)(2,1)}), bf16[32,16,1152]{2,1,0:T(8,128)(2,1)S(1)}, u32[]{:S(2)}, u32[]{:S(2)}) async-start(bf16[32,16,1152]{2,1,0:T(8,128)(2,1)} %copy-done.9), calls=%async_computation.1 | async-start | bytes 2359296 | tf_op jit(solution)/shard_map/all_to_all | solution.py:401
  76.4 2.5 %collective-permute-start.15 = (bf16[2048,128]{1,0:T(8,128)(2,1)S(1)}, bf16[2048,128]{1,0:T(8,128)(2,1)S(1)}, u32[]{:S(2)}, u32[]{:S(2)}) collective-permute-start(bf16[2048,128]{1,0:T(8,128)(2,1)S(1)} %copy-done.5), channel_id=1, source_target_pairs={{0,24},{8,0},{16,8},{24,16},{32,56},{40,32},{48,40},{56,48},{64,88... | collective-permute-start | bytes 1572872 | tf_op jit(solution)/shard_map/ppermute | solution.py:52
  79.0 0.4 collective-permute-start.16
  79.4 2.3 %collective-permute-start.17 = (bf16[1024,128]{1,0:T(8,128)(2,1)S(1)}, bf16[1024,128]{1,0:T(8,128)(2,1)S(1)}, u32[]{:S(2)}, u32[]{:S(2)}) collective-permute-start(bf16[1024,128]{1,0:T(8,128)(2,1)S(1)} %copy-done.20), channel_id=1, source_target_pairs={{0,6},{1,7},{2,0},{3,1},{4,2},{5,3},{6,4},{7,5},{8,14},{9,15},{10,... | collective-permute-start | bytes 786440 | tf_op jit(solution)/shard_map/ppermute | solution.py:47
  81.6 4.5 %collective-permute-start.19 = (bf16[512,128]{1,0:T(8,128)(2,1)}, bf16[512,128]{1,0:T(8,128)(2,1)S(1)}, u32[]{:S(2)}, u32[]{:S(2)}) collective-permute-start(bf16[512,128]{1,0:T(8,128)(2,1)} %bitcast.34), channel_id=1, source_target_pairs={{0,1},{1,0},{2,3},{3,2},{4,5},{5,4},{6,7},{7,6},{8,9},{9,8},{10,11... | collective-permute-start | bytes 393224 | tf_op jit(solution)/shard_map/ppermute | solution.py:47
  86.1 4.2 %collective-permute-start.20 = (bf16[512,128]{1,0:T(8,128)(2,1)}, bf16[512,128]{1,0:T(8,128)(2,1)S(1)}, u32[]{:S(2)}, u32[]{:S(2)}) collective-permute-start(bf16[512,128]{1,0:T(8,128)(2,1)} %bitcast.33), channel_id=1, source_target_pairs={{0,3},{1,2},{2,5},{3,4},{4,7},{5,6},{6,1},{7,0},{8,11},{9,10},{10,... | collective-permute-start | bytes 393224 | tf_op jit(solution)/shard_map/ppermute | solution.py:47
  90.3 3.0 %collective-permute-start.21 = (bf16[512,128]{1,0:T(8,128)(2,1)}, bf16[512,128]{1,0:T(8,128)(2,1)S(1)}, u32[]{:S(2)}, u32[]{:S(2)}) collective-permute-start(bf16[512,128]{1,0:T(8,128)(2,1)} %bitcast.32), channel_id=1, source_target_pairs={{0,7},{1,6},{2,1},{3,0},{4,3},{5,2},{6,5},{7,4},{8,15},{9,14},{10,... | collective-permute-start | bytes 393224 | tf_op jit(solution)/shard_map/ppermute | solution.py:47
  93.3 5.6 %collective-permute-done.15.refs_5_ = bf16[2048,128]{1,0:T(8,128)(2,1)S(1)} collective-permute-done((bf16[2048,128]{1,0:T(8,128)(2,1)S(1)}, bf16[2048,128]{1,0:T(8,128)(2,1)S(1)}, u32[]{:S(2)}, u32[]{:S(2)}) %collective-permute-start.15) | collective-permute-done | bytes 524320 | tf_op jit(solution)/shard_map/ppermute | solution.py:52
  98.9 0.3 collective-permute-start.18
  99.2 2.7 %collective-permute-done.14.refs_3_ = bf16[2048,128]{1,0:T(8,128)(2,1)S(1)} collective-permute-done((bf16[2048,128]{1,0:T(8,128)(2,1)S(1)}, bf16[2048,128]{1,0:T(8,128)(2,1)S(1)}, u32[]{:S(2)}, u32[]{:S(2)}) %collective-permute-start.14) | collective-permute-done | bytes 524320 | tf_op jit(solution)/shard_map/ppermute | solution.py:52
  101.9 3.5 %collective-permute-start.22 = (bf16[512,128]{1,0:T(8,128)(2,1)S(1)}, bf16[512,128]{1,0:T(8,128)(2,1)S(1)}, u32[]{:S(2)}, u32[]{:S(2)}) collective-permute-start(bf16[512,128]{1,0:T(8,128)(2,1)S(1)} %slice.27), channel_id=1, source_target_pairs={{0,7},{1,6},{2,1},{3,0},{4,3},{5,2},{6,5},{7,4},{8,15},{9,14},{10,... | collective-permute-start | bytes 393224 | tf_op jit(solution)/shard_map/ppermute | solution.py:47
  105.4 0.0 copy-start.3
  105.5 1.2 %copy-done.3 = bf16[4096,128]{1,0:T(8,128)(2,1)S(1)} copy-done((bf16[4096,128]{1,0:T(8,128)(2,1)S(1)}, bf16[4096,128]{1,0:T(8,128)(2,1)}, u32[]{:S(2)}) %copy-start.3) | copy-done | bytes 1048600
  106.7 1.0 copy-done.6
  107.7 1.0 copy-done.8
  108.8 0.9 copy-done.12
  109.7 0.9 copy-done.14
  110.6 5.1 %shard_map.146 = (bf16[512,1024]{1,0:T(8,128)(2,1)}, bf16[512,2048]{1,0:T(8,128)(2,1)S(1)}) custom-call(s32[4]{0:T(128)S(1)} %select_reduce_fusion.slots, s32[4]{0:T(128)S(1)} %and_select_fusion.2.quarters, bf16[4096,128]{1,0:T(8,128)(2,1)S(1)} %copy-done.3, bf16[4096,128]{1,0:T(8,128)(2,1)} %collective-permute-done.13.others, ...), custom_call_target="tpu_custom_call" | custom-call | tf_op jit(solution)/shard_map/pallas_call | solution.py:250
  115.7 2.1 %shard_map.147 = bf16[512,1024]{1,0:T(8,128)(2,1)} custom-call(s32[4]{0:T(128)S(1)} %select_reduce_fusion.slots, s32[4]{0:T(128)S(1)} %and_select_fusion.2.quarters, bf16[512,1024]{1,0:T(8,128)(2,1)} %get-tuple-element.62.near_ref, bf16[512,2048]{1,0:T(8,128)(2,1)S(1)} %get-tuple-element.63.weighted, ...), custom_call_target="tpu_custom_call", output_to_operand_aliasing={{}: (2, {})} | custom-call | tf_op jit(solution)/shard_map/pallas_call | solution.py:262
  117.8 0.8 shard_map.148
  (61 shorter events, 0.3 us)
Async XLA Ops:
  2.6 12.0 %copy-start.19 = (bf16[512,2,128]{2,1,0:T(2,128)(2,1)S(1)}, bf16[512,2,128]{2,1,0:T(2,128)(2,1)}, u32[]{:S(2)}) copy-start(bf16[512,2,128]{2,1,0:T(2,128)(2,1)} %param.13) | copy-start | bytes 786436
  2.6 12.8 %copy-start.22 = (s32[8,1]{0,1:T(1,128)S(1)}, s32[8,1]{0,1:T(1,128)}, u32[]{:S(2)}) copy-start(s32[8,1]{0,1:T(1,128)} %constant.150) | copy-start | bytes 100
  2.6 12.8 %copy-start.23 = (s32[8,1]{0,1:T(1,128)S(1)}, s32[8,1]{0,1:T(1,128)}, u32[]{:S(2)}) copy-start(s32[8,1]{0,1:T(1,128)} %constant.149) | copy-start | bytes 100
  2.6 45.6 %all-to-all-start = ((bf16[32,16,1280]{2,1,0:T(8,128)(2,1)}), bf16[32,16,1280]{2,1,0:T(8,128)(2,1)S(1)}, u32[]{:S(2)}, u32[]{:S(2)}) async-start(bf16[32,16,1280]{2,1,0:T(8,128)(2,1)} %shard_map.139), calls=%async_computation | async-start | bytes 2621440 | tf_op jit(solution)/shard_map/all_to_all | solution.py:329
  19.1 14.0 %collective-permute-start = (bf16[2048,128]{1,0:T(8,128)(2,1)}, bf16[2048,128]{1,0:T(8,128)(2,1)S(1)}, u32[]{:S(2)}, u32[]{:S(2)}) collective-permute-start(bf16[2048,128]{1,0:T(8,128)(2,1)} %get-tuple-element.40), channel_id=1, source_target_pairs={{0,2},{1,3},{2,4},{3,5},{4,6},{5,7},{6,0},{7,1},{8,10},{9,11},{10,... | collective-permute-start | bytes 1572872 | tf_op jit(solution)/shard_map/ppermute | solution.py:47
  20.4 12.8 %collective-permute-start.1 = (bf16[2048,128]{1,0:T(8,128)(2,1)}, bf16[2048,128]{1,0:T(8,128)(2,1)S(1)}, u32[]{:S(2)}, u32[]{:S(2)}) collective-permute-start(bf16[2048,128]{1,0:T(8,128)(2,1)} %get-tuple-element.41), channel_id=1, source_target_pairs={{0,6},{1,7},{2,0},{3,1},{4,2},{5,3},{6,4},{7,5},{8,14},{9,15},{10,... | collective-permute-start | bytes 1572872 | tf_op jit(solution)/shard_map/ppermute | solution.py:47
  33.2 11.4 %copy-start = (bf16[512,2,128]{2,0,1:T(8,128)(2,1)S(1)}, bf16[512,2,128]{2,0,1:T(8,128)(2,1)}, u32[]{:S(2)}) copy-start(bf16[512,2,128]{2,0,1:T(8,128)(2,1)} %copy.20) | copy-start | bytes 786436
  33.2 7.7 %collective-permute-start.2 = (bf16[1024,128]{1,0:T(8,128)(2,1)S(1)}, bf16[1024,128]{1,0:T(8,128)(2,1)S(1)}, u32[]{:S(2)}, u32[]{:S(2)}) collective-permute-start(bf16[1024,128]{1,0:T(8,128)(2,1)S(1)} %slice.24), channel_id=1, source_target_pairs={{0,2},{1,3},{2,4},{3,5},{4,6},{5,7},{6,0},{7,1},{8,10},{9,11},{10,... | collective-permute-start | bytes 786440 | tf_op jit(solution)/shard_map/ppermute | solution.py:47
  34.2 10.3 %collective-permute-start.6 = (bf16[1024,128]{1,0:T(8,128)(2,1)S(1)}, bf16[1024,128]{1,0:T(8,128)(2,1)S(1)}, u32[]{:S(2)}, u32[]{:S(2)}) collective-permute-start(bf16[1024,128]{1,0:T(8,128)(2,1)S(1)} %slice.25), channel_id=1, source_target_pairs={{0,7},{1,6},{2,1},{3,0},{4,3},{5,2},{6,5},{7,4},{8,15},{9,14},{10,... | collective-permute-start | bytes 786440 | tf_op jit(solution)/shard_map/ppermute | solution.py:47
  37.9 7.7 %collective-permute-start.3 = (bf16[512,128]{1,0:T(8,128)(2,1)}, bf16[512,128]{1,0:T(8,128)(2,1)S(1)}, u32[]{:S(2)}, u32[]{:S(2)}) collective-permute-start(bf16[512,128]{1,0:T(8,128)(2,1)} %get-tuple-element.43), channel_id=1, source_target_pairs={{0,1},{1,0},{2,3},{3,2},{4,5},{5,4},{6,7},{7,6},{8,9},{9,8},{10,11... | collective-permute-start | bytes 393224 | tf_op jit(solution)/shard_map/ppermute | solution.py:47
  37.9 7.7 %collective-permute-start.4 = (bf16[512,128]{1,0:T(8,128)(2,1)}, bf16[512,128]{1,0:T(8,128)(2,1)S(1)}, u32[]{:S(2)}, u32[]{:S(2)}) collective-permute-start(bf16[512,128]{1,0:T(8,128)(2,1)} %get-tuple-element.44), channel_id=1, source_target_pairs={{0,3},{1,2},{2,5},{3,4},{4,7},{5,6},{6,1},{7,0},{8,11},{9,10},{10,... | collective-permute-start | bytes 393224 | tf_op jit(solution)/shard_map/ppermute | solution.py:47
  38.4 8.9 %collective-permute-start.5 = (bf16[512,128]{1,0:T(8,128)(2,1)}, bf16[512,128]{1,0:T(8,128)(2,1)S(1)}, u32[]{:S(2)}, u32[]{:S(2)}) collective-permute-start(bf16[512,128]{1,0:T(8,128)(2,1)} %get-tuple-element.45), channel_id=1, source_target_pairs={{0,7},{1,6},{2,1},{3,0},{4,3},{5,2},{6,5},{7,4},{8,15},{9,14},{10,... | collective-permute-start | bytes 393224 | tf_op jit(solution)/shard_map/ppermute | solution.py:47
  40.9 0.9 copy-start.15
  41.9 12.3 %copy-start.7 = (bf16[2048,128]{1,0:T(8,128)(2,1)}, bf16[2048,128]{1,0:T(8,128)(2,1)S(1)}, u32[]{:S(2)}) copy-start(bf16[2048,128]{1,0:T(8,128)(2,1)S(1)} %shard_map.141.refs_0_) | copy-start | bytes 1572868
  44.5 4.6 %copy-start.24 = (s32[8]{0:T(128)S(1)}, s32[8]{0:T(128)}, u32[]{:S(2)}) copy-start(s32[8]{0:T(128)} %param.17) | copy-start | bytes 100
  44.5 4.6 %copy-start.25 = (s32[4]{0:T(128)S(1)}, s32[4]{0:T(128)}, u32[]{:S(2)}) copy-start(s32[4]{0:T(128)} %param.18) | copy-start | bytes 52
  44.5 4.8 %copy-start.16 = (s32[4]{0:T(128)S(1)}, s32[4]{0:T(128)}, u32[]{:S(2)}) copy-start(s32[4]{0:T(128)} %prompt.1) | copy-start | bytes 52
  44.5 4.8 %copy-start.17 = (f32[4]{0:T(128)S(1)}, f32[4]{0:T(128)}, u32[]{:S(2)}) copy-start(f32[4]{0:T(128)} %reward.1) | copy-start | bytes 52
  44.6 4.8 %copy-start.18 = (s32[4]{0:T(128)S(1)}, s32[4]{0:T(128)}, u32[]{:S(2)}) copy-start(s32[4]{0:T(128)} %live.1) | copy-start | bytes 52
  44.7 1.0 copy-start.2
  45.6 3.8 %copy-start.1 = (bf16[512,1024]{1,0:T(8,128)(2,1)S(1)}, bf16[512,1024]{1,0:T(8,128)(2,1)}, u32[]{:S(2)}) copy-start(bf16[512,1024]{1,0:T(8,128)(2,1)} %x_ref.3) | copy-start | bytes 3145732
  47.4 0.8 copy-start.4
  48.2 20.0 %collective-permute-start.13 = (bf16[4096,128]{1,0:T(8,128)(2,1)}, bf16[4096,128]{1,0:T(8,128)(2,1)}, u32[]{:S(2)}, u32[]{:S(2)}) collective-permute-start(bf16[4096,128]{1,0:T(8,128)(2,1)} %copy-done.2), channel_id=1, source_target_pairs={{0,1},{1,0},{2,3},{3,2},{4,5},{5,4},{6,7},{7,6},{8,9},{9,8},{10,11... | collective-permute-start | bytes 3145736 | tf_op jit(solution)/shard_map/ppermute | solution.py:47
  50.6 0.7 copy-start.13
  51.3 2.8 %collective-permute-start.7 = (f32[512,128]{1,0:T(8,128)S(1)}, f32[512,128]{1,0:T(8,128)S(1)}, u32[]{:S(2)}, u32[]{:S(2)}) collective-permute-start(f32[512,128]{1,0:T(8,128)S(1)} %get-tuple-element.48), channel_id=1, source_target_pairs={{0,1},{1,0},{2,3},{3,2},{4,5},{5,4},{6,7},{7,6},{8,9},{9,8},{10,11... | collective-permute-start | bytes 786440 | tf_op jit(solution)/shard_map/ppermute | solution.py:47
  51.4 16.0 %collective-permute-start.12 = (bf16[2048,128]{1,0:T(8,128)(2,1)S(1)}, bf16[2048,128]{1,0:T(8,128)(2,1)}, u32[]{:S(2)}, u32[]{:S(2)}) collective-permute-start(bf16[2048,128]{1,0:T(8,128)(2,1)S(1)} %shard_map.141.refs_0_), channel_id=1, source_target_pairs={{0,24},{8,0},{16,8},{24,16},{32,56},{40,32},{48,40},{56,48},{64,88... | collective-permute-start | bytes 1572872 | tf_op jit(solution)/shard_map/ppermute | solution.py:52
  54.2 14.0 %collective-permute-start.11 = (bf16[2048,128]{1,0:T(8,128)(2,1)S(1)}, bf16[2048,128]{1,0:T(8,128)(2,1)}, u32[]{:S(2)}, u32[]{:S(2)}) collective-permute-start(bf16[2048,128]{1,0:T(8,128)(2,1)S(1)} %shard_map.141.refs_0_), channel_id=1, source_target_pairs={{0,8},{8,16},{16,24},{24,0},{32,40},{40,48},{48,56},{56,32},{64,72... | collective-permute-start | bytes 1572872 | tf_op jit(solution)/shard_map/ppermute | solution.py:52
  54.2 5.8 %collective-permute-start.10 = (bf16[512,128]{1,0:T(8,128)(2,1)S(1)}, bf16[512,128]{1,0:T(8,128)(2,1)S(1)}, u32[]{:S(2)}, u32[]{:S(2)}) collective-permute-start(bf16[512,128]{1,0:T(8,128)(2,1)S(1)} %add_convert_fusion.own), channel_id=1, source_target_pairs={{0,4},{1,5},{2,6},{3,7},{4,0},{5,1},{6,2},{7,3},{8,12},{9,13},{10,... | collective-permute-start | bytes 393224 | tf_op jit(solution)/shard_map/ppermute | solution.py:47
  57.2 7.2 %collective-permute-start.9 = (bf16[512,128]{1,0:T(8,128)(2,1)S(1)}, bf16[512,128]{1,0:T(8,128)(2,1)S(1)}, u32[]{:S(2)}, u32[]{:S(2)}) collective-permute-start(bf16[512,128]{1,0:T(8,128)(2,1)S(1)} %add_convert_fusion.own), channel_id=1, source_target_pairs={{0,6},{1,7},{2,0},{3,1},{4,2},{5,3},{6,4},{7,5},{8,14},{9,15},{10,... | collective-permute-start | bytes 393224 | tf_op jit(solution)/shard_map/ppermute | solution.py:47
  60.1 5.5 %collective-permute-start.8 = (bf16[512,128]{1,0:T(8,128)(2,1)S(1)}, bf16[512,128]{1,0:T(8,128)(2,1)S(1)}, u32[]{:S(2)}, u32[]{:S(2)}) collective-permute-start(bf16[512,128]{1,0:T(8,128)(2,1)S(1)} %add_convert_fusion.own), channel_id=1, source_target_pairs={{0,2},{1,3},{2,4},{3,5},{4,6},{5,7},{6,0},{7,1},{8,10},{9,11},{10,... | collective-permute-start | bytes 393224 | tf_op jit(solution)/shard_map/ppermute | solution.py:47
  66.7 0.7 copy-start.11
  67.3 1.1 copy-start.9
  67.3 9.1 %copy-start.5 = (bf16[2048,128]{1,0:T(8,128)(2,1)S(1)}, bf16[2048,128]{1,0:T(8,128)(2,1)}, u32[]{:S(2)}) copy-start(bf16[2048,128]{1,0:T(8,128)(2,1)} %copy-done.4) | copy-start | bytes 1572868
  67.3 11.6 %copy-start.21 = (bf16[1024,128]{1,0:T(8,128)(2,1)S(1)}, bf16[1024,128]{1,0:T(8,128)(2,1)}, u32[]{:S(2)}) copy-start(bf16[1024,128]{1,0:T(8,128)(2,1)} %get-tuple-element.65) | copy-start | bytes 786436
  67.4 12.0 %copy-start.20 = (bf16[1024,128]{1,0:T(8,128)(2,1)S(1)}, bf16[1024,128]{1,0:T(8,128)(2,1)}, u32[]{:S(2)}) copy-start(bf16[1024,128]{1,0:T(8,128)(2,1)} %get-tuple-element.66) | copy-start | bytes 786436
  68.4 37.0 %copy-start.26 = (s32[4]{0:T(128)S(1)}, s32[4]{0:T(128)}, u32[]{:S(2)}) copy-start(s32[4]{0:T(128)} %constant.142.clone) | copy-start | bytes 52
  68.4 49.4 %all-to-all-start.1 = ((bf16[32,16,1152]{2,1,0:T(8,128)(2,1)}), bf16[32,16,1152]{2,1,0:T(8,128)(2,1)S(1)}, u32[]{:S(2)}, u32[]{:S(2)}) async-start(bf16[32,16,1152]{2,1,0:T(8,128)(2,1)} %copy-done.9), calls=%async_computation.1 | async-start | bytes 2359296 | tf_op jit(solution)/shard_map/all_to_all | solution.py:401
  76.4 22.4 %collective-permute-start.15 = (bf16[2048,128]{1,0:T(8,128)(2,1)S(1)}, bf16[2048,128]{1,0:T(8,128)(2,1)S(1)}, u32[]{:S(2)}, u32[]{:S(2)}) collective-permute-start(bf16[2048,128]{1,0:T(8,128)(2,1)S(1)} %copy-done.5), channel_id=1, source_target_pairs={{0,24},{8,0},{16,8},{24,16},{32,56},{40,32},{48,40},{56,48},{64,88... | collective-permute-start | bytes 1572872 | tf_op jit(solution)/shard_map/ppermute | solution.py:52
  79.0 23.0 %collective-permute-start.14 = (bf16[2048,128]{1,0:T(8,128)(2,1)S(1)}, bf16[2048,128]{1,0:T(8,128)(2,1)S(1)}, u32[]{:S(2)}, u32[]{:S(2)}) collective-permute-start(bf16[2048,128]{1,0:T(8,128)(2,1)S(1)} %copy-done.5), channel_id=1, source_target_pairs={{0,8},{8,16},{16,24},{24,0},{32,40},{40,48},{48,56},{56,32},{64,72... | collective-permute-start | bytes 1572872 | tf_op jit(solution)/shard_map/ppermute | solution.py:52
  79.0 7.2 %collective-permute-start.16 = (bf16[1024,128]{1,0:T(8,128)(2,1)S(1)}, bf16[1024,128]{1,0:T(8,128)(2,1)S(1)}, u32[]{:S(2)}, u32[]{:S(2)}) collective-permute-start(bf16[1024,128]{1,0:T(8,128)(2,1)S(1)} %copy-done.21), channel_id=1, source_target_pairs={{0,2},{1,3},{2,4},{3,5},{4,6},{5,7},{6,0},{7,1},{8,10},{9,11},{10,... | collective-permute-start | bytes 786440 | tf_op jit(solution)/shard_map/ppermute | solution.py:47
  79.4 11.0 %collective-permute-start.17 = (bf16[1024,128]{1,0:T(8,128)(2,1)S(1)}, bf16[1024,128]{1,0:T(8,128)(2,1)S(1)}, u32[]{:S(2)}, u32[]{:S(2)}) collective-permute-start(bf16[1024,128]{1,0:T(8,128)(2,1)S(1)} %copy-done.20), channel_id=1, source_target_pairs={{0,6},{1,7},{2,0},{3,1},{4,2},{5,3},{6,4},{7,5},{8,14},{9,15},{10,... | collective-permute-start | bytes 786440 | tf_op jit(solution)/shard_map/ppermute | solution.py:47
  81.6 34.0 %collective-permute-start.19 = (bf16[512,128]{1,0:T(8,128)(2,1)}, bf16[512,128]{1,0:T(8,128)(2,1)S(1)}, u32[]{:S(2)}, u32[]{:S(2)}) collective-permute-start(bf16[512,128]{1,0:T(8,128)(2,1)} %bitcast.34), channel_id=1, source_target_pairs={{0,1},{1,0},{2,3},{3,2},{4,5},{5,4},{6,7},{7,6},{8,9},{9,8},{10,11... | collective-permute-start | bytes 393224 | tf_op jit(solution)/shard_map/ppermute | solution.py:47
  86.1 29.6 %collective-permute-start.20 = (bf16[512,128]{1,0:T(8,128)(2,1)}, bf16[512,128]{1,0:T(8,128)(2,1)S(1)}, u32[]{:S(2)}, u32[]{:S(2)}) collective-permute-start(bf16[512,128]{1,0:T(8,128)(2,1)} %bitcast.33), channel_id=1, source_target_pairs={{0,3},{1,2},{2,5},{3,4},{4,7},{5,6},{6,1},{7,0},{8,11},{9,10},{10,... | collective-permute-start | bytes 393224 | tf_op jit(solution)/shard_map/ppermute | solution.py:47
  90.3 25.4 %collective-permute-start.21 = (bf16[512,128]{1,0:T(8,128)(2,1)}, bf16[512,128]{1,0:T(8,128)(2,1)S(1)}, u32[]{:S(2)}, u32[]{:S(2)}) collective-permute-start(bf16[512,128]{1,0:T(8,128)(2,1)} %bitcast.32), channel_id=1, source_target_pairs={{0,7},{1,6},{2,1},{3,0},{4,3},{5,2},{6,5},{7,4},{8,15},{9,14},{10,... | collective-permute-start | bytes 393224 | tf_op jit(solution)/shard_map/ppermute | solution.py:47
  98.9 16.8 %collective-permute-start.18 = (bf16[512,128]{1,0:T(8,128)(2,1)S(1)}, bf16[512,128]{1,0:T(8,128)(2,1)S(1)}, u32[]{:S(2)}, u32[]{:S(2)}) collective-permute-start(bf16[512,128]{1,0:T(8,128)(2,1)S(1)} %slice.26), channel_id=1, source_target_pairs={{0,2},{1,3},{2,4},{3,5},{4,6},{5,7},{6,0},{7,1},{8,10},{9,11},{10,... | collective-permute-start | bytes 393224 | tf_op jit(solution)/shard_map/ppermute | solution.py:47
  101.9 13.8 %collective-permute-start.22 = (bf16[512,128]{1,0:T(8,128)(2,1)S(1)}, bf16[512,128]{1,0:T(8,128)(2,1)S(1)}, u32[]{:S(2)}, u32[]{:S(2)}) collective-permute-start(bf16[512,128]{1,0:T(8,128)(2,1)S(1)} %slice.27), channel_id=1, source_target_pairs={{0,7},{1,6},{2,1},{3,0},{4,3},{5,2},{6,5},{7,4},{8,15},{9,14},{10,... | collective-permute-start | bytes 393224 | tf_op jit(solution)/shard_map/ppermute | solution.py:47
  105.4 1.2 %copy-start.3 = (bf16[4096,128]{1,0:T(8,128)(2,1)S(1)}, bf16[4096,128]{1,0:T(8,128)(2,1)}, u32[]{:S(2)}) copy-start(bf16[4096,128]{1,0:T(8,128)(2,1)} %copy-done.2) | copy-start | bytes 3145732
  106.7 1.0 copy-start.6
  107.7 1.0 copy-start.8
  108.8 0.9 copy-start.12
  109.7 0.9 copy-start.14
  110.6 5.1 %copy-start.10 = (bf16[2,256,128]{2,1,0:T(8,128)(2,1)S(1)}, bf16[2,256,128]{2,1,0:T(8,128)(2,1)}, u32[]{:S(2)}) copy-start(bf16[2,256,128]{2,1,0:T(8,128)(2,1)} %get-tuple-element.75) | copy-start | bytes 393220

commit v10 on v8

--- a/solution.py
+++ b/solution.py
@@ -88,11 +88,18 @@
 
 
 def assemble_kernel(cuts, *refs):
-    *pieces, out_ref = refs
+    *pieces, out_ref, done = refs
+    copies = []
     at = 0
-    for piece, (start, stop) in zip(pieces, cuts, strict=True):
-        out_ref[at : at + stop - start] = piece[start:stop]
-        at += stop - start
+    for i, (piece, (start, stop)) in enumerate(zip(pieces, cuts, strict=True)):
+        size = stop - start
+        source, target = piece.at[pl.ds(start, size)], out_ref.at[pl.ds(at, size)]
+        copies.append(pltpu.make_async_copy(source, target, done.at[i]))
+        at += size
+    for copy in copies:
+        copy.start()
+    for copy in copies:
+        copy.wait()
 
 
 def assemble(*pieces):
@@ -100,14 +107,13 @@
     cuts = [p[1:] for p in pieces]
     columns = arrays[0].shape[1]
     total = sum(stop - start for start, stop in cuts)
-    whole = lambda shape: pl.BlockSpec(shape, lambda i: (0,) * len(shape))
     return pl.pallas_call(
         functools.partial(assemble_kernel, cuts),
-        grid=(1,),
-        in_specs=[whole(v.shape) for v in arrays],
-        out_specs=whole((total, columns)),
+        in_specs=[pl.BlockSpec(memory_space=pl.ANY)] * len(arrays),
+        out_specs=pl.BlockSpec(memory_space=pltpu.HBM),
         out_shape=jax.ShapeDtypeStruct((total, columns), BF),
-        compiler_params=pltpu.CompilerParams(vmem_limit_bytes=24 * 2**20),
+        scratch_shapes=[pltpu.SemaphoreType.DMA((len(arrays),))],
+        compiler_params=pltpu.CompilerParams(vmem_limit_bytes=4 * 2**20),
     )(*arrays)
 
 

time: 117 us -> 118 us (level)
  Pallas kernels: 16.2 us -> 17.9 us
    pallas_call x2, Pallas kernels: 0.14 us -> 1.88 us  [assemble(): pl.pallas_call(functools.partial(assemble_kernel, cuts), in_specs=[pl.Blo...]
  transfers between devices with their start and end apart: 23 -> 23, of which waited for: 12 -> 12; matrix products, arithmetic and copies ran while one was open for 3% -> 3% of each run, Pallas kernels for 12% -> 13%
where the time goes in v10:
time: 118 us; the launch traced here: 117 us
  starting transfers between devices  47 us (40%)
  waiting for transfers between devices  39.2 us (33%)
  Pallas kernels  17.9 us (15%)
  local copies, waits for them, and re-layouts  11.5 us (10%)
    ppermute x19, waiting for transfers between devices, tensor_send(): return lax.ppermute(value, 'tensor', pairs)  25.6 us
    ppermute x19, starting transfers between devices, tensor_send(): return lax.ppermute(value, 'tensor', pairs)  23.3 us
    all_to_all x1, starting transfers between devices, shards(): gathered = lax.all_to_all(packed, 'dp', 0, 0)  11.8 us
    all_to_all x1, starting transfers between devices, shards(): terms = lax.all_to_all(terms, 'dp', 0, 0)  9.86 us
    unnamed x45, local copies, waits for them, and re-layouts  9.43 us
    all_to_all x1, waiting for transfers between devices, shards(): terms = lax.all_to_all(terms, 'dp', 0, 0)  8.35 us
    pallas_call x1, Pallas kernels, frozen_and_correction(): pl.pallas_call(near_kernel, grid_spec=pltpu.PrefetchScalarGridSpec(num_sc...  5.47 us
    ppermute x2, waiting for transfers between devices, x_send(): return lax.ppermute(value, 'dp', pairs)  5.21 us
  transfers between devices with their start and end apart: 23, of which 12 were waited for; matrix products, arithmetic and copies ran while one was open for 3% of the time, Pallas kernels for 13%

profile of v10, /device:TPU:2, one launch (start us, length us, event | category | flops | bytes accessed | tf_op | source)
XLA Modules:
  0.0 117.3 jit_solution(18219142830665638234)
XLA Ops:
  0.6 2.0 %shard_map.139 = bf16[32,16,1280]{2,1,0:T(8,128)(2,1)} custom-call(s32[1,4]{1,0:T(1,128)} %bitcast.26, f32[1,4]{1,0:T(1,128)} %bitcast.27, bf16[16,1024]{1,0:T(8,128)(2,1)} %down_ref.1, bf16[16,128]{1,0:T(8,128)(2,1)} %up_ref.1), custom_call_target="tpu_custom_call" | custom-call | tf_op jit(solution)/shard_map/pallas_call | solution.py:325
  2.6 11.8 %all-to-all-start = ((bf16[32,16,1280]{2,1,0:T(8,128)(2,1)}), bf16[32,16,1280]{2,1,0:T(8,128)(2,1)S(1)}, u32[]{:S(2)}, u32[]{:S(2)}) async-start(bf16[32,16,1280]{2,1,0:T(8,128)(2,1)} %shard_map.139), calls=%async_computation | async-start | bytes 2621440 | tf_op jit(solution)/shard_map/all_to_all | solution.py:335
  14.4 0.7 copy.20
  15.2 0.5 multiply_add_fusion.places
  15.7 3.3 %shard_map.140 = (bf16[2048,128]{1,0:T(8,128)(2,1)}, bf16[512,128]{1,0:T(8,128)(2,1)}, bf16[2048,128]{1,0:T(8,128)(2,1)}, bf16[512,128]{1,0:T(8,128)(2,1)}, bf16...) custom-call(s32[8]{0:T(128)} %multiply_add_fusion.places, bf16[2,8192,128]{2,1,0:T(8,128)(2,1)} %refs_7_.1, ...), custom_call_target="tpu_custom_call" | custom-call | tf_op jit(solution)/shard_map/pallas_call | solution.py:146
  19.0 1.6 %collective-permute-start = (bf16[2048,128]{1,0:T(8,128)(2,1)}, bf16[2048,128]{1,0:T(8,128)(2,1)S(1)}, u32[]{:S(2)}, u32[]{:S(2)}) collective-permute-start(bf16[2048,128]{1,0:T(8,128)(2,1)} %get-tuple-element.38), channel_id=1, source_target_pairs={{0,2},{1,3},{2,4},{3,5},{4,6},{5,7},{6,0},{7,1},{8,10},{9,11},{10,... | collective-permute-start | bytes 1572872 | tf_op jit(solution)/shard_map/ppermute | solution.py:47
  20.6 1.7 %collective-permute-start.1 = (bf16[2048,128]{1,0:T(8,128)(2,1)}, bf16[2048,128]{1,0:T(8,128)(2,1)S(1)}, u32[]{:S(2)}, u32[]{:S(2)}) collective-permute-start(bf16[2048,128]{1,0:T(8,128)(2,1)} %get-tuple-element.39), channel_id=1, source_target_pairs={{0,6},{1,7},{2,0},{3,1},{4,2},{5,3},{6,4},{7,5},{8,14},{9,15},{10,... | collective-permute-start | bytes 1572872 | tf_op jit(solution)/shard_map/ppermute | solution.py:47
  22.2 11.3 %collective-permute-done.refs_1_ = bf16[2048,128]{1,0:T(8,128)(2,1)S(1)} collective-permute-done((bf16[2048,128]{1,0:T(8,128)(2,1)}, bf16[2048,128]{1,0:T(8,128)(2,1)S(1)}, u32[]{:S(2)}, u32[]{:S(2)}) %collective-permute-start) | collective-permute-done | bytes 524320 | tf_op jit(solution)/shard_map/ppermute | solution.py:47
  33.6 0.0 collective-permute-done.1.refs_2_
  33.6 1.6 %collective-permute-start.2 = (bf16[1024,128]{1,0:T(8,128)(2,1)S(1)}, bf16[1024,128]{1,0:T(8,128)(2,1)S(1)}, u32[]{:S(2)}, u32[]{:S(2)}) collective-permute-start(bf16[1024,128]{1,0:T(8,128)(2,1)S(1)} %slice.24), channel_id=1, source_target_pairs={{0,2},{1,3},{2,4},{3,5},{4,6},{5,7},{6,0},{7,1},{8,10},{9,11},{10,... | collective-permute-start | bytes 786440 | tf_op jit(solution)/shard_map/ppermute | solution.py:47
  35.3 1.8 %collective-permute-start.3 = (bf16[512,128]{1,0:T(8,128)(2,1)}, bf16[512,128]{1,0:T(8,128)(2,1)S(1)}, u32[]{:S(2)}, u32[]{:S(2)}) collective-permute-start(bf16[512,128]{1,0:T(8,128)(2,1)} %get-tuple-element.41), channel_id=1, source_target_pairs={{0,1},{1,0},{2,3},{3,2},{4,5},{5,4},{6,7},{7,6},{8,9},{9,8},{10,11... | collective-permute-start | bytes 393224 | tf_op jit(solution)/shard_map/ppermute | solution.py:47
  37.1 3.0 %collective-permute-start.5 = (bf16[512,128]{1,0:T(8,128)(2,1)}, bf16[512,128]{1,0:T(8,128)(2,1)S(1)}, u32[]{:S(2)}, u32[]{:S(2)}) collective-permute-start(bf16[512,128]{1,0:T(8,128)(2,1)} %get-tuple-element.43), channel_id=1, source_target_pairs={{0,7},{1,6},{2,1},{3,0},{4,3},{5,2},{6,5},{7,4},{8,15},{9,14},{10,... | collective-permute-start | bytes 393224 | tf_op jit(solution)/shard_map/ppermute | solution.py:47
  40.0 1.5 %collective-permute-done.2.refs_3_ = bf16[1024,128]{1,0:T(8,128)(2,1)S(1)} collective-permute-done((bf16[1024,128]{1,0:T(8,128)(2,1)S(1)}, bf16[1024,128]{1,0:T(8,128)(2,1)S(1)}, u32[]{:S(2)}, u32[]{:S(2)}) %collective-permute-start.2) | collective-permute-done | bytes 262176 | tf_op jit(solution)/shard_map/ppermute | solution.py:47
  41.6 2.3 %collective-permute-done.6.refs_7_.refs_4_ = bf16[1024,128]{1,0:T(8,128)(2,1)S(1)} collective-permute-done((bf16[1024,128]{1,0:T(8,128)(2,1)S(1)}, bf16[1024,128]{1,0:T(8,128)(2,1)S(1)}, u32[]{:S(2)}, u32[]{:S(2)}) %collective-permute-start.6) | collective-permute-done | bytes 262176 | tf_op jit(solution)/shard_map/ppermute | solution.py:47
  43.9 0.4 shard_map.142.cots
  44.3 0.0 copy-start.4
  44.4 1.0 copy-done.4
  45.3 0.0 collective-permute-done.3.refs_4_
  45.3 1.2 %collective-permute-done.5.refs_6_ = bf16[512,128]{1,0:T(8,128)(2,1)S(1)} collective-permute-done((bf16[512,128]{1,0:T(8,128)(2,1)}, bf16[512,128]{1,0:T(8,128)(2,1)S(1)}, u32[]{:S(2)}, u32[]{:S(2)}) %collective-permute-start.5) | collective-permute-done | bytes 131104 | tf_op jit(solution)/shard_map/ppermute | solution.py:47
  46.6 0.0 copy-start.13
  46.6 0.0 copy-start.14
  46.6 0.0 copy-start.15
  46.6 1.4 %shard_map.141.refs_0_ = bf16[4096,128]{1,0:T(8,128)(2,1)S(1)} custom-call(bf16[512,128]{1,0:T(8,128)(2,1)S(1)} %copy-done.12, bf16[2048,128]{1,0:T(8,128)(2,1)S(1)} %collective-permute-done.refs_1_, bf16[2048,128]{1,0:T(8,128)(2,1)S(1)} %collective-permute-done.1.refs_2_, bf16[1024,128]{1,0:T(8,128)(2,1)S(1)} %collective-permute-done.2.refs_3_, ...), custom_call_target="tpu_custom_call" | custom-call | tf_op jit(solution)/shard_map/pallas_call | solution.py:110
  48.0 1.0 copy-done.2
  49.0 0.0 collective-permute-start.13
  49.0 0.5 collective-permute-start.12
  49.6 1.5 %collective-permute-start.11 = (bf16[4096,128]{1,0:T(8,128)(2,1)}, bf16[4096,128]{1,0:T(8,128)(2,1)}, u32[]{:S(2)}, u32[]{:S(2)}) collective-permute-start(bf16[4096,128]{1,0:T(8,128)(2,1)} %copy-done.2), channel_id=1, source_target_pairs={{0,8},{8,16},{16,24},{24,0},{32,40},{40,48},{48,56},{56,32},{64,72... | collective-permute-start | bytes 3145736 | tf_op jit(solution)/shard_map/ppermute | solution.py:52
  51.1 0.2 select_reduce_fusion.slots
  51.3 1.2 %shard_map.143 = (f32[512,128]{1,0:T(8,128)S(1)}, bf16[512,128]{1,0:T(8,128)(2,1)S(1)}, f32[512,1]{1,0:T(8,128)S(1)}) custom-call(s32[4]{0:T(128)S(1)} %select_reduce_fusion.slots, s32[4]{0:T(128)S(1)} %copy-done.15, s32[4]{0:T(128)S(1)} %copy-done.13, f32[4]{0:T(128)S(1)} %copy-done.14, bf16[32,16,1280]{2,1,0:T(8,128)(2,1)S(1)} %all-to-all-done.gathered_ref, ...), custom_call_target="tpu_custom_call" | custom-call | flops 67108864 | bytes 1048576 | tf_op jit(solution)/shard_map/pallas_call | solution.py:376
  52.5 0.7 copy-done.10
  53.2 1.5 %collective-permute-done.7 = f32[512,128]{1,0:T(8,128)S(1)} collective-permute-done((f32[512,128]{1,0:T(8,128)S(1)}, f32[512,128]{1,0:T(8,128)S(1)}, u32[]{:S(2)}, u32[]{:S(2)}) %collective-permute-start.7) | collective-permute-done | bytes 262176 | tf_op jit(solution)/shard_map/ppermute | solution.py:47
  54.8 1.9 %collective-permute-start.10 = (bf16[512,128]{1,0:T(8,128)(2,1)S(1)}, bf16[512,128]{1,0:T(8,128)(2,1)S(1)}, u32[]{:S(2)}, u32[]{:S(2)}) collective-permute-start(bf16[512,128]{1,0:T(8,128)(2,1)S(1)} %add_convert_fusion.own), channel_id=1, source_target_pairs={{0,4},{1,5},{2,6},{3,7},{4,0},{5,1},{6,2},{7,3},{8,12},{9,13},{10,... | collective-permute-start | bytes 393224 | tf_op jit(solution)/shard_map/ppermute | solution.py:47
  56.8 2.4 %collective-permute-start.9 = (bf16[512,128]{1,0:T(8,128)(2,1)S(1)}, bf16[512,128]{1,0:T(8,128)(2,1)S(1)}, u32[]{:S(2)}, u32[]{:S(2)}) collective-permute-start(bf16[512,128]{1,0:T(8,128)(2,1)S(1)} %add_convert_fusion.own), channel_id=1, source_target_pairs={{0,6},{1,7},{2,0},{3,1},{4,2},{5,3},{6,4},{7,5},{8,14},{9,15},{10,... | collective-permute-start | bytes 393224 | tf_op jit(solution)/shard_map/ppermute | solution.py:47
  59.1 2.8 %collective-permute-done.10.third = bf16[512,128]{1,0:T(8,128)(2,1)S(1)} collective-permute-done((bf16[512,128]{1,0:T(8,128)(2,1)S(1)}, bf16[512,128]{1,0:T(8,128)(2,1)S(1)}, u32[]{:S(2)}, u32[]{:S(2)}) %collective-permute-start.10) | collective-permute-done | bytes 131104 | tf_op jit(solution)/shard_map/ppermute | solution.py:47
  61.9 2.4 %collective-permute-start.8 = (bf16[512,128]{1,0:T(8,128)(2,1)S(1)}, bf16[512,128]{1,0:T(8,128)(2,1)S(1)}, u32[]{:S(2)}, u32[]{:S(2)}) collective-permute-start(bf16[512,128]{1,0:T(8,128)(2,1)S(1)} %add_convert_fusion.own), channel_id=1, source_target_pairs={{0,2},{1,3},{2,4},{3,5},{4,6},{5,7},{6,0},{7,1},{8,10},{9,11},{10,... | collective-permute-start | bytes 393224 | tf_op jit(solution)/shard_map/ppermute | solution.py:47
  64.3 2.1 %constant_dynamic-slice_fusion = (bf16[2,256,128]{2,1,0:T(8,128)(2,1)}, bf16[2,256,128]{2,1,0:T(8,128)(2,1)}, bf16[2,256,128]{2,1,0:T(8,128)(2,1)S(1)}, bf16[2,2...) fusion(bf16[2,8192,128]{2,1,0:T(8,128)(2,1)} %refs_7_.1, ...), kind=kLoop, calls=%fused_computation.10 | loop fusion | bytes 2097184 | tf_op jit(solution)/shard_map/dynamic_slice | solution.py:368
  66.5 0.0 collective-permute-done.9.second
  66.5 1.7 %collective-permute-done.8.first = bf16[512,128]{1,0:T(8,128)(2,1)S(1)} collective-permute-done((bf16[512,128]{1,0:T(8,128)(2,1)S(1)}, bf16[512,128]{1,0:T(8,128)(2,1)S(1)}, u32[]{:S(2)}, u32[]{:S(2)}) %collective-permute-start.8) | collective-permute-done | bytes 131104 | tf_op jit(solution)/shard_map/ppermute | solution.py:47
  68.1 1.1 shard_map.144
  69.3 1.1 copy-done.6
  70.3 0.6 copy-done.8
  71.0 4.0 %collective-permute-done.12.refs_2_ = bf16[4096,128]{1,0:T(8,128)(2,1)} collective-permute-done((bf16[4096,128]{1,0:T(8,128)(2,1)}, bf16[4096,128]{1,0:T(8,128)(2,1)}, u32[]{:S(2)}, u32[]{:S(2)}) %collective-permute-start.12) | collective-permute-done | bytes 1048608 | tf_op jit(solution)/shard_map/ppermute | solution.py:52
  74.9 1.2 %collective-permute-done.11.refs_1_ = bf16[4096,128]{1,0:T(8,128)(2,1)} collective-permute-done((bf16[4096,128]{1,0:T(8,128)(2,1)}, bf16[4096,128]{1,0:T(8,128)(2,1)}, u32[]{:S(2)}, u32[]{:S(2)}) %collective-permute-start.11) | collective-permute-done | bytes 1048608 | tf_op jit(solution)/shard_map/ppermute | solution.py:52
  76.2 9.9 %all-to-all-start.1 = ((bf16[32,16,1152]{2,1,0:T(8,128)(2,1)}), bf16[32,16,1152]{2,1,0:T(8,128)(2,1)S(1)}, u32[]{:S(2)}, u32[]{:S(2)}) async-start(bf16[32,16,1152]{2,1,0:T(8,128)(2,1)} %copy-done.6), calls=%async_computation.1 | async-start | bytes 2359296 | tf_op jit(solution)/shard_map/all_to_all | solution.py:406
  86.0 1.4 %collective-permute-start.14 = (bf16[1024,128]{1,0:T(8,128)(2,1)S(1)}, bf16[1024,128]{1,0:T(8,128)(2,1)S(1)}, u32[]{:S(2)}, u32[]{:S(2)}) collective-permute-start(bf16[1024,128]{1,0:T(8,128)(2,1)S(1)} %get-tuple-element.61), channel_id=1, source_target_pairs={{0,2},{1,3},{2,4},{3,5},{4,6},{5,7},{6,0},{7,1},{8,10},{9,11},{10,... | collective-permute-start | bytes 786440 | tf_op jit(solution)/shard_map/ppermute | solution.py:47
  87.5 1.9 %collective-permute-start.15 = (bf16[1024,128]{1,0:T(8,128)(2,1)S(1)}, bf16[1024,128]{1,0:T(8,128)(2,1)S(1)}, u32[]{:S(2)}, u32[]{:S(2)}) collective-permute-start(bf16[1024,128]{1,0:T(8,128)(2,1)S(1)} %get-tuple-element.62), channel_id=1, source_target_pairs={{0,6},{1,7},{2,0},{3,1},{4,2},{5,3},{6,4},{7,5},{8,14},{9,15},{10,... | collective-permute-start | bytes 786440 | tf_op jit(solution)/shard_map/ppermute | solution.py:47
  89.4 0.0 collective-permute-start.17
  89.4 0.2 collective-permute-start.18
  89.6 2.7 %collective-permute-start.19 = (bf16[512,128]{1,0:T(8,128)(2,1)S(1)}, bf16[512,128]{1,0:T(8,128)(2,1)S(1)}, u32[]{:S(2)}, u32[]{:S(2)}) collective-permute-start(bf16[512,128]{1,0:T(8,128)(2,1)S(1)} %bitcast.32), channel_id=1, source_target_pairs={{0,7},{1,6},{2,1},{3,0},{4,3},{5,2},{6,5},{7,4},{8,15},{9,14},{10,... | collective-permute-start | bytes 393224 | tf_op jit(solution)/shard_map/ppermute | solution.py:47
  92.3 2.9 %collective-permute-done.14.refs_1_ = bf16[1024,128]{1,0:T(8,128)(2,1)S(1)} collective-permute-done((bf16[1024,128]{1,0:T(8,128)(2,1)S(1)}, bf16[1024,128]{1,0:T(8,128)(2,1)S(1)}, u32[]{:S(2)}, u32[]{:S(2)}) %collective-permute-start.14) | collective-permute-done | bytes 262176 | tf_op jit(solution)/shard_map/ppermute | solution.py:47
  95.2 0.3 collective-permute-done.15.refs_2_
  95.5 0.7 collective-permute-start.16
  96.3 0.0 collective-permute-start.20
  96.3 1.2 %copy-done.3 = bf16[4096,128]{1,0:T(8,128)(2,1)S(1)} copy-done((bf16[4096,128]{1,0:T(8,128)(2,1)S(1)}, bf16[4096,128]{1,0:T(8,128)(2,1)}, u32[]{:S(2)}) %copy-start.3) | copy-done | bytes 1048600
  97.5 1.2 %copy-done.5 = bf16[4096,128]{1,0:T(8,128)(2,1)S(1)} copy-done((bf16[4096,128]{1,0:T(8,128)(2,1)S(1)}, bf16[4096,128]{1,0:T(8,128)(2,1)}, u32[]{:S(2)}) %copy-start.5) | copy-done | bytes 1048600
  98.7 0.9 copy-done.9
  99.6 0.9 copy-done.11
  100.6 5.5 %shard_map.145 = (bf16[512,1024]{1,0:T(8,128)(2,1)}, bf16[512,2048]{1,0:T(8,128)(2,1)S(1)}) custom-call(s32[4]{0:T(128)S(1)} %select_reduce_fusion.slots, s32[4]{0:T(128)S(1)} %and_select_fusion.2.quarters, bf16[4096,128]{1,0:T(8,128)(2,1)S(1)} %copy-done.5, bf16[4096,128]{1,0:T(8,128)(2,1)} %collective-permute-done.13.others, ...), custom_call_target="tpu_custom_call" | custom-call | tf_op jit(solution)/shard_map/pallas_call | solution.py:256
  106.0 0.0 collective-permute-done.17.refs_4_
  106.1 0.0 collective-permute-done.18.refs_5_
  106.1 0.0 collective-permute-done.19.refs_6_
  106.1 2.1 %shard_map.146 = bf16[512,1024]{1,0:T(8,128)(2,1)} custom-call(s32[4]{0:T(128)S(1)} %select_reduce_fusion.slots, s32[4]{0:T(128)S(1)} %and_select_fusion.2.quarters, bf16[512,1024]{1,0:T(8,128)(2,1)} %get-tuple-element.58.near_ref, bf16[512,2048]{1,0:T(8,128)(2,1)S(1)} %get-tuple-element.59.weighted, ...), custom_call_target="tpu_custom_call", output_to_operand_aliasing={{}: (2, {})} | custom-call | tf_op jit(solution)/shard_map/pallas_call | solution.py:268
  108.2 8.3 %all-to-all-done.1.terms_ref = bf16[32,16,1152]{2,1,0:T(8,128)(2,1)S(1)} async-done(((bf16[32,16,1152]{2,1,0:T(8,128)(2,1)}), bf16[32,16,1152]{2,1,0:T(8,128)(2,1)S(1)}, u32[]{:S(2)}, u32[]{:S(2)}) %all-to-all-start.1) | async-done | bytes 1179680 | tf_op jit(solution)/shard_map/all_to_all | solution.py:406
  116.5 0.8 shard_map.147
  (46 shorter events, 0.2 us)
Async XLA Ops:
  2.6 11.8 %copy-start.16 = (bf16[512,2,128]{2,1,0:T(2,128)(2,1)S(1)}, bf16[512,2,128]{2,1,0:T(2,128)(2,1)}, u32[]{:S(2)}) copy-start(bf16[512,2,128]{2,1,0:T(2,128)(2,1)} %param.13) | copy-start | bytes 786436
  2.6 12.5 %copy-start.17 = (s32[8,1]{0,1:T(1,128)S(1)}, s32[8,1]{0,1:T(1,128)}, u32[]{:S(2)}) copy-start(s32[8,1]{0,1:T(1,128)} %constant.150) | copy-start | bytes 100
  2.6 12.5 %copy-start.18 = (s32[8,1]{0,1:T(1,128)S(1)}, s32[8,1]{0,1:T(1,128)}, u32[]{:S(2)}) copy-start(s32[8,1]{0,1:T(1,128)} %constant.149) | copy-start | bytes 100
  2.6 46.4 %all-to-all-start = ((bf16[32,16,1280]{2,1,0:T(8,128)(2,1)}), bf16[32,16,1280]{2,1,0:T(8,128)(2,1)S(1)}, u32[]{:S(2)}, u32[]{:S(2)}) async-start(bf16[32,16,1280]{2,1,0:T(8,128)(2,1)} %shard_map.139), calls=%async_computation | async-start | bytes 2621440 | tf_op jit(solution)/shard_map/all_to_all | solution.py:335
  15.7 28.2 %copy-start = (bf16[512,2,128]{2,0,1:T(8,128)(2,1)S(1)}, bf16[512,2,128]{2,0,1:T(8,128)(2,1)}, u32[]{:S(2)}) copy-start(bf16[512,2,128]{2,0,1:T(8,128)(2,1)} %copy.20) | copy-start | bytes 786436
  19.0 14.6 %collective-permute-start = (bf16[2048,128]{1,0:T(8,128)(2,1)}, bf16[2048,128]{1,0:T(8,128)(2,1)S(1)}, u32[]{:S(2)}, u32[]{:S(2)}) collective-permute-start(bf16[2048,128]{1,0:T(8,128)(2,1)} %get-tuple-element.38), channel_id=1, source_target_pairs={{0,2},{1,3},{2,4},{3,5},{4,6},{5,7},{6,0},{7,1},{8,10},{9,11},{10,... | collective-permute-start | bytes 1572872 | tf_op jit(solution)/shard_map/ppermute | solution.py:47
  20.6 13.0 %collective-permute-start.1 = (bf16[2048,128]{1,0:T(8,128)(2,1)}, bf16[2048,128]{1,0:T(8,128)(2,1)S(1)}, u32[]{:S(2)}, u32[]{:S(2)}) collective-permute-start(bf16[2048,128]{1,0:T(8,128)(2,1)} %get-tuple-element.39), channel_id=1, source_target_pairs={{0,6},{1,7},{2,0},{3,1},{4,2},{5,3},{6,4},{7,5},{8,14},{9,15},{10,... | collective-permute-start | bytes 1572872 | tf_op jit(solution)/shard_map/ppermute | solution.py:47
  33.6 7.9 %collective-permute-start.2 = (bf16[1024,128]{1,0:T(8,128)(2,1)S(1)}, bf16[1024,128]{1,0:T(8,128)(2,1)S(1)}, u32[]{:S(2)}, u32[]{:S(2)}) collective-permute-start(bf16[1024,128]{1,0:T(8,128)(2,1)S(1)} %slice.24), channel_id=1, source_target_pairs={{0,2},{1,3},{2,4},{3,5},{4,6},{5,7},{6,0},{7,1},{8,10},{9,11},{10,... | collective-permute-start | bytes 786440 | tf_op jit(solution)/shard_map/ppermute | solution.py:47
  35.3 8.6 %collective-permute-start.6 = (bf16[1024,128]{1,0:T(8,128)(2,1)S(1)}, bf16[1024,128]{1,0:T(8,128)(2,1)S(1)}, u32[]{:S(2)}, u32[]{:S(2)}) collective-permute-start(bf16[1024,128]{1,0:T(8,128)(2,1)S(1)} %slice.25), channel_id=1, source_target_pairs={{0,7},{1,6},{2,1},{3,0},{4,3},{5,2},{6,5},{7,4},{8,15},{9,14},{10,... | collective-permute-start | bytes 786440 | tf_op jit(solution)/shard_map/ppermute | solution.py:47
  35.3 10.0 %collective-permute-start.3 = (bf16[512,128]{1,0:T(8,128)(2,1)}, bf16[512,128]{1,0:T(8,128)(2,1)S(1)}, u32[]{:S(2)}, u32[]{:S(2)}) collective-permute-start(bf16[512,128]{1,0:T(8,128)(2,1)} %get-tuple-element.41), channel_id=1, source_target_pairs={{0,1},{1,0},{2,3},{3,2},{4,5},{5,4},{6,7},{7,6},{8,9},{9,8},{10,11... | collective-permute-start | bytes 393224 | tf_op jit(solution)/shard_map/ppermute | solution.py:47
  37.1 8.3 %collective-permute-start.4 = (bf16[512,128]{1,0:T(8,128)(2,1)}, bf16[512,128]{1,0:T(8,128)(2,1)S(1)}, u32[]{:S(2)}, u32[]{:S(2)}) collective-permute-start(bf16[512,128]{1,0:T(8,128)(2,1)} %get-tuple-element.42), channel_id=1, source_target_pairs={{0,3},{1,2},{2,5},{3,4},{4,7},{5,6},{6,1},{7,0},{8,11},{9,10},{10,... | collective-permute-start | bytes 393224 | tf_op jit(solution)/shard_map/ppermute | solution.py:47
  37.1 9.5 %collective-permute-start.5 = (bf16[512,128]{1,0:T(8,128)(2,1)}, bf16[512,128]{1,0:T(8,128)(2,1)S(1)}, u32[]{:S(2)}, u32[]{:S(2)}) collective-permute-start(bf16[512,128]{1,0:T(8,128)(2,1)} %get-tuple-element.43), channel_id=1, source_target_pairs={{0,7},{1,6},{2,1},{3,0},{4,3},{5,2},{6,5},{7,4},{8,15},{9,14},{10,... | collective-permute-start | bytes 393224 | tf_op jit(solution)/shard_map/ppermute | solution.py:47
  43.9 2.6 %copy-start.12 = (bf16[512,128]{1,0:T(8,128)(2,1)S(1)}, bf16[512,128]{1,0:T(8,128)(2,1)}, u32[]{:S(2)}) copy-start(bf16[512,128]{1,0:T(8,128)(2,1)} %get-tuple-element.37.refs_0_) | copy-start | bytes 393220
  44.3 1.0 copy-start.4
  46.5 4.5 %copy-start.19 = (s32[8]{0:T(128)S(1)}, s32[8]{0:T(128)}, u32[]{:S(2)}) copy-start(s32[8]{0:T(128)} %param.17) | copy-start | bytes 100
  46.5 4.5 %copy-start.20 = (s32[4]{0:T(128)S(1)}, s32[4]{0:T(128)}, u32[]{:S(2)}) copy-start(s32[4]{0:T(128)} %param.18) | copy-start | bytes 52
  46.5 4.7 %copy-start.1 = (bf16[512,1024]{1,0:T(8,128)(2,1)S(1)}, bf16[512,1024]{1,0:T(8,128)(2,1)}, u32[]{:S(2)}) copy-start(bf16[512,1024]{1,0:T(8,128)(2,1)} %x_ref.3) | copy-start | bytes 3145732
  46.6 4.7 %copy-start.13 = (s32[4]{0:T(128)S(1)}, s32[4]{0:T(128)}, u32[]{:S(2)}) copy-start(s32[4]{0:T(128)} %prompt.1) | copy-start | bytes 52
  46.6 4.7 %copy-start.14 = (f32[4]{0:T(128)S(1)}, f32[4]{0:T(128)}, u32[]{:S(2)}) copy-start(f32[4]{0:T(128)} %reward.1) | copy-start | bytes 52
  46.6 4.7 %copy-start.15 = (s32[4]{0:T(128)S(1)}, s32[4]{0:T(128)}, u32[]{:S(2)}) copy-start(s32[4]{0:T(128)} %live.1) | copy-start | bytes 52
  48.0 1.0 copy-start.2
  49.0 21.9 %collective-permute-start.13 = (bf16[4096,128]{1,0:T(8,128)(2,1)}, bf16[4096,128]{1,0:T(8,128)(2,1)}, u32[]{:S(2)}, u32[]{:S(2)}) collective-permute-start(bf16[4096,128]{1,0:T(8,128)(2,1)} %copy-done.4), channel_id=1, source_target_pairs={{0,1},{1,0},{2,3},{3,2},{4,5},{5,4},{6,7},{7,6},{8,9},{9,8},{10,11... | collective-permute-start | bytes 3145736 | tf_op jit(solution)/shard_map/ppermute | solution.py:47
  49.0 25.9 %collective-permute-start.12 = (bf16[4096,128]{1,0:T(8,128)(2,1)}, bf16[4096,128]{1,0:T(8,128)(2,1)}, u32[]{:S(2)}, u32[]{:S(2)}) collective-permute-start(bf16[4096,128]{1,0:T(8,128)(2,1)} %copy-done.2), channel_id=1, source_target_pairs={{0,24},{8,0},{16,8},{24,16},{32,56},{40,32},{48,40},{56,48},{64,88... | collective-permute-start | bytes 3145736 | tf_op jit(solution)/shard_map/ppermute | solution.py:52
  49.6 26.6 %collective-permute-start.11 = (bf16[4096,128]{1,0:T(8,128)(2,1)}, bf16[4096,128]{1,0:T(8,128)(2,1)}, u32[]{:S(2)}, u32[]{:S(2)}) collective-permute-start(bf16[4096,128]{1,0:T(8,128)(2,1)} %copy-done.2), channel_id=1, source_target_pairs={{0,8},{8,16},{16,24},{24,0},{32,40},{40,48},{48,56},{56,32},{64,72... | collective-permute-start | bytes 3145736 | tf_op jit(solution)/shard_map/ppermute | solution.py:52
  52.5 0.7 copy-start.10
  53.2 1.5 %collective-permute-start.7 = (f32[512,128]{1,0:T(8,128)S(1)}, f32[512,128]{1,0:T(8,128)S(1)}, u32[]{:S(2)}, u32[]{:S(2)}) collective-permute-start(f32[512,128]{1,0:T(8,128)S(1)} %get-tuple-element.46), channel_id=1, source_target_pairs={{0,1},{1,0},{2,3},{3,2},{4,5},{5,4},{6,7},{7,6},{8,9},{9,8},{10,11... | collective-permute-start | bytes 786440 | tf_op jit(solution)/shard_map/ppermute | solution.py:47
  54.8 7.1 %collective-permute-start.10 = (bf16[512,128]{1,0:T(8,128)(2,1)S(1)}, bf16[512,128]{1,0:T(8,128)(2,1)S(1)}, u32[]{:S(2)}, u32[]{:S(2)}) collective-permute-start(bf16[512,128]{1,0:T(8,128)(2,1)S(1)} %add_convert_fusion.own), channel_id=1, source_target_pairs={{0,4},{1,5},{2,6},{3,7},{4,0},{5,1},{6,2},{7,3},{8,12},{9,13},{10,... | collective-permute-start | bytes 393224 | tf_op jit(solution)/shard_map/ppermute | solution.py:47
  56.8 9.7 %collective-permute-start.9 = (bf16[512,128]{1,0:T(8,128)(2,1)S(1)}, bf16[512,128]{1,0:T(8,128)(2,1)S(1)}, u32[]{:S(2)}, u32[]{:S(2)}) collective-permute-start(bf16[512,128]{1,0:T(8,128)(2,1)S(1)} %add_convert_fusion.own), channel_id=1, source_target_pairs={{0,6},{1,7},{2,0},{3,1},{4,2},{5,3},{6,4},{7,5},{8,14},{9,15},{10,... | collective-permute-start | bytes 393224 | tf_op jit(solution)/shard_map/ppermute | solution.py:47
  61.9 6.2 %collective-permute-start.8 = (bf16[512,128]{1,0:T(8,128)(2,1)S(1)}, bf16[512,128]{1,0:T(8,128)(2,1)S(1)}, u32[]{:S(2)}, u32[]{:S(2)}) collective-permute-start(bf16[512,128]{1,0:T(8,128)(2,1)S(1)} %add_convert_fusion.own), channel_id=1, source_target_pairs={{0,2},{1,3},{2,4},{3,5},{4,6},{5,7},{6,0},{7,1},{8,10},{9,11},{10,... | collective-permute-start | bytes 393224 | tf_op jit(solution)/shard_map/ppermute | solution.py:47
  69.3 1.1 copy-start.6
  70.3 0.6 copy-start.8
  76.2 20.1 %copy-start.21 = (s32[4]{0:T(128)S(1)}, s32[4]{0:T(128)}, u32[]{:S(2)}) copy-start(s32[4]{0:T(128)} %constant.142.clone) | copy-start | bytes 52
  76.2 40.4 %all-to-all-start.1 = ((bf16[32,16,1152]{2,1,0:T(8,128)(2,1)}), bf16[32,16,1152]{2,1,0:T(8,128)(2,1)S(1)}, u32[]{:S(2)}, u32[]{:S(2)}) async-start(bf16[32,16,1152]{2,1,0:T(8,128)(2,1)} %copy-done.6), calls=%async_computation.1 | async-start | bytes 2359296 | tf_op jit(solution)/shard_map/all_to_all | solution.py:406
  86.0 9.2 %collective-permute-start.14 = (bf16[1024,128]{1,0:T(8,128)(2,1)S(1)}, bf16[1024,128]{1,0:T(8,128)(2,1)S(1)}, u32[]{:S(2)}, u32[]{:S(2)}) collective-permute-start(bf16[1024,128]{1,0:T(8,128)(2,1)S(1)} %get-tuple-element.61), channel_id=1, source_target_pairs={{0,2},{1,3},{2,4},{3,5},{4,6},{5,7},{6,0},{7,1},{8,10},{9,11},{10,... | collective-permute-start | bytes 786440 | tf_op jit(solution)/shard_map/ppermute | solution.py:47
  87.5 8.1 %collective-permute-start.15 = (bf16[1024,128]{1,0:T(8,128)(2,1)S(1)}, bf16[1024,128]{1,0:T(8,128)(2,1)S(1)}, u32[]{:S(2)}, u32[]{:S(2)}) collective-permute-start(bf16[1024,128]{1,0:T(8,128)(2,1)S(1)} %get-tuple-element.62), channel_id=1, source_target_pairs={{0,6},{1,7},{2,0},{3,1},{4,2},{5,3},{6,4},{7,5},{8,14},{9,15},{10,... | collective-permute-start | bytes 786440 | tf_op jit(solution)/shard_map/ppermute | solution.py:47
  89.4 16.7 %collective-permute-start.17 = (bf16[512,128]{1,0:T(8,128)(2,1)}, bf16[512,128]{1,0:T(8,128)(2,1)S(1)}, u32[]{:S(2)}, u32[]{:S(2)}) collective-permute-start(bf16[512,128]{1,0:T(8,128)(2,1)} %bitcast.34), channel_id=1, source_target_pairs={{0,1},{1,0},{2,3},{3,2},{4,5},{5,4},{6,7},{7,6},{8,9},{9,8},{10,11... | collective-permute-start | bytes 393224 | tf_op jit(solution)/shard_map/ppermute | solution.py:47
  89.4 16.7 %collective-permute-start.18 = (bf16[512,128]{1,0:T(8,128)(2,1)S(1)}, bf16[512,128]{1,0:T(8,128)(2,1)S(1)}, u32[]{:S(2)}, u32[]{:S(2)}) collective-permute-start(bf16[512,128]{1,0:T(8,128)(2,1)S(1)} %bitcast.33), channel_id=1, source_target_pairs={{0,3},{1,2},{2,5},{3,4},{4,7},{5,6},{6,1},{7,0},{8,11},{9,10},{10,... | collective-permute-start | bytes 393224 | tf_op jit(solution)/shard_map/ppermute | solution.py:47
  89.6 16.4 %collective-permute-start.19 = (bf16[512,128]{1,0:T(8,128)(2,1)S(1)}, bf16[512,128]{1,0:T(8,128)(2,1)S(1)}, u32[]{:S(2)}, u32[]{:S(2)}) collective-permute-start(bf16[512,128]{1,0:T(8,128)(2,1)S(1)} %bitcast.32), channel_id=1, source_target_pairs={{0,7},{1,6},{2,1},{3,0},{4,3},{5,2},{6,5},{7,4},{8,15},{9,14},{10,... | collective-permute-start | bytes 393224 | tf_op jit(solution)/shard_map/ppermute | solution.py:47
  95.5 10.5 %collective-permute-start.16 = (bf16[512,128]{1,0:T(8,128)(2,1)S(1)}, bf16[512,128]{1,0:T(8,128)(2,1)S(1)}, u32[]{:S(2)}, u32[]{:S(2)}) collective-permute-start(bf16[512,128]{1,0:T(8,128)(2,1)S(1)} %slice.26), channel_id=1, source_target_pairs={{0,2},{1,3},{2,4},{3,5},{4,6},{5,7},{6,0},{7,1},{8,10},{9,11},{10,... | collective-permute-start | bytes 393224 | tf_op jit(solution)/shard_map/ppermute | solution.py:47
  96.3 9.8 %collective-permute-start.20 = (bf16[512,128]{1,0:T(8,128)(2,1)S(1)}, bf16[512,128]{1,0:T(8,128)(2,1)S(1)}, u32[]{:S(2)}, u32[]{:S(2)}) collective-permute-start(bf16[512,128]{1,0:T(8,128)(2,1)S(1)} %slice.27), channel_id=1, source_target_pairs={{0,7},{1,6},{2,1},{3,0},{4,3},{5,2},{6,5},{7,4},{8,15},{9,14},{10,... | collective-permute-start | bytes 393224 | tf_op jit(solution)/shard_map/ppermute | solution.py:47
  96.3 1.2 %copy-start.3 = (bf16[4096,128]{1,0:T(8,128)(2,1)S(1)}, bf16[4096,128]{1,0:T(8,128)(2,1)}, u32[]{:S(2)}) copy-start(bf16[4096,128]{1,0:T(8,128)(2,1)} %copy-done.2) | copy-start | bytes 3145732
  97.5 1.2 %copy-start.5 = (bf16[4096,128]{1,0:T(8,128)(2,1)S(1)}, bf16[4096,128]{1,0:T(8,128)(2,1)}, u32[]{:S(2)}) copy-start(bf16[4096,128]{1,0:T(8,128)(2,1)} %copy-done.4) | copy-start | bytes 3145732
  98.7 0.9 copy-start.9
  99.6 0.9 copy-start.11
  100.6 5.5 %copy-start.7 = (bf16[2,256,128]{2,1,0:T(8,128)(2,1)S(1)}, bf16[2,256,128]{2,1,0:T(8,128)(2,1)}, u32[]{:S(2)}) copy-start(bf16[2,256,128]{2,1,0:T(8,128)(2,1)} %get-tuple-element.71) | copy-start | bytes 393220

commit v11 on v8

--- a/solution.py
+++ b/solution.py
@@ -107,7 +107,7 @@
         in_specs=[whole(v.shape) for v in arrays],
         out_specs=whole((total, columns)),
         out_shape=jax.ShapeDtypeStruct((total, columns), BF),
-        compiler_params=pltpu.CompilerParams(vmem_limit_bytes=24 * 2**20),
+        compiler_params=pltpu.CompilerParams(vmem_limit_bytes=FULL_VMEM),
     )(*arrays)
 
 

time: 117 us -> 120 us (1.026)
  Pallas kernels: 16.2 us -> 21 us
  waiting for transfers between devices: 39.9 us -> 37 us
  starting transfers between devices: 46.6 us -> 47.9 us
    pallas_call x2, Pallas kernels: 0.14 us -> 5.12 us  [assemble(): pl.pallas_call(functools.partial(assemble_kernel, cuts), grid=(1,), in_sp...]
    ppermute x19, waiting for transfers between devices: 26.4 us -> 24.6 us  [tensor_send(): return lax.ppermute(value, 'tensor', pairs)]
    unnamed x45 -> x53, local copies, waits for them, and re-layouts: 9.43 us -> 9.5 us
  transfers between devices with their start and end apart: 23 -> 23, of which waited for: 12 -> 11; matrix products, arithmetic and copies ran while one was open for 3% -> 3% of each run, Pallas kernels for 12% -> 15%
where the time goes in v11:
time: 120 us; the launch traced here: 119 us
  starting transfers between devices  47.9 us (40%)
  waiting for transfers between devices  37 us (31%)
  Pallas kernels  21 us (18%)
  local copies, waits for them, and re-layouts  11.6 us (10%)
    ppermute x19, waiting for transfers between devices, tensor_send(): return lax.ppermute(value, 'tensor', pairs)  24.6 us
    ppermute x19, starting transfers between devices, tensor_send(): return lax.ppermute(value, 'tensor', pairs)  24.2 us
    all_to_all x1, starting transfers between devices, shards(): gathered = lax.all_to_all(packed, 'dp', 0, 0)  11.8 us
    all_to_all x1, starting transfers between devices, shards(): terms = lax.all_to_all(terms, 'dp', 0, 0)  9.86 us
    unnamed x53, local copies, waits for them, and re-layouts  9.5 us
    all_to_all x1, waiting for transfers between devices, shards(): terms = lax.all_to_all(terms, 'dp', 0, 0)  7.3 us
    pallas_call x1, Pallas kernels, frozen_and_correction(): pl.pallas_call(near_kernel, grid_spec=pltpu.PrefetchScalarGridSpec(num_sc...  5.47 us
    ppermute x2, waiting for transfers between devices, x_send(): return lax.ppermute(value, 'dp', pairs)  5.12 us
  transfers between devices with their start and end apart: 23, of which 11 were waited for; matrix products, arithmetic and copies ran while one was open for 3% of the time, Pallas kernels for 15%

profile of v11, /device:TPU:2, one launch (start us, length us, event | category | flops | bytes accessed | tf_op | source)
XLA Modules:
  0.0 119.2 jit_solution(2001122767735805270)
XLA Ops:
  0.6 2.0 %shard_map.139 = bf16[32,16,1280]{2,1,0:T(8,128)(2,1)} custom-call(s32[1,4]{1,0:T(1,128)} %bitcast.26, f32[1,4]{1,0:T(1,128)} %bitcast.27, bf16[16,1024]{1,0:T(8,128)(2,1)} %down_ref.1, bf16[16,128]{1,0:T(8,128)(2,1)} %up_ref.1), custom_call_target="tpu_custom_call" | custom-call | tf_op jit(solution)/shard_map/pallas_call | solution.py:319
  2.6 11.8 %all-to-all-start = ((bf16[32,16,1280]{2,1,0:T(8,128)(2,1)}), bf16[32,16,1280]{2,1,0:T(8,128)(2,1)S(1)}, u32[]{:S(2)}, u32[]{:S(2)}) async-start(bf16[32,16,1280]{2,1,0:T(8,128)(2,1)} %shard_map.139), calls=%async_computation | async-start | bytes 2621440 | tf_op jit(solution)/shard_map/all_to_all | solution.py:329
  14.4 0.7 copy.20
  15.2 0.5 multiply_add_fusion.places
  15.7 3.2 %shard_map.140 = (bf16[2048,128]{1,0:T(8,128)(2,1)}, bf16[512,128]{1,0:T(8,128)(2,1)}, bf16[2048,128]{1,0:T(8,128)(2,1)}, bf16[512,128]{1,0:T(8,128)(2,1)}, bf16...) custom-call(s32[8]{0:T(128)} %multiply_add_fusion.places, bf16[2,8192,128]{2,1,0:T(8,128)(2,1)} %refs_7_.1, ...), custom_call_target="tpu_custom_call" | custom-call | tf_op jit(solution)/shard_map/pallas_call | solution.py:140
  18.9 1.6 %collective-permute-start = (bf16[2048,128]{1,0:T(8,128)(2,1)}, bf16[2048,128]{1,0:T(8,128)(2,1)S(1)}, u32[]{:S(2)}, u32[]{:S(2)}) collective-permute-start(bf16[2048,128]{1,0:T(8,128)(2,1)} %get-tuple-element.38), channel_id=1, source_target_pairs={{0,2},{1,3},{2,4},{3,5},{4,6},{5,7},{6,0},{7,1},{8,10},{9,11},{10,... | collective-permute-start | bytes 1572872 | tf_op jit(solution)/shard_map/ppermute | solution.py:47
  20.5 1.7 %collective-permute-start.1 = (bf16[2048,128]{1,0:T(8,128)(2,1)}, bf16[2048,128]{1,0:T(8,128)(2,1)S(1)}, u32[]{:S(2)}, u32[]{:S(2)}) collective-permute-start(bf16[2048,128]{1,0:T(8,128)(2,1)} %get-tuple-element.39), channel_id=1, source_target_pairs={{0,6},{1,7},{2,0},{3,1},{4,2},{5,3},{6,4},{7,5},{8,14},{9,15},{10,... | collective-permute-start | bytes 1572872 | tf_op jit(solution)/shard_map/ppermute | solution.py:47
  22.1 11.3 %collective-permute-done.refs_1_ = bf16[2048,128]{1,0:T(8,128)(2,1)S(1)} collective-permute-done((bf16[2048,128]{1,0:T(8,128)(2,1)}, bf16[2048,128]{1,0:T(8,128)(2,1)S(1)}, u32[]{:S(2)}, u32[]{:S(2)}) %collective-permute-start) | collective-permute-done | bytes 524320 | tf_op jit(solution)/shard_map/ppermute | solution.py:47
  33.5 0.0 collective-permute-done.1.refs_2_
  33.5 1.6 %collective-permute-start.2 = (bf16[1024,128]{1,0:T(8,128)(2,1)S(1)}, bf16[1024,128]{1,0:T(8,128)(2,1)S(1)}, u32[]{:S(2)}, u32[]{:S(2)}) collective-permute-start(bf16[1024,128]{1,0:T(8,128)(2,1)S(1)} %slice.24), channel_id=1, source_target_pairs={{0,2},{1,3},{2,4},{3,5},{4,6},{5,7},{6,0},{7,1},{8,10},{9,11},{10,... | collective-permute-start | bytes 786440 | tf_op jit(solution)/shard_map/ppermute | solution.py:47
  35.2 0.0 collective-permute-start.6
  35.2 1.8 %collective-permute-start.3 = (bf16[512,128]{1,0:T(8,128)(2,1)}, bf16[512,128]{1,0:T(8,128)(2,1)S(1)}, u32[]{:S(2)}, u32[]{:S(2)}) collective-permute-start(bf16[512,128]{1,0:T(8,128)(2,1)} %get-tuple-element.41), channel_id=1, source_target_pairs={{0,1},{1,0},{2,3},{3,2},{4,5},{5,4},{6,7},{7,6},{8,9},{9,8},{10,11... | collective-permute-start | bytes 393224 | tf_op jit(solution)/shard_map/ppermute | solution.py:47
  37.0 0.0 collective-permute-start.4
  37.0 3.0 %collective-permute-start.5 = (bf16[512,128]{1,0:T(8,128)(2,1)}, bf16[512,128]{1,0:T(8,128)(2,1)S(1)}, u32[]{:S(2)}, u32[]{:S(2)}) collective-permute-start(bf16[512,128]{1,0:T(8,128)(2,1)} %get-tuple-element.43), channel_id=1, source_target_pairs={{0,7},{1,6},{2,1},{3,0},{4,3},{5,2},{6,5},{7,4},{8,15},{9,14},{10,... | collective-permute-start | bytes 393224 | tf_op jit(solution)/shard_map/ppermute | solution.py:47
  39.9 1.5 %collective-permute-done.2.refs_3_ = bf16[1024,128]{1,0:T(8,128)(2,1)S(1)} collective-permute-done((bf16[1024,128]{1,0:T(8,128)(2,1)S(1)}, bf16[1024,128]{1,0:T(8,128)(2,1)S(1)}, u32[]{:S(2)}, u32[]{:S(2)}) %collective-permute-start.2) | collective-permute-done | bytes 262176 | tf_op jit(solution)/shard_map/ppermute | solution.py:47
  41.5 2.3 %collective-permute-done.6.refs_7_.refs_4_ = bf16[1024,128]{1,0:T(8,128)(2,1)S(1)} collective-permute-done((bf16[1024,128]{1,0:T(8,128)(2,1)S(1)}, bf16[1024,128]{1,0:T(8,128)(2,1)S(1)}, u32[]{:S(2)}, u32[]{:S(2)}) %collective-permute-start.6) | collective-permute-done | bytes 262176 | tf_op jit(solution)/shard_map/ppermute | solution.py:47
  43.8 0.7 copy-done.16
  44.5 2.5 %shard_map.142.cots = bf16[4096,128]{1,0:T(8,128)(2,1)} custom-call(bf16[1024,128]{1,0:T(8,128)(2,1)} %bitcast.23, bf16[2048,128]{1,0:T(8,128)(2,1)} %copy-done.13, bf16[2048,128]{1,0:T(8,128)(2,1)} %copy-done.14, bf16[1024,128]{1,0:T(8,128)(2,1)} %copy-done.15, bf16[1024,128]{1,0:T(8,128)(2,1)} %copy-done.16), custom_call_target="tpu_custom_call" | custom-call | tf_op jit(solution)/shard_map/pallas_call | solution.py:104
  47.0 0.0 collective-permute-done.3.refs_4_
  47.0 0.0 collective-permute-done.5.refs_6_
  47.0 0.7 copy-done.19
  47.7 0.6 copy-done.20
  48.3 0.0 copy-start.1
  48.3 0.0 copy-start.10
  48.3 0.0 copy-start.11
  48.3 0.0 copy-start.12
  48.4 2.7 %shard_map.141.refs_0_ = bf16[4096,128]{1,0:T(8,128)(2,1)} custom-call(bf16[512,128]{1,0:T(8,128)(2,1)} %get-tuple-element.37.refs_0_, bf16[2048,128]{1,0:T(8,128)(2,1)} %copy-done.13, bf16[2048,128]{1,0:T(8,128)(2,1)} %copy-done.14, bf16[1024,128]{1,0:T(8,128)(2,1)} %copy-done.15, bf16[512,128]{1,0:T(8,128)(2,1)} %copy-done.18, ...), custom_call_target="tpu_custom_call" | custom-call | tf_op jit(solution)/shard_map/pallas_call | solution.py:104
  51.0 0.0 all-to-all-done.gathered_ref
  51.0 0.0 collective-permute-start.13
  51.0 0.6 collective-permute-start.12
  51.6 1.5 %collective-permute-start.11 = (bf16[4096,128]{1,0:T(8,128)(2,1)}, bf16[4096,128]{1,0:T(8,128)(2,1)}, u32[]{:S(2)}, u32[]{:S(2)}) collective-permute-start(bf16[4096,128]{1,0:T(8,128)(2,1)} %shard_map.141.refs_0_), channel_id=1, source_target_pairs={{0,8},{8,16},{16,24},{24,0},{32,40},{40,48},{48,56},{56,32},{64,72... | collective-permute-start | bytes 3145736 | tf_op jit(solution)/shard_map/ppermute | solution.py:52
  53.1 0.2 select_reduce_fusion.slots
  53.4 1.2 %shard_map.143 = (f32[512,128]{1,0:T(8,128)S(1)}, bf16[512,128]{1,0:T(8,128)(2,1)S(1)}, f32[512,1]{1,0:T(8,128)S(1)}) custom-call(s32[4]{0:T(128)S(1)} %select_reduce_fusion.slots, s32[4]{0:T(128)S(1)} %copy-done.12, s32[4]{0:T(128)S(1)} %copy-done.10, f32[4]{0:T(128)S(1)} %copy-done.11, bf16[32,16,1280]{2,1,0:T(8,128)(2,1)S(1)} %all-to-all-done.gathered_ref, ...), custom_call_target="tpu_custom_call" | custom-call | flops 67108864 | bytes 1048576 | tf_op jit(solution)/shard_map/pallas_call | solution.py:370
  54.6 0.7 copy-done.8
  55.3 0.0 collective-permute-start.7
  55.3 1.5 %collective-permute-done.7 = f32[512,128]{1,0:T(8,128)S(1)} collective-permute-done((f32[512,128]{1,0:T(8,128)S(1)}, f32[512,128]{1,0:T(8,128)S(1)}, u32[]{:S(2)}, u32[]{:S(2)}) %collective-permute-start.7) | collective-permute-done | bytes 262176 | tf_op jit(solution)/shard_map/ppermute | solution.py:47
  56.9 3.0 %collective-permute-start.10 = (bf16[512,128]{1,0:T(8,128)(2,1)S(1)}, bf16[512,128]{1,0:T(8,128)(2,1)S(1)}, u32[]{:S(2)}, u32[]{:S(2)}) collective-permute-start(bf16[512,128]{1,0:T(8,128)(2,1)S(1)} %add_convert_fusion.own), channel_id=1, source_target_pairs={{0,4},{1,5},{2,6},{3,7},{4,0},{5,1},{6,2},{7,3},{8,12},{9,13},{10,... | collective-permute-start | bytes 393224 | tf_op jit(solution)/shard_map/ppermute | solution.py:47
  59.9 1.2 %collective-permute-start.9 = (bf16[512,128]{1,0:T(8,128)(2,1)S(1)}, bf16[512,128]{1,0:T(8,128)(2,1)S(1)}, u32[]{:S(2)}, u32[]{:S(2)}) collective-permute-start(bf16[512,128]{1,0:T(8,128)(2,1)S(1)} %add_convert_fusion.own), channel_id=1, source_target_pairs={{0,6},{1,7},{2,0},{3,1},{4,2},{5,3},{6,4},{7,5},{8,14},{9,15},{10,... | collective-permute-start | bytes 393224 | tf_op jit(solution)/shard_map/ppermute | solution.py:47
  61.1 2.9 %collective-permute-done.10.third = bf16[512,128]{1,0:T(8,128)(2,1)S(1)} collective-permute-done((bf16[512,128]{1,0:T(8,128)(2,1)S(1)}, bf16[512,128]{1,0:T(8,128)(2,1)S(1)}, u32[]{:S(2)}, u32[]{:S(2)}) %collective-permute-start.10) | collective-permute-done | bytes 131104 | tf_op jit(solution)/shard_map/ppermute | solution.py:47
  64.0 2.3 %collective-permute-start.8 = (bf16[512,128]{1,0:T(8,128)(2,1)S(1)}, bf16[512,128]{1,0:T(8,128)(2,1)S(1)}, u32[]{:S(2)}, u32[]{:S(2)}) collective-permute-start(bf16[512,128]{1,0:T(8,128)(2,1)S(1)} %add_convert_fusion.own), channel_id=1, source_target_pairs={{0,2},{1,3},{2,4},{3,5},{4,6},{5,7},{6,0},{7,1},{8,10},{9,11},{10,... | collective-permute-start | bytes 393224 | tf_op jit(solution)/shard_map/ppermute | solution.py:47
  66.3 2.1 %constant_dynamic-slice_fusion = (bf16[2,256,128]{2,1,0:T(8,128)(2,1)}, bf16[2,256,128]{2,1,0:T(8,128)(2,1)}, bf16[2,256,128]{2,1,0:T(8,128)(2,1)S(1)}, bf16[2,2...) fusion(bf16[2,8192,128]{2,1,0:T(8,128)(2,1)} %refs_7_.1, ...), kind=kLoop, calls=%fused_computation.10 | loop fusion | bytes 2097184 | tf_op jit(solution)/shard_map/dynamic_slice | solution.py:362
  68.4 0.0 collective-permute-done.9.second
  68.4 1.8 %collective-permute-done.8.first = bf16[512,128]{1,0:T(8,128)(2,1)S(1)} collective-permute-done((bf16[512,128]{1,0:T(8,128)(2,1)S(1)}, bf16[512,128]{1,0:T(8,128)(2,1)S(1)}, u32[]{:S(2)}, u32[]{:S(2)}) %collective-permute-start.8) | collective-permute-done | bytes 131104 | tf_op jit(solution)/shard_map/ppermute | solution.py:47
  70.2 1.1 shard_map.144
  71.3 1.1 copy-done.4
  72.4 0.6 copy-done.6
  73.1 3.9 %collective-permute-done.12.refs_2_ = bf16[4096,128]{1,0:T(8,128)(2,1)} collective-permute-done((bf16[4096,128]{1,0:T(8,128)(2,1)}, bf16[4096,128]{1,0:T(8,128)(2,1)}, u32[]{:S(2)}, u32[]{:S(2)}) %collective-permute-start.12) | collective-permute-done | bytes 1048608 | tf_op jit(solution)/shard_map/ppermute | solution.py:52
  76.9 1.2 %collective-permute-done.11.refs_1_ = bf16[4096,128]{1,0:T(8,128)(2,1)} collective-permute-done((bf16[4096,128]{1,0:T(8,128)(2,1)}, bf16[4096,128]{1,0:T(8,128)(2,1)}, u32[]{:S(2)}, u32[]{:S(2)}) %collective-permute-start.11) | collective-permute-done | bytes 1048608 | tf_op jit(solution)/shard_map/ppermute | solution.py:52
  78.2 9.9 %all-to-all-start.1 = ((bf16[32,16,1152]{2,1,0:T(8,128)(2,1)}), bf16[32,16,1152]{2,1,0:T(8,128)(2,1)S(1)}, u32[]{:S(2)}, u32[]{:S(2)}) async-start(bf16[32,16,1152]{2,1,0:T(8,128)(2,1)} %copy-done.4), calls=%async_computation.1 | async-start | bytes 2359296 | tf_op jit(solution)/shard_map/all_to_all | solution.py:400
  88.0 1.2 %collective-permute-start.14 = (bf16[1024,128]{1,0:T(8,128)(2,1)S(1)}, bf16[1024,128]{1,0:T(8,128)(2,1)S(1)}, u32[]{:S(2)}, u32[]{:S(2)}) collective-permute-start(bf16[1024,128]{1,0:T(8,128)(2,1)S(1)} %get-tuple-element.61), channel_id=1, source_target_pairs={{0,2},{1,3},{2,4},{3,5},{4,6},{5,7},{6,0},{7,1},{8,10},{9,11},{10,... | collective-permute-start | bytes 786440 | tf_op jit(solution)/shard_map/ppermute | solution.py:47
  89.3 2.1 %collective-permute-start.15 = (bf16[1024,128]{1,0:T(8,128)(2,1)S(1)}, bf16[1024,128]{1,0:T(8,128)(2,1)S(1)}, u32[]{:S(2)}, u32[]{:S(2)}) collective-permute-start(bf16[1024,128]{1,0:T(8,128)(2,1)S(1)} %get-tuple-element.62), channel_id=1, source_target_pairs={{0,6},{1,7},{2,0},{3,1},{4,2},{5,3},{6,4},{7,5},{8,14},{9,15},{10,... | collective-permute-start | bytes 786440 | tf_op jit(solution)/shard_map/ppermute | solution.py:47
  91.4 0.1 collective-permute-start.18
  91.4 2.9 %collective-permute-start.19 = (bf16[512,128]{1,0:T(8,128)(2,1)S(1)}, bf16[512,128]{1,0:T(8,128)(2,1)S(1)}, u32[]{:S(2)}, u32[]{:S(2)}) collective-permute-start(bf16[512,128]{1,0:T(8,128)(2,1)S(1)} %bitcast.32), channel_id=1, source_target_pairs={{0,7},{1,6},{2,1},{3,0},{4,3},{5,2},{6,5},{7,4},{8,15},{9,14},{10,... | collective-permute-start | bytes 393224 | tf_op jit(solution)/shard_map/ppermute | solution.py:47
  94.3 2.8 %collective-permute-done.14.refs_1_ = bf16[1024,128]{1,0:T(8,128)(2,1)S(1)} collective-permute-done((bf16[1024,128]{1,0:T(8,128)(2,1)S(1)}, bf16[1024,128]{1,0:T(8,128)(2,1)S(1)}, u32[]{:S(2)}, u32[]{:S(2)}) %collective-permute-start.14) | collective-permute-done | bytes 262176 | tf_op jit(solution)/shard_map/ppermute | solution.py:47
  97.1 0.3 collective-permute-done.15.refs_2_
  97.4 1.8 %collective-permute-start.16 = (bf16[512,128]{1,0:T(8,128)(2,1)S(1)}, bf16[512,128]{1,0:T(8,128)(2,1)S(1)}, u32[]{:S(2)}, u32[]{:S(2)}) collective-permute-start(bf16[512,128]{1,0:T(8,128)(2,1)S(1)} %slice.26), channel_id=1, source_target_pairs={{0,2},{1,3},{2,4},{3,5},{4,6},{5,7},{6,0},{7,1},{8,10},{9,11},{10,... | collective-permute-start | bytes 393224 | tf_op jit(solution)/shard_map/ppermute | solution.py:47
  99.2 1.2 %copy-done.2 = bf16[4096,128]{1,0:T(8,128)(2,1)S(1)} copy-done((bf16[4096,128]{1,0:T(8,128)(2,1)S(1)}, bf16[4096,128]{1,0:T(8,128)(2,1)}, u32[]{:S(2)}) %copy-start.2) | copy-done | bytes 1048600
  100.5 1.2 %copy-done.3 = bf16[4096,128]{1,0:T(8,128)(2,1)S(1)} copy-done((bf16[4096,128]{1,0:T(8,128)(2,1)S(1)}, bf16[4096,128]{1,0:T(8,128)(2,1)}, u32[]{:S(2)}) %copy-start.3) | copy-done | bytes 1048600
  101.7 0.9 copy-done.7
  102.6 0.9 copy-done.9
  103.5 5.5 %shard_map.145 = (bf16[512,1024]{1,0:T(8,128)(2,1)}, bf16[512,2048]{1,0:T(8,128)(2,1)S(1)}) custom-call(s32[4]{0:T(128)S(1)} %select_reduce_fusion.slots, s32[4]{0:T(128)S(1)} %and_select_fusion.2.quarters, bf16[4096,128]{1,0:T(8,128)(2,1)S(1)} %copy-done.3, bf16[4096,128]{1,0:T(8,128)(2,1)} %collective-permute-done.13.others, ...), custom_call_target="tpu_custom_call" | custom-call | tf_op jit(solution)/shard_map/pallas_call | solution.py:250
  109.1 2.1 %shard_map.146 = bf16[512,1024]{1,0:T(8,128)(2,1)} custom-call(s32[4]{0:T(128)S(1)} %select_reduce_fusion.slots, s32[4]{0:T(128)S(1)} %and_select_fusion.2.quarters, bf16[512,1024]{1,0:T(8,128)(2,1)} %get-tuple-element.58.near_ref, bf16[512,2048]{1,0:T(8,128)(2,1)S(1)} %get-tuple-element.59.weighted, ...), custom_call_target="tpu_custom_call", output_to_operand_aliasing={{}: (2, {})} | custom-call | tf_op jit(solution)/shard_map/pallas_call | solution.py:262
  111.2 7.3 %all-to-all-done.1.terms_ref = bf16[32,16,1152]{2,1,0:T(8,128)(2,1)S(1)} async-done(((bf16[32,16,1152]{2,1,0:T(8,128)(2,1)}), bf16[32,16,1152]{2,1,0:T(8,128)(2,1)S(1)}, u32[]{:S(2)}, u32[]{:S(2)}) %all-to-all-start.1) | async-done | bytes 1179680 | tf_op jit(solution)/shard_map/all_to_all | solution.py:400
  118.5 0.8 shard_map.147
  (54 shorter events, 0.2 us)
Async XLA Ops:
  2.6 11.8 %copy-start.17 = (bf16[512,2,128]{2,1,0:T(2,128)(2,1)S(1)}, bf16[512,2,128]{2,1,0:T(2,128)(2,1)}, u32[]{:S(2)}) copy-start(bf16[512,2,128]{2,1,0:T(2,128)(2,1)} %param.13) | copy-start | bytes 786436
  2.6 12.5 %copy-start.21 = (s32[8,1]{0,1:T(1,128)S(1)}, s32[8,1]{0,1:T(1,128)}, u32[]{:S(2)}) copy-start(s32[8,1]{0,1:T(1,128)} %constant.150) | copy-start | bytes 100
  2.6 12.5 %copy-start.22 = (s32[8,1]{0,1:T(1,128)S(1)}, s32[8,1]{0,1:T(1,128)}, u32[]{:S(2)}) copy-start(s32[8,1]{0,1:T(1,128)} %constant.149) | copy-start | bytes 100
  2.6 48.4 %all-to-all-start = ((bf16[32,16,1280]{2,1,0:T(8,128)(2,1)}), bf16[32,16,1280]{2,1,0:T(8,128)(2,1)S(1)}, u32[]{:S(2)}, u32[]{:S(2)}) async-start(bf16[32,16,1280]{2,1,0:T(8,128)(2,1)} %shard_map.139), calls=%async_computation | async-start | bytes 2621440 | tf_op jit(solution)/shard_map/all_to_all | solution.py:329
  18.9 14.6 %collective-permute-start = (bf16[2048,128]{1,0:T(8,128)(2,1)}, bf16[2048,128]{1,0:T(8,128)(2,1)S(1)}, u32[]{:S(2)}, u32[]{:S(2)}) collective-permute-start(bf16[2048,128]{1,0:T(8,128)(2,1)} %get-tuple-element.38), channel_id=1, source_target_pairs={{0,2},{1,3},{2,4},{3,5},{4,6},{5,7},{6,0},{7,1},{8,10},{9,11},{10,... | collective-permute-start | bytes 1572872 | tf_op jit(solution)/shard_map/ppermute | solution.py:47
  20.5 13.0 %collective-permute-start.1 = (bf16[2048,128]{1,0:T(8,128)(2,1)}, bf16[2048,128]{1,0:T(8,128)(2,1)S(1)}, u32[]{:S(2)}, u32[]{:S(2)}) collective-permute-start(bf16[2048,128]{1,0:T(8,128)(2,1)} %get-tuple-element.39), channel_id=1, source_target_pairs={{0,6},{1,7},{2,0},{3,1},{4,2},{5,3},{6,4},{7,5},{8,14},{9,15},{10,... | collective-permute-start | bytes 1572872 | tf_op jit(solution)/shard_map/ppermute | solution.py:47
  33.5 10.3 %copy-start.13 = (bf16[2048,128]{1,0:T(8,128)(2,1)}, bf16[2048,128]{1,0:T(8,128)(2,1)S(1)}, u32[]{:S(2)}) copy-start(bf16[2048,128]{1,0:T(8,128)(2,1)S(1)} %collective-permute-done.refs_1_) | copy-start | bytes 1572868
  33.5 10.3 %copy-start.14 = (bf16[2048,128]{1,0:T(8,128)(2,1)}, bf16[2048,128]{1,0:T(8,128)(2,1)S(1)}, u32[]{:S(2)}) copy-start(bf16[2048,128]{1,0:T(8,128)(2,1)S(1)} %collective-permute-done.1.refs_2_) | copy-start | bytes 1572868
  33.5 7.9 %collective-permute-start.2 = (bf16[1024,128]{1,0:T(8,128)(2,1)S(1)}, bf16[1024,128]{1,0:T(8,128)(2,1)S(1)}, u32[]{:S(2)}, u32[]{:S(2)}) collective-permute-start(bf16[1024,128]{1,0:T(8,128)(2,1)S(1)} %slice.24), channel_id=1, source_target_pairs={{0,2},{1,3},{2,4},{3,5},{4,6},{5,7},{6,0},{7,1},{8,10},{9,11},{10,... | collective-permute-start | bytes 786440 | tf_op jit(solution)/shard_map/ppermute | solution.py:47
  35.2 8.6 %collective-permute-start.6 = (bf16[1024,128]{1,0:T(8,128)(2,1)S(1)}, bf16[1024,128]{1,0:T(8,128)(2,1)S(1)}, u32[]{:S(2)}, u32[]{:S(2)}) collective-permute-start(bf16[1024,128]{1,0:T(8,128)(2,1)S(1)} %slice.25), channel_id=1, source_target_pairs={{0,7},{1,6},{2,1},{3,0},{4,3},{5,2},{6,5},{7,4},{8,15},{9,14},{10,... | collective-permute-start | bytes 786440 | tf_op jit(solution)/shard_map/ppermute | solution.py:47
  35.2 11.8 %collective-permute-start.3 = (bf16[512,128]{1,0:T(8,128)(2,1)}, bf16[512,128]{1,0:T(8,128)(2,1)S(1)}, u32[]{:S(2)}, u32[]{:S(2)}) collective-permute-start(bf16[512,128]{1,0:T(8,128)(2,1)} %get-tuple-element.41), channel_id=1, source_target_pairs={{0,1},{1,0},{2,3},{3,2},{4,5},{5,4},{6,7},{7,6},{8,9},{9,8},{10,11... | collective-permute-start | bytes 393224 | tf_op jit(solution)/shard_map/ppermute | solution.py:47
  37.0 10.0 %collective-permute-start.4 = (bf16[512,128]{1,0:T(8,128)(2,1)}, bf16[512,128]{1,0:T(8,128)(2,1)S(1)}, u32[]{:S(2)}, u32[]{:S(2)}) collective-permute-start(bf16[512,128]{1,0:T(8,128)(2,1)} %get-tuple-element.42), channel_id=1, source_target_pairs={{0,3},{1,2},{2,5},{3,4},{4,7},{5,6},{6,1},{7,0},{8,11},{9,10},{10,... | collective-permute-start | bytes 393224 | tf_op jit(solution)/shard_map/ppermute | solution.py:47
  37.0 10.0 %collective-permute-start.5 = (bf16[512,128]{1,0:T(8,128)(2,1)}, bf16[512,128]{1,0:T(8,128)(2,1)S(1)}, u32[]{:S(2)}, u32[]{:S(2)}) collective-permute-start(bf16[512,128]{1,0:T(8,128)(2,1)} %get-tuple-element.43), channel_id=1, source_target_pairs={{0,7},{1,6},{2,1},{3,0},{4,3},{5,2},{6,5},{7,4},{8,15},{9,14},{10,... | collective-permute-start | bytes 393224 | tf_op jit(solution)/shard_map/ppermute | solution.py:47
  41.5 2.3 %copy-start.15 = (bf16[1024,128]{1,0:T(8,128)(2,1)}, bf16[1024,128]{1,0:T(8,128)(2,1)S(1)}, u32[]{:S(2)}) copy-start(bf16[1024,128]{1,0:T(8,128)(2,1)S(1)} %collective-permute-done.2.refs_3_) | copy-start | bytes 786436
  43.8 0.7 copy-start.16
  47.0 1.3 %copy-start.18 = (bf16[512,128]{1,0:T(8,128)(2,1)}, bf16[512,128]{1,0:T(8,128)(2,1)S(1)}, u32[]{:S(2)}) copy-start(bf16[512,128]{1,0:T(8,128)(2,1)S(1)} %collective-permute-done.3.refs_4_) | copy-start | bytes 393220
  47.0 0.7 copy-start.19
  47.7 0.6 copy-start.20
  48.3 4.8 %copy-start.23 = (s32[8]{0:T(128)S(1)}, s32[8]{0:T(128)}, u32[]{:S(2)}) copy-start(s32[8]{0:T(128)} %param.17) | copy-start | bytes 100
  48.3 4.8 %copy-start.24 = (s32[4]{0:T(128)S(1)}, s32[4]{0:T(128)}, u32[]{:S(2)}) copy-start(s32[4]{0:T(128)} %param.18) | copy-start | bytes 52
  48.3 5.0 %copy-start = (bf16[512,2,128]{2,0,1:T(8,128)(2,1)S(1)}, bf16[512,2,128]{2,0,1:T(8,128)(2,1)}, u32[]{:S(2)}) copy-start(bf16[512,2,128]{2,0,1:T(8,128)(2,1)} %copy.20) | copy-start | bytes 786436
  48.3 5.0 %copy-start.1 = (bf16[512,1024]{1,0:T(8,128)(2,1)S(1)}, bf16[512,1024]{1,0:T(8,128)(2,1)}, u32[]{:S(2)}) copy-start(bf16[512,1024]{1,0:T(8,128)(2,1)} %x_ref.3) | copy-start | bytes 3145732
  48.3 5.0 %copy-start.10 = (s32[4]{0:T(128)S(1)}, s32[4]{0:T(128)}, u32[]{:S(2)}) copy-start(s32[4]{0:T(128)} %prompt.1) | copy-start | bytes 52
  48.3 5.0 %copy-start.11 = (f32[4]{0:T(128)S(1)}, f32[4]{0:T(128)}, u32[]{:S(2)}) copy-start(f32[4]{0:T(128)} %reward.1) | copy-start | bytes 52
  48.3 5.0 %copy-start.12 = (s32[4]{0:T(128)S(1)}, s32[4]{0:T(128)}, u32[]{:S(2)}) copy-start(s32[4]{0:T(128)} %live.1) | copy-start | bytes 52
  51.0 22.0 %collective-permute-start.13 = (bf16[4096,128]{1,0:T(8,128)(2,1)}, bf16[4096,128]{1,0:T(8,128)(2,1)}, u32[]{:S(2)}, u32[]{:S(2)}) collective-permute-start(bf16[4096,128]{1,0:T(8,128)(2,1)} %shard_map.142.cots), channel_id=1, source_target_pairs={{0,1},{1,0},{2,3},{3,2},{4,5},{5,4},{6,7},{7,6},{8,9},{9,8},{10,11... | collective-permute-start | bytes 3145736 | tf_op jit(solution)/shard_map/ppermute | solution.py:47
  51.0 25.9 %collective-permute-start.12 = (bf16[4096,128]{1,0:T(8,128)(2,1)}, bf16[4096,128]{1,0:T(8,128)(2,1)}, u32[]{:S(2)}, u32[]{:S(2)}) collective-permute-start(bf16[4096,128]{1,0:T(8,128)(2,1)} %shard_map.141.refs_0_), channel_id=1, source_target_pairs={{0,24},{8,0},{16,8},{24,16},{32,56},{40,32},{48,40},{56,48},{64,88... | collective-permute-start | bytes 3145736 | tf_op jit(solution)/shard_map/ppermute | solution.py:52
  51.6 26.6 %collective-permute-start.11 = (bf16[4096,128]{1,0:T(8,128)(2,1)}, bf16[4096,128]{1,0:T(8,128)(2,1)}, u32[]{:S(2)}, u32[]{:S(2)}) collective-permute-start(bf16[4096,128]{1,0:T(8,128)(2,1)} %shard_map.141.refs_0_), channel_id=1, source_target_pairs={{0,8},{8,16},{16,24},{24,0},{32,40},{40,48},{48,56},{56,32},{64,72... | collective-permute-start | bytes 3145736 | tf_op jit(solution)/shard_map/ppermute | solution.py:52
  54.6 0.7 copy-start.8
  55.3 1.5 %collective-permute-start.7 = (f32[512,128]{1,0:T(8,128)S(1)}, f32[512,128]{1,0:T(8,128)S(1)}, u32[]{:S(2)}, u32[]{:S(2)}) collective-permute-start(f32[512,128]{1,0:T(8,128)S(1)} %get-tuple-element.46), channel_id=1, source_target_pairs={{0,1},{1,0},{2,3},{3,2},{4,5},{5,4},{6,7},{7,6},{8,9},{9,8},{10,11... | collective-permute-start | bytes 786440 | tf_op jit(solution)/shard_map/ppermute | solution.py:47
  56.9 7.1 %collective-permute-start.10 = (bf16[512,128]{1,0:T(8,128)(2,1)S(1)}, bf16[512,128]{1,0:T(8,128)(2,1)S(1)}, u32[]{:S(2)}, u32[]{:S(2)}) collective-permute-start(bf16[512,128]{1,0:T(8,128)(2,1)S(1)} %add_convert_fusion.own), channel_id=1, source_target_pairs={{0,4},{1,5},{2,6},{3,7},{4,0},{5,1},{6,2},{7,3},{8,12},{9,13},{10,... | collective-permute-start | bytes 393224 | tf_op jit(solution)/shard_map/ppermute | solution.py:47
  59.9 8.5 %collective-permute-start.9 = (bf16[512,128]{1,0:T(8,128)(2,1)S(1)}, bf16[512,128]{1,0:T(8,128)(2,1)S(1)}, u32[]{:S(2)}, u32[]{:S(2)}) collective-permute-start(bf16[512,128]{1,0:T(8,128)(2,1)S(1)} %add_convert_fusion.own), channel_id=1, source_target_pairs={{0,6},{1,7},{2,0},{3,1},{4,2},{5,3},{6,4},{7,5},{8,14},{9,15},{10,... | collective-permute-start | bytes 393224 | tf_op jit(solution)/shard_map/ppermute | solution.py:47
  64.0 6.2 %collective-permute-start.8 = (bf16[512,128]{1,0:T(8,128)(2,1)S(1)}, bf16[512,128]{1,0:T(8,128)(2,1)S(1)}, u32[]{:S(2)}, u32[]{:S(2)}) collective-permute-start(bf16[512,128]{1,0:T(8,128)(2,1)S(1)} %add_convert_fusion.own), channel_id=1, source_target_pairs={{0,2},{1,3},{2,4},{3,5},{4,6},{5,7},{6,0},{7,1},{8,10},{9,11},{10,... | collective-permute-start | bytes 393224 | tf_op jit(solution)/shard_map/ppermute | solution.py:47
  71.3 1.1 copy-start.4
  72.4 0.6 copy-start.6
  78.2 21.0 %copy-start.25 = (s32[4]{0:T(128)S(1)}, s32[4]{0:T(128)}, u32[]{:S(2)}) copy-start(s32[4]{0:T(128)} %constant.142.clone) | copy-start | bytes 52
  78.2 40.3 %all-to-all-start.1 = ((bf16[32,16,1152]{2,1,0:T(8,128)(2,1)}), bf16[32,16,1152]{2,1,0:T(8,128)(2,1)S(1)}, u32[]{:S(2)}, u32[]{:S(2)}) async-start(bf16[32,16,1152]{2,1,0:T(8,128)(2,1)} %copy-done.4), calls=%async_computation.1 | async-start | bytes 2359296 | tf_op jit(solution)/shard_map/all_to_all | solution.py:400
  88.0 9.0 %collective-permute-start.14 = (bf16[1024,128]{1,0:T(8,128)(2,1)S(1)}, bf16[1024,128]{1,0:T(8,128)(2,1)S(1)}, u32[]{:S(2)}, u32[]{:S(2)}) collective-permute-start(bf16[1024,128]{1,0:T(8,128)(2,1)S(1)} %get-tuple-element.61), channel_id=1, source_target_pairs={{0,2},{1,3},{2,4},{3,5},{4,6},{5,7},{6,0},{7,1},{8,10},{9,11},{10,... | collective-permute-start | bytes 786440 | tf_op jit(solution)/shard_map/ppermute | solution.py:47
  89.3 8.1 %collective-permute-start.15 = (bf16[1024,128]{1,0:T(8,128)(2,1)S(1)}, bf16[1024,128]{1,0:T(8,128)(2,1)S(1)}, u32[]{:S(2)}, u32[]{:S(2)}) collective-permute-start(bf16[1024,128]{1,0:T(8,128)(2,1)S(1)} %get-tuple-element.62), channel_id=1, source_target_pairs={{0,6},{1,7},{2,0},{3,1},{4,2},{5,3},{6,4},{7,5},{8,14},{9,15},{10,... | collective-permute-start | bytes 786440 | tf_op jit(solution)/shard_map/ppermute | solution.py:47
  91.4 17.7 %collective-permute-start.17 = (bf16[512,128]{1,0:T(8,128)(2,1)}, bf16[512,128]{1,0:T(8,128)(2,1)S(1)}, u32[]{:S(2)}, u32[]{:S(2)}) collective-permute-start(bf16[512,128]{1,0:T(8,128)(2,1)} %bitcast.34), channel_id=1, source_target_pairs={{0,1},{1,0},{2,3},{3,2},{4,5},{5,4},{6,7},{7,6},{8,9},{9,8},{10,11... | collective-permute-start | bytes 393224 | tf_op jit(solution)/shard_map/ppermute | solution.py:47
  91.4 17.7 %collective-permute-start.18 = (bf16[512,128]{1,0:T(8,128)(2,1)S(1)}, bf16[512,128]{1,0:T(8,128)(2,1)S(1)}, u32[]{:S(2)}, u32[]{:S(2)}) collective-permute-start(bf16[512,128]{1,0:T(8,128)(2,1)S(1)} %bitcast.33), channel_id=1, source_target_pairs={{0,3},{1,2},{2,5},{3,4},{4,7},{5,6},{6,1},{7,0},{8,11},{9,10},{10,... | collective-permute-start | bytes 393224 | tf_op jit(solution)/shard_map/ppermute | solution.py:47
  91.4 17.6 %collective-permute-start.19 = (bf16[512,128]{1,0:T(8,128)(2,1)S(1)}, bf16[512,128]{1,0:T(8,128)(2,1)S(1)}, u32[]{:S(2)}, u32[]{:S(2)}) collective-permute-start(bf16[512,128]{1,0:T(8,128)(2,1)S(1)} %bitcast.32), channel_id=1, source_target_pairs={{0,7},{1,6},{2,1},{3,0},{4,3},{5,2},{6,5},{7,4},{8,15},{9,14},{10,... | collective-permute-start | bytes 393224 | tf_op jit(solution)/shard_map/ppermute | solution.py:47
  97.4 11.6 %collective-permute-start.16 = (bf16[512,128]{1,0:T(8,128)(2,1)S(1)}, bf16[512,128]{1,0:T(8,128)(2,1)S(1)}, u32[]{:S(2)}, u32[]{:S(2)}) collective-permute-start(bf16[512,128]{1,0:T(8,128)(2,1)S(1)} %slice.26), channel_id=1, source_target_pairs={{0,2},{1,3},{2,4},{3,5},{4,6},{5,7},{6,0},{7,1},{8,10},{9,11},{10,... | collective-permute-start | bytes 393224 | tf_op jit(solution)/shard_map/ppermute | solution.py:47
  99.2 9.8 %collective-permute-start.20 = (bf16[512,128]{1,0:T(8,128)(2,1)S(1)}, bf16[512,128]{1,0:T(8,128)(2,1)S(1)}, u32[]{:S(2)}, u32[]{:S(2)}) collective-permute-start(bf16[512,128]{1,0:T(8,128)(2,1)S(1)} %slice.27), channel_id=1, source_target_pairs={{0,7},{1,6},{2,1},{3,0},{4,3},{5,2},{6,5},{7,4},{8,15},{9,14},{10,... | collective-permute-start | bytes 393224 | tf_op jit(solution)/shard_map/ppermute | solution.py:47
  99.2 1.2 %copy-start.2 = (bf16[4096,128]{1,0:T(8,128)(2,1)S(1)}, bf16[4096,128]{1,0:T(8,128)(2,1)}, u32[]{:S(2)}) copy-start(bf16[4096,128]{1,0:T(8,128)(2,1)} %shard_map.141.refs_0_) | copy-start | bytes 3145732
  100.5 1.2 %copy-start.3 = (bf16[4096,128]{1,0:T(8,128)(2,1)S(1)}, bf16[4096,128]{1,0:T(8,128)(2,1)}, u32[]{:S(2)}) copy-start(bf16[4096,128]{1,0:T(8,128)(2,1)} %shard_map.142.cots) | copy-start | bytes 3145732
  101.7 0.9 copy-start.7
  102.6 0.9 copy-start.9
  103.5 5.5 %copy-start.5 = (bf16[2,256,128]{2,1,0:T(8,128)(2,1)S(1)}, bf16[2,256,128]{2,1,0:T(8,128)(2,1)}, u32[]{:S(2)}) copy-start(bf16[2,256,128]{2,1,0:T(8,128)(2,1)} %get-tuple-element.71) | copy-start | bytes 393220
